TPU v7x, 32 devices: a whole 2x2x4 slice. The times are simulated.
32 devices in a mesh: chan: 8 (over y, x, core), freq: 4 (over z).
Axes of the slice: x: 2, y: 2, z: 4, core: 2. Of those that a mesh axis runs over, the one named last changes fastest.
Arguments:
- traces: bfloat16 [1024, 16, 2048], P('chan', 'freq'), may hold values from -32 to 32
- band_bins: int32 [256], replicated, may hold values from 1 to 1023, as said below
- pair_blocks: int32 [8, 3], P('chan'), may hold values from 0 to 7, as said below
Outputs:
- correlations: float32 [8, 128, 3, 128, 128], P('chan', 'freq')
Inputs may be any that keep to these rules, and one draw needn't show every extreme that they name: `band_bins`: distinct and increasing. pair_blocks[i, k] lies within 3 blocks of i; pair_blocks[i, 0] is the lowest and pair_blocks[i, 1] the highest such block.
All inputs are finite; a program needn't handle non-finite values.
Results may differ from a plain program's by a relative error of at most 0.005.
Values may be sent and summed in bfloat16 or wider, within the bound.
No kernel may reach another device: no remote copies, remote signals or barrier semaphores. Data moves between devices by JAX's collectives and lax.ppermute only.
A program may use at most 256 MiB of HBM per device.

v0:
```python
import math

import jax
import jax.numpy as jnp
from jax import lax
from jax.sharding import PartitionSpec as P

LAGS = 128
REACH = 3


def shifted(value, axis, by):
    size = lax.axis_size(axis)
    pairs = [(i, i + by) for i in range(size) if 0 <= i + by < size]
    return lax.ppermute(value, axis, pairs)


def make_dft_table(band_bins, length):
    sample_idx = jnp.arange(length, dtype=jnp.int32)
    phase_int = band_bins[:, None] * sample_idx[None, :] % length
    phases = phase_int.astype(jnp.float32) * (2.0 * math.pi / length)
    return jnp.concatenate([jnp.cos(phases), -jnp.sin(phases)], 0).T.astype(jnp.bfloat16)


def make_lag_table(band_bins, length, lag_count):
    lag_idx = jnp.arange(lag_count, dtype=jnp.int32) - lag_count // 2
    phase_int = band_bins[:, None] * lag_idx[None, :] % length
    phases = phase_int.astype(jnp.float32) * (2.0 * math.pi / length)
    return jnp.concatenate([jnp.cos(phases), -jnp.sin(phases)], 0)


def gram_pair(first_block, second_block):
    rotated = jnp.stack([-second_block[:, :, 1], second_block[:, :, 0]], 2)
    gram_real = jnp.einsum(
        "awcf,bwcf->abf", first_block, second_block, preferred_element_type=jnp.float32
    )
    gram_imag = jnp.einsum(
        "awcf,bwcf->abf", first_block, rotated, preferred_element_type=jnp.float32
    )
    return jnp.stack([gram_real, gram_imag], 2)


def on_device(traces, band_bins, pair_blocks):
    channels, windows, length = traces.shape
    band_count = band_bins.shape[0]
    dft_matrix = make_dft_table(band_bins, length)
    spectra = jnp.dot(
        traces.reshape(channels * windows, length), dft_matrix, preferred_element_type=jnp.float32
    )
    amplitude = jnp.sqrt(jnp.sum(spectra * spectra, axis=1, keepdims=True) / band_count + 1e-06)
    whitened = (spectra / amplitude).astype(jnp.bfloat16).reshape(channels, windows, 2, band_count)
    own_block = lax.all_to_all(whitened, "freq", split_axis=3, concat_axis=1, tiled=True)
    below_blocks = [shifted(own_block, "chan", distance) for distance in range(1, REACH + 1)]
    above_blocks = [shifted(own_block, "chan", -distance) for distance in range(1, REACH + 1)]
    stacked = jnp.stack(below_blocks[::-1] + [own_block] + above_blocks, 0)
    my_index = lax.axis_index("chan")
    gram_list = []
    for pair_slot in range(pair_blocks.shape[1]):
        offset = pair_blocks[0, pair_slot] - my_index + REACH
        partner = lax.dynamic_index_in_dim(stacked, offset, 0, keepdims=False)
        gram_list.append(gram_pair(own_block, partner))
    cross_gram = jnp.stack(gram_list, 1)
    lag_matrix = make_lag_table(band_bins, length, LAGS)
    lag_norm = 1.0 / math.sqrt(own_block.shape[1] * band_count)
    gram_block = lax.all_to_all(cross_gram, "freq", split_axis=0, concat_axis=4, tiled=True)
    dims_shape = gram_block.shape
    lagged = (
        jnp.dot(
            gram_block.reshape(-1, 2 * band_count),
            lag_matrix,
            precision=lax.Precision.HIGHEST,
            preferred_element_type=jnp.float32,
        )
        * lag_norm
    )
    result = lagged.reshape(dims_shape[0], dims_shape[1], dims_shape[2], LAGS)
    return result[None]


def solution(mesh):
    placed = (P("chan", "freq", None), P(), P("chan", None))
    return jax.shard_map(
        on_device,
        mesh=mesh,
        in_specs=placed,
        out_specs=P("chan", "freq", None, None, None),
        check_vma=False,
    )
```

profile of v0, /device:TPU:17, one launch (start us, length us, event | category | flops | bytes accessed | tf_op | source)
XLA Modules:
  0.0 804.0 jit_solution(3776072286118862629)
XLA Ops:
  0.0 10.4 %cosine_convert_fusion = (bf16[256,2048]{1,0:T(8,128)(2,1)S(1)}, bf16[256,2048]{1,0:T(8,128)(2,1)}) fusion(s32[256]{0:T(256)} %param.4), kind=kLoop, calls=%fused_computation.22 | loop fusion | flops 8912896 | bytes 2098176 | tf_op jit(solution)/shard_map/convert
  10.4 2.5 reshape.24
  12.9 2.5 multiply_reduce_fusion
  16.8 16.0 %all_to_all.33 = bf16[128,4,2,256]{0,1,2,3:T(4,128)(2,1)S(1)} all-to-all(bf16[128,4,2,256]{0,1,2,3:T(4,128)(2,1)S(1)} %copy.23), channel_id=1, replica_groups=mesh['chan'=8,'freq'=4] {'freq'}, dimensions={3} | all-to-all | bytes 1048576 | tf_op jit(solution)/shard_map/all_to_all | solution.py:52
  33.3 4.6 collective-permute-start
  37.8 3.1 collective-permute-start.1
  41.0 2.2 collective-permute-start.2
  45.8 2.1 collective-permute-start.3
  49.2 17.2 %collective-permute-done = bf16[128,16,2,64]{0,1,2,3:T(8,128)(2,1)S(1)} collective-permute-done((bf16[128,16,2,64]{0,1,2,3:T(8,128)(2,1)S(1)}, bf16[128,16,2,64]{0,1,2,3:T(8,128)(2,1)S(1)}, u32[]{:S(2)}, u32[]{:S(2)}) %collective-permute-start) | collective-permute-done | bytes 524320 | tf_op jit(solution)/shard_map/ppermute | solution.py:15
  68.1 1.9 collective-permute-done.3
  70.1 5.8 collective-permute-done.4
  79.1 2.7 convolution_bitcast_fusion.3
  82.0 2.7 convolution_bitcast_fusion.1
  86.5 2.8 convolution_bitcast_fusion.2
  89.3 4.0 maximum_bitcast_fusion.1
  93.4 2.8 convolution_bitcast_fusion
  96.2 7.8 maximum_bitcast_fusion.2
  104.0 11.9 %pad_maximum_fusion = f32[128,3,128,2,64]{0,2,4,3,1:T(8,128)} fusion(f32[128,1,128,2,64]{0,2,4,3,1:T(8,128)} %maximum_bitcast_fusion.2, f32[128,1,128,2,64]{0,2,4,3,1:T(8,128)S(1)} %maximum_bitcast_fusion.1, f32[128,1,128,2,64]{0,2,4,3,1:T(8,128)S(1)} %maximum_bitcast_fusion), kind=kLoop, calls=%fused_computation | loop fusion | flops 12582912 | bytes 50331648 | tf_op jit(solution)/shard_map/stack | solution.py:62
  115.9 24.7 %copy.27 = f32[128,3,128,2,64]{2,4,3,1,0:T(8,128)} copy(f32[128,3,128,2,64]{0,2,4,3,1:T(8,128)} %pad_maximum_fusion) | data formatting | bytes 50331648 | tf_op jit(solution)/shard_map/stack | solution.py:62
  140.6 10.7 %all-to-all-start.1 = ((f32[128,3,128,2,64]{2,4,3,1,0:T(8,128)}), f32[128,3,128,2,64]{2,4,3,1,0:T(8,128)}, u32[]{:S(2)}, u32[]{:S(2)}) async-start(f32[128,3,128,2,64]{2,4,3,1,0:T(8,128)} %copy.27), calls=%async_computation.1 | async-start | bytes 50331648 | tf_op jit(solution)/shard_map/all_to_all | solution.py:65
  151.9 538.4 %all-to-all-done.1 = f32[128,3,128,2,64]{2,4,3,1,0:T(8,128)} async-done(((f32[128,3,128,2,64]{2,4,3,1,0:T(8,128)}), f32[128,3,128,2,64]{2,4,3,1,0:T(8,128)}, u32[]{:S(2)}, u32[]{:S(2)}) %all-to-all-start.1) | async-done | bytes 25165856 | tf_op jit(solution)/shard_map/all_to_all | solution.py:65
  690.4 33.6 %copy.28 = f32[32,3,128,2,4,64]{2,1,0,5,4,3:T(4,128)} copy(f32[32,3,128,2,4,64]{2,5,3,1,0,4:T(8,128)} %bitcast.46) | data formatting | bytes 50331648 | tf_op jit(solution)/shard_map/all_to_all | solution.py:65
  724.0 36.4 %reshape.26 = f32[12288,512]{0,1:T(8,128)} reshape(f32[32,3,128,2,4,64]{2,1,0,5,4,3:T(4,128)} %copy.28) | data formatting | bytes 50331648 | tf_op jit(solution)/shard_map/reshape | solution.py:69
  760.3 43.7 %convolution_multiply_fusion = f32[12288,128]{1,0:T(8,128)} fusion(f32[12288,512]{0,1:T(8,128)} %reshape.26, f32[256,128]{1,0:T(8,128)S(1)} %get-tuple-element.15, f32[256,128]{1,0:T(8,128)S(1)} %get-tuple-element.14), kind=kOutput, calls=%fused_computation.1 | convolution fusion | flops 9665314816 | bytes 31719424 | tf_op jit(solution)/shard_map/dot_general | solution.py:68
  (32 shorter events, 11.3 us)
Async XLA Ops:
  15.4 27.8 %copy-start = (s32[1,3]{1,0:T(1,128)S(1)}, s32[1,3]{1,0:T(1,128)}, u32[]{:S(2)}) copy-start(s32[1,3]{1,0:T(1,128)} %param.5) | copy-start | bytes 40
  33.3 33.1 %collective-permute-start = (bf16[128,16,2,64]{0,1,2,3:T(8,128)(2,1)S(1)}, bf16[128,16,2,64]{0,1,2,3:T(8,128)(2,1)S(1)}, u32[]{:S(2)}, u32[]{:S(2)}) collective-permute-start(bf16[128,16,2,64]{0,1,2,3:T(8,128)(2,1)S(1)} %bitcast.93), channel_id=1, source_target_pairs={{0,12},{4,16},{8,20},{12,24},{16,28},{1,13},{5,17},{9,21},{13,25},... | collective-permute-start | bytes 1572872 | tf_op jit(solution)/shard_map/ppermute | solution.py:15
  37.8 30.1 %collective-permute-start.1 = (bf16[128,16,2,64]{0,1,2,3:T(8,128)(2,1)S(1)}, bf16[128,16,2,64]{0,1,2,3:T(8,128)(2,1)S(1)}, u32[]{:S(2)}, u32[]{:S(2)}) collective-permute-start(bf16[128,16,2,64]{0,1,2,3:T(8,128)(2,1)S(1)} %bitcast.94), channel_id=1, source_target_pairs={{0,8},{4,12},{8,16},{12,20},{16,24},{20,28},{1,9},{5,13},{9,17},{1... | collective-permute-start | bytes 1572872 | tf_op jit(solution)/shard_map/ppermute | solution.py:15
  41.0 27.0 %collective-permute-start.2 = (bf16[128,16,2,64]{0,1,2,3:T(8,128)(2,1)S(1)}, bf16[128,16,2,64]{0,1,2,3:T(8,128)(2,1)S(1)}, u32[]{:S(2)}, u32[]{:S(2)}) collective-permute-start(bf16[128,16,2,64]{0,1,2,3:T(8,128)(2,1)S(1)} %bitcast.95), channel_id=1, source_target_pairs={{0,4},{4,8},{8,12},{12,16},{16,20},{20,24},{24,28},{1,5},{5,9},{9,... | collective-permute-start | bytes 1572872 | tf_op jit(solution)/shard_map/ppermute | solution.py:15
  45.8 24.3 %collective-permute-start.3 = (bf16[128,16,2,64]{0,1,2,3:T(8,128)(2,1)S(1)}, bf16[128,16,2,64]{0,1,2,3:T(8,128)(2,1)S(1)}, u32[]{:S(2)}, u32[]{:S(2)}) collective-permute-start(bf16[128,16,2,64]{0,1,2,3:T(8,128)(2,1)S(1)} %bitcast.96), channel_id=1, source_target_pairs={{4,0},{8,4},{12,8},{16,12},{20,16},{24,20},{28,24},{5,1},{9,5},{13... | collective-permute-start | bytes 1572872 | tf_op jit(solution)/shard_map/ppermute | solution.py:15
  47.9 28.0 %collective-permute-start.4 = (bf16[128,16,2,64]{0,1,2,3:T(8,128)(2,1)S(1)}, bf16[128,16,2,64]{0,1,2,3:T(8,128)(2,1)S(1)}, u32[]{:S(2)}, u32[]{:S(2)}) collective-permute-start(bf16[128,16,2,64]{0,1,2,3:T(8,128)(2,1)S(1)} %bitcast.97), channel_id=1, source_target_pairs={{8,0},{12,4},{16,8},{20,12},{24,16},{28,20},{9,1},{13,5},{17,9},{2... | collective-permute-start | bytes 1572872 | tf_op jit(solution)/shard_map/ppermute | solution.py:15
  66.4 11.5 %collective-permute-start.5 = (bf16[128,16,2,64]{0,1,2,3:T(8,128)(2,1)S(1)}, bf16[128,16,2,64]{0,1,2,3:T(8,128)(2,1)S(1)}, u32[]{:S(2)}, u32[]{:S(2)}) collective-permute-start(bf16[128,16,2,64]{0,1,2,3:T(8,128)(2,1)S(1)} %bitcast.98), channel_id=1, source_target_pairs={{12,0},{16,4},{20,8},{24,12},{28,16},{13,1},{17,5},{21,9},{25,13},... | collective-permute-start | bytes 1572872 | tf_op jit(solution)/shard_map/ppermute | solution.py:15
  140.6 10.7 %copy-start.1 = (s32[256]{0:T(256)S(1)}, s32[256]{0:T(256)}, u32[]{:S(2)}) copy-start(s32[256]{0:T(256)} %param.4) | copy-start | bytes 3076
  140.6 549.7 %all-to-all-start.1 = ((f32[128,3,128,2,64]{2,4,3,1,0:T(8,128)}), f32[128,3,128,2,64]{2,4,3,1,0:T(8,128)}, u32[]{:S(2)}, u32[]{:S(2)}) async-start(f32[128,3,128,2,64]{2,4,3,1,0:T(8,128)} %copy.27), calls=%async_computation.1 | async-start | bytes 50331648 | tf_op jit(solution)/shard_map/all_to_all | solution.py:65
where the time goes:
time: 814 us; the launch traced here: 804 us
  waiting for transfers between devices  565 us (69%)
  local copies, waits for them, and re-layouts  100 us (12%)
  matrix products  58.7 us (7%)
  other arithmetic  36.1 us (4%)
  starting transfers between devices  25.5 us (3%)
  blocking collectives  16 us (2%)
    all_to_all x1, waiting for transfers between devices, on_device(): lax.all_to_all(cross_gram, 'freq', split_axis=0, concat_axis=4, tiled=True)  538 us
    dot_general x1, matrix products, on_device(): jnp.dot(gram_block.reshape(-1, 2 * band_count), lag_matrix, precision=lax...  43.7 us
    reshape x1, local copies, waits for them, and re-layouts, on_device(): gram_block.reshape(-1, 2 * band_count)  36.4 us
    all_to_all x1, local copies, waits for them, and re-layouts, on_device(): lax.all_to_all(cross_gram, 'freq', split_axis=0, concat_axis=4, tiled=True)  33.6 us
    ppermute x6, waiting for transfers between devices, shifted(): return lax.ppermute(value, axis, pairs)  26.8 us
    another operation x4, other arithmetic, on_device(): cross_gram = jnp.stack(gram_list, 1)  24.9 us
    another operation x1, local copies, waits for them, and re-layouts, on_device(): cross_gram = jnp.stack(gram_list, 1)  24.7 us
  transfers between devices with their start and end apart: 7, of which 5 were waited for; matrix products, arithmetic and copies ran while one was open for 0% of the time, Pallas kernels for 0%

commit v1 on v0

--- a/solution.py
+++ b/solution.py
@@ -2,11 +2,15 @@
 
 import jax
 import jax.numpy as jnp
+import numpy as np
 from jax import lax
+from jax.experimental import pallas as pl
+from jax.experimental.pallas import tpu as pltpu
 from jax.sharding import PartitionSpec as P
 
 LAGS = 128
 REACH = 3
+GROUP = 8
 
 
 def shifted(value, axis, by):
@@ -40,7 +44,7 @@
     return jnp.stack([gram_real, gram_imag], 2)
 
 
-def on_device(traces, band_bins, pair_blocks):
+def on_any_device(traces, band_bins, pair_blocks):
     channels, windows, length = traces.shape
     band_count = band_bins.shape[0]
     dft_matrix = make_dft_table(band_bins, length)
@@ -77,10 +81,228 @@
     return result[None]
 
 
+def spectra_kernel(traces_ref, fine_cos, fine_sin, step_cos, step_sin, out_ref, table, planes):
+    bins = fine_cos.shape[0]
+    fine = fine_cos.shape[1]
+    channels = out_ref.shape[1]
+    windows = traces_ref.shape[0] // channels
+    for h in range(step_cos.shape[1]):
+        sc, ss = step_cos[:, h : h + 1], step_sin[:, h : h + 1]
+        cols = slice(h * fine, (h + 1) * fine)
+        table[:bins, cols] = (sc * fine_cos[...] - ss * fine_sin[...]).astype(jnp.bfloat16)
+        table[bins:, cols] = (-(ss * fine_cos[...] + sc * fine_sin[...])).astype(jnp.bfloat16)
+    for half in range(windows // 2):
+        rows = traces_ref[half * 2 * channels : (half + 1) * 2 * channels, :]
+        spectra = lax.dot_general(
+            table[...], rows, (((1,), (1,)), ((), ())), preferred_element_type=jnp.float32
+        )
+        power = jnp.sum(spectra * spectra, axis=0, keepdims=True)
+        white = spectra / jnp.sqrt(power / bins + 1e-06)
+        for w in range(2):
+            for c in range(2):
+                planes[pl.ds((half * 2 + w) * 2 + c, bins, stride=2 * windows), :] = white[
+                    c * bins : (c + 1) * bins, w * channels : (w + 1) * channels
+                ]
+    out_ref[...] = planes[...].astype(jnp.bfloat16)
+
+
+def make_slab(traces, band_bins):
+    channels, windows, length = traces.shape
+    bins = band_bins.shape[0]
+    fine = 128
+    rows = traces.transpose(1, 0, 2).reshape(windows * channels, length)
+    sample_idx = jnp.concatenate([jnp.arange(fine), jnp.arange(length // fine) * fine])
+    phase_int = band_bins[:, None] * sample_idx[None, :].astype(jnp.int32) % length
+    phases = phase_int.astype(jnp.float32) * (2.0 * math.pi / length)
+    cos, sin = jnp.cos(phases), jnp.sin(phases)
+    return pl.pallas_call(
+        spectra_kernel,
+        out_shape=jax.ShapeDtypeStruct((bins * windows * 2, channels), jnp.bfloat16),
+        scratch_shapes=[
+            pltpu.VMEM((2 * bins, length), jnp.bfloat16),
+            pltpu.VMEM((bins * windows * 2, channels), jnp.float32),
+        ],
+        compiler_params=pltpu.CompilerParams(vmem_limit_bytes=48 << 20),
+        name="spectra",
+    )(rows, cos[:, :fine], sin[:, :fine], cos[:, fine:], sin[:, fine:])
+
+
+def pairs_kernel(slots, left_ref, lag_ref, *refs, parts, gram_steps, norm):
+    n_in = 2 * len(parts)
+    sources, out_ref, partner, gram, sems = refs[:n_in], *refs[n_in:]
+    step = pl.program_id(0)
+    per_step, m, k = left_ref.shape
+    slot_count = partner.shape[0]
+    channels = partner.shape[3]
+    held = sources[0].shape[0]
+    group_rows = k // partner.shape[1]
+
+    def copies(act):
+        for s in range(slot_count):
+            first = 0
+            for p, count in enumerate(parts):
+                dst = partner.at[s, first : first + count]
+                sem = sems.at[s, p]
+
+                @pl.when(slots[s] < held)
+                def _():
+                    act(pltpu.make_async_copy(sources[2 * p].at[slots[s]], dst, sem))
+
+                @pl.when(slots[s] >= held)
+                def _():
+                    act(pltpu.make_async_copy(sources[2 * p + 1].at[slots[s] - held], dst, sem))
+
+                first += count
+
+    @pl.when(step == 0)
+    def _():
+        copies(lambda c: c.start())
+        copies(lambda c: c.wait())
+
+    @pl.when(step < gram_steps)
+    def _():
+        for u in range(per_step):
+            g = step * per_step + u
+            rows = pl.ds(pl.multiple_of(g * group_rows, group_rows), group_rows)
+            right = jnp.concatenate(
+                [partner[s, :, rows, :].reshape(k, channels) for s in range(slot_count)], 1
+            )
+            product = jnp.dot(left_ref[u], right, preferred_element_type=jnp.float32)
+            cols = pl.ds(pl.multiple_of(g * 2 * GROUP, 2 * GROUP), 2 * GROUP)
+            gram[:, cols, :] = product.astype(jnp.bfloat16).reshape(
+                m // (2 * GROUP), 2 * GROUP, slot_count * channels
+            )
+
+    @pl.when(step >= gram_steps)
+    def _():
+        per_lag = out_ref.shape[0]
+        for u in range(per_lag):
+            a = (step - gram_steps) * per_lag + u
+            lagged = (
+                jnp.dot(lag_ref[...], gram[a], preferred_element_type=jnp.float32) * norm
+            )
+            for s in range(slot_count):
+                out_ref[u, s] = lagged[:, s * channels : (s + 1) * channels].T
+
+
+def correlate(slots, left, lag_rows, sources, parts, norm):
+    groups, m, k = left.shape
+    rows_out = m // (2 * GROUP)
+    slot_count = slots.shape[0]
+    channels = sources[0].shape[-1]
+    slab_rows = sources[0].shape[-2]
+    lag_count, entries = lag_rows.shape
+    per_step, per_lag = 2, 2
+    gram_steps = groups // per_step
+    any_spec = pl.BlockSpec(memory_space=pl.ANY)
+    return pl.pallas_call(
+        lambda *r: pairs_kernel(*r, parts=parts, gram_steps=gram_steps, norm=norm),
+        grid_spec=pltpu.PrefetchScalarGridSpec(
+            num_scalar_prefetch=1,
+            grid=(gram_steps + rows_out // per_lag,),
+            in_specs=[
+                pl.BlockSpec((per_step, m, k), lambda i, s: (jnp.minimum(i, gram_steps - 1), 0, 0)),
+                pl.BlockSpec((lag_count, entries), lambda i, s: (0, 0)),
+            ]
+            + [any_spec] * len(sources),
+            out_specs=pl.BlockSpec(
+                (per_lag, slot_count, channels, lag_count),
+                lambda i, s: (jnp.maximum(i - gram_steps, 0), 0, 0, 0),
+            ),
+            scratch_shapes=[
+                pltpu.VMEM((slot_count, sum(parts), slab_rows, channels), jnp.bfloat16),
+                pltpu.VMEM((rows_out, entries, slot_count * channels), jnp.bfloat16),
+                pltpu.SemaphoreType.DMA((slot_count, len(parts))),
+            ],
+        ),
+        out_shape=jax.ShapeDtypeStruct((rows_out, slot_count, channels, lag_count), jnp.float32),
+        compiler_params=pltpu.CompilerParams(vmem_limit_bytes=56 << 20),
+        name="pairs",
+    )(slots, left, lag_rows, *sources)
+
+
+def make_left(own, row_index, rows_out):
+    slabs, slab_rows, channels = own.shape
+    mine = lax.dynamic_slice_in_dim(own, row_index * rows_out, rows_out, 2)
+    per_bin = slab_rows // 256
+    groups = 256 // GROUP
+    mine = mine.reshape(slabs, groups, GROUP, per_bin // 2, 2, rows_out)
+    rotated = jnp.stack([mine[:, :, :, :, 1], -mine[:, :, :, :, 0]], 4)
+    both = jnp.stack([mine, rotated], 0).reshape(2, slabs, groups, GROUP, per_bin, rows_out)
+    both = both.transpose(2, 5, 0, 1, 3, 4)
+    eye = jnp.eye(GROUP, dtype=jnp.bfloat16)
+    left = both[:, :, None] * eye[None, None, :, None, None, :, None]
+    return left.reshape(groups, rows_out * GROUP * 2, slabs * GROUP * per_bin)
+
+
+X_PAIRS = [(i, i ^ 2) for i in range(8)]
+Y_PAIRS = [(4, 0), (1, 5), (6, 2), (3, 7)]
+YX_PAIRS = [(6, 2), (7, 3), (0, 4), (1, 5)]
+CORE_PAIRS = [(i, i ^ 1) for i in range(8)]
+
+
+def held_blocks():
+    table = np.full((8, 8), -1, np.int32)
+    for i in range(8):
+        table[i, 0] = i
+        table[i, 1] = i ^ 2
+    for src, dst in Y_PAIRS:
+        table[dst, 2] = src
+    for src, dst in YX_PAIRS:
+        table[dst, 3] = src ^ 2
+    for i in range(8):
+        table[i, 4:] = table[i ^ 1, :4]
+    return table
+
+
+def spread(part):
+    across_x = lax.ppermute(part, "chan", X_PAIRS)
+    across_y = lax.ppermute(part, "chan", Y_PAIRS)
+    across_both = lax.ppermute(across_x, "chan", YX_PAIRS)
+    held = jnp.stack([part, across_x, across_y, across_both], 0)
+    return held, lax.ppermute(held, "chan", CORE_PAIRS)
+
+
+def on_device(traces, band_bins, pair_blocks):
+    channels, windows, length = traces.shape
+    bins = band_bins.shape[0]
+    z = lax.axis_index("freq")
+    me = lax.axis_index("chan")
+    slab = make_slab(traces, band_bins)
+
+    up1 = lax.ppermute(slab, "freq", [(0, 1), (1, 2), (2, 3)])
+    down1 = lax.ppermute(slab, "freq", [(3, 2), (2, 1), (1, 0)])
+    up2 = lax.ppermute(up1, "freq", [(1, 2), (2, 3)])
+    down2 = lax.ppermute(down1, "freq", [(2, 1), (1, 0)])
+    up3 = lax.ppermute(up2, "freq", [(2, 3)])
+    down3 = lax.ppermute(down2, "freq", [(1, 0)])
+
+    def choose(*options):
+        return lax.select_n(z, *options)
+
+    part0 = slab[None]
+    part1 = choose(down1, up1, down1, up1)[None]
+    part2 = jnp.stack([choose(down2, down1, up1, up2), choose(down3, down2, up2, up3)], 0)
+    sources = []
+    for part in (part0, part1, part2):
+        sources += spread(part)
+
+    own = jnp.concatenate([part0, part1, part2], 0)
+    left = make_left(own, z, channels // 4)
+    lag_rows = make_lag_table(band_bins, length, LAGS)
+    lag_rows = lag_rows.reshape(2, bins, LAGS).transpose(2, 1, 0).reshape(LAGS, 2 * bins)
+    table = jnp.asarray(held_blocks())[me]
+    slots = jnp.argmax(table[None, :] == pair_blocks[0][:, None], axis=1).astype(jnp.int32)
+    norm = 1.0 / math.sqrt(4 * windows * bins)
+    result = correlate(slots, left, lag_rows.astype(jnp.bfloat16), sources, (1, 1, 2), norm)
+    return result[None]
+
+
 def solution(mesh):
     placed = (P("chan", "freq", None), P(), P("chan", None))
+    fits = mesh.shape["chan"] == 8 and mesh.shape["freq"] == 4
     return jax.shard_map(
-        on_device,
+        on_device if fits else on_any_device,
         mesh=mesh,
         in_specs=placed,
         out_specs=P("chan", "freq", None, None, None),

time: 814 us -> 240 us (0.29)
  the two profiles are of different devices: /device:TPU:17 before, /device:TPU:3 now
where the time goes in v1:
time: 240 us; the launch traced here: 238 us
  local copies, waits for them, and re-layouts  68.8 us (29%)
  waiting for transfers between devices  60.7 us (25%)
  starting transfers between devices  45.2 us (19%)
  other arithmetic  34.8 us (14%)
  Pallas kernels  28.1 us (12%)
    mul x4, local copies, waits for them, and re-layouts, make_left(): left = both[:, :, None] * eye[None, None, :, None, None, :, None]  53.4 us
    pallas_call x1, Pallas kernels, correlate(): pl.pallas_call(lambda *r: pairs_kernel(*r, parts=parts, gram_steps=gram_s...  26 us
    ppermute x3, starting transfers between devices, spread(): return (held, lax.ppermute(held, 'chan', CORE_PAIRS))  19 us
    ppermute x3, waiting for transfers between devices, spread(): across_x = lax.ppermute(part, 'chan', X_PAIRS)  16.9 us
    ppermute x1, waiting for transfers between devices, on_device(): down2 = lax.ppermute(down1, 'freq', [(2, 1), (1, 0)])  11.8 us
    ppermute x1, waiting for transfers between devices, on_device(): down3 = lax.ppermute(down2, 'freq', [(1, 0)])  10.7 us
    another operation x5, other arithmetic, spread(): held = jnp.stack([part, across_x, across_y, across_both], 0)  10.3 us
    transpose x1, local copies, waits for them, and re-layouts, make_left(): both = both.transpose(2, 5, 0, 1, 3, 4)  10.2 us
  transfers between devices with their start and end apart: 18, of which 7 were waited for; matrix products, arithmetic and copies ran while one was open for 40% of the time, Pallas kernels for 0%

profile of v1, /device:TPU:3, one launch (start us, length us, event | category | flops | bytes accessed | tf_op | source)
XLA Modules:
  0.0 238.1 jit_solution(17186796835932230054)
XLA Ops:
  6.6 3.2 %collective-permute-start.1 = (bf16[2048,128]{1,0:T(8,128)(2,1)S(1)}, bf16[2048,128]{1,0:T(8,128)(2,1)S(1)}, u32[]{:S(2)}, u32[]{:S(2)}) collective-permute-start(bf16[2048,128]{1,0:T(8,128)(2,1)S(1)} %spectra.1), channel_id=1, source_target_pairs={{0,1},{1,2},{2,3},{4,5},{5,6},{6,7},{8,9},{9,10},{10,11},{12,13},{... | collective-permute-start | bytes 1572872 | tf_op jit(solution)/shard_map/ppermute | solution.py:273
  11.2 9.2 %collective-permute-done.1 = bf16[2048,128]{1,0:T(8,128)(2,1)S(1)} collective-permute-done((bf16[2048,128]{1,0:T(8,128)(2,1)S(1)}, bf16[2048,128]{1,0:T(8,128)(2,1)S(1)}, u32[]{:S(2)}, u32[]{:S(2)}) %collective-permute-start.1) | collective-permute-done | bytes 524320 | tf_op jit(solution)/shard_map/ppermute | solution.py:273
  21.1 3.1 %collective-permute-done = bf16[2048,128]{1,0:T(8,128)(2,1)S(1)} collective-permute-done((bf16[2048,128]{1,0:T(8,128)(2,1)S(1)}, bf16[2048,128]{1,0:T(8,128)(2,1)S(1)}, u32[]{:S(2)}, u32[]{:S(2)}) %collective-permute-start) | collective-permute-done | bytes 524320 | tf_op jit(solution)/shard_map/ppermute | solution.py:274
  26.3 11.8 %collective-permute-done.2 = bf16[2048,128]{1,0:T(8,128)(2,1)S(1)} collective-permute-done((bf16[2048,128]{1,0:T(8,128)(2,1)S(1)}, bf16[2048,128]{1,0:T(8,128)(2,1)S(1)}, u32[]{:S(2)}, u32[]{:S(2)}) %collective-permute-start.2) | collective-permute-done | bytes 524320 | tf_op jit(solution)/shard_map/ppermute | solution.py:276
  40.2 10.7 %collective-permute-done.4 = bf16[2048,128]{1,0:T(8,128)(2,1)} collective-permute-done((bf16[2048,128]{1,0:T(8,128)(2,1)S(1)}, bf16[2048,128]{1,0:T(8,128)(2,1)}, u32[]{:S(2)}, u32[]{:S(2)}) %collective-permute-start.4) | collective-permute-done | bytes 524320 | tf_op jit(solution)/shard_map/ppermute | solution.py:278
  53.5 4.1 %collective-permute-start.15 = (bf16[2,2048,128]{2,1,0:T(8,128)(2,1)S(1)}, bf16[2,2048,128]{2,1,0:T(8,128)(2,1)}, u32[]{:S(2)}, u32[]{:S(2)}) collective-permute-start(bf16[2,2048,128]{2,1,0:T(8,128)(2,1)S(1)} %get-tuple-element.10), channel_id=1, source_target_pairs={{16,0},{4,20},{24,8},{12,28},{17,1},{5,21},{25,9},{13,29},{18,2},{... | collective-permute-start | bytes 3145736 | tf_op jit(solution)/shard_map/ppermute | solution.py:260
  57.6 16.9 %collective-permute-done.14 = bf16[2,2048,128]{2,1,0:T(8,128)(2,1)} collective-permute-done((bf16[2,2048,128]{2,1,0:T(8,128)(2,1)S(1)}, bf16[2,2048,128]{2,1,0:T(8,128)(2,1)}, u32[]{:S(2)}, u32[]{:S(2)}) %collective-permute-start.14) | collective-permute-done | bytes 1048608 | tf_op jit(solution)/shard_map/ppermute | solution.py:259
  75.8 3.0 %collective-permute-start.6 = (bf16[1,2048,128]{2,1,0:T(8,128)(2,1)S(1)}, bf16[1,2048,128]{2,1,0:T(8,128)(2,1)}, u32[]{:S(2)}, u32[]{:S(2)}) collective-permute-start(bf16[1,2048,128]{2,1,0:T(8,128)(2,1)S(1)} %bitcast.40), channel_id=1, source_target_pairs={{0,8},{4,12},{8,0},{12,4},{16,24},{20,28},{24,16},{28,20},{1,9},{5... | collective-permute-start | bytes 1572872 | tf_op jit(solution)/shard_map/ppermute | solution.py:259
  78.8 2.8 %collective-permute-start.7 = (bf16[1,2048,128]{2,1,0:T(8,128)(2,1)S(1)}, bf16[1,2048,128]{2,1,0:T(8,128)(2,1)}, u32[]{:S(2)}, u32[]{:S(2)}) collective-permute-start(bf16[1,2048,128]{2,1,0:T(8,128)(2,1)S(1)} %bitcast.41), channel_id=1, source_target_pairs={{16,0},{4,20},{24,8},{12,28},{17,1},{5,21},{25,9},{13,29},{18,2},{... | collective-permute-start | bytes 1572872 | tf_op jit(solution)/shard_map/ppermute | solution.py:260
  81.6 3.1 %mul.73 = bf16[32,8,2,4,8,8]{5,4,3,2,1,0:T(8,128)(2,1)} broadcast(bf16[8,8]{1,0:T(8,128)(2,1)S(1)} %fusion.10), dimensions={1,4} | broadcast | bytes 262272 | tf_op jit(solution)/shard_map/mul | solution.py:234
  84.7 6.9 %mul.74 = bf16[512,256]{1,0:T(8,128)(2,1)S(1)} reshape(bf16[32,8,2,4,8,8]{5,4,3,2,1,0:T(8,128)(2,1)} %mul.73) | data formatting | bytes 524288 | tf_op jit(solution)/shard_map/mul | solution.py:234
  96.9 3.6 %pad_maximum_fusion.r_7_ = bf16[4,2,2048,128]{3,2,1,0:T(8,128)(2,1)} fusion(bf16[1,2,2048,128]{3,2,1,0:T(8,128)(2,1)} %bitcast.27, bf16[1,2,2048,128]{3,2,1,0:T(8,128)(2,1)} %bitcast.26, bf16[1,2,2048,128]{3,2,1,0:T(8,128)(2,1)} %bitcast.25, bf16[1,2,2048,128]{3,2,1,0:T(8,128)(2,1)S(1)} %get-tuple-element.9), kind=kLoop, calls=%fused_computation.1 | loop fusion | flops 6291456 | bytes 8388608 | tf_op jit(solution)/shard_map/stack | solution.py:262
  100.5 10.1 %collective-permute-start.17 = (bf16[4,2,2048,128]{3,2,1,0:T(8,128)(2,1)}, bf16[4,2,2048,128]{3,2,1,0:T(8,128)(2,1)}, u32[]{:S(2)}, u32[]{:S(2)}) collective-permute-start(bf16[4,2,2048,128]{3,2,1,0:T(8,128)(2,1)} %pad_maximum_fusion.r_7_), channel_id=1, source_target_pairs={{0,4},{4,0},{8,12},{12,8},{16,20},{20,16},{24,28},{28,24},{1,5},{5... | collective-permute-start | bytes 12582920 | tf_op jit(solution)/shard_map/ppermute | solution.py:263
  117.5 3.4 %collective-permute-start.9 = (bf16[4,1,2048,128]{3,2,1,0:T(8,128)(2,1)S(1)}, bf16[4,1,2048,128]{3,2,1,0:T(8,128)(2,1)}, u32[]{:S(2)}, u32[]{:S(2)}) collective-permute-start(bf16[4,1,2048,128]{3,2,1,0:T(8,128)(2,1)S(1)} %pad_maximum_fusion.2.r_3_), channel_id=1, source_target_pairs={{0,4},{4,0},{8,12},{12,8},{16,20},{20,16},{24,28},{28,24},{1,5},{5... | collective-permute-start | bytes 6291464 | tf_op jit(solution)/shard_map/ppermute | solution.py:263
  122.6 7.8 %collective-permute-done.12 = bf16[1,2048,128]{2,1,0:T(8,128)(2,1)S(1)} collective-permute-done((bf16[1,2048,128]{2,1,0:T(8,128)(2,1)}, bf16[1,2048,128]{2,1,0:T(8,128)(2,1)S(1)}, u32[]{:S(2)}, u32[]{:S(2)}) %collective-permute-start.12) | collective-permute-done | bytes 524320 | tf_op jit(solution)/shard_map/ppermute | solution.py:261
  133.0 5.5 %collective-permute-start.13 = (bf16[4,1,2048,128]{3,2,1,0:T(8,128)(2,1)}, bf16[4,1,2048,128]{3,2,1,0:T(8,128)(2,1)}, u32[]{:S(2)}, u32[]{:S(2)}) collective-permute-start(bf16[4,1,2048,128]{3,2,1,0:T(8,128)(2,1)} %pad_maximum_fusion.3.r_5_), channel_id=1, source_target_pairs={{0,4},{4,0},{8,12},{12,8},{16,20},{20,16},{24,28},{28,24},{1,5},{5... | collective-permute-start | bytes 6291464 | tf_op jit(solution)/shard_map/ppermute | solution.py:263
  138.5 3.8 %fusion.13 = (bf16[4,32,8,4,1,32]{5,4,3,2,1,0:T(2,128)(2,1)S(1)}, bf16[4,32,8,4,1,32]{5,4,3,2,1,0:T(2,128)(2,1)S(1)}) fusion(bf16[4,32,8,4,2,32]{5,4,3,2,1,0:T(2,128)(2,1)S(1)} %bitcast.45), kind=kLoop, calls=%fused_computation.46 | loop fusion | flops 131072 | bytes 1048576 | tf_op jit(solution)/shard_map/slice | solution.py:230
  142.3 5.6 %pad_maximum_fusion.1 = bf16[4,32,8,4,2,32]{5,4,3,2,1,0:T(2,128)(2,1)S(1)} fusion(bf16[4,32,8,4,1,32]{5,4,3,2,1,0:T(2,128)(2,1)S(1)} %get-tuple-element.8, bf16[4,32,8,4,1,32]{5,4,3,2,1,0:T(2,128)(2,1)S(1)} %get-tuple-element.7), kind=kLoop, calls=%fused_computation.7 | loop fusion | flops 1048576 | bytes 1048576 | tf_op jit(solution)/shard_map/stack | solution.py:230
  147.9 3.0 %maximum_bitcast_fusion = bf16[32,32,2,4,8,8]{1,5,4,0,3,2:T(8,128)(2,1)} fusion(bf16[1,4,32,8,8,32]{5,4,3,2,1,0:T(8,128)(2,1)S(1)} %bitcast.47, bf16[1,4,32,8,8,32]{5,4,3,2,1,0:T(8,128)(2,1)S(1)} %bitcast.46), kind=kLoop, calls=%fused_computation | loop fusion | flops 524288 | bytes 2097152 | tf_op jit(solution)/shard_map/transpose | solution.py:232
  150.9 10.2 %copy.22 = bf16[32,32,2,4,8,8]{0,5,4,3,2,1:T(8,128)(2,1)} copy(bf16[32,32,2,4,8,8]{1,5,4,0,3,2:T(8,128)(2,1)} %maximum_bitcast_fusion) | data formatting | bytes 2097152 | tf_op jit(solution)/shard_map/transpose | solution.py:232
  161.1 12.7 %mul.71 = bf16[32,32,8,2,4,8,8]{0,6,5,4,3,2,1:T(8,128)(2,1)} broadcast(bf16[32,32,2,4,8,8]{0,5,4,3,2,1:T(8,128)(2,1)} %copy.22), dimensions={0,1,3,4,5,6} | broadcast | bytes 9437184 | tf_op jit(solution)/shard_map/mul | solution.py:234
  173.8 30.7 %copy.23 = bf16[32,512,256]{2,1,0:T(8,128)(2,1)} copy(bf16[32,512,256]{0,2,1:T(8,128)(2,1)} %bitcast.44) | data formatting | bytes 16777216 | tf_op jit(solution)/shard_map/mul | solution.py:234
  204.5 7.4 %broadcast_multiply_fusion.r_1_ = bf16[32,512,256]{2,1,0:T(8,128)(2,1)} fusion(bf16[32,512,256]{2,1,0:T(8,128)(2,1)} %copy.23, bf16[512,256]{1,0:T(8,128)(2,1)S(1)} %mul.74), kind=kLoop, calls=%fused_computation.2 | loop fusion | flops 4194304 | bytes 17039360 | tf_op jit(solution)/shard_map/mul | solution.py:234
  211.9 26.0 %pairs.1 = f32[32,3,128,128]{3,2,1,0:T(8,128)} custom-call(s32[3]{0:T(128)} %get-tuple-element.6.r_0_, bf16[32,512,256]{2,1,0:T(8,128)(2,1)} %broadcast_multiply_fusion.r_1_, bf16[128,512]{1,0:T(8,128)(2,1)} %copy.25.r_2_, bf16[4,1,2048,128]{3,2,1,0:T(8,128)(2,1)} %copy-done, bf16[4,1,2048,128]{3,2,1,0:T(8,128)(2,1)} %collective-permute-done.9.r_4_, ...), custom_call_target="tpu_custom_call" | custom-call | tf_op jit(solution)/shard_map/pairs/pallas_call | solution.py:198
  (60 shorter events, 32.9 us)
Async XLA Ops:
  6.6 13.8 %collective-permute-start.1 = (bf16[2048,128]{1,0:T(8,128)(2,1)S(1)}, bf16[2048,128]{1,0:T(8,128)(2,1)S(1)}, u32[]{:S(2)}, u32[]{:S(2)}) collective-permute-start(bf16[2048,128]{1,0:T(8,128)(2,1)S(1)} %spectra.1), channel_id=1, source_target_pairs={{0,1},{1,2},{2,3},{4,5},{5,6},{6,7},{8,9},{9,10},{10,11},{12,13},{... | collective-permute-start | bytes 1572872 | tf_op jit(solution)/shard_map/ppermute | solution.py:273
  9.9 14.4 %collective-permute-start = (bf16[2048,128]{1,0:T(8,128)(2,1)S(1)}, bf16[2048,128]{1,0:T(8,128)(2,1)S(1)}, u32[]{:S(2)}, u32[]{:S(2)}) collective-permute-start(bf16[2048,128]{1,0:T(8,128)(2,1)S(1)} %spectra.1), channel_id=1, source_target_pairs={{3,2},{2,1},{1,0},{7,6},{6,5},{5,4},{11,10},{10,9},{9,8},{15,14},{... | collective-permute-start | bytes 1572872 | tf_op jit(solution)/shard_map/ppermute | solution.py:274
  20.4 5.1 %collective-permute-start.3 = (bf16[2048,128]{1,0:T(8,128)(2,1)S(1)}, bf16[2048,128]{1,0:T(8,128)(2,1)S(1)}, u32[]{:S(2)}, u32[]{:S(2)}) collective-permute-start(bf16[2048,128]{1,0:T(8,128)(2,1)S(1)} %collective-permute-done.1), channel_id=1, source_target_pairs={{1,2},{2,3},{5,6},{6,7},{9,10},{10,11},{13,14},{14,15},{17,18},{18... | collective-permute-start | bytes 1572872 | tf_op jit(solution)/shard_map/ppermute | solution.py:275
  24.2 13.8 %collective-permute-start.2 = (bf16[2048,128]{1,0:T(8,128)(2,1)S(1)}, bf16[2048,128]{1,0:T(8,128)(2,1)S(1)}, u32[]{:S(2)}, u32[]{:S(2)}) collective-permute-start(bf16[2048,128]{1,0:T(8,128)(2,1)S(1)} %collective-permute-done), channel_id=1, source_target_pairs={{2,1},{1,0},{6,5},{5,4},{10,9},{9,8},{14,13},{13,12},{18,17},{17,1... | collective-permute-start | bytes 1572872 | tf_op jit(solution)/shard_map/ppermute | solution.py:276
  25.5 13.8 %collective-permute-start.5 = (bf16[2048,128]{1,0:T(8,128)(2,1)S(1)}, bf16[2048,128]{1,0:T(8,128)(2,1)S(1)}, u32[]{:S(2)}, u32[]{:S(2)}) collective-permute-start(bf16[2048,128]{1,0:T(8,128)(2,1)S(1)} %collective-permute-done.3), channel_id=1, source_target_pairs={{2,3},{6,7},{10,11},{14,15},{18,19},{22,23},{26,27},{30,31}} | collective-permute-start | bytes 1572872 | tf_op jit(solution)/shard_map/ppermute | solution.py:277
  38.1 12.8 %collective-permute-start.4 = (bf16[2048,128]{1,0:T(8,128)(2,1)S(1)}, bf16[2048,128]{1,0:T(8,128)(2,1)}, u32[]{:S(2)}, u32[]{:S(2)}) collective-permute-start(bf16[2048,128]{1,0:T(8,128)(2,1)S(1)} %collective-permute-done.2), channel_id=1, source_target_pairs={{1,0},{5,4},{9,8},{13,12},{17,16},{21,20},{25,24},{29,28}} | collective-permute-start | bytes 1572872 | tf_op jit(solution)/shard_map/ppermute | solution.py:278
  53.1 22.7 %copy-start.1 = (bf16[1,2048,128]{2,1,0:T(8,128)(2,1)}, bf16[1,2048,128]{2,1,0:T(8,128)(2,1)S(1)}, u32[]{:S(2)}) copy-start(bf16[1,2048,128]{2,1,0:T(8,128)(2,1)S(1)} %get-tuple-element.14) | copy-start | bytes 1572868
  53.2 21.3 %collective-permute-start.14 = (bf16[2,2048,128]{2,1,0:T(8,128)(2,1)S(1)}, bf16[2,2048,128]{2,1,0:T(8,128)(2,1)}, u32[]{:S(2)}, u32[]{:S(2)}) collective-permute-start(bf16[2,2048,128]{2,1,0:T(8,128)(2,1)S(1)} %get-tuple-element.10), channel_id=1, source_target_pairs={{0,8},{4,12},{8,0},{12,4},{16,24},{20,28},{24,16},{28,20},{1,9},{5... | collective-permute-start | bytes 3145736 | tf_op jit(solution)/shard_map/ppermute | solution.py:259
  53.5 42.3 %collective-permute-start.15 = (bf16[2,2048,128]{2,1,0:T(8,128)(2,1)S(1)}, bf16[2,2048,128]{2,1,0:T(8,128)(2,1)}, u32[]{:S(2)}, u32[]{:S(2)}) collective-permute-start(bf16[2,2048,128]{2,1,0:T(8,128)(2,1)S(1)} %get-tuple-element.10), channel_id=1, source_target_pairs={{16,0},{4,20},{24,8},{12,28},{17,1},{5,21},{25,9},{13,29},{18,2},{... | collective-permute-start | bytes 3145736 | tf_op jit(solution)/shard_map/ppermute | solution.py:260
  74.5 22.4 %collective-permute-start.16 = (bf16[2,2048,128]{2,1,0:T(8,128)(2,1)}, bf16[2,2048,128]{2,1,0:T(8,128)(2,1)}, u32[]{:S(2)}, u32[]{:S(2)}) collective-permute-start(bf16[2,2048,128]{2,1,0:T(8,128)(2,1)} %collective-permute-done.14), channel_id=1, source_target_pairs={{24,8},{28,12},{0,16},{4,20},{25,9},{29,13},{1,17},{5,21},{26,10},... | collective-permute-start | bytes 3145736 | tf_op jit(solution)/shard_map/ppermute | solution.py:261
  75.8 16.4 %collective-permute-start.6 = (bf16[1,2048,128]{2,1,0:T(8,128)(2,1)S(1)}, bf16[1,2048,128]{2,1,0:T(8,128)(2,1)}, u32[]{:S(2)}, u32[]{:S(2)}) collective-permute-start(bf16[1,2048,128]{2,1,0:T(8,128)(2,1)S(1)} %bitcast.40), channel_id=1, source_target_pairs={{0,8},{4,12},{8,0},{12,4},{16,24},{20,28},{24,16},{28,20},{1,9},{5... | collective-permute-start | bytes 1572872 | tf_op jit(solution)/shard_map/ppermute | solution.py:259
  78.8 36.9 %collective-permute-start.7 = (bf16[1,2048,128]{2,1,0:T(8,128)(2,1)S(1)}, bf16[1,2048,128]{2,1,0:T(8,128)(2,1)}, u32[]{:S(2)}, u32[]{:S(2)}) collective-permute-start(bf16[1,2048,128]{2,1,0:T(8,128)(2,1)S(1)} %bitcast.41), channel_id=1, source_target_pairs={{16,0},{4,20},{24,8},{12,28},{17,1},{5,21},{25,9},{13,29},{18,2},{... | collective-permute-start | bytes 1572872 | tf_op jit(solution)/shard_map/ppermute | solution.py:260
  84.7 6.9 %copy-start.5 = (s32[256]{0:T(256)S(1)}, s32[256]{0:T(256)}, u32[]{:S(2)}) copy-start(s32[256]{0:T(256)} %param.5) | copy-start | bytes 3076
  92.2 23.5 %collective-permute-start.8 = (bf16[1,2048,128]{2,1,0:T(8,128)(2,1)}, bf16[1,2048,128]{2,1,0:T(8,128)(2,1)}, u32[]{:S(2)}, u32[]{:S(2)}) collective-permute-start(bf16[1,2048,128]{2,1,0:T(8,128)(2,1)} %collective-permute-done.6), channel_id=1, source_target_pairs={{24,8},{28,12},{0,16},{4,20},{25,9},{29,13},{1,17},{5,21},{26,10},... | collective-permute-start | bytes 1572872 | tf_op jit(solution)/shard_map/ppermute | solution.py:261
  93.5 20.7 %collective-permute-start.10 = (bf16[1,2048,128]{2,1,0:T(8,128)(2,1)}, bf16[1,2048,128]{2,1,0:T(8,128)(2,1)}, u32[]{:S(2)}, u32[]{:S(2)}) collective-permute-start(bf16[1,2048,128]{2,1,0:T(8,128)(2,1)} %get-tuple-element.12), channel_id=1, source_target_pairs={{0,8},{4,12},{8,0},{12,4},{16,24},{20,28},{24,16},{28,20},{1,9},{5... | collective-permute-start | bytes 1572872 | tf_op jit(solution)/shard_map/ppermute | solution.py:259
  96.9 15.3 %copy-start.6 = (s32[1,3]{1,0:T(1,128)S(1)}, s32[1,3]{1,0:T(1,128)}, u32[]{:S(2)}) copy-start(s32[1,3]{1,0:T(1,128)} %param.6) | copy-start | bytes 40
  100.5 111.3 %collective-permute-start.17 = (bf16[4,2,2048,128]{3,2,1,0:T(8,128)(2,1)}, bf16[4,2,2048,128]{3,2,1,0:T(8,128)(2,1)}, u32[]{:S(2)}, u32[]{:S(2)}) collective-permute-start(bf16[4,2,2048,128]{3,2,1,0:T(8,128)(2,1)} %pad_maximum_fusion.r_7_), channel_id=1, source_target_pairs={{0,4},{4,0},{8,12},{12,8},{16,20},{20,16},{24,28},{28,24},{1,5},{5... | collective-permute-start | bytes 12582920 | tf_op jit(solution)/shard_map/ppermute | solution.py:263
  112.9 9.7 %collective-permute-start.11 = (bf16[1,2048,128]{2,1,0:T(8,128)(2,1)}, bf16[1,2048,128]{2,1,0:T(8,128)(2,1)S(1)}, u32[]{:S(2)}, u32[]{:S(2)}) collective-permute-start(bf16[1,2048,128]{2,1,0:T(8,128)(2,1)} %get-tuple-element.12), channel_id=1, source_target_pairs={{16,0},{4,20},{24,8},{12,28},{17,1},{5,21},{25,9},{13,29},{18,2},{... | collective-permute-start | bytes 1572872 | tf_op jit(solution)/shard_map/ppermute | solution.py:260
  114.3 16.1 %collective-permute-start.12 = (bf16[1,2048,128]{2,1,0:T(8,128)(2,1)}, bf16[1,2048,128]{2,1,0:T(8,128)(2,1)S(1)}, u32[]{:S(2)}, u32[]{:S(2)}) collective-permute-start(bf16[1,2048,128]{2,1,0:T(8,128)(2,1)} %collective-permute-done.10), channel_id=1, source_target_pairs={{24,8},{28,12},{0,16},{4,20},{25,9},{29,13},{1,17},{5,21},{26,10},... | collective-permute-start | bytes 1572872 | tf_op jit(solution)/shard_map/ppermute | solution.py:261
  115.8 5.2 %copy-start.2 = (bf16[1,2048,128]{2,1,0:T(8,128)(2,1)S(1)}, bf16[1,2048,128]{2,1,0:T(8,128)(2,1)}, u32[]{:S(2)}) copy-start(bf16[1,2048,128]{2,1,0:T(8,128)(2,1)} %copy-done.1) | copy-start | bytes 1572868
  117.4 5.1 %copy-start = (bf16[4,1,2048,128]{3,2,1,0:T(8,128)(2,1)}, bf16[4,1,2048,128]{3,2,1,0:T(8,128)(2,1)S(1)}, u32[]{:S(2)}) copy-start(bf16[4,1,2048,128]{3,2,1,0:T(8,128)(2,1)S(1)} %pad_maximum_fusion.2.r_3_) | copy-start | bytes 6291460
  117.5 12.9 %copy-start.3 = (bf16[1,1,2048,128]{3,2,1,0:T(8,128)(2,1)S(1)}, bf16[1,1,2048,128]{3,2,1,0:T(8,128)(2,1)}, u32[]{:S(2)}) copy-start(bf16[1,1,2048,128]{3,2,1,0:T(8,128)(2,1)} %get-tuple-element.11) | copy-start | bytes 1572868
  117.5 94.4 %collective-permute-start.9 = (bf16[4,1,2048,128]{3,2,1,0:T(8,128)(2,1)S(1)}, bf16[4,1,2048,128]{3,2,1,0:T(8,128)(2,1)}, u32[]{:S(2)}, u32[]{:S(2)}) collective-permute-start(bf16[4,1,2048,128]{3,2,1,0:T(8,128)(2,1)S(1)} %pad_maximum_fusion.2.r_3_), channel_id=1, source_target_pairs={{0,4},{4,0},{8,12},{12,8},{16,20},{20,16},{24,28},{28,24},{1,5},{5... | collective-permute-start | bytes 6291464 | tf_op jit(solution)/shard_map/ppermute | solution.py:263
  133.0 78.9 %collective-permute-start.13 = (bf16[4,1,2048,128]{3,2,1,0:T(8,128)(2,1)}, bf16[4,1,2048,128]{3,2,1,0:T(8,128)(2,1)}, u32[]{:S(2)}, u32[]{:S(2)}) collective-permute-start(bf16[4,1,2048,128]{3,2,1,0:T(8,128)(2,1)} %pad_maximum_fusion.3.r_5_), channel_id=1, source_target_pairs={{0,4},{4,0},{8,12},{12,8},{16,20},{20,16},{24,28},{28,24},{1,5},{5... | collective-permute-start | bytes 6291464 | tf_op jit(solution)/shard_map/ppermute | solution.py:263
  (1 other events, 0.8 us)

commit v2 on v1

--- a/solution.py
+++ b/solution.py
@@ -82,9 +82,8 @@
 
 
 def spectra_kernel(traces_ref, fine_cos, fine_sin, step_cos, step_sin, out_ref, table, planes):
-    bins = fine_cos.shape[0]
-    fine = fine_cos.shape[1]
-    channels = out_ref.shape[1]
+    bins, fine = fine_cos.shape
+    groups, _, channels = planes.shape
     windows = traces_ref.shape[0] // channels
     for h in range(step_cos.shape[1]):
         sc, ss = step_cos[:, h : h + 1], step_sin[:, h : h + 1]
@@ -100,10 +99,11 @@
         white = spectra / jnp.sqrt(power / bins + 1e-06)
         for w in range(2):
             for c in range(2):
-                planes[pl.ds((half * 2 + w) * 2 + c, bins, stride=2 * windows), :] = white[
+                first = c * GROUP * windows + half * 2 + w
+                planes[:, pl.ds(first, GROUP, stride=windows), :] = white[
                     c * bins : (c + 1) * bins, w * channels : (w + 1) * channels
-                ]
-    out_ref[...] = planes[...].astype(jnp.bfloat16)
+                ].reshape(groups, GROUP, channels)
+    out_ref[...] = planes[...].reshape(out_ref.shape).astype(jnp.bfloat16)
 
 
 def make_slab(traces, band_bins):
@@ -120,39 +120,96 @@
         out_shape=jax.ShapeDtypeStruct((bins * windows * 2, channels), jnp.bfloat16),
         scratch_shapes=[
             pltpu.VMEM((2 * bins, length), jnp.bfloat16),
-            pltpu.VMEM((bins * windows * 2, channels), jnp.float32),
+            pltpu.VMEM((bins // GROUP, GROUP * windows * 2, channels), jnp.float32),
         ],
         compiler_params=pltpu.CompilerParams(vmem_limit_bytes=48 << 20),
         name="spectra",
     )(rows, cos[:, :fine], sin[:, :fine], cos[:, fine:], sin[:, fine:])
 
 
+def left_kernel(z, *refs, per_step):
+    slabs, (out_ref, choice, mask) = refs[:-3], refs[-3:]
+    m, k = mask.shape
+    channels = slabs[0].shape[1]
+    group_rows = k // len(slabs)
+    half = group_rows // 2
+    rows_out = m // (2 * GROUP)
+
+    @pl.when(pl.program_id(0) == 0)
+    def _():
+        row = lax.broadcasted_iota(jnp.int32, (m, 2 * channels), 0)
+        col = lax.broadcasted_iota(jnp.int32, (m, 2 * channels), 1)
+        wanted = row // (2 * GROUP) + z[0] * rows_out + (row % 2) * channels
+        choice[...] = jnp.where(col == wanted, 1.0, 0.0).astype(jnp.bfloat16)
+        row = lax.broadcasted_iota(jnp.int32, (m, k), 0)
+        col = lax.broadcasted_iota(jnp.int32, (m, k), 1)
+        bin_of_col = col % half // (half // GROUP)
+        mask[...] = jnp.where(bin_of_col == row // 2 % GROUP, 1.0, 0.0)
+
+    for u in range(per_step):
+        pieces = []
+        for slab in slabs:
+            real = slab[u * group_rows : u * group_rows + half, :]
+            imag = slab[u * group_rows + half : (u + 1) * group_rows, :]
+            pieces.append(jnp.concatenate([real, imag], 1))
+            pieces.append(jnp.concatenate([imag, -real], 1))
+        both = jnp.concatenate(pieces, 0)
+        rows = lax.dot_general(
+            choice[...], both, (((1,), (1,)), ((), ())), preferred_element_type=jnp.float32
+        )
+        out_ref[u] = (rows * mask[...]).astype(jnp.bfloat16)
+
+
+def make_left(slabs, z, rows_out, bins):
+    slab_rows, channels = slabs[0].shape
+    groups = bins // GROUP
+    m, k = rows_out * GROUP * 2, slab_rows // groups * len(slabs)
+    per_step = 4
+    return pl.pallas_call(
+        lambda *r: left_kernel(*r, per_step=per_step),
+        grid_spec=pltpu.PrefetchScalarGridSpec(
+            num_scalar_prefetch=1,
+            grid=(groups // per_step,),
+            in_specs=[
+                pl.BlockSpec((slab_rows // groups * per_step, channels), lambda i, s: (i, 0))
+            ]
+            * len(slabs),
+            out_specs=pl.BlockSpec((per_step, m, k), lambda i, s: (i, 0, 0)),
+            scratch_shapes=[
+                pltpu.VMEM((m, 2 * channels), jnp.bfloat16),
+                pltpu.VMEM((m, k), jnp.float32),
+            ],
+        ),
+        out_shape=jax.ShapeDtypeStruct((groups, m, k), jnp.bfloat16),
+        compiler_params=pltpu.CompilerParams(vmem_limit_bytes=32 << 20),
+        name="left",
+    )(z.reshape(1), *slabs)
+
+
 def pairs_kernel(slots, left_ref, lag_ref, *refs, parts, gram_steps, norm):
-    n_in = 2 * len(parts)
-    sources, out_ref, partner, gram, sems = refs[:n_in], *refs[n_in:]
+    n_in = sum(len(part) for part in parts)
+    sources, (out_ref, partner, gram, sems) = refs[:n_in], refs[n_in:]
     step = pl.program_id(0)
     per_step, m, k = left_ref.shape
     slot_count = partner.shape[0]
     channels = partner.shape[3]
-    held = sources[0].shape[0]
     group_rows = k // partner.shape[1]
 
     def copies(act):
         for s in range(slot_count):
-            first = 0
-            for p, count in enumerate(parts):
-                dst = partner.at[s, first : first + count]
-                sem = sems.at[s, p]
-
-                @pl.when(slots[s] < held)
-                def _():
-                    act(pltpu.make_async_copy(sources[2 * p].at[slots[s]], dst, sem))
-
-                @pl.when(slots[s] >= held)
-                def _():
-                    act(pltpu.make_async_copy(sources[2 * p + 1].at[slots[s] - held], dst, sem))
-
-                first += count
+            ref = 0
+            for r, part in enumerate(parts):
+                slot = slots[s * len(parts) + r]
+                first = 0
+                for count in part:
+
+                    @pl.when((slot >= first) & (slot < first + count))
+                    def _():
+                        source = sources[ref].at[slot - first]
+                        act(pltpu.make_async_copy(source, partner.at[s, r], sems.at[s, r]))
+
+                    first += count
+                    ref += 1
 
     @pl.when(step == 0)
     def _():
@@ -185,16 +242,15 @@
                 out_ref[u, s] = lagged[:, s * channels : (s + 1) * channels].T
 
 
-def correlate(slots, left, lag_rows, sources, parts, norm):
+def correlate(slots, left, lag_rows, sources, slot_count, norm):
     groups, m, k = left.shape
     rows_out = m // (2 * GROUP)
-    slot_count = slots.shape[0]
-    channels = sources[0].shape[-1]
-    slab_rows = sources[0].shape[-2]
+    parts = [[value.shape[0] for value in part] for part in sources]
+    flat = [value for part in sources for value in part]
+    slab_rows, channels = flat[0].shape[1:]
     lag_count, entries = lag_rows.shape
     per_step, per_lag = 2, 2
     gram_steps = groups // per_step
-    any_spec = pl.BlockSpec(memory_space=pl.ANY)
     return pl.pallas_call(
         lambda *r: pairs_kernel(*r, parts=parts, gram_steps=gram_steps, norm=norm),
         grid_spec=pltpu.PrefetchScalarGridSpec(
@@ -204,13 +260,13 @@
                 pl.BlockSpec((per_step, m, k), lambda i, s: (jnp.minimum(i, gram_steps - 1), 0, 0)),
                 pl.BlockSpec((lag_count, entries), lambda i, s: (0, 0)),
             ]
-            + [any_spec] * len(sources),
+            + [pl.BlockSpec(memory_space=pl.ANY)] * len(flat),
             out_specs=pl.BlockSpec(
                 (per_lag, slot_count, channels, lag_count),
                 lambda i, s: (jnp.maximum(i - gram_steps, 0), 0, 0, 0),
             ),
             scratch_shapes=[
-                pltpu.VMEM((slot_count, sum(parts), slab_rows, channels), jnp.bfloat16),
+                pltpu.VMEM((slot_count, len(parts), slab_rows, channels), jnp.bfloat16),
                 pltpu.VMEM((rows_out, entries, slot_count * channels), jnp.bfloat16),
                 pltpu.SemaphoreType.DMA((slot_count, len(parts))),
             ],
@@ -218,49 +274,33 @@
         out_shape=jax.ShapeDtypeStruct((rows_out, slot_count, channels, lag_count), jnp.float32),
         compiler_params=pltpu.CompilerParams(vmem_limit_bytes=56 << 20),
         name="pairs",
-    )(slots, left, lag_rows, *sources)
-
-
-def make_left(own, row_index, rows_out):
-    slabs, slab_rows, channels = own.shape
-    mine = lax.dynamic_slice_in_dim(own, row_index * rows_out, rows_out, 2)
-    per_bin = slab_rows // 256
-    groups = 256 // GROUP
-    mine = mine.reshape(slabs, groups, GROUP, per_bin // 2, 2, rows_out)
-    rotated = jnp.stack([mine[:, :, :, :, 1], -mine[:, :, :, :, 0]], 4)
-    both = jnp.stack([mine, rotated], 0).reshape(2, slabs, groups, GROUP, per_bin, rows_out)
-    both = both.transpose(2, 5, 0, 1, 3, 4)
-    eye = jnp.eye(GROUP, dtype=jnp.bfloat16)
-    left = both[:, :, None] * eye[None, None, :, None, None, :, None]
-    return left.reshape(groups, rows_out * GROUP * 2, slabs * GROUP * per_bin)
+    )(slots, left, lag_rows, *flat)
 
 
 X_PAIRS = [(i, i ^ 2) for i in range(8)]
 Y_PAIRS = [(4, 0), (1, 5), (6, 2), (3, 7)]
-YX_PAIRS = [(6, 2), (7, 3), (0, 4), (1, 5)]
+X_ON = [(0, 2), (7, 5)]
+Y_ON = [(7, 3), (0, 4)]
+Y_ON_ALL = Y_ON + [(6, 2), (1, 5)]
 CORE_PAIRS = [(i, i ^ 1) for i in range(8)]
 
 
-def held_blocks():
-    table = np.full((8, 8), -1, np.int32)
-    for i in range(8):
-        table[i, 0] = i
-        table[i, 1] = i ^ 2
-    for src, dst in Y_PAIRS:
-        table[dst, 2] = src
-    for src, dst in YX_PAIRS:
-        table[dst, 3] = src ^ 2
-    for i in range(8):
-        table[i, 4:] = table[i ^ 1, :4]
-    return table
-
-
-def spread(part):
-    across_x = lax.ppermute(part, "chan", X_PAIRS)
-    across_y = lax.ppermute(part, "chan", Y_PAIRS)
-    across_both = lax.ppermute(across_x, "chan", YX_PAIRS)
-    held = jnp.stack([part, across_x, across_y, across_both], 0)
-    return held, lax.ppermute(held, "chan", CORE_PAIRS)
+def hop(entry, pairs):
+    value, ids = entry
+    moved = np.full_like(ids, -1)
+    for src, dst in pairs:
+        moved[:, dst] = ids[:, src]
+    return lax.ppermute(value, "chan", pairs), moved
+
+
+def join(*entries):
+    values, ids = zip(*entries)
+    return jnp.concatenate(values, 0), np.concatenate(ids, 0)
+
+
+def together(*entries):
+    values = lax.optimization_barrier(tuple(value for value, _ in entries))
+    return [(value, ids) for value, (_, ids) in zip(values, entries)]
 
 
 def on_device(traces, band_bins, pair_blocks):
@@ -268,33 +308,65 @@
     bins = band_bins.shape[0]
     z = lax.axis_index("freq")
     me = lax.axis_index("chan")
-    slab = make_slab(traces, band_bins)
-
-    up1 = lax.ppermute(slab, "freq", [(0, 1), (1, 2), (2, 3)])
-    down1 = lax.ppermute(slab, "freq", [(3, 2), (2, 1), (1, 0)])
-    up2 = lax.ppermute(up1, "freq", [(1, 2), (2, 3)])
-    down2 = lax.ppermute(down1, "freq", [(2, 1), (1, 0)])
-    up3 = lax.ppermute(up2, "freq", [(2, 3)])
-    down3 = lax.ppermute(down2, "freq", [(1, 0)])
-
-    def choose(*options):
-        return lax.select_n(z, *options)
-
-    part0 = slab[None]
-    part1 = choose(down1, up1, down1, up1)[None]
-    part2 = jnp.stack([choose(down2, down1, up1, up2), choose(down3, down2, up2, up3)], 0)
-    sources = []
-    for part in (part0, part1, part2):
-        sources += spread(part)
-
-    own = jnp.concatenate([part0, part1, part2], 0)
-    left = make_left(own, z, channels // 4)
+    own = np.arange(8)[None]
+
+    def along_z(entry, pairs):
+        return lax.ppermute(entry[0], "freq", pairs), entry[1]
+
+    def choose(*entries):
+        return lax.select_n(z, *[value for value, _ in entries]), entries[0][1]
+
     lag_rows = make_lag_table(band_bins, length, LAGS)
     lag_rows = lag_rows.reshape(2, bins, LAGS).transpose(2, 1, 0).reshape(LAGS, 2 * bins)
-    table = jnp.asarray(held_blocks())[me]
-    slots = jnp.argmax(table[None, :] == pair_blocks[0][:, None], axis=1).astype(jnp.int32)
+    lag_rows = lag_rows.astype(jnp.bfloat16)
+    q0 = make_slab(traces, band_bins)[None], own
+
+    up1, down1 = along_z(q0, [(0, 1), (1, 2), (2, 3)]), along_z(q0, [(3, 2), (2, 1), (1, 0)])
+    x0, y0 = hop(q0, X_PAIRS), hop(q0, Y_PAIRS)
+    up1, down1, x0, y0 = together(up1, down1, x0, y0)
+
+    q1 = choose(down1, up1, down1, up1)
+    up2, down2 = along_z(up1, [(1, 2), (2, 3)]), along_z(down1, [(2, 1), (1, 0)])
+    x1, y1, c0 = hop(q1, X_PAIRS), hop(q1, Y_PAIRS), hop(x0, Y_ON_ALL)
+    up2, down2, x1, y1, c0 = together(up2, down2, x1, y1, c0)
+
+    q2 = choose(down2, down1, up1, up2)
+    up3, down3 = along_z(up2, [(2, 3)]), along_z(down2, [(1, 0)])
+    x2, y2, c1 = hop(q2, X_PAIRS), hop(q2, Y_PAIRS), hop(x1, Y_ON_ALL)
+    other0 = hop(join(q0, x0, y0, c0), CORE_PAIRS)
+    up3, down3, x2, y2, c1, other0 = together(up3, down3, x2, y2, c1, other0)
+
+    q3 = choose(down3, down2, up2, up3)
+    x3, y3, c2 = hop(q3, X_PAIRS), hop(q3, Y_PAIRS), hop(x2, Y_ON_ALL)
+    other1 = hop(join(q1, x1, y1, c1), CORE_PAIRS)
+    left = make_left([q[0][0] for q in (q0, q1, q2, q3)], z, channels // 4, bins)
+    x3, y3, c2, other1, (left, _) = together(x3, y3, c2, other1, (left, None))
+
+    c3, d3 = hop(x3, Y_ON), hop(y3, X_ON)
+    other2, other3 = hop(join(q2, x2, y2, c2), CORE_PAIRS), hop(join(q3, x3, y3), CORE_PAIRS)
+    c3, d3, other2, other3 = together(c3, d3, other2, other3)
+    late3 = hop(join(c3, d3), CORE_PAIRS)
+
+    held = [
+        [q0, x0, y0, c0, other0],
+        [q1, x1, y1, c1, other1],
+        [q2, x2, y2, c2, other2],
+        [q3, x3, y3, c3, d3, other3, late3],
+    ]
+    ids = [np.concatenate([entry[1] for entry in part], 0) for part in held]
+    most = max(len(rows) for rows in ids)
+    table = np.stack([np.pad(rows, ((0, most - len(rows)), (0, 0)), constant_values=-1) for rows in ids])
+    mine = jnp.asarray(table.transpose(2, 0, 1), jnp.int32)[me]
+    slots = jnp.argmax(mine[None] == pair_blocks[0][:, None, None], axis=2).astype(jnp.int32)
     norm = 1.0 / math.sqrt(4 * windows * bins)
-    result = correlate(slots, left, lag_rows.astype(jnp.bfloat16), sources, (1, 1, 2), norm)
+    result = correlate(
+        slots.reshape(-1),
+        left,
+        lag_rows,
+        [[entry[0] for entry in part] for part in held],
+        pair_blocks.shape[1],
+        norm,
+    )
     return result[None]
 
 

time: 240 us -> 147 us (0.61)
  the two profiles are of different devices: /device:TPU:3 before, /device:TPU:17 now
where the time goes in v2:
time: 147 us; the launch traced here: 145 us
  starting transfers between devices  48.6 us (33%)
  waiting for transfers between devices  46.5 us (32%)
  Pallas kernels  32.1 us (22%)
  local copies, waits for them, and re-layouts  12.8 us (9%)
  other arithmetic  4.49 us (3%)
    ppermute x18, waiting for transfers between devices, hop(): return (lax.ppermute(value, 'chan', pairs), moved)  38.1 us
    ppermute x18, starting transfers between devices, hop(): return (lax.ppermute(value, 'chan', pairs), moved)  35.6 us
    pallas_call x1, Pallas kernels, correlate(): pl.pallas_call(lambda *r: pairs_kernel(*r, parts=parts, gram_steps=gram_s...  26.1 us
    ppermute x6, starting transfers between devices, along_z(): return (lax.ppermute(entry[0], 'freq', pairs), entry[1])  13.1 us
    ppermute x6, waiting for transfers between devices, along_z(): return (lax.ppermute(entry[0], 'freq', pairs), entry[1])  8.47 us
    unnamed x46, local copies, waits for them, and re-layouts  7.74 us
    pallas_call x1, Pallas kernels, make_left(): pl.pallas_call(lambda *r: left_kernel(*r, per_step=per_step), grid_spec=p...  4.04 us
  transfers between devices with their start and end apart: 24, of which 13 were waited for; matrix products, arithmetic and copies ran while one was open for 3% of the time, Pallas kernels for 3%

profile of v2, /device:TPU:17, one launch (start us, length us, event | category | flops | bytes accessed | tf_op | source)
XLA Modules:
  0.0 145.0 jit_solution(10473925414275366255)
XLA Ops:
  1.9 2.7 %copy.9 = bf16[4,128,2048]{2,1,0:T(8,128)(2,1)S(1)} copy(bf16[4,128,2048]{2,0,1:T(4,128)(2,1)} %bitcast.25) | data formatting | bytes 4194304 | tf_op jit(solution)/shard_map/transpose | solution.py:113
  6.6 3.2 %collective-permute-start.3 = (bf16[1,2048,128]{2,1,0:T(8,128)(2,1)S(1)}, bf16[1,2048,128]{2,1,0:T(8,128)(2,1)S(1)}, u32[]{:S(2)}, u32[]{:S(2)}) collective-permute-start(bf16[1,2048,128]{2,1,0:T(8,128)(2,1)S(1)} %bitcast.17), channel_id=1, source_target_pairs={{16,0},{4,20},{24,8},{12,28},{17,1},{5,21},{25,9},{13,29},{18,2},{... | collective-permute-start | bytes 1572872 | tf_op jit(solution)/shard_map/ppermute | solution.py:293
  11.0 2.1 %collective-permute-start.1 = (bf16[1,2048,128]{2,1,0:T(8,128)(2,1)S(1)}, bf16[1,2048,128]{2,1,0:T(8,128)(2,1)S(1)}, u32[]{:S(2)}, u32[]{:S(2)}) collective-permute-start(bf16[1,2048,128]{2,1,0:T(8,128)(2,1)S(1)} %bitcast.19), channel_id=1, source_target_pairs={{3,2},{2,1},{1,0},{7,6},{6,5},{5,4},{11,10},{10,9},{9,8},{15,14},{... | collective-permute-start | bytes 1572872 | tf_op jit(solution)/shard_map/ppermute | solution.py:314
  13.1 3.2 %collective-permute-start = (bf16[1,2048,128]{2,1,0:T(8,128)(2,1)S(1)}, bf16[1,2048,128]{2,1,0:T(8,128)(2,1)S(1)}, u32[]{:S(2)}, u32[]{:S(2)}) collective-permute-start(bf16[1,2048,128]{2,1,0:T(8,128)(2,1)S(1)} %bitcast.20), channel_id=1, source_target_pairs={{0,1},{1,2},{2,3},{4,5},{5,6},{6,7},{8,9},{9,10},{10,11},{12,13},{... | collective-permute-start | bytes 1572872 | tf_op jit(solution)/shard_map/ppermute | solution.py:314
  16.4 6.6 %collective-permute-done.2.r_4_ = bf16[1,2048,128]{2,1,0:T(8,128)(2,1)S(1)} collective-permute-done((bf16[1,2048,128]{2,1,0:T(8,128)(2,1)S(1)}, bf16[1,2048,128]{2,1,0:T(8,128)(2,1)S(1)}, u32[]{:S(2)}, u32[]{:S(2)}) %collective-permute-start.2) | collective-permute-done | bytes 524320 | tf_op jit(solution)/shard_map/ppermute | solution.py:293
  23.0 3.4 %collective-permute-done.1 = bf16[1,2048,128]{2,1,0:T(8,128)(2,1)S(1)} collective-permute-done((bf16[1,2048,128]{2,1,0:T(8,128)(2,1)S(1)}, bf16[1,2048,128]{2,1,0:T(8,128)(2,1)S(1)}, u32[]{:S(2)}, u32[]{:S(2)}) %collective-permute-start.1) | collective-permute-done | bytes 524320 | tf_op jit(solution)/shard_map/ppermute | solution.py:314
  26.4 2.2 %collective-permute-done = bf16[1,2048,128]{2,1,0:T(8,128)(2,1)S(1)} collective-permute-done((bf16[1,2048,128]{2,1,0:T(8,128)(2,1)S(1)}, bf16[1,2048,128]{2,1,0:T(8,128)(2,1)S(1)}, u32[]{:S(2)}, u32[]{:S(2)}) %collective-permute-start) | collective-permute-done | bytes 524320 | tf_op jit(solution)/shard_map/ppermute | solution.py:314
  30.3 3.2 %collective-permute-start.4 = (bf16[1,2048,128]{2,1,0:T(8,128)(2,1)S(1)}, bf16[1,2048,128]{2,1,0:T(8,128)(2,1)S(1)}, u32[]{:S(2)}, u32[]{:S(2)}) collective-permute-start(bf16[1,2048,128]{2,1,0:T(8,128)(2,1)S(1)} %collective-permute-done), channel_id=1, source_target_pairs={{1,2},{2,3},{5,6},{6,7},{9,10},{10,11},{13,14},{14,15},{17,18},{18... | collective-permute-start | bytes 1572872 | tf_op jit(solution)/shard_map/ppermute | solution.py:314
  33.5 2.1 %collective-permute-start.5 = (bf16[1,2048,128]{2,1,0:T(8,128)(2,1)S(1)}, bf16[1,2048,128]{2,1,0:T(8,128)(2,1)S(1)}, u32[]{:S(2)}, u32[]{:S(2)}) collective-permute-start(bf16[1,2048,128]{2,1,0:T(8,128)(2,1)S(1)} %collective-permute-done.1), channel_id=1, source_target_pairs={{2,1},{1,0},{6,5},{5,4},{10,9},{9,8},{14,13},{13,12},{18,17},{17,1... | collective-permute-start | bytes 1572872 | tf_op jit(solution)/shard_map/ppermute | solution.py:314
  37.0 6.2 %collective-permute-done.6.r_9_ = bf16[1,2048,128]{2,1,0:T(8,128)(2,1)S(1)} collective-permute-done((bf16[1,2048,128]{2,1,0:T(8,128)(2,1)S(1)}, bf16[1,2048,128]{2,1,0:T(8,128)(2,1)S(1)}, u32[]{:S(2)}, u32[]{:S(2)}) %collective-permute-start.6) | collective-permute-done | bytes 524320 | tf_op jit(solution)/shard_map/ppermute | solution.py:293
  46.7 3.2 %collective-permute-start.14 = (bf16[4,2048,128]{2,1,0:T(8,128)(2,1)S(1)}, bf16[4,2048,128]{2,1,0:T(8,128)(2,1)}, u32[]{:S(2)}, u32[]{:S(2)}) collective-permute-start(bf16[4,2048,128]{2,1,0:T(8,128)(2,1)S(1)} %pad_maximum_fusion), channel_id=1, source_target_pairs={{0,4},{4,0},{8,12},{12,8},{16,20},{20,16},{24,28},{28,24},{1,5},{5... | collective-permute-start | bytes 6291464 | tf_op jit(solution)/shard_map/ppermute | solution.py:293
  50.0 4.1 %collective-permute-start.12 = (bf16[1,2048,128]{2,1,0:T(8,128)(2,1)S(1)}, bf16[1,2048,128]{2,1,0:T(8,128)(2,1)S(1)}, u32[]{:S(2)}, u32[]{:S(2)}) collective-permute-start(bf16[1,2048,128]{2,1,0:T(8,128)(2,1)S(1)} %select_select_fusion.1.r_13_), channel_id=1, source_target_pairs={{16,0},{4,20},{24,8},{12,28},{17,1},{5,21},{25,9},{13,29},{18,2},{... | collective-permute-start | bytes 1572872 | tf_op jit(solution)/shard_map/ppermute | solution.py:293
  57.9 2.3 %collective-permute-done.12.r_15_ = bf16[1,2048,128]{2,1,0:T(8,128)(2,1)S(1)} collective-permute-done((bf16[1,2048,128]{2,1,0:T(8,128)(2,1)S(1)}, bf16[1,2048,128]{2,1,0:T(8,128)(2,1)S(1)}, u32[]{:S(2)}, u32[]{:S(2)}) %collective-permute-start.12) | collective-permute-done | bytes 524320 | tf_op jit(solution)/shard_map/ppermute | solution.py:293
  60.2 4.1 %collective-permute-start.13 = (bf16[1,2048,128]{2,1,0:T(8,128)(2,1)S(1)}, bf16[1,2048,128]{2,1,0:T(8,128)(2,1)S(1)}, u32[]{:S(2)}, u32[]{:S(2)}) collective-permute-start(bf16[1,2048,128]{2,1,0:T(8,128)(2,1)S(1)} %collective-permute-done.6.r_9_), channel_id=1, source_target_pairs={{28,12},{0,16},{24,8},{4,20},{29,13},{1,17},{25,9},{5,21},{30,14},... | collective-permute-start | bytes 1572872 | tf_op jit(solution)/shard_map/ppermute | solution.py:293
  64.3 3.6 %collective-permute-done.11.r_14_ = bf16[1,2048,128]{2,1,0:T(8,128)(2,1)S(1)} collective-permute-done((bf16[1,2048,128]{2,1,0:T(8,128)(2,1)S(1)}, bf16[1,2048,128]{2,1,0:T(8,128)(2,1)S(1)}, u32[]{:S(2)}, u32[]{:S(2)}) %collective-permute-start.11) | collective-permute-done | bytes 524320 | tf_op jit(solution)/shard_map/ppermute | solution.py:293
  68.2 6.7 %collective-permute-done.13.r_11_ = bf16[1,2048,128]{2,1,0:T(8,128)(2,1)S(1)} collective-permute-done((bf16[1,2048,128]{2,1,0:T(8,128)(2,1)S(1)}, bf16[1,2048,128]{2,1,0:T(8,128)(2,1)S(1)}, u32[]{:S(2)}, u32[]{:S(2)}) %collective-permute-start.13) | collective-permute-done | bytes 524320 | tf_op jit(solution)/shard_map/ppermute | solution.py:293
  75.9 3.8 %collective-permute-start.16 = (bf16[1,2048,128]{2,1,0:T(8,128)(2,1)S(1)}, bf16[1,2048,128]{2,1,0:T(8,128)(2,1)S(1)}, u32[]{:S(2)}, u32[]{:S(2)}) collective-permute-start(bf16[1,2048,128]{2,1,0:T(8,128)(2,1)S(1)} %select_select_fusion.r_18_), channel_id=1, source_target_pairs={{16,0},{4,20},{24,8},{12,28},{17,1},{5,21},{25,9},{13,29},{18,2},{... | collective-permute-start | bytes 1572872 | tf_op jit(solution)/shard_map/ppermute | solution.py:293
  81.4 4.0 %left.1.r_1_ = bf16[32,512,256]{2,1,0:T(8,128)(2,1)S(1)} custom-call(s32[1]{0:T(128)} %bitcast.5.r_0_, bf16[2048,128]{1,0:T(8,128)(2,1)S(1)} %spectra.1.r_1_, bf16[2048,128]{1,0:T(8,128)(2,1)S(1)} %bitcast.15, bf16[2048,128]{1,0:T(8,128)(2,1)S(1)} %bitcast.23, bf16[2048,128]{1,0:T(8,128)(2,1)S(1)} %bitcast.16), custom_call_target="tpu_custom_call" | custom-call | tf_op jit(solution)/shard_map/left/pallas_call | solution.py:168
  85.5 3.3 %copy-done = bf16[32,512,256]{2,1,0:T(8,128)(2,1)} copy-done((bf16[32,512,256]{2,1,0:T(8,128)(2,1)}, bf16[32,512,256]{2,1,0:T(8,128)(2,1)S(1)}, u32[]{:S(2)}) %copy-start) | copy-done | bytes 8388632
  88.8 3.7 %collective-permute-done.15.r_19_ = bf16[1,2048,128]{2,1,0:T(8,128)(2,1)S(1)} collective-permute-done((bf16[1,2048,128]{2,1,0:T(8,128)(2,1)S(1)}, bf16[1,2048,128]{2,1,0:T(8,128)(2,1)S(1)}, u32[]{:S(2)}, u32[]{:S(2)}) %collective-permute-start.15) | collective-permute-done | bytes 524320 | tf_op jit(solution)/shard_map/ppermute | solution.py:293
  92.4 4.6 %collective-permute-done.17.r_16_ = bf16[1,2048,128]{2,1,0:T(8,128)(2,1)S(1)} collective-permute-done((bf16[1,2048,128]{2,1,0:T(8,128)(2,1)S(1)}, bf16[1,2048,128]{2,1,0:T(8,128)(2,1)S(1)}, u32[]{:S(2)}, u32[]{:S(2)}) %collective-permute-start.17) | collective-permute-done | bytes 524320 | tf_op jit(solution)/shard_map/ppermute | solution.py:293
  100.8 4.2 %collective-permute-done.22.r_23_ = bf16[3,2048,128]{2,1,0:T(8,128)(2,1)S(1)} collective-permute-done((bf16[3,2048,128]{2,1,0:T(8,128)(2,1)S(1)}, bf16[3,2048,128]{2,1,0:T(8,128)(2,1)S(1)}, u32[]{:S(2)}, u32[]{:S(2)}) %collective-permute-start.22) | collective-permute-done | bytes 1572896 | tf_op jit(solution)/shard_map/ppermute | solution.py:293
  106.3 8.0 %collective-permute-start.23 = (bf16[2,2048,128]{2,1,0:T(8,128)(2,1)S(1)}, bf16[2,2048,128]{2,1,0:T(8,128)(2,1)S(1)}, u32[]{:S(2)}, u32[]{:S(2)}) collective-permute-start(bf16[2,2048,128]{2,1,0:T(8,128)(2,1)S(1)} %pad_maximum_fusion.4), channel_id=1, source_target_pairs={{0,4},{4,0},{8,12},{12,8},{16,20},{20,16},{24,28},{28,24},{1,5},{5... | collective-permute-start | bytes 3145736 | tf_op jit(solution)/shard_map/ppermute | solution.py:293
  118.9 26.1 %pairs.1 = f32[32,3,128,128]{3,2,1,0:T(8,128)} custom-call(s32[12]{0:T(128)} %reshape.20.r_0_, bf16[32,512,256]{2,1,0:T(8,128)(2,1)} %copy-done, bf16[128,512]{1,0:T(8,128)(2,1)} %copy.11.r_2_, bf16[1,2048,128]{2,1,0:T(8,128)(2,1)} %bitcast.22, bf16[1,2048,128]{2,1,0:T(8,128)(2,1)} %copy-done.10, bf16[1,2048,128]{2,1,0:T(8,128)(2,1)} %copy-done.9, ...), custom_call_target="tpu_custom_call" | custom-call | tf_op jit(solution)/shard_map/pairs/pallas_call | solution.py:254
  (98 shorter events, 27.7 us)
Async XLA Ops:
  6.6 9.8 %collective-permute-start.3 = (bf16[1,2048,128]{2,1,0:T(8,128)(2,1)S(1)}, bf16[1,2048,128]{2,1,0:T(8,128)(2,1)S(1)}, u32[]{:S(2)}, u32[]{:S(2)}) collective-permute-start(bf16[1,2048,128]{2,1,0:T(8,128)(2,1)S(1)} %bitcast.17), channel_id=1, source_target_pairs={{16,0},{4,20},{24,8},{12,28},{17,1},{5,21},{25,9},{13,29},{18,2},{... | collective-permute-start | bytes 1572872 | tf_op jit(solution)/shard_map/ppermute | solution.py:293
  9.7 13.3 %collective-permute-start.2 = (bf16[1,2048,128]{2,1,0:T(8,128)(2,1)S(1)}, bf16[1,2048,128]{2,1,0:T(8,128)(2,1)S(1)}, u32[]{:S(2)}, u32[]{:S(2)}) collective-permute-start(bf16[1,2048,128]{2,1,0:T(8,128)(2,1)S(1)} %bitcast.18), channel_id=1, source_target_pairs={{0,8},{4,12},{8,0},{12,4},{16,24},{20,28},{24,16},{28,20},{1,9},{5... | collective-permute-start | bytes 1572872 | tf_op jit(solution)/shard_map/ppermute | solution.py:293
  11.0 15.4 %collective-permute-start.1 = (bf16[1,2048,128]{2,1,0:T(8,128)(2,1)S(1)}, bf16[1,2048,128]{2,1,0:T(8,128)(2,1)S(1)}, u32[]{:S(2)}, u32[]{:S(2)}) collective-permute-start(bf16[1,2048,128]{2,1,0:T(8,128)(2,1)S(1)} %bitcast.19), channel_id=1, source_target_pairs={{3,2},{2,1},{1,0},{7,6},{6,5},{5,4},{11,10},{10,9},{9,8},{15,14},{... | collective-permute-start | bytes 1572872 | tf_op jit(solution)/shard_map/ppermute | solution.py:314
  13.1 15.5 %collective-permute-start = (bf16[1,2048,128]{2,1,0:T(8,128)(2,1)S(1)}, bf16[1,2048,128]{2,1,0:T(8,128)(2,1)S(1)}, u32[]{:S(2)}, u32[]{:S(2)}) collective-permute-start(bf16[1,2048,128]{2,1,0:T(8,128)(2,1)S(1)} %bitcast.20), channel_id=1, source_target_pairs={{0,1},{1,2},{2,3},{4,5},{5,6},{6,7},{8,9},{9,10},{10,11},{12,13},{... | collective-permute-start | bytes 1572872 | tf_op jit(solution)/shard_map/ppermute | solution.py:314
  28.6 8.3 %collective-permute-start.7 = (bf16[1,2048,128]{2,1,0:T(8,128)(2,1)S(1)}, bf16[1,2048,128]{2,1,0:T(8,128)(2,1)S(1)}, u32[]{:S(2)}, u32[]{:S(2)}) collective-permute-start(bf16[1,2048,128]{2,1,0:T(8,128)(2,1)S(1)} %select_select_fusion.2.r_8_), channel_id=1, source_target_pairs={{16,0},{4,20},{24,8},{12,28},{17,1},{5,21},{25,9},{13,29},{18,2},{... | collective-permute-start | bytes 1572872 | tf_op jit(solution)/shard_map/ppermute | solution.py:293
  30.0 13.2 %collective-permute-start.6 = (bf16[1,2048,128]{2,1,0:T(8,128)(2,1)S(1)}, bf16[1,2048,128]{2,1,0:T(8,128)(2,1)S(1)}, u32[]{:S(2)}, u32[]{:S(2)}) collective-permute-start(bf16[1,2048,128]{2,1,0:T(8,128)(2,1)S(1)} %select_select_fusion.2.r_8_), channel_id=1, source_target_pairs={{0,8},{4,12},{8,0},{12,4},{16,24},{20,28},{24,16},{28,20},{1,9},{5... | collective-permute-start | bytes 1572872 | tf_op jit(solution)/shard_map/ppermute | solution.py:293
  30.3 14.7 %collective-permute-start.4 = (bf16[1,2048,128]{2,1,0:T(8,128)(2,1)S(1)}, bf16[1,2048,128]{2,1,0:T(8,128)(2,1)S(1)}, u32[]{:S(2)}, u32[]{:S(2)}) collective-permute-start(bf16[1,2048,128]{2,1,0:T(8,128)(2,1)S(1)} %collective-permute-done), channel_id=1, source_target_pairs={{1,2},{2,3},{5,6},{6,7},{9,10},{10,11},{13,14},{14,15},{17,18},{18... | collective-permute-start | bytes 1572872 | tf_op jit(solution)/shard_map/ppermute | solution.py:314
  33.5 12.4 %collective-permute-start.5 = (bf16[1,2048,128]{2,1,0:T(8,128)(2,1)S(1)}, bf16[1,2048,128]{2,1,0:T(8,128)(2,1)S(1)}, u32[]{:S(2)}, u32[]{:S(2)}) collective-permute-start(bf16[1,2048,128]{2,1,0:T(8,128)(2,1)S(1)} %collective-permute-done.1), channel_id=1, source_target_pairs={{2,1},{1,0},{6,5},{5,4},{10,9},{9,8},{14,13},{13,12},{18,17},{17,1... | collective-permute-start | bytes 1572872 | tf_op jit(solution)/shard_map/ppermute | solution.py:314
  35.6 10.3 %collective-permute-start.8 = (bf16[1,2048,128]{2,1,0:T(8,128)(2,1)S(1)}, bf16[1,2048,128]{2,1,0:T(8,128)(2,1)S(1)}, u32[]{:S(2)}, u32[]{:S(2)}) collective-permute-start(bf16[1,2048,128]{2,1,0:T(8,128)(2,1)S(1)} %collective-permute-done.2.r_4_), channel_id=1, source_target_pairs={{28,12},{0,16},{24,8},{4,20},{29,13},{1,17},{25,9},{5,21},{30,14},... | collective-permute-start | bytes 1572872 | tf_op jit(solution)/shard_map/ppermute | solution.py:293
  46.7 28.3 %collective-permute-start.14 = (bf16[4,2048,128]{2,1,0:T(8,128)(2,1)S(1)}, bf16[4,2048,128]{2,1,0:T(8,128)(2,1)}, u32[]{:S(2)}, u32[]{:S(2)}) collective-permute-start(bf16[4,2048,128]{2,1,0:T(8,128)(2,1)S(1)} %pad_maximum_fusion), channel_id=1, source_target_pairs={{0,4},{4,0},{8,12},{12,8},{16,20},{20,16},{24,28},{28,24},{1,5},{5... | collective-permute-start | bytes 6291464 | tf_op jit(solution)/shard_map/ppermute | solution.py:293
  50.0 10.2 %collective-permute-start.12 = (bf16[1,2048,128]{2,1,0:T(8,128)(2,1)S(1)}, bf16[1,2048,128]{2,1,0:T(8,128)(2,1)S(1)}, u32[]{:S(2)}, u32[]{:S(2)}) collective-permute-start(bf16[1,2048,128]{2,1,0:T(8,128)(2,1)S(1)} %select_select_fusion.1.r_13_), channel_id=1, source_target_pairs={{16,0},{4,20},{24,8},{12,28},{17,1},{5,21},{25,9},{13,29},{18,2},{... | collective-permute-start | bytes 1572872 | tf_op jit(solution)/shard_map/ppermute | solution.py:293
  54.1 13.9 %collective-permute-start.11 = (bf16[1,2048,128]{2,1,0:T(8,128)(2,1)S(1)}, bf16[1,2048,128]{2,1,0:T(8,128)(2,1)S(1)}, u32[]{:S(2)}, u32[]{:S(2)}) collective-permute-start(bf16[1,2048,128]{2,1,0:T(8,128)(2,1)S(1)} %select_select_fusion.1.r_13_), channel_id=1, source_target_pairs={{0,8},{4,12},{8,0},{12,4},{16,24},{20,28},{24,16},{28,20},{1,9},{5... | collective-permute-start | bytes 1572872 | tf_op jit(solution)/shard_map/ppermute | solution.py:293
  55.4 12.8 %collective-permute-start.9 = (bf16[1,2048,128]{2,1,0:T(8,128)(2,1)S(1)}, bf16[1,2048,128]{2,1,0:T(8,128)(2,1)S(1)}, u32[]{:S(2)}, u32[]{:S(2)}) collective-permute-start(bf16[1,2048,128]{2,1,0:T(8,128)(2,1)S(1)} %collective-permute-done.4), channel_id=1, source_target_pairs={{2,3},{6,7},{10,11},{14,15},{18,19},{22,23},{26,27},{30,31}} | collective-permute-start | bytes 1572872 | tf_op jit(solution)/shard_map/ppermute | solution.py:314
  57.2 11.0 %collective-permute-start.10 = (bf16[1,2048,128]{2,1,0:T(8,128)(2,1)S(1)}, bf16[1,2048,128]{2,1,0:T(8,128)(2,1)S(1)}, u32[]{:S(2)}, u32[]{:S(2)}) collective-permute-start(bf16[1,2048,128]{2,1,0:T(8,128)(2,1)S(1)} %collective-permute-done.5), channel_id=1, source_target_pairs={{1,0},{5,4},{9,8},{13,12},{17,16},{21,20},{25,24},{29,28}} | collective-permute-start | bytes 1572872 | tf_op jit(solution)/shard_map/ppermute | solution.py:314
  60.2 14.7 %collective-permute-start.13 = (bf16[1,2048,128]{2,1,0:T(8,128)(2,1)S(1)}, bf16[1,2048,128]{2,1,0:T(8,128)(2,1)S(1)}, u32[]{:S(2)}, u32[]{:S(2)}) collective-permute-start(bf16[1,2048,128]{2,1,0:T(8,128)(2,1)S(1)} %collective-permute-done.6.r_9_), channel_id=1, source_target_pairs={{28,12},{0,16},{24,8},{4,20},{29,13},{1,17},{25,9},{5,21},{30,14},... | collective-permute-start | bytes 1572872 | tf_op jit(solution)/shard_map/ppermute | solution.py:293
  75.7 21.3 %collective-permute-start.18 = (bf16[4,2048,128]{2,1,0:T(8,128)(2,1)S(1)}, bf16[4,2048,128]{2,1,0:T(8,128)(2,1)S(1)}, u32[]{:S(2)}, u32[]{:S(2)}) collective-permute-start(bf16[4,2048,128]{2,1,0:T(8,128)(2,1)S(1)} %pad_maximum_fusion.1), channel_id=1, source_target_pairs={{0,4},{4,0},{8,12},{12,8},{16,20},{20,16},{24,28},{28,24},{1,5},{5... | collective-permute-start | bytes 6291464 | tf_op jit(solution)/shard_map/ppermute | solution.py:293
  75.9 12.9 %collective-permute-start.16 = (bf16[1,2048,128]{2,1,0:T(8,128)(2,1)S(1)}, bf16[1,2048,128]{2,1,0:T(8,128)(2,1)S(1)}, u32[]{:S(2)}, u32[]{:S(2)}) collective-permute-start(bf16[1,2048,128]{2,1,0:T(8,128)(2,1)S(1)} %select_select_fusion.r_18_), channel_id=1, source_target_pairs={{16,0},{4,20},{24,8},{12,28},{17,1},{5,21},{25,9},{13,29},{18,2},{... | collective-permute-start | bytes 1572872 | tf_op jit(solution)/shard_map/ppermute | solution.py:293
  79.7 12.7 %collective-permute-start.15 = (bf16[1,2048,128]{2,1,0:T(8,128)(2,1)S(1)}, bf16[1,2048,128]{2,1,0:T(8,128)(2,1)S(1)}, u32[]{:S(2)}, u32[]{:S(2)}) collective-permute-start(bf16[1,2048,128]{2,1,0:T(8,128)(2,1)S(1)} %select_select_fusion.r_18_), channel_id=1, source_target_pairs={{0,8},{4,12},{8,0},{12,4},{16,24},{20,28},{24,16},{28,20},{1,9},{5... | collective-permute-start | bytes 1572872 | tf_op jit(solution)/shard_map/ppermute | solution.py:293
  80.1 17.0 %collective-permute-start.17 = (bf16[1,2048,128]{2,1,0:T(8,128)(2,1)S(1)}, bf16[1,2048,128]{2,1,0:T(8,128)(2,1)S(1)}, u32[]{:S(2)}, u32[]{:S(2)}) collective-permute-start(bf16[1,2048,128]{2,1,0:T(8,128)(2,1)S(1)} %collective-permute-done.11.r_14_), channel_id=1, source_target_pairs={{28,12},{0,16},{24,8},{4,20},{29,13},{1,17},{25,9},{5,21},{30,14},... | collective-permute-start | bytes 1572872 | tf_op jit(solution)/shard_map/ppermute | solution.py:293
  98.6 6.4 %collective-permute-start.21 = (bf16[4,2048,128]{2,1,0:T(8,128)(2,1)S(1)}, bf16[4,2048,128]{2,1,0:T(8,128)(2,1)}, u32[]{:S(2)}, u32[]{:S(2)}) collective-permute-start(bf16[4,2048,128]{2,1,0:T(8,128)(2,1)S(1)} %pad_maximum_fusion.2), channel_id=1, source_target_pairs={{0,4},{4,0},{8,12},{12,8},{16,20},{20,16},{24,28},{28,24},{1,5},{5... | collective-permute-start | bytes 6291464 | tf_op jit(solution)/shard_map/ppermute | solution.py:293
  99.0 6.0 %collective-permute-start.22 = (bf16[3,2048,128]{2,1,0:T(8,128)(2,1)S(1)}, bf16[3,2048,128]{2,1,0:T(8,128)(2,1)S(1)}, u32[]{:S(2)}, u32[]{:S(2)}) collective-permute-start(bf16[3,2048,128]{2,1,0:T(8,128)(2,1)S(1)} %pad_maximum_fusion.3), channel_id=1, source_target_pairs={{0,4},{4,0},{8,12},{12,8},{16,20},{20,16},{24,28},{28,24},{1,5},{5... | collective-permute-start | bytes 4718600 | tf_op jit(solution)/shard_map/ppermute | solution.py:293
  99.4 1.4 collective-permute-start.19
  100.1 0.7 collective-permute-start.20
  106.3 11.6 %collective-permute-start.23 = (bf16[2,2048,128]{2,1,0:T(8,128)(2,1)S(1)}, bf16[2,2048,128]{2,1,0:T(8,128)(2,1)S(1)}, u32[]{:S(2)}, u32[]{:S(2)}) collective-permute-start(bf16[2,2048,128]{2,1,0:T(8,128)(2,1)S(1)} %pad_maximum_fusion.4), channel_id=1, source_target_pairs={{0,4},{4,0},{8,12},{12,8},{16,20},{20,16},{24,28},{28,24},{1,5},{5... | collective-permute-start | bytes 3145736 | tf_op jit(solution)/shard_map/ppermute | solution.py:293
  (23 other events, 482.2 us)

commit v3 on v0

--- a/solution.py
+++ b/solution.py
@@ -2,11 +2,15 @@
 
 import jax
 import jax.numpy as jnp
+import numpy as np
 from jax import lax
+from jax.experimental import pallas as pl
+from jax.experimental.pallas import tpu as pltpu
 from jax.sharding import PartitionSpec as P
 
 LAGS = 128
 REACH = 3
+GROUP = 8
 
 
 def shifted(value, axis, by):
@@ -40,7 +44,7 @@
     return jnp.stack([gram_real, gram_imag], 2)
 
 
-def on_device(traces, band_bins, pair_blocks):
+def on_any_device(traces, band_bins, pair_blocks):
     channels, windows, length = traces.shape
     band_count = band_bins.shape[0]
     dft_matrix = make_dft_table(band_bins, length)
@@ -77,10 +81,347 @@
     return result[None]
 
 
+def spectra_kernel(traces_ref, fine_cos, fine_sin, step_cos, step_sin, out_ref, table, planes):
+    bins, fine = fine_cos.shape
+    groups, _, channels = planes.shape
+    windows = traces_ref.shape[0] // channels
+    for h in range(step_cos.shape[1]):
+        sc, ss = step_cos[:, h : h + 1], step_sin[:, h : h + 1]
+        cols = slice(h * fine, (h + 1) * fine)
+        table[:bins, cols] = (sc * fine_cos[...] - ss * fine_sin[...]).astype(jnp.bfloat16)
+        table[bins:, cols] = (-(ss * fine_cos[...] + sc * fine_sin[...])).astype(jnp.bfloat16)
+    for half in range(windows // 2):
+        rows = traces_ref[half * 2 * channels : (half + 1) * 2 * channels, :]
+        spectra = lax.dot_general(
+            table[...], rows, (((1,), (1,)), ((), ())), preferred_element_type=jnp.float32
+        )
+        power = jnp.sum(spectra * spectra, axis=0, keepdims=True)
+        white = spectra / jnp.sqrt(power / bins + 1e-06)
+        for w in range(2):
+            for c in range(2):
+                first = c * GROUP * windows + half * 2 + w
+                planes[:, pl.ds(first, GROUP, stride=windows), :] = white[
+                    c * bins : (c + 1) * bins, w * channels : (w + 1) * channels
+                ].reshape(groups, GROUP, channels)
+    out_ref[...] = planes[...].reshape(out_ref.shape).astype(jnp.bfloat16)
+
+
+def make_slab(traces, band_bins):
+    channels, windows, length = traces.shape
+    bins = band_bins.shape[0]
+    fine = 128
+    rows = traces.transpose(1, 0, 2).reshape(windows * channels, length)
+    sample_idx = jnp.concatenate([jnp.arange(fine), jnp.arange(length // fine) * fine])
+    phase_int = band_bins[:, None] * sample_idx[None, :].astype(jnp.int32) % length
+    phases = phase_int.astype(jnp.float32) * (2.0 * math.pi / length)
+    cos, sin = jnp.cos(phases), jnp.sin(phases)
+    return pl.pallas_call(
+        spectra_kernel,
+        out_shape=jax.ShapeDtypeStruct((bins * windows * 2, channels), jnp.bfloat16),
+        scratch_shapes=[
+            pltpu.VMEM((2 * bins, length), jnp.bfloat16),
+            pltpu.VMEM((bins // GROUP, GROUP * windows * 2, channels), jnp.float32),
+        ],
+        compiler_params=pltpu.CompilerParams(vmem_limit_bytes=48 << 20),
+        name="spectra",
+    )(rows, cos[:, :fine], sin[:, :fine], cos[:, fine:], sin[:, fine:])
+
+
+def left_kernel(z, *refs, per_step):
+    slabs, (out_ref, choice, mask) = refs[:-3], refs[-3:]
+    m, k = mask.shape
+    channels = slabs[0].shape[1]
+    group_rows = k // len(slabs)
+    half = group_rows // 2
+    rows_out = m // (2 * GROUP)
+
+    @pl.when(pl.program_id(0) == 0)
+    def _():
+        row = lax.broadcasted_iota(jnp.int32, (m, 2 * channels), 0)
+        col = lax.broadcasted_iota(jnp.int32, (m, 2 * channels), 1)
+        wanted = row // (2 * GROUP) + z[0] * rows_out + (row % 2) * channels
+        choice[...] = jnp.where(col == wanted, 1.0, 0.0).astype(jnp.bfloat16)
+        row = lax.broadcasted_iota(jnp.int32, (m, k), 0)
+        col = lax.broadcasted_iota(jnp.int32, (m, k), 1)
+        bin_of_col = col % half // (half // GROUP)
+        mask[...] = jnp.where(bin_of_col == row // 2 % GROUP, 1.0, 0.0)
+
+    for u in range(per_step):
+        pieces = []
+        for slab in slabs:
+            real = slab[u * group_rows : u * group_rows + half, :]
+            imag = slab[u * group_rows + half : (u + 1) * group_rows, :]
+            pieces.append(jnp.concatenate([real, imag], 1))
+            pieces.append(jnp.concatenate([imag, -real], 1))
+        both = jnp.concatenate(pieces, 0)
+        rows = lax.dot_general(
+            choice[...], both, (((1,), (1,)), ((), ())), preferred_element_type=jnp.float32
+        )
+        out_ref[u] = (rows * mask[...]).astype(jnp.bfloat16)
+
+
+def make_left(slabs, z, rows_out, bins):
+    slab_rows, channels = slabs[0].shape
+    groups = bins // GROUP
+    m, k = rows_out * GROUP * 2, slab_rows // groups * len(slabs)
+    per_step = 4
+    return pl.pallas_call(
+        lambda *r: left_kernel(*r, per_step=per_step),
+        grid_spec=pltpu.PrefetchScalarGridSpec(
+            num_scalar_prefetch=1,
+            grid=(groups // per_step,),
+            in_specs=[
+                pl.BlockSpec((slab_rows // groups * per_step, channels), lambda i, s: (i, 0))
+            ]
+            * len(slabs),
+            out_specs=pl.BlockSpec((per_step, m, k), lambda i, s: (i, 0, 0)),
+            scratch_shapes=[
+                pltpu.VMEM((m, 2 * channels), jnp.bfloat16),
+                pltpu.VMEM((m, k), jnp.float32),
+            ],
+        ),
+        out_shape=jax.ShapeDtypeStruct((groups, m, k), jnp.bfloat16),
+        compiler_params=pltpu.CompilerParams(vmem_limit_bytes=32 << 20),
+        name="left",
+    )(z.reshape(1), *slabs)
+
+
+CHUNKS = 4
+GROUP_UNROLL = 4
+ROW_UNROLL = 4
+
+
+def pairs_kernel(slots, left_ref, lag_ref, *refs, arrays, norm):
+    sources, (out_ref, partner, gram, stage, in_sems, out_sems) = refs[: len(arrays)], refs[len(arrays) :]
+    groups, m, k = left_ref.shape
+    slot_count, slabs, slab_rows, channels = partner.shape
+    group_rows = k // slabs
+    chunk_rows = slab_rows // CHUNKS
+    lanes = slot_count * channels
+
+    def fetch(source, s, r, chunk):
+        rows = pl.ds(chunk * chunk_rows, chunk_rows)
+        return pltpu.make_async_copy(source.at[rows], partner.at[s, r, rows], in_sems.at[chunk, s, r])
+
+    for s in range(slot_count):
+        for r in range(slabs):
+            slot = slots[s * slabs + r]
+            for source, (first, count, holds) in zip(sources, arrays):
+                if r in holds:
+
+                    @pl.when((slot >= first) & (slot < first + count))
+                    def _():
+                        for chunk in range(CHUNKS):
+                            fetch(source.at[slot - first], s, r, chunk).start()
+
+    per_chunk = groups // CHUNKS
+
+    for chunk in range(CHUNKS):
+        for s in range(slot_count):
+            for r in range(slabs):
+                fetch(sources[0].at[0], s, r, chunk).wait()
+
+        @pl.loop(0, per_chunk // GROUP_UNROLL)
+        def _(i):
+            for u in range(GROUP_UNROLL):
+                g = chunk * per_chunk + i * GROUP_UNROLL + u
+                rows = pl.ds(pl.multiple_of(g * group_rows, group_rows), group_rows)
+                right = jnp.concatenate(
+                    [partner[s, :, rows, :].reshape(k, channels) for s in range(slot_count)], 1
+                )
+                product = jnp.dot(left_ref[g], right, preferred_element_type=jnp.float32)
+                cols = pl.ds(pl.multiple_of(g * 2 * GROUP, 2 * GROUP), 2 * GROUP)
+                gram[:, cols, :] = product.astype(jnp.bfloat16).reshape(
+                    m // (2 * GROUP), 2 * GROUP, lanes
+                )
+
+    steps = gram.shape[0] // ROW_UNROLL
+
+    def write(i, b):
+        return pltpu.make_async_copy(
+            stage.at[b], out_ref.at[pl.ds(i * ROW_UNROLL, ROW_UNROLL)], out_sems.at[b]
+        )
+
+    @pl.loop(0, steps)
+    def _(i):
+        b = lax.rem(i, 2)
+
+        @pl.when(i >= 2)
+        def _():
+            write(i - 2, b).wait()
+
+        for u in range(ROW_UNROLL):
+            lagged = jnp.dot(
+                lag_ref[...], gram[i * ROW_UNROLL + u], preferred_element_type=jnp.float32
+            )
+            for s in range(slot_count):
+                stage[b, u, s] = (lagged[:, s * channels : (s + 1) * channels] * norm).T
+        write(i, b).start()
+
+    for i in range(steps - 2, steps):
+        write(i, i % 2).wait()
+
+
+def correlate(slots, left, lag_rows, held, slot_count, norm):
+    groups, m, k = left.shape
+    rows_out = m // (2 * GROUP)
+    arrays, first = [], 0
+    for value, holds in held:
+        arrays.append((first, value.shape[0], holds))
+        first += value.shape[0]
+    slab_rows, channels = held[0][0].shape[1:]
+    slabs = slots.shape[0] // slot_count
+    lag_count, entries = lag_rows.shape
+    anywhere = pl.BlockSpec(memory_space=pl.ANY)
+    in_vmem = pl.BlockSpec(memory_space=pltpu.VMEM)
+    return pl.pallas_call(
+        lambda *r: pairs_kernel(*r, arrays=arrays, norm=norm),
+        in_specs=[pl.BlockSpec(memory_space=pltpu.SMEM), in_vmem, in_vmem] + [anywhere] * len(held),
+        out_specs=anywhere,
+        scratch_shapes=[
+            pltpu.VMEM((slot_count, slabs, slab_rows, channels), jnp.bfloat16),
+            pltpu.VMEM((rows_out, entries, slot_count * channels), jnp.bfloat16),
+            pltpu.VMEM((2, ROW_UNROLL, slot_count, channels, lag_count), jnp.float32),
+            pltpu.SemaphoreType.DMA((CHUNKS, slot_count, slabs)),
+            pltpu.SemaphoreType.DMA((2,)),
+        ],
+        out_shape=jax.ShapeDtypeStruct((rows_out, slot_count, channels, lag_count), jnp.float32),
+        compiler_params=pltpu.CompilerParams(vmem_limit_bytes=36 << 20),
+        name="pairs",
+    )(slots, left, lag_rows, *[value for value, _ in held])
+
+
+X_PAIRS = [(i, i ^ 2) for i in range(8)]
+Y_PAIRS = [(4, 0), (1, 5), (6, 2), (3, 7)]
+Y_ON = [(7, 3), (0, 4)]
+X_ON = [(0, 2), (7, 5)]
+CORE_PAIRS = [(i, i ^ 1) for i in range(8)]
+
+
+def moved(what, pairs):
+    after = [[None] * 8 for _ in what]
+    for src, dst in pairs:
+        for old, new in zip(what, after):
+            new[dst] = old[src]
+    return after
+
+
+class Held:
+    def __init__(self, value, what):
+        self.value, self.what = value, what
+
+    def hop(self, pairs):
+        return Held(lax.ppermute(self.value, "chan", pairs), moved(self.what, pairs))
+
+
+def join(*parts):
+    return Held(jnp.concatenate([p.value for p in parts], 0), [w for p in parts for w in p.what])
+
+
+def where_device(me, devices, first, second):
+    here = jnp.asarray(np.isin(np.arange(8), devices))[me]
+    what = [
+        [one[i] if i in devices else other[i] for i in range(8)]
+        for one, other in zip(first.what, second.what)
+    ]
+    return Held(jnp.where(here, first.value, second.value), what)
+
+
+def together(*parts):
+    return lax.optimization_barrier(parts)
+
+
+jax.tree_util.register_pytree_node(
+    Held,
+    lambda held: ((held.value,), tuple(tuple(row) for row in held.what)),
+    lambda what, children: Held(children[0], [list(row) for row in what]),
+)
+
+
+def on_device(traces, band_bins, pair_blocks):
+    channels, windows, length = traces.shape
+    bins = band_bins.shape[0]
+    z = lax.axis_index("freq")
+    me = lax.axis_index("chan")
+    slot_count = pair_blocks.shape[1]
+
+    lag_idx = jnp.arange(LAGS, dtype=jnp.int32) - LAGS // 2
+    phases = (lag_idx[:, None] * band_bins[None, :] % length).astype(jnp.float32)
+    phases = phases * (2.0 * math.pi / length)
+    lag_rows = jnp.stack([jnp.cos(phases), -jnp.sin(phases)], 2).reshape(LAGS, 2 * bins)
+    lag_rows = lag_rows.astype(jnp.bfloat16)
+
+    def along_z(value, pairs):
+        return lax.ppermute(value, "freq", pairs)
+
+    def slab_of(value, r):
+        return Held(value, [[(i, r) for i in range(8)]])
+
+    def over_y(straight, came_over_x):
+        mixed = where_device(me, [0, 7], came_over_x, straight)
+        return mixed.hop(Y_PAIRS + Y_ON)
+
+    s0 = make_slab(traces, band_bins)[None]
+    q0 = slab_of(s0, 0)
+    y0 = q0.hop(Y_PAIRS)
+    down1, up1 = along_z(s0, [(3, 2), (2, 1), (1, 0)]), along_z(s0, [(0, 1), (1, 2), (2, 3)])
+    x0 = q0.hop(X_PAIRS)
+    y0, down1, up1, x0, lag_rows = together(y0, down1, up1, x0, lag_rows)
+
+    q1 = slab_of(lax.select_n(z, down1, up1, down1, up1), 1)
+    up2, down2 = along_z(up1, [(1, 2), (2, 3)]), along_z(down1, [(2, 1), (1, 0)])
+    y1 = over_y(q1, x0)
+    e0 = y0.hop(X_ON)
+    x1 = q1.hop(X_PAIRS)
+    up2, down2, y1, e0, x1 = together(up2, down2, y1, e0, x1)
+
+    q2 = slab_of(lax.select_n(z, down2, down1, up1, up2), 2)
+    last = along_z(jnp.where(z == 2, up2, down2), [(2, 3), (1, 0)])
+    a = join(q0, x0, y0, q1, x1, y1, e0).hop(CORE_PAIRS)
+    y2 = over_y(q2, x1)
+    e1 = y1.hop(X_ON)
+    x2 = q2.hop(X_PAIRS)
+    last, a, y2, e1, x2 = together(last, a, y2, e1, x2)
+
+    q3 = slab_of(lax.select_n(z, last, down2, up2, last), 3)
+    b = join(q2, x2, y2, e1).hop(CORE_PAIRS)
+    y3 = over_y(q3, x2)
+    e2 = y2.hop(X_ON)
+    x3 = q3.hop(X_PAIRS)
+    left = make_left([q.value[0] for q in (q0, q1, q2, q3)], z, channels // 4, bins)
+    b, y3, e2, x3, left = together(b, y3, e2, x3, left)
+
+    c = join(q3, x3, y3, e2).hop(CORE_PAIRS)
+    y4, e3 = x3.hop(Y_ON), y3.hop(X_ON)
+
+    held = [q0, q1, q2, q3, x0, x1, x2, x3, y0, y1, y2, y3, y4, e0, e1, e2, e3, a, b, c]
+    whats = [h.what for h in held] + [moved(y4.what + e3.what, CORE_PAIRS)]
+    table = np.zeros((8, 8, 4), np.int32)
+    all_holds = [set() for _ in whats]
+    index = sum(len(what) for what in whats)
+    for what, holds in zip(reversed(whats), reversed(all_holds)):
+        for item in reversed(what):
+            index -= 1
+            for device, block_slab in enumerate(item):
+                if block_slab is not None:
+                    table[device, block_slab[0], block_slab[1]] = index
+                    holds.add(block_slab[1])
+    mine = jnp.asarray(table)[me]
+    slots = jnp.concatenate([mine[pair_blocks[0, s]] for s in range(slot_count)])
+
+    y4, e3, c, slots = together(y4, e3, c, slots)
+    d = join(y4, e3).hop(CORE_PAIRS)
+    held = [q0, q1, q2, q3, x0, x1, x2, x3, y0, y1, y2, y3, y4, e0, e1, e2, e3, a, b, c, d]
+    places = [(h.value, holds) for h, holds in zip(held, all_holds)]
+    norm = 1.0 / math.sqrt(4 * windows * bins)
+    return correlate(slots, left, lag_rows, places, slot_count, norm)[None]
+
+
 def solution(mesh):
     placed = (P("chan", "freq", None), P(), P("chan", None))
+    fits = mesh.shape["chan"] == 8 and mesh.shape["freq"] == 4
     return jax.shard_map(
-        on_device,
+        on_device if fits else on_any_device,
         mesh=mesh,
         in_specs=placed,
         out_specs=P("chan", "freq", None, None, None),

time: 814 us -> 170 us (0.21); the launches traced: 804 us -> 168 us
  waiting for transfers between devices: 565 us -> 38.3 us
  local copies, waits for them, and re-layouts: 100 us -> 25.5 us
  matrix products: 58.7 us -> 0 us
  Pallas kernels: 0 us -> 29.4 us
  starting transfers between devices: 25.5 us -> 51.7 us
  other arithmetic: 36.1 us -> 17.4 us
  blocking collectives: 16 us -> 0 us
    all_to_all x1 -> x0, waiting for transfers between devices: 538 us -> none  [on_device(): lax.all_to_all(cross_gram, 'freq', split_axis=0, concat_axis=4, tiled=True)]
    dot_general x8 -> x0, matrix products: 58.7 us -> none  [the longest x1 43.7 us: on_device(): jnp.dot(gram_block.reshape(-1, 2 * band_count), lag_matrix, precision=lax...]
    reshape x4 -> x0, local copies, waits for them, and re-layouts: 39.9 us -> none  [the longest x1 36.4 us: on_device(): gram_block.reshape(-1, 2 * band_count)]
    ppermute x6 -> x22, starting transfers between devices: 14.8 us -> 51.7 us  [the longest x17 38.2 us: hop(): lax.ppermute(self.value, 'chan', pairs)]
    another operation x5 -> x2, other arithmetic: 35.3 us -> 0.62 us  [the longest x4 24.9 us: on_device(): cross_gram = jnp.stack(gram_list, 1)]
    all_to_all x3 -> x0, local copies, waits for them, and re-layouts: 34.1 us -> none  [the longest x1 33.6 us: on_device(): lax.all_to_all(cross_gram, 'freq', split_axis=0, concat_axis=4, tiled=True)]
    pallas_call x0 -> x3, Pallas kernels: none -> 29.4 us  [the longest x1 23.5 us: correlate(): pl.pallas_call(lambda *r: pairs_kernel(*r, arrays=arrays, norm=norm), in_...]
    another operation x2 -> x1, local copies, waits for them, and re-layouts: 24.8 us -> 0.12 us  [on_device(): jnp.stack([jnp.cos(phases), -jnp.sin(phases)], 2).reshape(LAGS, 2 * bins)]
  transfers between devices with their start and end apart: 7 -> 22, of which waited for: 5 -> 11; matrix products, arithmetic and copies ran while one was open for 0% -> 5% of each run, Pallas kernels for 0% -> 2%
where the time goes in v3:
time: 170 us; the launch traced here: 168 us
  starting transfers between devices  51.7 us (30%)
  waiting for transfers between devices  38.3 us (23%)
  Pallas kernels  29.4 us (17%)
  local copies, waits for them, and re-layouts  25.5 us (15%)
  other arithmetic  17.4 us (10%)
  between operations  6.16 us (4%)
    ppermute x17, starting transfers between devices, hop(): lax.ppermute(self.value, 'chan', pairs)  38.2 us
    ppermute x17, waiting for transfers between devices, hop(): lax.ppermute(self.value, 'chan', pairs)  31.2 us
    pallas_call x1, Pallas kernels, correlate(): pl.pallas_call(lambda *r: pairs_kernel(*r, arrays=arrays, norm=norm), in_...  23.5 us
    unnamed x46, local copies, waits for them, and re-layouts  19.5 us
    ppermute x5, starting transfers between devices, along_z(): return lax.ppermute(value, 'freq', pairs)  13.5 us
    select_n x3, other arithmetic, where_device(): return Held(jnp.where(here, first.value, second.value), what)  7.45 us
    ppermute x5, waiting for transfers between devices, along_z(): return lax.ppermute(value, 'freq', pairs)  7.06 us
    concatenate x3, other arithmetic, join(): jnp.concatenate([p.value for p in parts], 0)  6.06 us
  transfers between devices with their start and end apart: 22, of which 11 were waited for; matrix products, arithmetic and copies ran while one was open for 5% of the time, Pallas kernels for 2%

profile of v3, /device:TPU:17, one launch (start us, length us, event | category | flops | bytes accessed | tf_op | source)
XLA Modules:
  0.0 168.4 jit_solution(1536848907245089151)
XLA Ops:
  1.9 2.8 %copy.11 = bf16[4,128,2048]{2,1,0:T(8,128)(2,1)S(1)} copy(bf16[4,128,2048]{2,0,1:T(4,128)(2,1)} %bitcast.29) | data formatting | bytes 4194304 | tf_op jit(solution)/shard_map/transpose | solution.py:113
  7.9 3.2 %collective-permute-start.2 = (bf16[1,2048,128]{2,1,0:T(8,128)(2,1)S(1)}, bf16[1,2048,128]{2,1,0:T(8,128)(2,1)}, u32[]{:S(2)}, u32[]{:S(2)}) collective-permute-start(bf16[1,2048,128]{2,1,0:T(8,128)(2,1)S(1)} %bitcast.21), channel_id=1, source_target_pairs={{0,1},{1,2},{2,3},{4,5},{5,6},{6,7},{8,9},{9,10},{10,11},{12,13},{... | collective-permute-start | bytes 1572872 | tf_op jit(solution)/shard_map/ppermute | solution.py:355
  13.1 3.2 %collective-permute-start = (bf16[1,2048,128]{2,1,0:T(8,128)(2,1)S(1)}, bf16[1,2048,128]{2,1,0:T(8,128)(2,1)S(1)}, u32[]{:S(2)}, u32[]{:S(2)}) collective-permute-start(bf16[1,2048,128]{2,1,0:T(8,128)(2,1)S(1)} %bitcast.23), channel_id=1, source_target_pairs={{16,0},{4,20},{24,8},{12,28},{17,1},{5,21},{25,9},{13,29},{18,2},{... | collective-permute-start | bytes 1572872 | tf_op jit(solution)/shard_map/ppermute | solution.py:314
  19.5 2.8 %collective-permute-done.2 = bf16[1,2048,128]{2,1,0:T(8,128)(2,1)} collective-permute-done((bf16[1,2048,128]{2,1,0:T(8,128)(2,1)S(1)}, bf16[1,2048,128]{2,1,0:T(8,128)(2,1)}, u32[]{:S(2)}, u32[]{:S(2)}) %collective-permute-start.2) | collective-permute-done | bytes 524320 | tf_op jit(solution)/shard_map/ppermute | solution.py:355
  22.3 2.9 %collective-permute-done.1 = bf16[1,2048,128]{2,1,0:T(8,128)(2,1)} collective-permute-done((bf16[1,2048,128]{2,1,0:T(8,128)(2,1)S(1)}, bf16[1,2048,128]{2,1,0:T(8,128)(2,1)}, u32[]{:S(2)}, u32[]{:S(2)}) %collective-permute-start.1) | collective-permute-done | bytes 524320 | tf_op jit(solution)/shard_map/ppermute | solution.py:355
  27.2 5.0 %collective-permute-start.5 = (bf16[1,2048,128]{2,1,0:T(8,128)(2,1)}, bf16[1,2048,128]{2,1,0:T(8,128)(2,1)}, u32[]{:S(2)}, u32[]{:S(2)}) collective-permute-start(bf16[1,2048,128]{2,1,0:T(8,128)(2,1)} %collective-permute-done.1), channel_id=1, source_target_pairs={{2,1},{1,0},{6,5},{5,4},{10,9},{9,8},{14,13},{13,12},{18,17},{17,1... | collective-permute-start | bytes 1572872 | tf_op jit(solution)/shard_map/ppermute | solution.py:355
  36.5 4.6 %collective-permute-start.6 = (bf16[1,2048,128]{2,1,0:T(8,128)(2,1)}, bf16[1,2048,128]{2,1,0:T(8,128)(2,1)}, u32[]{:S(2)}, u32[]{:S(2)}) collective-permute-start(bf16[1,2048,128]{2,1,0:T(8,128)(2,1)} %broadcast_select_fusion.3), channel_id=1, source_target_pairs={{16,0},{4,20},{24,8},{12,28},{28,12},{0,16},{17,1},{5,21},{25,9},{... | collective-permute-start | bytes 1572872 | tf_op jit(solution)/shard_map/ppermute | solution.py:314
  42.4 6.9 %collective-permute-done.6.r_12_ = bf16[1,2048,128]{2,1,0:T(8,128)(2,1)} collective-permute-done((bf16[1,2048,128]{2,1,0:T(8,128)(2,1)}, bf16[1,2048,128]{2,1,0:T(8,128)(2,1)}, u32[]{:S(2)}, u32[]{:S(2)}) %collective-permute-start.6) | collective-permute-done | bytes 524320 | tf_op jit(solution)/shard_map/ppermute | solution.py:314
  49.3 4.9 %collective-permute-done.8.r_8_ = bf16[1,2048,128]{2,1,0:T(8,128)(2,1)S(1)} collective-permute-done((bf16[1,2048,128]{2,1,0:T(8,128)(2,1)S(1)}, bf16[1,2048,128]{2,1,0:T(8,128)(2,1)S(1)}, u32[]{:S(2)}, u32[]{:S(2)}) %collective-permute-start.8) | collective-permute-done | bytes 524320 | tf_op jit(solution)/shard_map/ppermute | solution.py:314
  54.2 3.4 %broadcast_select_fusion.2 = (bf16[1,2048,128]{2,1,0:T(8,128)(2,1)S(1)}, bf16[1,2048,128]{2,1,0:T(8,128)(2,1)S(1)}, bf16[1,2048,128]{2,1,0:T(8,128)(2,1)S(1)}, bf16[7,2048,128]{2,1,0:T(8,128)(2,1)}) fusion(bf16[1,2048,128]{2,1,0:T(8,128)(2,1)S(1)} %collective-permute-done.8.r_8_, pred[]{:T(512)} %bitcast.4, bf16[1,2048,128]{2,1,0:T(8,128)(2,1)} %collective-permute-done.2, ...), kind=kLoop, calls=%fused_computation.8 | loop fusion | flops 1310720 | bytes 4719108 | tf_op jit(solution)/shard_map/jit(_where)/select_n | solution.py:327
  64.6 2.2 %collective-permute-start.13 = (bf16[1,2048,128]{2,1,0:T(8,128)(2,1)S(1)}, bf16[1,2048,128]{2,1,0:T(8,128)(2,1)S(1)}, u32[]{:S(2)}, u32[]{:S(2)}) collective-permute-start(bf16[1,2048,128]{2,1,0:T(8,128)(2,1)S(1)} %get-tuple-element.56.r_5_), channel_id=1, source_target_pairs={{0,8},{4,12},{8,0},{12,4},{16,24},{20,28},{24,16},{28,20},{1,9},{5... | collective-permute-start | bytes 1572872 | tf_op jit(solution)/shard_map/ppermute | solution.py:314
  67.5 7.1 %collective-permute-done.11.r_13_ = bf16[1,2048,128]{2,1,0:T(8,128)(2,1)S(1)} collective-permute-done((bf16[1,2048,128]{2,1,0:T(8,128)(2,1)S(1)}, bf16[1,2048,128]{2,1,0:T(8,128)(2,1)S(1)}, u32[]{:S(2)}, u32[]{:S(2)}) %collective-permute-start.11) | collective-permute-done | bytes 524320 | tf_op jit(solution)/shard_map/ppermute | solution.py:314
  76.0 3.3 %collective-permute-done.13.r_9_ = bf16[1,2048,128]{2,1,0:T(8,128)(2,1)S(1)} collective-permute-done((bf16[1,2048,128]{2,1,0:T(8,128)(2,1)S(1)}, bf16[1,2048,128]{2,1,0:T(8,128)(2,1)S(1)}, u32[]{:S(2)}, u32[]{:S(2)}) %collective-permute-start.13) | collective-permute-done | bytes 524320 | tf_op jit(solution)/shard_map/ppermute | solution.py:314
  82.2 5.3 %collective-permute-start.14 = (bf16[4,2048,128]{2,1,0:T(8,128)(2,1)S(1)}, bf16[4,2048,128]{2,1,0:T(8,128)(2,1)S(1)}, u32[]{:S(2)}, u32[]{:S(2)}) collective-permute-start(bf16[4,2048,128]{2,1,0:T(8,128)(2,1)S(1)} %pad_maximum_fusion), channel_id=1, source_target_pairs={{0,4},{4,0},{8,12},{12,8},{16,20},{20,16},{24,28},{28,24},{1,5},{5... | collective-permute-start | bytes 6291464 | tf_op jit(solution)/shard_map/ppermute | solution.py:314
  89.5 4.3 %collective-permute-start.15 = (bf16[1,2048,128]{2,1,0:T(8,128)(2,1)S(1)}, bf16[1,2048,128]{2,1,0:T(8,128)(2,1)}, u32[]{:S(2)}, u32[]{:S(2)}) collective-permute-start(bf16[1,2048,128]{2,1,0:T(8,128)(2,1)S(1)} %get-tuple-element.53), channel_id=1, source_target_pairs={{16,0},{4,20},{24,8},{12,28},{28,12},{0,16},{17,1},{5,21},{25,9},{... | collective-permute-start | bytes 1572872 | tf_op jit(solution)/shard_map/ppermute | solution.py:314
  95.3 4.0 %left.1.r_1_ = bf16[32,512,256]{2,1,0:T(8,128)(2,1)S(1)} custom-call(s32[1]{0:T(128)} %bitcast.5.r_0_, bf16[2048,128]{1,0:T(8,128)(2,1)S(1)} %spectra.1.r_1_, bf16[2048,128]{1,0:T(8,128)(2,1)S(1)} %bitcast.25, bf16[2048,128]{1,0:T(8,128)(2,1)S(1)} %bitcast.26, bf16[2048,128]{1,0:T(8,128)(2,1)S(1)} %bitcast.27), custom_call_target="tpu_custom_call" | custom-call | tf_op jit(solution)/shard_map/left/pallas_call | solution.py:168
  99.3 3.3 %copy-done = bf16[32,512,256]{2,1,0:T(8,128)(2,1)} copy-done((bf16[32,512,256]{2,1,0:T(8,128)(2,1)}, bf16[32,512,256]{2,1,0:T(8,128)(2,1)S(1)}, u32[]{:S(2)}) %copy-start) | copy-done | bytes 8388632
  103.7 3.7 %collective-permute-done.17.r_10_ = bf16[1,2048,128]{2,1,0:T(8,128)(2,1)} collective-permute-done((bf16[1,2048,128]{2,1,0:T(8,128)(2,1)S(1)}, bf16[1,2048,128]{2,1,0:T(8,128)(2,1)}, u32[]{:S(2)}, u32[]{:S(2)}) %collective-permute-start.17) | collective-permute-done | bytes 524320 | tf_op jit(solution)/shard_map/ppermute | solution.py:314
  107.4 3.5 %pad_maximum_fusion.1 = bf16[4,2048,128]{2,1,0:T(8,128)(2,1)} fusion(bf16[1,2048,128]{2,1,0:T(8,128)(2,1)S(1)} %collective-permute-done.16.r_18_, bf16[1,2048,128]{2,1,0:T(8,128)(2,1)} %collective-permute-done.15.r_14_, bf16[1,2048,128]{2,1,0:T(8,128)(2,1)} %collective-permute-done.17.r_10_, bf16[1,2048,128]{2,1,0:T(8,128)(2,1)S(1)} %get-tuple-element.54.r_6_), kind=kLoop, calls=%fused_computation.1 | loop fusion | flops 3145728 | bytes 4194304 | tf_op jit(solution)/shard_map/concatenate | solution.py:318
  111.8 4.1 %collective-permute-start.20 = (bf16[4,2048,128]{2,1,0:T(8,128)(2,1)}, bf16[4,2048,128]{2,1,0:T(8,128)(2,1)}, u32[]{:S(2)}, u32[]{:S(2)}) collective-permute-start(bf16[4,2048,128]{2,1,0:T(8,128)(2,1)} %pad_maximum_fusion.1), channel_id=1, source_target_pairs={{0,4},{4,0},{8,12},{12,8},{16,20},{20,16},{24,28},{28,24},{1,5},{5... | collective-permute-start | bytes 6291464 | tf_op jit(solution)/shard_map/ppermute | solution.py:314
  126.0 2.3 %pad_maximum_fusion.2 = bf16[2,2048,128]{2,1,0:T(8,128)(2,1)} fusion(bf16[1,2048,128]{2,1,0:T(8,128)(2,1)} %collective-permute-done.19.r_19_, bf16[1,2048,128]{2,1,0:T(8,128)(2,1)} %collective-permute-done.18.r_15_), kind=kLoop, calls=%fused_computation.2 | loop fusion | flops 524288 | bytes 2097152 | tf_op jit(solution)/shard_map/concatenate | solution.py:318
  128.3 4.0 %collective-permute-start.21 = (bf16[2,2048,128]{2,1,0:T(8,128)(2,1)}, bf16[2,2048,128]{2,1,0:T(8,128)(2,1)}, u32[]{:S(2)}, u32[]{:S(2)}) collective-permute-start(bf16[2,2048,128]{2,1,0:T(8,128)(2,1)} %pad_maximum_fusion.2), channel_id=1, source_target_pairs={{0,4},{4,0},{8,12},{12,8},{16,20},{20,16},{24,28},{28,24},{1,5},{5... | collective-permute-start | bytes 3145736 | tf_op jit(solution)/shard_map/ppermute | solution.py:314
  132.4 2.5 %collective-permute-done.21.r_23_ = bf16[2,2048,128]{2,1,0:T(8,128)(2,1)} collective-permute-done((bf16[2,2048,128]{2,1,0:T(8,128)(2,1)}, bf16[2,2048,128]{2,1,0:T(8,128)(2,1)}, u32[]{:S(2)}, u32[]{:S(2)}) %collective-permute-start.21) | collective-permute-done | bytes 1048608 | tf_op jit(solution)/shard_map/ppermute | solution.py:314
  144.8 23.5 %pairs.1 = f32[32,3,128,128]{3,2,1,0:T(8,128)} custom-call(s32[12]{0:T(128)S(1)} %pad_add_fusion.1.r_0_, bf16[32,512,256]{2,1,0:T(8,128)(2,1)} %copy-done, bf16[128,512]{1,0:T(8,128)(2,1)S(1)} %copy.13.r_2_, bf16[1,2048,128]{2,1,0:T(8,128)(2,1)S(1)} %bitcast.24, bf16[1,2048,128]{2,1,0:T(8,128)(2,1)S(1)} %get-tuple-element.58.r_4_, ...), custom_call_target="tpu_custom_call" | custom-call | tf_op jit(solution)/shard_map/pairs/pallas_call | solution.py:277
  (95 shorter events, 49.8 us)
Async XLA Ops:
  6.6 13.0 %collective-permute-start.3 = (bf16[1,2048,128]{2,1,0:T(8,128)(2,1)S(1)}, bf16[1,2048,128]{2,1,0:T(8,128)(2,1)S(1)}, u32[]{:S(2)}, u32[]{:S(2)}) collective-permute-start(bf16[1,2048,128]{2,1,0:T(8,128)(2,1)S(1)} %bitcast.20), channel_id=1, source_target_pairs={{0,8},{4,12},{8,0},{12,4},{16,24},{20,28},{24,16},{28,20},{1,9},{5... | collective-permute-start | bytes 1572872 | tf_op jit(solution)/shard_map/ppermute | solution.py:314
  7.9 14.5 %collective-permute-start.2 = (bf16[1,2048,128]{2,1,0:T(8,128)(2,1)S(1)}, bf16[1,2048,128]{2,1,0:T(8,128)(2,1)}, u32[]{:S(2)}, u32[]{:S(2)}) collective-permute-start(bf16[1,2048,128]{2,1,0:T(8,128)(2,1)S(1)} %bitcast.21), channel_id=1, source_target_pairs={{0,1},{1,2},{2,3},{4,5},{5,6},{6,7},{8,9},{9,10},{10,11},{12,13},{... | collective-permute-start | bytes 1572872 | tf_op jit(solution)/shard_map/ppermute | solution.py:355
  11.1 14.2 %collective-permute-start.1 = (bf16[1,2048,128]{2,1,0:T(8,128)(2,1)S(1)}, bf16[1,2048,128]{2,1,0:T(8,128)(2,1)}, u32[]{:S(2)}, u32[]{:S(2)}) collective-permute-start(bf16[1,2048,128]{2,1,0:T(8,128)(2,1)S(1)} %bitcast.22), channel_id=1, source_target_pairs={{3,2},{2,1},{1,0},{7,6},{6,5},{5,4},{11,10},{10,9},{9,8},{15,14},{... | collective-permute-start | bytes 1572872 | tf_op jit(solution)/shard_map/ppermute | solution.py:355
  13.1 12.1 %collective-permute-start = (bf16[1,2048,128]{2,1,0:T(8,128)(2,1)S(1)}, bf16[1,2048,128]{2,1,0:T(8,128)(2,1)S(1)}, u32[]{:S(2)}, u32[]{:S(2)}) collective-permute-start(bf16[1,2048,128]{2,1,0:T(8,128)(2,1)S(1)} %bitcast.23), channel_id=1, source_target_pairs={{16,0},{4,20},{24,8},{12,28},{17,1},{5,21},{25,9},{13,29},{18,2},{... | collective-permute-start | bytes 1572872 | tf_op jit(solution)/shard_map/ppermute | solution.py:314
  25.2 29.0 %copy-start.5 = (bf16[1,2048,128]{2,1,0:T(8,128)(2,1)}, bf16[1,2048,128]{2,1,0:T(8,128)(2,1)S(1)}, u32[]{:S(2)}) copy-start(bf16[1,2048,128]{2,1,0:T(8,128)(2,1)S(1)} %collective-permute-done.r_11_) | copy-start | bytes 1572868
  25.2 17.1 %collective-permute-start.4 = (bf16[1,2048,128]{2,1,0:T(8,128)(2,1)}, bf16[1,2048,128]{2,1,0:T(8,128)(2,1)}, u32[]{:S(2)}, u32[]{:S(2)}) collective-permute-start(bf16[1,2048,128]{2,1,0:T(8,128)(2,1)} %collective-permute-done.2), channel_id=1, source_target_pairs={{1,2},{2,3},{5,6},{6,7},{9,10},{10,11},{13,14},{14,15},{17,18},{18... | collective-permute-start | bytes 1572872 | tf_op jit(solution)/shard_map/ppermute | solution.py:355
  27.2 15.2 %collective-permute-start.5 = (bf16[1,2048,128]{2,1,0:T(8,128)(2,1)}, bf16[1,2048,128]{2,1,0:T(8,128)(2,1)}, u32[]{:S(2)}, u32[]{:S(2)}) collective-permute-start(bf16[1,2048,128]{2,1,0:T(8,128)(2,1)} %collective-permute-done.1), channel_id=1, source_target_pairs={{2,1},{1,0},{6,5},{5,4},{10,9},{9,8},{14,13},{13,12},{18,17},{17,1... | collective-permute-start | bytes 1572872 | tf_op jit(solution)/shard_map/ppermute | solution.py:355
  32.1 10.3 %collective-permute-start.7 = (bf16[1,2048,128]{2,1,0:T(8,128)(2,1)S(1)}, bf16[1,2048,128]{2,1,0:T(8,128)(2,1)S(1)}, u32[]{:S(2)}, u32[]{:S(2)}) collective-permute-start(bf16[1,2048,128]{2,1,0:T(8,128)(2,1)S(1)} %collective-permute-done.r_11_), channel_id=1, source_target_pairs={{0,8},{28,20},{1,9},{29,21},{2,10},{30,22},{3,11},{31,23}} | collective-permute-start | bytes 1572872 | tf_op jit(solution)/shard_map/ppermute | solution.py:314
  36.5 12.8 %collective-permute-start.6 = (bf16[1,2048,128]{2,1,0:T(8,128)(2,1)}, bf16[1,2048,128]{2,1,0:T(8,128)(2,1)}, u32[]{:S(2)}, u32[]{:S(2)}) collective-permute-start(bf16[1,2048,128]{2,1,0:T(8,128)(2,1)} %broadcast_select_fusion.3), channel_id=1, source_target_pairs={{16,0},{4,20},{24,8},{12,28},{28,12},{0,16},{17,1},{5,21},{25,9},{... | collective-permute-start | bytes 1572872 | tf_op jit(solution)/shard_map/ppermute | solution.py:314
  41.0 13.2 %collective-permute-start.8 = (bf16[1,2048,128]{2,1,0:T(8,128)(2,1)S(1)}, bf16[1,2048,128]{2,1,0:T(8,128)(2,1)S(1)}, u32[]{:S(2)}, u32[]{:S(2)}) collective-permute-start(bf16[1,2048,128]{2,1,0:T(8,128)(2,1)S(1)} %get-tuple-element.58.r_4_), channel_id=1, source_target_pairs={{0,8},{4,12},{8,0},{12,4},{16,24},{20,28},{24,16},{28,20},{1,9},{5... | collective-permute-start | bytes 1572872 | tf_op jit(solution)/shard_map/ppermute | solution.py:314
  54.2 27.2 %copy-start.3 = (bf16[1,2048,128]{2,1,0:T(8,128)(2,1)}, bf16[1,2048,128]{2,1,0:T(8,128)(2,1)S(1)}, u32[]{:S(2)}) copy-start(bf16[1,2048,128]{2,1,0:T(8,128)(2,1)S(1)} %collective-permute-done.8.r_8_) | copy-start | bytes 1572868
  60.3 19.0 %collective-permute-start.10 = (bf16[7,2048,128]{2,1,0:T(8,128)(2,1)}, bf16[7,2048,128]{2,1,0:T(8,128)(2,1)S(1)}, u32[]{:S(2)}, u32[]{:S(2)}) collective-permute-start(bf16[7,2048,128]{2,1,0:T(8,128)(2,1)} %constant_dynamic-update-slice_fusion), channel_id=1, source_target_pairs={{0,4},{4,0},{8,12},{12,8},{16,20},{20,16},{24,28},{28,24},{1,5},{5... | collective-permute-start | bytes 11010056 | tf_op jit(solution)/shard_map/ppermute | solution.py:314
  61.4 13.1 %collective-permute-start.11 = (bf16[1,2048,128]{2,1,0:T(8,128)(2,1)S(1)}, bf16[1,2048,128]{2,1,0:T(8,128)(2,1)S(1)}, u32[]{:S(2)}, u32[]{:S(2)}) collective-permute-start(bf16[1,2048,128]{2,1,0:T(8,128)(2,1)S(1)} %get-tuple-element.55), channel_id=1, source_target_pairs={{16,0},{4,20},{24,8},{12,28},{28,12},{0,16},{17,1},{5,21},{25,9},{... | collective-permute-start | bytes 1572872 | tf_op jit(solution)/shard_map/ppermute | solution.py:314
  63.3 12.7 %collective-permute-start.9 = (bf16[1,2048,128]{2,1,0:T(8,128)(2,1)S(1)}, bf16[1,2048,128]{2,1,0:T(8,128)(2,1)S(1)}, u32[]{:S(2)}, u32[]{:S(2)}) collective-permute-start(bf16[1,2048,128]{2,1,0:T(8,128)(2,1)S(1)} %get-tuple-element.59), channel_id=1, source_target_pairs={{2,3},{1,0},{6,7},{5,4},{10,11},{9,8},{14,15},{13,12},{18,19},{17,... | collective-permute-start | bytes 1572872 | tf_op jit(solution)/shard_map/ppermute | solution.py:355
  64.6 14.6 %collective-permute-start.13 = (bf16[1,2048,128]{2,1,0:T(8,128)(2,1)S(1)}, bf16[1,2048,128]{2,1,0:T(8,128)(2,1)S(1)}, u32[]{:S(2)}, u32[]{:S(2)}) collective-permute-start(bf16[1,2048,128]{2,1,0:T(8,128)(2,1)S(1)} %get-tuple-element.56.r_5_), channel_id=1, source_target_pairs={{0,8},{4,12},{8,0},{12,4},{16,24},{20,28},{24,16},{28,20},{1,9},{5... | collective-permute-start | bytes 1572872 | tf_op jit(solution)/shard_map/ppermute | solution.py:314
  66.8 12.4 %collective-permute-start.12 = (bf16[1,2048,128]{2,1,0:T(8,128)(2,1)}, bf16[1,2048,128]{2,1,0:T(8,128)(2,1)S(1)}, u32[]{:S(2)}, u32[]{:S(2)}) collective-permute-start(bf16[1,2048,128]{2,1,0:T(8,128)(2,1)} %collective-permute-done.6.r_12_), channel_id=1, source_target_pairs={{0,8},{28,20},{1,9},{29,21},{2,10},{30,22},{3,11},{31,23}} | collective-permute-start | bytes 1572872 | tf_op jit(solution)/shard_map/ppermute | solution.py:314
  82.2 25.2 %collective-permute-start.14 = (bf16[4,2048,128]{2,1,0:T(8,128)(2,1)S(1)}, bf16[4,2048,128]{2,1,0:T(8,128)(2,1)S(1)}, u32[]{:S(2)}, u32[]{:S(2)}) collective-permute-start(bf16[4,2048,128]{2,1,0:T(8,128)(2,1)S(1)} %pad_maximum_fusion), channel_id=1, source_target_pairs={{0,4},{4,0},{8,12},{12,8},{16,20},{20,16},{24,28},{28,24},{1,5},{5... | collective-permute-start | bytes 6291464 | tf_op jit(solution)/shard_map/ppermute | solution.py:314
  89.5 14.2 %collective-permute-start.15 = (bf16[1,2048,128]{2,1,0:T(8,128)(2,1)S(1)}, bf16[1,2048,128]{2,1,0:T(8,128)(2,1)}, u32[]{:S(2)}, u32[]{:S(2)}) collective-permute-start(bf16[1,2048,128]{2,1,0:T(8,128)(2,1)S(1)} %get-tuple-element.53), channel_id=1, source_target_pairs={{16,0},{4,20},{24,8},{12,28},{28,12},{0,16},{17,1},{5,21},{25,9},{... | collective-permute-start | bytes 1572872 | tf_op jit(solution)/shard_map/ppermute | solution.py:314
  93.8 13.6 %collective-permute-start.17 = (bf16[1,2048,128]{2,1,0:T(8,128)(2,1)S(1)}, bf16[1,2048,128]{2,1,0:T(8,128)(2,1)}, u32[]{:S(2)}, u32[]{:S(2)}) collective-permute-start(bf16[1,2048,128]{2,1,0:T(8,128)(2,1)S(1)} %get-tuple-element.54.r_6_), channel_id=1, source_target_pairs={{0,8},{4,12},{8,0},{12,4},{16,24},{20,28},{24,16},{28,20},{1,9},{5... | collective-permute-start | bytes 1572872 | tf_op jit(solution)/shard_map/ppermute | solution.py:314
  93.8 13.6 %collective-permute-start.16 = (bf16[1,2048,128]{2,1,0:T(8,128)(2,1)S(1)}, bf16[1,2048,128]{2,1,0:T(8,128)(2,1)S(1)}, u32[]{:S(2)}, u32[]{:S(2)}) collective-permute-start(bf16[1,2048,128]{2,1,0:T(8,128)(2,1)S(1)} %collective-permute-done.11.r_13_), channel_id=1, source_target_pairs={{0,8},{28,20},{1,9},{29,21},{2,10},{30,22},{3,11},{31,23}} | collective-permute-start | bytes 1572872 | tf_op jit(solution)/shard_map/ppermute | solution.py:314
  111.8 14.3 %collective-permute-start.20 = (bf16[4,2048,128]{2,1,0:T(8,128)(2,1)}, bf16[4,2048,128]{2,1,0:T(8,128)(2,1)}, u32[]{:S(2)}, u32[]{:S(2)}) collective-permute-start(bf16[4,2048,128]{2,1,0:T(8,128)(2,1)} %pad_maximum_fusion.1), channel_id=1, source_target_pairs={{0,4},{4,0},{8,12},{12,8},{16,20},{20,16},{24,28},{28,24},{1,5},{5... | collective-permute-start | bytes 6291464 | tf_op jit(solution)/shard_map/ppermute | solution.py:314
  115.9 10.1 %collective-permute-start.18 = (bf16[1,2048,128]{2,1,0:T(8,128)(2,1)}, bf16[1,2048,128]{2,1,0:T(8,128)(2,1)}, u32[]{:S(2)}, u32[]{:S(2)}) collective-permute-start(bf16[1,2048,128]{2,1,0:T(8,128)(2,1)} %collective-permute-done.17.r_10_), channel_id=1, source_target_pairs={{28,12},{0,16},{29,13},{1,17},{30,14},{2,18},{31,15},{3,19}} | collective-permute-start | bytes 1572872 | tf_op jit(solution)/shard_map/ppermute | solution.py:314
  117.4 8.7 %collective-permute-start.19 = (bf16[1,2048,128]{2,1,0:T(8,128)(2,1)}, bf16[1,2048,128]{2,1,0:T(8,128)(2,1)}, u32[]{:S(2)}, u32[]{:S(2)}) collective-permute-start(bf16[1,2048,128]{2,1,0:T(8,128)(2,1)} %collective-permute-done.15.r_14_), channel_id=1, source_target_pairs={{0,8},{28,20},{1,9},{29,21},{2,10},{30,22},{3,11},{31,23}} | collective-permute-start | bytes 1572872 | tf_op jit(solution)/shard_map/ppermute | solution.py:314
  128.3 6.6 %collective-permute-start.21 = (bf16[2,2048,128]{2,1,0:T(8,128)(2,1)}, bf16[2,2048,128]{2,1,0:T(8,128)(2,1)}, u32[]{:S(2)}, u32[]{:S(2)}) collective-permute-start(bf16[2,2048,128]{2,1,0:T(8,128)(2,1)} %pad_maximum_fusion.2), channel_id=1, source_target_pairs={{0,4},{4,0},{8,12},{12,8},{16,20},{20,16},{24,28},{28,24},{1,5},{5... | collective-permute-start | bytes 3145736 | tf_op jit(solution)/shard_map/ppermute | solution.py:314
  (19 other events, 91.2 us)

commit v4 on v3

--- a/solution.py
+++ b/solution.py
@@ -186,14 +186,15 @@
     )(z.reshape(1), *slabs)
 
 
-CHUNKS = 4
+CHUNKS = 2
 GROUP_UNROLL = 4
 ROW_UNROLL = 4
 
 
 def pairs_kernel(slots, left_ref, lag_ref, *refs, arrays, norm):
-    sources, (out_ref, partner, gram, stage, in_sems, out_sems) = refs[: len(arrays)], refs[len(arrays) :]
-    groups, m, k = left_ref.shape
+    sources, refs = refs[: len(arrays)], refs[len(arrays) :]
+    out_ref, partner, left, gram, stage, in_sems, left_sems, out_sems = refs
+    groups, m, k = left.shape
     slot_count, slabs, slab_rows, channels = partner.shape
     group_rows = k // slabs
     chunk_rows = slab_rows // CHUNKS
@@ -216,7 +217,15 @@
 
     per_chunk = groups // CHUNKS
 
+    def fetch_left(chunk):
+        some = pl.ds(chunk * per_chunk, per_chunk)
+        return pltpu.make_async_copy(left_ref.at[some], left.at[some], left_sems.at[chunk])
+
     for chunk in range(CHUNKS):
+        fetch_left(chunk).start()
+
+    for chunk in range(CHUNKS):
+        fetch_left(chunk).wait()
         for s in range(slot_count):
             for r in range(slabs):
                 fetch(sources[0].at[0], s, r, chunk).wait()
@@ -229,7 +238,7 @@
                 right = jnp.concatenate(
                     [partner[s, :, rows, :].reshape(k, channels) for s in range(slot_count)], 1
                 )
-                product = jnp.dot(left_ref[g], right, preferred_element_type=jnp.float32)
+                product = jnp.dot(left[g], right, preferred_element_type=jnp.float32)
                 cols = pl.ds(pl.multiple_of(g * 2 * GROUP, 2 * GROUP), 2 * GROUP)
                 gram[:, cols, :] = product.astype(jnp.bfloat16).reshape(
                     m // (2 * GROUP), 2 * GROUP, lanes
@@ -276,17 +285,19 @@
     in_vmem = pl.BlockSpec(memory_space=pltpu.VMEM)
     return pl.pallas_call(
         lambda *r: pairs_kernel(*r, arrays=arrays, norm=norm),
-        in_specs=[pl.BlockSpec(memory_space=pltpu.SMEM), in_vmem, in_vmem] + [anywhere] * len(held),
+        in_specs=[pl.BlockSpec(memory_space=pltpu.SMEM), anywhere, in_vmem] + [anywhere] * len(held),
         out_specs=anywhere,
         scratch_shapes=[
             pltpu.VMEM((slot_count, slabs, slab_rows, channels), jnp.bfloat16),
+            pltpu.VMEM((groups, m, k), jnp.bfloat16),
             pltpu.VMEM((rows_out, entries, slot_count * channels), jnp.bfloat16),
             pltpu.VMEM((2, ROW_UNROLL, slot_count, channels, lag_count), jnp.float32),
             pltpu.SemaphoreType.DMA((CHUNKS, slot_count, slabs)),
+            pltpu.SemaphoreType.DMA((CHUNKS,)),
             pltpu.SemaphoreType.DMA((2,)),
         ],
         out_shape=jax.ShapeDtypeStruct((rows_out, slot_count, channels, lag_count), jnp.float32),
-        compiler_params=pltpu.CompilerParams(vmem_limit_bytes=36 << 20),
+        compiler_params=pltpu.CompilerParams(vmem_limit_bytes=58 << 20),
         name="pairs",
     )(slots, left, lag_rows, *[value for value, _ in held])
 
@@ -294,6 +305,7 @@
 X_PAIRS = [(i, i ^ 2) for i in range(8)]
 Y_PAIRS = [(4, 0), (1, 5), (6, 2), (3, 7)]
 Y_ON = [(7, 3), (0, 4)]
+Y_ON_ALL = Y_ON + [(6, 2), (1, 5)]
 X_ON = [(0, 2), (7, 5)]
 CORE_PAIRS = [(i, i ^ 1) for i in range(8)]
 
@@ -318,15 +330,6 @@
     return Held(jnp.concatenate([p.value for p in parts], 0), [w for p in parts for w in p.what])
 
 
-def where_device(me, devices, first, second):
-    here = jnp.asarray(np.isin(np.arange(8), devices))[me]
-    what = [
-        [one[i] if i in devices else other[i] for i in range(8)]
-        for one, other in zip(first.what, second.what)
-    ]
-    return Held(jnp.where(here, first.value, second.value), what)
-
-
 def together(*parts):
     return lax.optimization_barrier(parts)
 
@@ -357,45 +360,42 @@
     def slab_of(value, r):
         return Held(value, [[(i, r) for i in range(8)]])
 
-    def over_y(straight, came_over_x):
-        mixed = where_device(me, [0, 7], came_over_x, straight)
-        return mixed.hop(Y_PAIRS + Y_ON)
-
     s0 = make_slab(traces, band_bins)[None]
     q0 = slab_of(s0, 0)
+    down1, up1 = along_z(s0, [(3, 2), (2, 1), (1, 0)]), along_z(s0, [(0, 1), (1, 2), (2, 3)])
     y0 = q0.hop(Y_PAIRS)
-    down1, up1 = along_z(s0, [(3, 2), (2, 1), (1, 0)]), along_z(s0, [(0, 1), (1, 2), (2, 3)])
     x0 = q0.hop(X_PAIRS)
     y0, down1, up1, x0, lag_rows = together(y0, down1, up1, x0, lag_rows)
 
     q1 = slab_of(lax.select_n(z, down1, up1, down1, up1), 1)
     up2, down2 = along_z(up1, [(1, 2), (2, 3)]), along_z(down1, [(2, 1), (1, 0)])
-    y1 = over_y(q1, x0)
-    e0 = y0.hop(X_ON)
     x1 = q1.hop(X_PAIRS)
-    up2, down2, y1, e0, x1 = together(up2, down2, y1, e0, x1)
+    y1 = q1.hop(Y_PAIRS)
+    c0 = x0.hop(Y_ON_ALL)
+    up2, down2, y1, c0, x1 = together(up2, down2, y1, c0, x1)
 
     q2 = slab_of(lax.select_n(z, down2, down1, up1, up2), 2)
     last = along_z(jnp.where(z == 2, up2, down2), [(2, 3), (1, 0)])
-    a = join(q0, x0, y0, q1, x1, y1, e0).hop(CORE_PAIRS)
-    y2 = over_y(q2, x1)
-    e1 = y1.hop(X_ON)
+    a0 = join(q0, x0, y0, c0).hop(CORE_PAIRS)
     x2 = q2.hop(X_PAIRS)
-    last, a, y2, e1, x2 = together(last, a, y2, e1, x2)
+    y2 = q2.hop(Y_PAIRS)
+    c1 = x1.hop(Y_ON_ALL)
+    last, a0, y2, c1, x2 = together(last, a0, y2, c1, x2)
 
     q3 = slab_of(lax.select_n(z, last, down2, up2, last), 3)
-    b = join(q2, x2, y2, e1).hop(CORE_PAIRS)
-    y3 = over_y(q3, x2)
-    e2 = y2.hop(X_ON)
+    a1 = join(q1, x1, y1, c1).hop(CORE_PAIRS)
+    a2 = join(q2, x2, y2).hop(CORE_PAIRS)
     x3 = q3.hop(X_PAIRS)
+    y3 = q3.hop(Y_PAIRS)
+    c2 = x2.hop(Y_ON_ALL)
     left = make_left([q.value[0] for q in (q0, q1, q2, q3)], z, channels // 4, bins)
-    b, y3, e2, x3, left = together(b, y3, e2, x3, left)
-
-    c = join(q3, x3, y3, e2).hop(CORE_PAIRS)
-    y4, e3 = x3.hop(Y_ON), y3.hop(X_ON)
-
-    held = [q0, q1, q2, q3, x0, x1, x2, x3, y0, y1, y2, y3, y4, e0, e1, e2, e3, a, b, c]
-    whats = [h.what for h in held] + [moved(y4.what + e3.what, CORE_PAIRS)]
+    a1, a2, y3, c2, x3, left = together(a1, a2, y3, c2, x3, left)
+
+    a3 = join(c2, q3, x3, y3).hop(CORE_PAIRS)
+    c3, d3 = x3.hop(Y_ON), y3.hop(X_ON)
+
+    held = [q0, q1, q2, q3, x0, x1, x2, x3, y0, y1, y2, y3, c0, c1, c2, c3, d3, a0, a1, a2, a3]
+    whats = [h.what for h in held] + [moved(c3.what + d3.what, CORE_PAIRS)]
     table = np.zeros((8, 8, 4), np.int32)
     all_holds = [set() for _ in whats]
     index = sum(len(what) for what in whats)
@@ -409,9 +409,9 @@
     mine = jnp.asarray(table)[me]
     slots = jnp.concatenate([mine[pair_blocks[0, s]] for s in range(slot_count)])
 
-    y4, e3, c, slots = together(y4, e3, c, slots)
-    d = join(y4, e3).hop(CORE_PAIRS)
-    held = [q0, q1, q2, q3, x0, x1, x2, x3, y0, y1, y2, y3, y4, e0, e1, e2, e3, a, b, c, d]
+    c3, d3, a3, slots = together(c3, d3, a3, slots)
+    a4 = join(c3, d3).hop(CORE_PAIRS)
+    held = [q0, q1, q2, q3, x0, x1, x2, x3, y0, y1, y2, y3, c0, c1, c2, c3, d3, a0, a1, a2, a3, a4]
     places = [(h.value, holds) for h, holds in zip(held, all_holds)]
     norm = 1.0 / math.sqrt(4 * windows * bins)
     return correlate(slots, left, lag_rows, places, slot_count, norm)[None]

time: 170 us -> 140 us (0.82)
  local copies, waits for them, and re-layouts: 25.5 us -> 12.7 us
  starting transfers between devices: 51.7 us -> 42.7 us
  other arithmetic: 17.4 us -> 10 us
  Pallas kernels: 29.4 us -> 23.2 us
  waiting for transfers between devices: 38.3 us -> 43.8 us
    unnamed x46 -> x56, local copies, waits for them, and re-layouts: 19.5 us -> 7.61 us
    ppermute x5, waiting for transfers between devices: 7.06 us -> 17.8 us  [along_z(): return lax.ppermute(value, 'freq', pairs)]
    ppermute x17 -> x18, starting transfers between devices: 38.2 us -> 31.6 us  [hop(): lax.ppermute(self.value, 'chan', pairs)]
    pallas_call x1, Pallas kernels: 23.5 us -> 17.2 us  [correlate(): pl.pallas_call(lambda *r: pairs_kernel(*r, arrays=arrays, norm=norm), in_...]
    ppermute x17 -> x18, waiting for transfers between devices: 31.2 us -> 26 us  [hop(): lax.ppermute(self.value, 'chan', pairs)]
    select_n x3, other arithmetic: 7.45 us -> 3.2 us  [the longest x1 1.68 us: on_device(): q2 = slab_of(lax.select_n(z, down2, down1, up1, up2), 2)]
    ppermute x5, starting transfers between devices: 13.5 us -> 11.1 us  [along_z(): return lax.ppermute(value, 'freq', pairs)]
    concatenate x3 -> x5, other arithmetic: 6.06 us -> 3.87 us  [join(): jnp.concatenate([p.value for p in parts], 0)]
  transfers between devices with their start and end apart: 22 -> 23, of which waited for: 11 -> 12; matrix products, arithmetic and copies ran while one was open for 5% -> 4% of each run, Pallas kernels for 2% -> 3%
where the time goes in v4:
time: 140 us; the launch traced here: 139 us
  waiting for transfers between devices  43.8 us (31%)
  starting transfers between devices  42.7 us (30%)
  Pallas kernels  23.2 us (17%)
  local copies, waits for them, and re-layouts  12.7 us (9%)
  other arithmetic  10 us (7%)
  between operations  6 us (4%)
    ppermute x18, starting transfers between devices, hop(): lax.ppermute(self.value, 'chan', pairs)  31.6 us
    ppermute x18, waiting for transfers between devices, hop(): lax.ppermute(self.value, 'chan', pairs)  26 us
    ppermute x5, waiting for transfers between devices, along_z(): return lax.ppermute(value, 'freq', pairs)  17.8 us
    pallas_call x1, Pallas kernels, correlate(): pl.pallas_call(lambda *r: pairs_kernel(*r, arrays=arrays, norm=norm), in_...  17.2 us
    ppermute x5, starting transfers between devices, along_z(): return lax.ppermute(value, 'freq', pairs)  11.1 us
    unnamed x56, local copies, waits for them, and re-layouts  7.61 us
    pallas_call x1, Pallas kernels, make_left(): pl.pallas_call(lambda *r: left_kernel(*r, per_step=per_step), grid_spec=p...  4.03 us
    concatenate x5, other arithmetic, join(): jnp.concatenate([p.value for p in parts], 0)  3.87 us
  transfers between devices with their start and end apart: 23, of which 12 were waited for; matrix products, arithmetic and copies ran while one was open for 4% of the time, Pallas kernels for 3%

profile of v4, /device:TPU:17, one launch (start us, length us, event | category | flops | bytes accessed | tf_op | source)
XLA Modules:
  0.0 138.5 jit_solution(1412053062461424937)
XLA Ops:
  1.9 2.7 %copy.8 = bf16[4,128,2048]{2,1,0:T(8,128)(2,1)S(1)} copy(bf16[4,128,2048]{2,0,1:T(4,128)(2,1)} %bitcast.28) | data formatting | bytes 4194304 | tf_op jit(solution)/shard_map/transpose | solution.py:113
  4.6 1.9 %spectra.1.r_1_ = bf16[2048,128]{1,0:T(8,128)(2,1)S(1)} custom-call(bf16[512,2048]{1,0:T(8,128)(2,1)S(1)} %bitcast.27, f32[256,128]{1,0:T(8,128)S(1)} %slice.28.fine_cos, f32[256,128]{1,0:T(8,128)S(1)} %slice.29.fine_sin, f32[256,16]{1,0:T(8,128)S(1)} %slice.30.step_cos, f32[256,16]{1,0:T(8,128)S(1)} %slice.31.step_sin), custom_call_target="tpu_custom_call" | custom-call | tf_op jit(solution)/shard_map/spectra/pallas_call | solution.py:118
  7.8 3.2 %collective-permute-start.2 = (bf16[1,2048,128]{2,1,0:T(8,128)(2,1)S(1)}, bf16[1,2048,128]{2,1,0:T(8,128)(2,1)}, u32[]{:S(2)}, u32[]{:S(2)}) collective-permute-start(bf16[1,2048,128]{2,1,0:T(8,128)(2,1)S(1)} %bitcast.21), channel_id=1, source_target_pairs={{0,1},{1,2},{2,3},{4,5},{5,6},{6,7},{8,9},{9,10},{10,11},{12,13},{... | collective-permute-start | bytes 1572872 | tf_op jit(solution)/shard_map/ppermute | solution.py:358
  11.1 2.1 %collective-permute-start.1 = (bf16[1,2048,128]{2,1,0:T(8,128)(2,1)S(1)}, bf16[1,2048,128]{2,1,0:T(8,128)(2,1)}, u32[]{:S(2)}, u32[]{:S(2)}) collective-permute-start(bf16[1,2048,128]{2,1,0:T(8,128)(2,1)S(1)} %bitcast.22), channel_id=1, source_target_pairs={{3,2},{2,1},{1,0},{7,6},{6,5},{5,4},{11,10},{10,9},{9,8},{15,14},{... | collective-permute-start | bytes 1572872 | tf_op jit(solution)/shard_map/ppermute | solution.py:358
  13.1 3.2 %collective-permute-start = (bf16[1,2048,128]{2,1,0:T(8,128)(2,1)S(1)}, bf16[1,2048,128]{2,1,0:T(8,128)(2,1)S(1)}, u32[]{:S(2)}, u32[]{:S(2)}) collective-permute-start(bf16[1,2048,128]{2,1,0:T(8,128)(2,1)S(1)} %bitcast.23), channel_id=1, source_target_pairs={{16,0},{4,20},{24,8},{12,28},{17,1},{5,21},{25,9},{13,29},{18,2},{... | collective-permute-start | bytes 1572872 | tf_op jit(solution)/shard_map/ppermute | solution.py:326
  17.1 2.4 %collective-permute-done.3.r_7_ = bf16[1,2048,128]{2,1,0:T(8,128)(2,1)S(1)} collective-permute-done((bf16[1,2048,128]{2,1,0:T(8,128)(2,1)S(1)}, bf16[1,2048,128]{2,1,0:T(8,128)(2,1)S(1)}, u32[]{:S(2)}, u32[]{:S(2)}) %collective-permute-start.3) | collective-permute-done | bytes 524320 | tf_op jit(solution)/shard_map/ppermute | solution.py:326
  19.5 2.8 %collective-permute-done.2 = bf16[1,2048,128]{2,1,0:T(8,128)(2,1)} collective-permute-done((bf16[1,2048,128]{2,1,0:T(8,128)(2,1)S(1)}, bf16[1,2048,128]{2,1,0:T(8,128)(2,1)}, u32[]{:S(2)}, u32[]{:S(2)}) %collective-permute-start.2) | collective-permute-done | bytes 524320 | tf_op jit(solution)/shard_map/ppermute | solution.py:358
  22.3 2.9 %collective-permute-done.1 = bf16[1,2048,128]{2,1,0:T(8,128)(2,1)} collective-permute-done((bf16[1,2048,128]{2,1,0:T(8,128)(2,1)S(1)}, bf16[1,2048,128]{2,1,0:T(8,128)(2,1)}, u32[]{:S(2)}, u32[]{:S(2)}) %collective-permute-start.1) | collective-permute-done | bytes 524320 | tf_op jit(solution)/shard_map/ppermute | solution.py:358
  27.0 3.2 %collective-permute-start.6 = (bf16[1,2048,128]{2,1,0:T(8,128)(2,1)S(1)}, bf16[1,2048,128]{2,1,0:T(8,128)(2,1)S(1)}, u32[]{:S(2)}, u32[]{:S(2)}) collective-permute-start(bf16[1,2048,128]{2,1,0:T(8,128)(2,1)S(1)} %select_select_fusion.2.r_4_), channel_id=1, source_target_pairs={{16,0},{4,20},{24,8},{12,28},{17,1},{5,21},{25,9},{13,29},{18,2},{... | collective-permute-start | bytes 1572872 | tf_op jit(solution)/shard_map/ppermute | solution.py:326
  30.2 2.1 %collective-permute-start.5 = (bf16[1,2048,128]{2,1,0:T(8,128)(2,1)}, bf16[1,2048,128]{2,1,0:T(8,128)(2,1)S(1)}, u32[]{:S(2)}, u32[]{:S(2)}) collective-permute-start(bf16[1,2048,128]{2,1,0:T(8,128)(2,1)} %collective-permute-done.1), channel_id=1, source_target_pairs={{2,1},{1,0},{6,5},{5,4},{10,9},{9,8},{14,13},{13,12},{18,17},{17,1... | collective-permute-start | bytes 1572872 | tf_op jit(solution)/shard_map/ppermute | solution.py:358
  32.3 1.9 %collective-permute-start.4 = (bf16[1,2048,128]{2,1,0:T(8,128)(2,1)}, bf16[1,2048,128]{2,1,0:T(8,128)(2,1)S(1)}, u32[]{:S(2)}, u32[]{:S(2)}) collective-permute-start(bf16[1,2048,128]{2,1,0:T(8,128)(2,1)} %collective-permute-done.2), channel_id=1, source_target_pairs={{1,2},{2,3},{5,6},{6,7},{9,10},{10,11},{13,14},{14,15},{17,18},{18... | collective-permute-start | bytes 1572872 | tf_op jit(solution)/shard_map/ppermute | solution.py:358
  35.6 2.5 %collective-permute-done.8.r_8_ = bf16[1,2048,128]{2,1,0:T(8,128)(2,1)S(1)} collective-permute-done((bf16[1,2048,128]{2,1,0:T(8,128)(2,1)S(1)}, bf16[1,2048,128]{2,1,0:T(8,128)(2,1)S(1)}, u32[]{:S(2)}, u32[]{:S(2)}) %collective-permute-start.8) | collective-permute-done | bytes 524320 | tf_op jit(solution)/shard_map/ppermute | solution.py:326
  38.8 4.5 %collective-permute-done.5 = bf16[1,2048,128]{2,1,0:T(8,128)(2,1)S(1)} collective-permute-done((bf16[1,2048,128]{2,1,0:T(8,128)(2,1)}, bf16[1,2048,128]{2,1,0:T(8,128)(2,1)S(1)}, u32[]{:S(2)}, u32[]{:S(2)}) %collective-permute-start.5) | collective-permute-done | bytes 524320 | tf_op jit(solution)/shard_map/ppermute | solution.py:358
  44.2 2.9 %collective-permute-done.4 = bf16[1,2048,128]{2,1,0:T(8,128)(2,1)S(1)} collective-permute-done((bf16[1,2048,128]{2,1,0:T(8,128)(2,1)}, bf16[1,2048,128]{2,1,0:T(8,128)(2,1)S(1)}, u32[]{:S(2)}, u32[]{:S(2)}) %collective-permute-start.4) | collective-permute-done | bytes 524320 | tf_op jit(solution)/shard_map/ppermute | solution.py:358
  54.7 3.9 %collective-permute-start.13 = (bf16[1,2048,128]{2,1,0:T(8,128)(2,1)S(1)}, bf16[1,2048,128]{2,1,0:T(8,128)(2,1)S(1)}, u32[]{:S(2)}, u32[]{:S(2)}) collective-permute-start(bf16[1,2048,128]{2,1,0:T(8,128)(2,1)S(1)} %get-tuple-element.55.r_5_), channel_id=1, source_target_pairs={{0,8},{4,12},{8,0},{12,4},{16,24},{20,28},{24,16},{28,20},{1,9},{5... | collective-permute-start | bytes 1572872 | tf_op jit(solution)/shard_map/ppermute | solution.py:326
  61.2 4.8 %collective-permute-done.9 = bf16[1,2048,128]{2,1,0:T(8,128)(2,1)S(1)} collective-permute-done((bf16[1,2048,128]{2,1,0:T(8,128)(2,1)S(1)}, bf16[1,2048,128]{2,1,0:T(8,128)(2,1)S(1)}, u32[]{:S(2)}, u32[]{:S(2)}) %collective-permute-start.9) | collective-permute-done | bytes 524320 | tf_op jit(solution)/shard_map/ppermute | solution.py:358
  65.9 4.6 %collective-permute-done.13.r_9_ = bf16[1,2048,128]{2,1,0:T(8,128)(2,1)S(1)} collective-permute-done((bf16[1,2048,128]{2,1,0:T(8,128)(2,1)S(1)}, bf16[1,2048,128]{2,1,0:T(8,128)(2,1)S(1)}, u32[]{:S(2)}, u32[]{:S(2)}) %collective-permute-start.13) | collective-permute-done | bytes 524320 | tf_op jit(solution)/shard_map/ppermute | solution.py:326
  70.6 6.6 %collective-permute-done.12.r_16_ = bf16[1,2048,128]{2,1,0:T(8,128)(2,1)S(1)} collective-permute-done((bf16[1,2048,128]{2,1,0:T(8,128)(2,1)S(1)}, bf16[1,2048,128]{2,1,0:T(8,128)(2,1)S(1)}, u32[]{:S(2)}, u32[]{:S(2)}) %collective-permute-start.12) | collective-permute-done | bytes 524320 | tf_op jit(solution)/shard_map/ppermute | solution.py:326
  78.7 3.4 %collective-permute-start.18 = (bf16[1,2048,128]{2,1,0:T(8,128)(2,1)S(1)}, bf16[1,2048,128]{2,1,0:T(8,128)(2,1)S(1)}, u32[]{:S(2)}, u32[]{:S(2)}) collective-permute-start(bf16[1,2048,128]{2,1,0:T(8,128)(2,1)S(1)} %select_select_fusion.r_6_), channel_id=1, source_target_pairs={{0,8},{4,12},{8,0},{12,4},{16,24},{20,28},{24,16},{28,20},{1,9},{5... | collective-permute-start | bytes 1572872 | tf_op jit(solution)/shard_map/ppermute | solution.py:326
  84.8 4.0 %left.1.r_1_ = bf16[32,512,256]{2,1,0:T(8,128)(2,1)S(1)} custom-call(s32[1]{0:T(128)} %bitcast.4.r_0_, bf16[2048,128]{1,0:T(8,128)(2,1)S(1)} %spectra.1.r_1_, bf16[2048,128]{1,0:T(8,128)(2,1)S(1)} %bitcast.18, bf16[2048,128]{1,0:T(8,128)(2,1)S(1)} %bitcast.19, bf16[2048,128]{1,0:T(8,128)(2,1)S(1)} %bitcast.26), custom_call_target="tpu_custom_call" | custom-call | tf_op jit(solution)/shard_map/left/pallas_call | solution.py:168
  88.8 3.3 %copy-done = bf16[32,512,256]{2,1,0:T(8,128)(2,1)} copy-done((bf16[32,512,256]{2,1,0:T(8,128)(2,1)}, bf16[32,512,256]{2,1,0:T(8,128)(2,1)S(1)}, u32[]{:S(2)}) %copy-start) | copy-done | bytes 8388632
  93.8 6.8 %collective-permute-done.17.r_17_ = bf16[1,2048,128]{2,1,0:T(8,128)(2,1)S(1)} collective-permute-done((bf16[1,2048,128]{2,1,0:T(8,128)(2,1)S(1)}, bf16[1,2048,128]{2,1,0:T(8,128)(2,1)S(1)}, u32[]{:S(2)}, u32[]{:S(2)}) %collective-permute-start.17) | collective-permute-done | bytes 524320 | tf_op jit(solution)/shard_map/ppermute | solution.py:326
  112.4 5.6 %collective-permute-start.22 = (bf16[2,2048,128]{2,1,0:T(8,128)(2,1)S(1)}, bf16[2,2048,128]{2,1,0:T(8,128)(2,1)S(1)}, u32[]{:S(2)}, u32[]{:S(2)}) collective-permute-start(bf16[2,2048,128]{2,1,0:T(8,128)(2,1)S(1)} %pad_maximum_fusion.4), channel_id=1, source_target_pairs={{0,4},{4,0},{8,12},{12,8},{16,20},{20,16},{24,28},{28,24},{1,5},{5... | collective-permute-start | bytes 3145736 | tf_op jit(solution)/shard_map/ppermute | solution.py:326
  121.3 17.2 %pairs.1 = f32[32,3,128,128]{3,2,1,0:T(8,128)} custom-call(s32[12]{0:T(128)} %pad_add_fusion.1.r_0_, bf16[32,512,256]{2,1,0:T(8,128)(2,1)} %copy-done, bf16[128,512]{1,0:T(8,128)(2,1)} %copy.10.r_2_, bf16[1,2048,128]{2,1,0:T(8,128)(2,1)} %bitcast.25, bf16[1,2048,128]{2,1,0:T(8,128)(2,1)} %copy-done.1, bf16[1,2048,128]{2,1,0:T(8,128)(2,1)} %copy-done.2, ...), custom_call_target="tpu_custom_call" | custom-call | tf_op jit(solution)/shard_map/pairs/pallas_call | solution.py:286
  (106 shorter events, 34.1 us)
Async XLA Ops:
  6.6 78.2 %copy-start.3 = (bf16[2048,128]{1,0:T(8,128)(2,1)}, bf16[2048,128]{1,0:T(8,128)(2,1)S(1)}, u32[]{:S(2)}) copy-start(bf16[2048,128]{1,0:T(8,128)(2,1)S(1)} %spectra.1.r_1_) | copy-start | bytes 1572868
  6.6 13.0 %collective-permute-start.3 = (bf16[1,2048,128]{2,1,0:T(8,128)(2,1)S(1)}, bf16[1,2048,128]{2,1,0:T(8,128)(2,1)S(1)}, u32[]{:S(2)}, u32[]{:S(2)}) collective-permute-start(bf16[1,2048,128]{2,1,0:T(8,128)(2,1)S(1)} %bitcast.20), channel_id=1, source_target_pairs={{0,8},{4,12},{8,0},{12,4},{16,24},{20,28},{24,16},{28,20},{1,9},{5... | collective-permute-start | bytes 1572872 | tf_op jit(solution)/shard_map/ppermute | solution.py:326
  7.8 14.5 %collective-permute-start.2 = (bf16[1,2048,128]{2,1,0:T(8,128)(2,1)S(1)}, bf16[1,2048,128]{2,1,0:T(8,128)(2,1)}, u32[]{:S(2)}, u32[]{:S(2)}) collective-permute-start(bf16[1,2048,128]{2,1,0:T(8,128)(2,1)S(1)} %bitcast.21), channel_id=1, source_target_pairs={{0,1},{1,2},{2,3},{4,5},{5,6},{6,7},{8,9},{9,10},{10,11},{12,13},{... | collective-permute-start | bytes 1572872 | tf_op jit(solution)/shard_map/ppermute | solution.py:358
  11.1 14.2 %collective-permute-start.1 = (bf16[1,2048,128]{2,1,0:T(8,128)(2,1)S(1)}, bf16[1,2048,128]{2,1,0:T(8,128)(2,1)}, u32[]{:S(2)}, u32[]{:S(2)}) collective-permute-start(bf16[1,2048,128]{2,1,0:T(8,128)(2,1)S(1)} %bitcast.22), channel_id=1, source_target_pairs={{3,2},{2,1},{1,0},{7,6},{6,5},{5,4},{11,10},{10,9},{9,8},{15,14},{... | collective-permute-start | bytes 1572872 | tf_op jit(solution)/shard_map/ppermute | solution.py:358
  13.1 12.1 %collective-permute-start = (bf16[1,2048,128]{2,1,0:T(8,128)(2,1)S(1)}, bf16[1,2048,128]{2,1,0:T(8,128)(2,1)S(1)}, u32[]{:S(2)}, u32[]{:S(2)}) collective-permute-start(bf16[1,2048,128]{2,1,0:T(8,128)(2,1)S(1)} %bitcast.23), channel_id=1, source_target_pairs={{16,0},{4,20},{24,8},{12,28},{17,1},{5,21},{25,9},{13,29},{18,2},{... | collective-permute-start | bytes 1572872 | tf_op jit(solution)/shard_map/ppermute | solution.py:326
  26.7 11.3 %collective-permute-start.8 = (bf16[1,2048,128]{2,1,0:T(8,128)(2,1)S(1)}, bf16[1,2048,128]{2,1,0:T(8,128)(2,1)S(1)}, u32[]{:S(2)}, u32[]{:S(2)}) collective-permute-start(bf16[1,2048,128]{2,1,0:T(8,128)(2,1)S(1)} %select_select_fusion.2.r_4_), channel_id=1, source_target_pairs={{0,8},{4,12},{8,0},{12,4},{16,24},{20,28},{24,16},{28,20},{1,9},{5... | collective-permute-start | bytes 1572872 | tf_op jit(solution)/shard_map/ppermute | solution.py:326
  27.0 11.0 %collective-permute-start.6 = (bf16[1,2048,128]{2,1,0:T(8,128)(2,1)S(1)}, bf16[1,2048,128]{2,1,0:T(8,128)(2,1)S(1)}, u32[]{:S(2)}, u32[]{:S(2)}) collective-permute-start(bf16[1,2048,128]{2,1,0:T(8,128)(2,1)S(1)} %select_select_fusion.2.r_4_), channel_id=1, source_target_pairs={{16,0},{4,20},{24,8},{12,28},{17,1},{5,21},{25,9},{13,29},{18,2},{... | collective-permute-start | bytes 1572872 | tf_op jit(solution)/shard_map/ppermute | solution.py:326
  30.2 13.1 %collective-permute-start.5 = (bf16[1,2048,128]{2,1,0:T(8,128)(2,1)}, bf16[1,2048,128]{2,1,0:T(8,128)(2,1)S(1)}, u32[]{:S(2)}, u32[]{:S(2)}) collective-permute-start(bf16[1,2048,128]{2,1,0:T(8,128)(2,1)} %collective-permute-done.1), channel_id=1, source_target_pairs={{2,1},{1,0},{6,5},{5,4},{10,9},{9,8},{14,13},{13,12},{18,17},{17,1... | collective-permute-start | bytes 1572872 | tf_op jit(solution)/shard_map/ppermute | solution.py:358
  32.3 14.7 %collective-permute-start.4 = (bf16[1,2048,128]{2,1,0:T(8,128)(2,1)}, bf16[1,2048,128]{2,1,0:T(8,128)(2,1)S(1)}, u32[]{:S(2)}, u32[]{:S(2)}) collective-permute-start(bf16[1,2048,128]{2,1,0:T(8,128)(2,1)} %collective-permute-done.2), channel_id=1, source_target_pairs={{1,2},{2,3},{5,6},{6,7},{9,10},{10,11},{13,14},{14,15},{17,18},{18... | collective-permute-start | bytes 1572872 | tf_op jit(solution)/shard_map/ppermute | solution.py:358
  34.2 13.6 %collective-permute-start.7 = (bf16[1,2048,128]{2,1,0:T(8,128)(2,1)S(1)}, bf16[1,2048,128]{2,1,0:T(8,128)(2,1)S(1)}, u32[]{:S(2)}, u32[]{:S(2)}) collective-permute-start(bf16[1,2048,128]{2,1,0:T(8,128)(2,1)S(1)} %collective-permute-done.3.r_7_), channel_id=1, source_target_pairs={{28,12},{0,16},{24,8},{4,20},{29,13},{1,17},{25,9},{5,21},{30,14},... | collective-permute-start | bytes 1572872 | tf_op jit(solution)/shard_map/ppermute | solution.py:326
  49.4 27.7 %collective-permute-start.10 = (bf16[4,2048,128]{2,1,0:T(8,128)(2,1)}, bf16[4,2048,128]{2,1,0:T(8,128)(2,1)}, u32[]{:S(2)}, u32[]{:S(2)}) collective-permute-start(bf16[4,2048,128]{2,1,0:T(8,128)(2,1)} %pad_maximum_fusion), channel_id=1, source_target_pairs={{0,4},{4,0},{8,12},{12,8},{16,20},{20,16},{24,28},{28,24},{1,5},{5... | collective-permute-start | bytes 6291464 | tf_op jit(solution)/shard_map/ppermute | solution.py:326
  52.9 13.1 %collective-permute-start.9 = (bf16[1,2048,128]{2,1,0:T(8,128)(2,1)S(1)}, bf16[1,2048,128]{2,1,0:T(8,128)(2,1)S(1)}, u32[]{:S(2)}, u32[]{:S(2)}) collective-permute-start(bf16[1,2048,128]{2,1,0:T(8,128)(2,1)S(1)} %get-tuple-element.56), channel_id=1, source_target_pairs={{2,3},{1,0},{6,7},{5,4},{10,11},{9,8},{14,15},{13,12},{18,19},{17,... | collective-permute-start | bytes 1572872 | tf_op jit(solution)/shard_map/ppermute | solution.py:358
  54.7 15.9 %collective-permute-start.13 = (bf16[1,2048,128]{2,1,0:T(8,128)(2,1)S(1)}, bf16[1,2048,128]{2,1,0:T(8,128)(2,1)S(1)}, u32[]{:S(2)}, u32[]{:S(2)}) collective-permute-start(bf16[1,2048,128]{2,1,0:T(8,128)(2,1)S(1)} %get-tuple-element.55.r_5_), channel_id=1, source_target_pairs={{0,8},{4,12},{8,0},{12,4},{16,24},{20,28},{24,16},{28,20},{1,9},{5... | collective-permute-start | bytes 1572872 | tf_op jit(solution)/shard_map/ppermute | solution.py:326
  58.5 12.1 %collective-permute-start.11 = (bf16[1,2048,128]{2,1,0:T(8,128)(2,1)S(1)}, bf16[1,2048,128]{2,1,0:T(8,128)(2,1)S(1)}, u32[]{:S(2)}, u32[]{:S(2)}) collective-permute-start(bf16[1,2048,128]{2,1,0:T(8,128)(2,1)S(1)} %get-tuple-element.55.r_5_), channel_id=1, source_target_pairs={{16,0},{4,20},{24,8},{12,28},{17,1},{5,21},{25,9},{13,29},{18,2},{... | collective-permute-start | bytes 1572872 | tf_op jit(solution)/shard_map/ppermute | solution.py:326
  59.8 17.3 %collective-permute-start.12 = (bf16[1,2048,128]{2,1,0:T(8,128)(2,1)S(1)}, bf16[1,2048,128]{2,1,0:T(8,128)(2,1)S(1)}, u32[]{:S(2)}, u32[]{:S(2)}) collective-permute-start(bf16[1,2048,128]{2,1,0:T(8,128)(2,1)S(1)} %copy-done.12), channel_id=1, source_target_pairs={{28,12},{0,16},{24,8},{4,20},{29,13},{1,17},{25,9},{5,21},{30,14},... | collective-permute-start | bytes 1572872 | tf_op jit(solution)/shard_map/ppermute | solution.py:326
  77.4 23.1 %collective-permute-start.14 = (bf16[4,2048,128]{2,1,0:T(8,128)(2,1)S(1)}, bf16[4,2048,128]{2,1,0:T(8,128)(2,1)S(1)}, u32[]{:S(2)}, u32[]{:S(2)}) collective-permute-start(bf16[4,2048,128]{2,1,0:T(8,128)(2,1)S(1)} %pad_maximum_fusion.1), channel_id=1, source_target_pairs={{0,4},{4,0},{8,12},{12,8},{16,20},{20,16},{24,28},{28,24},{1,5},{5... | collective-permute-start | bytes 6291464 | tf_op jit(solution)/shard_map/ppermute | solution.py:326
  77.9 22.6 %collective-permute-start.15 = (bf16[3,2048,128]{2,1,0:T(8,128)(2,1)S(1)}, bf16[3,2048,128]{2,1,0:T(8,128)(2,1)S(1)}, u32[]{:S(2)}, u32[]{:S(2)}) collective-permute-start(bf16[3,2048,128]{2,1,0:T(8,128)(2,1)S(1)} %pad_maximum_fusion.3), channel_id=1, source_target_pairs={{0,4},{4,0},{8,12},{12,8},{16,20},{20,16},{24,28},{28,24},{1,5},{5... | collective-permute-start | bytes 4718600 | tf_op jit(solution)/shard_map/ppermute | solution.py:326
  78.7 15.0 %collective-permute-start.18 = (bf16[1,2048,128]{2,1,0:T(8,128)(2,1)S(1)}, bf16[1,2048,128]{2,1,0:T(8,128)(2,1)S(1)}, u32[]{:S(2)}, u32[]{:S(2)}) collective-permute-start(bf16[1,2048,128]{2,1,0:T(8,128)(2,1)S(1)} %select_select_fusion.r_6_), channel_id=1, source_target_pairs={{0,8},{4,12},{8,0},{12,4},{16,24},{20,28},{24,16},{28,20},{1,9},{5... | collective-permute-start | bytes 1572872 | tf_op jit(solution)/shard_map/ppermute | solution.py:326
  82.1 11.7 %collective-permute-start.16 = (bf16[1,2048,128]{2,1,0:T(8,128)(2,1)S(1)}, bf16[1,2048,128]{2,1,0:T(8,128)(2,1)S(1)}, u32[]{:S(2)}, u32[]{:S(2)}) collective-permute-start(bf16[1,2048,128]{2,1,0:T(8,128)(2,1)S(1)} %select_select_fusion.r_6_), channel_id=1, source_target_pairs={{16,0},{4,20},{24,8},{12,28},{17,1},{5,21},{25,9},{13,29},{18,2},{... | collective-permute-start | bytes 1572872 | tf_op jit(solution)/shard_map/ppermute | solution.py:326
  83.4 17.1 %collective-permute-start.17 = (bf16[1,2048,128]{2,1,0:T(8,128)(2,1)S(1)}, bf16[1,2048,128]{2,1,0:T(8,128)(2,1)S(1)}, u32[]{:S(2)}, u32[]{:S(2)}) collective-permute-start(bf16[1,2048,128]{2,1,0:T(8,128)(2,1)S(1)} %collective-permute-done.13.r_9_), channel_id=1, source_target_pairs={{28,12},{0,16},{24,8},{4,20},{29,13},{1,17},{25,9},{5,21},{30,14},... | collective-permute-start | bytes 1572872 | tf_op jit(solution)/shard_map/ppermute | solution.py:326
  102.7 9.6 %collective-permute-start.21 = (bf16[4,2048,128]{2,1,0:T(8,128)(2,1)}, bf16[4,2048,128]{2,1,0:T(8,128)(2,1)}, u32[]{:S(2)}, u32[]{:S(2)}) collective-permute-start(bf16[4,2048,128]{2,1,0:T(8,128)(2,1)} %pad_maximum_fusion.2), channel_id=1, source_target_pairs={{0,4},{4,0},{8,12},{12,8},{16,20},{20,16},{24,28},{28,24},{1,5},{5... | collective-permute-start | bytes 6291464 | tf_op jit(solution)/shard_map/ppermute | solution.py:326
  103.3 9.0 %collective-permute-start.19 = (bf16[1,2048,128]{2,1,0:T(8,128)(2,1)S(1)}, bf16[1,2048,128]{2,1,0:T(8,128)(2,1)S(1)}, u32[]{:S(2)}, u32[]{:S(2)}) collective-permute-start(bf16[1,2048,128]{2,1,0:T(8,128)(2,1)S(1)} %collective-permute-done.18.r_10_), channel_id=1, source_target_pairs={{28,12},{0,16},{29,13},{1,17},{30,14},{2,18},{31,15},{3,19}} | collective-permute-start | bytes 1572872 | tf_op jit(solution)/shard_map/ppermute | solution.py:326
  104.0 8.2 %collective-permute-start.20 = (bf16[1,2048,128]{2,1,0:T(8,128)(2,1)S(1)}, bf16[1,2048,128]{2,1,0:T(8,128)(2,1)S(1)}, u32[]{:S(2)}, u32[]{:S(2)}) collective-permute-start(bf16[1,2048,128]{2,1,0:T(8,128)(2,1)S(1)} %collective-permute-done.16.r_14_), channel_id=1, source_target_pairs={{0,8},{28,20},{1,9},{29,21},{2,10},{30,22},{3,11},{31,23}} | collective-permute-start | bytes 1572872 | tf_op jit(solution)/shard_map/ppermute | solution.py:326
  112.4 7.9 %collective-permute-start.22 = (bf16[2,2048,128]{2,1,0:T(8,128)(2,1)S(1)}, bf16[2,2048,128]{2,1,0:T(8,128)(2,1)S(1)}, u32[]{:S(2)}, u32[]{:S(2)}) collective-permute-start(bf16[2,2048,128]{2,1,0:T(8,128)(2,1)S(1)} %pad_maximum_fusion.4), channel_id=1, source_target_pairs={{0,4},{4,0},{8,12},{12,8},{16,20},{20,16},{24,28},{28,24},{1,5},{5... | collective-permute-start | bytes 3145736 | tf_op jit(solution)/shard_map/ppermute | solution.py:326
  (27 other events, 314.6 us)

commit v5 on v4

--- a/solution.py
+++ b/solution.py
@@ -122,7 +122,7 @@
             pltpu.VMEM((2 * bins, length), jnp.bfloat16),
             pltpu.VMEM((bins // GROUP, GROUP * windows * 2, channels), jnp.float32),
         ],
-        compiler_params=pltpu.CompilerParams(vmem_limit_bytes=48 << 20),
+        compiler_params=pltpu.CompilerParams(vmem_limit_bytes=12 << 20),
         name="spectra",
     )(rows, cos[:, :fine], sin[:, :fine], cos[:, fine:], sin[:, fine:])
 
@@ -181,7 +181,7 @@
             ],
         ),
         out_shape=jax.ShapeDtypeStruct((groups, m, k), jnp.bfloat16),
-        compiler_params=pltpu.CompilerParams(vmem_limit_bytes=32 << 20),
+        compiler_params=pltpu.CompilerParams(vmem_limit_bytes=10 << 20),
         name="left",
     )(z.reshape(1), *slabs)
 
@@ -193,8 +193,8 @@
 
 def pairs_kernel(slots, left_ref, lag_ref, *refs, arrays, norm):
     sources, refs = refs[: len(arrays)], refs[len(arrays) :]
-    out_ref, partner, left, gram, stage, in_sems, left_sems, out_sems = refs
-    groups, m, k = left.shape
+    out_ref, partner, gram, stage, in_sems, out_sems = refs
+    groups, m, k = left_ref.shape
     slot_count, slabs, slab_rows, channels = partner.shape
     group_rows = k // slabs
     chunk_rows = slab_rows // CHUNKS
@@ -217,15 +217,7 @@
 
     per_chunk = groups // CHUNKS
 
-    def fetch_left(chunk):
-        some = pl.ds(chunk * per_chunk, per_chunk)
-        return pltpu.make_async_copy(left_ref.at[some], left.at[some], left_sems.at[chunk])
-
     for chunk in range(CHUNKS):
-        fetch_left(chunk).start()
-
-    for chunk in range(CHUNKS):
-        fetch_left(chunk).wait()
         for s in range(slot_count):
             for r in range(slabs):
                 fetch(sources[0].at[0], s, r, chunk).wait()
@@ -238,7 +230,7 @@
                 right = jnp.concatenate(
                     [partner[s, :, rows, :].reshape(k, channels) for s in range(slot_count)], 1
                 )
-                product = jnp.dot(left[g], right, preferred_element_type=jnp.float32)
+                product = jnp.dot(left_ref[g], right, preferred_element_type=jnp.float32)
                 cols = pl.ds(pl.multiple_of(g * 2 * GROUP, 2 * GROUP), 2 * GROUP)
                 gram[:, cols, :] = product.astype(jnp.bfloat16).reshape(
                     m // (2 * GROUP), 2 * GROUP, lanes
@@ -285,19 +277,17 @@
     in_vmem = pl.BlockSpec(memory_space=pltpu.VMEM)
     return pl.pallas_call(
         lambda *r: pairs_kernel(*r, arrays=arrays, norm=norm),
-        in_specs=[pl.BlockSpec(memory_space=pltpu.SMEM), anywhere, in_vmem] + [anywhere] * len(held),
+        in_specs=[pl.BlockSpec(memory_space=pltpu.SMEM), in_vmem, in_vmem] + [anywhere] * len(held),
         out_specs=anywhere,
         scratch_shapes=[
             pltpu.VMEM((slot_count, slabs, slab_rows, channels), jnp.bfloat16),
-            pltpu.VMEM((groups, m, k), jnp.bfloat16),
             pltpu.VMEM((rows_out, entries, slot_count * channels), jnp.bfloat16),
             pltpu.VMEM((2, ROW_UNROLL, slot_count, channels, lag_count), jnp.float32),
             pltpu.SemaphoreType.DMA((CHUNKS, slot_count, slabs)),
-            pltpu.SemaphoreType.DMA((CHUNKS,)),
             pltpu.SemaphoreType.DMA((2,)),
         ],
         out_shape=jax.ShapeDtypeStruct((rows_out, slot_count, channels, lag_count), jnp.float32),
-        compiler_params=pltpu.CompilerParams(vmem_limit_bytes=58 << 20),
+        compiler_params=pltpu.CompilerParams(vmem_limit_bytes=25 << 20),
         name="pairs",
     )(slots, left, lag_rows, *[value for value, _ in held])
 
@@ -362,9 +352,9 @@
 
     s0 = make_slab(traces, band_bins)[None]
     q0 = slab_of(s0, 0)
-    down1, up1 = along_z(s0, [(3, 2), (2, 1), (1, 0)]), along_z(s0, [(0, 1), (1, 2), (2, 3)])
     y0 = q0.hop(Y_PAIRS)
     x0 = q0.hop(X_PAIRS)
+    down1, up1 = along_z(s0, [(3, 2), (2, 1), (1, 0)]), along_z(s0, [(0, 1), (1, 2), (2, 3)])
     y0, down1, up1, x0, lag_rows = together(y0, down1, up1, x0, lag_rows)
 
     q1 = slab_of(lax.select_n(z, down1, up1, down1, up1), 1)
@@ -406,8 +396,11 @@
                 if block_slab is not None:
                     table[device, block_slab[0], block_slab[1]] = index
                     holds.add(block_slab[1])
-    mine = jnp.asarray(table)[me]
-    slots = jnp.concatenate([mine[pair_blocks[0, s]] for s in range(slot_count)])
+    ids = np.arange(8, dtype=np.int32)
+    wanted = (ids[None, None, :, None] == pair_blocks[0][:, None, None, None]) & (
+        ids[None, :, None, None] == me
+    )
+    slots = jnp.sum(jnp.where(wanted, table[None], 0), axis=(1, 2)).reshape(-1)
 
     c3, d3, a3, slots = together(c3, d3, a3, slots)
     a4 = join(c3, d3).hop(CORE_PAIRS)

time: 140 us -> 157 us (1.12)
  local copies, waits for them, and re-layouts: 12.7 us -> 26.6 us
  starting transfers between devices: 42.7 us -> 49.3 us
  between operations: 6 us -> 0.33 us
  Pallas kernels: 23.2 us -> 20.6 us
  waiting for transfers between devices: 43.8 us -> 45.9 us
  other arithmetic: 10 us -> 11.7 us
    unnamed x56 -> x68, local copies, waits for them, and re-layouts: 7.61 us -> 23.5 us
    ppermute x18, starting transfers between devices: 31.6 us -> 38.1 us  [hop(): lax.ppermute(self.value, 'chan', pairs)]
    concatenate x5, other arithmetic: 3.87 us -> 7.08 us  [join(): jnp.concatenate([p.value for p in parts], 0)]
    pallas_call x1, Pallas kernels: 17.2 us -> 14.6 us  [correlate(): pl.pallas_call(lambda *r: pairs_kernel(*r, arrays=arrays, norm=norm), in_...]
  transfers between devices with their start and end apart: 23 -> 23, of which waited for: 12 -> 13; matrix products, arithmetic and copies ran while one was open for 4% -> 2% of each run, Pallas kernels for 3% -> 3%
where the time goes in v5:
time: 157 us; the launch traced here: 154 us
  starting transfers between devices  49.3 us (31%)
  waiting for transfers between devices  45.9 us (29%)
  local copies, waits for them, and re-layouts  26.6 us (17%)
  Pallas kernels  20.6 us (13%)
  other arithmetic  11.7 us (7%)
    ppermute x18, starting transfers between devices, hop(): lax.ppermute(self.value, 'chan', pairs)  38.1 us
    ppermute x18, waiting for transfers between devices, hop(): lax.ppermute(self.value, 'chan', pairs)  27.1 us
    unnamed x68, local copies, waits for them, and re-layouts  23.5 us
    ppermute x5, waiting for transfers between devices, along_z(): return lax.ppermute(value, 'freq', pairs)  18.8 us
    pallas_call x1, Pallas kernels, correlate(): pl.pallas_call(lambda *r: pairs_kernel(*r, arrays=arrays, norm=norm), in_...  14.6 us
    ppermute x5, starting transfers between devices, along_z(): return lax.ppermute(value, 'freq', pairs)  11.2 us
    concatenate x5, other arithmetic, join(): jnp.concatenate([p.value for p in parts], 0)  7.08 us
    pallas_call x1, Pallas kernels, make_left(): pl.pallas_call(lambda *r: left_kernel(*r, per_step=per_step), grid_spec=p...  4.04 us
  transfers between devices with their start and end apart: 23, of which 13 were waited for; matrix products, arithmetic and copies ran while one was open for 2% of the time, Pallas kernels for 3%

profile of v5, /device:TPU:17, one launch (start us, length us, event | category | flops | bytes accessed | tf_op | source)
XLA Modules:
  0.0 154.4 jit_solution(10506691525497458656)
XLA Ops:
  1.9 2.7 %copy.12 = bf16[4,128,2048]{2,1,0:T(8,128)(2,1)S(1)} copy(bf16[4,128,2048]{2,0,1:T(4,128)(2,1)} %bitcast.22) | data formatting | bytes 4194304 | tf_op jit(solution)/shard_map/transpose | solution.py:113
  7.8 3.2 %collective-permute-start.2 = (bf16[1,2048,128]{2,1,0:T(8,128)(2,1)S(1)}, bf16[1,2048,128]{2,1,0:T(8,128)(2,1)S(1)}, u32[]{:S(2)}, u32[]{:S(2)}) collective-permute-start(bf16[1,2048,128]{2,1,0:T(8,128)(2,1)S(1)} %bitcast.15), channel_id=1, source_target_pairs={{0,1},{1,2},{2,3},{4,5},{5,6},{6,7},{8,9},{9,10},{10,11},{12,13},{... | collective-permute-start | bytes 1572872 | tf_op jit(solution)/shard_map/ppermute | solution.py:348
  13.1 3.2 %collective-permute-start = (bf16[1,2048,128]{2,1,0:T(8,128)(2,1)S(1)}, bf16[1,2048,128]{2,1,0:T(8,128)(2,1)S(1)}, u32[]{:S(2)}, u32[]{:S(2)}) collective-permute-start(bf16[1,2048,128]{2,1,0:T(8,128)(2,1)S(1)} %bitcast.17), channel_id=1, source_target_pairs={{16,0},{4,20},{24,8},{12,28},{17,1},{5,21},{25,9},{13,29},{18,2},{... | collective-permute-start | bytes 1572872 | tf_op jit(solution)/shard_map/ppermute | solution.py:316
  17.1 2.3 %collective-permute-done.3.r_7_ = bf16[1,2048,128]{2,1,0:T(8,128)(2,1)S(1)} collective-permute-done((bf16[1,2048,128]{2,1,0:T(8,128)(2,1)S(1)}, bf16[1,2048,128]{2,1,0:T(8,128)(2,1)S(1)}, u32[]{:S(2)}, u32[]{:S(2)}) %collective-permute-start.3) | collective-permute-done | bytes 524320 | tf_op jit(solution)/shard_map/ppermute | solution.py:316
  19.4 2.8 %collective-permute-done.2 = bf16[1,2048,128]{2,1,0:T(8,128)(2,1)S(1)} collective-permute-done((bf16[1,2048,128]{2,1,0:T(8,128)(2,1)S(1)}, bf16[1,2048,128]{2,1,0:T(8,128)(2,1)S(1)}, u32[]{:S(2)}, u32[]{:S(2)}) %collective-permute-start.2) | collective-permute-done | bytes 524320 | tf_op jit(solution)/shard_map/ppermute | solution.py:348
  22.2 2.9 %collective-permute-done.1 = bf16[1,2048,128]{2,1,0:T(8,128)(2,1)S(1)} collective-permute-done((bf16[1,2048,128]{2,1,0:T(8,128)(2,1)S(1)}, bf16[1,2048,128]{2,1,0:T(8,128)(2,1)S(1)}, u32[]{:S(2)}, u32[]{:S(2)}) %collective-permute-start.1) | collective-permute-done | bytes 524320 | tf_op jit(solution)/shard_map/ppermute | solution.py:348
  25.5 3.2 %collective-permute-start.6 = (bf16[1,2048,128]{2,1,0:T(8,128)(2,1)S(1)}, bf16[1,2048,128]{2,1,0:T(8,128)(2,1)S(1)}, u32[]{:S(2)}, u32[]{:S(2)}) collective-permute-start(bf16[1,2048,128]{2,1,0:T(8,128)(2,1)S(1)} %select_select_fusion.2.r_4_), channel_id=1, source_target_pairs={{16,0},{4,20},{24,8},{12,28},{17,1},{5,21},{25,9},{13,29},{18,2},{... | collective-permute-start | bytes 1572872 | tf_op jit(solution)/shard_map/ppermute | solution.py:316
  28.7 2.1 %collective-permute-start.5 = (bf16[1,2048,128]{2,1,0:T(8,128)(2,1)S(1)}, bf16[1,2048,128]{2,1,0:T(8,128)(2,1)S(1)}, u32[]{:S(2)}, u32[]{:S(2)}) collective-permute-start(bf16[1,2048,128]{2,1,0:T(8,128)(2,1)S(1)} %collective-permute-done.1), channel_id=1, source_target_pairs={{2,1},{1,0},{6,5},{5,4},{10,9},{9,8},{14,13},{13,12},{18,17},{17,1... | collective-permute-start | bytes 1572872 | tf_op jit(solution)/shard_map/ppermute | solution.py:348
  34.0 2.5 %collective-permute-done.8.r_8_ = bf16[1,2048,128]{2,1,0:T(8,128)(2,1)S(1)} collective-permute-done((bf16[1,2048,128]{2,1,0:T(8,128)(2,1)S(1)}, bf16[1,2048,128]{2,1,0:T(8,128)(2,1)S(1)}, u32[]{:S(2)}, u32[]{:S(2)}) %collective-permute-start.8) | collective-permute-done | bytes 524320 | tf_op jit(solution)/shard_map/ppermute | solution.py:316
  37.3 4.2 %collective-permute-done.5 = bf16[1,2048,128]{2,1,0:T(8,128)(2,1)S(1)} collective-permute-done((bf16[1,2048,128]{2,1,0:T(8,128)(2,1)S(1)}, bf16[1,2048,128]{2,1,0:T(8,128)(2,1)S(1)}, u32[]{:S(2)}, u32[]{:S(2)}) %collective-permute-start.5) | collective-permute-done | bytes 524320 | tf_op jit(solution)/shard_map/ppermute | solution.py:348
  41.5 3.8 %collective-permute-done.4 = bf16[1,2048,128]{2,1,0:T(8,128)(2,1)S(1)} collective-permute-done((bf16[1,2048,128]{2,1,0:T(8,128)(2,1)S(1)}, bf16[1,2048,128]{2,1,0:T(8,128)(2,1)S(1)}, u32[]{:S(2)}, u32[]{:S(2)}) %collective-permute-start.4) | collective-permute-done | bytes 524320 | tf_op jit(solution)/shard_map/ppermute | solution.py:348
  52.9 3.4 %collective-permute-start.13 = (bf16[1,2048,128]{2,1,0:T(8,128)(2,1)S(1)}, bf16[1,2048,128]{2,1,0:T(8,128)(2,1)S(1)}, u32[]{:S(2)}, u32[]{:S(2)}) collective-permute-start(bf16[1,2048,128]{2,1,0:T(8,128)(2,1)S(1)} %get-tuple-element.55.r_5_), channel_id=1, source_target_pairs={{0,8},{4,12},{8,0},{12,4},{16,24},{20,28},{24,16},{28,20},{1,9},{5... | collective-permute-start | bytes 1572872 | tf_op jit(solution)/shard_map/ppermute | solution.py:316
  59.1 5.2 %collective-permute-done.9 = bf16[1,2048,128]{2,1,0:T(8,128)(2,1)S(1)} collective-permute-done((bf16[1,2048,128]{2,1,0:T(8,128)(2,1)S(1)}, bf16[1,2048,128]{2,1,0:T(8,128)(2,1)S(1)}, u32[]{:S(2)}, u32[]{:S(2)}) %collective-permute-start.9) | collective-permute-done | bytes 524320 | tf_op jit(solution)/shard_map/ppermute | solution.py:348
  64.2 4.2 %collective-permute-done.13.r_9_ = bf16[1,2048,128]{2,1,0:T(8,128)(2,1)S(1)} collective-permute-done((bf16[1,2048,128]{2,1,0:T(8,128)(2,1)S(1)}, bf16[1,2048,128]{2,1,0:T(8,128)(2,1)S(1)}, u32[]{:S(2)}, u32[]{:S(2)}) %collective-permute-start.13) | collective-permute-done | bytes 524320 | tf_op jit(solution)/shard_map/ppermute | solution.py:316
  68.5 6.6 %collective-permute-done.12.r_16_ = bf16[1,2048,128]{2,1,0:T(8,128)(2,1)S(1)} collective-permute-done((bf16[1,2048,128]{2,1,0:T(8,128)(2,1)S(1)}, bf16[1,2048,128]{2,1,0:T(8,128)(2,1)S(1)}, u32[]{:S(2)}, u32[]{:S(2)}) %collective-permute-start.12) | collective-permute-done | bytes 524320 | tf_op jit(solution)/shard_map/ppermute | solution.py:316
  77.9 3.2 %collective-permute-start.18 = (bf16[1,2048,128]{2,1,0:T(8,128)(2,1)S(1)}, bf16[1,2048,128]{2,1,0:T(8,128)(2,1)S(1)}, u32[]{:S(2)}, u32[]{:S(2)}) collective-permute-start(bf16[1,2048,128]{2,1,0:T(8,128)(2,1)S(1)} %select_select_fusion.r_6_), channel_id=1, source_target_pairs={{0,8},{4,12},{8,0},{12,4},{16,24},{20,28},{24,16},{28,20},{1,9},{5... | collective-permute-start | bytes 1572872 | tf_op jit(solution)/shard_map/ppermute | solution.py:316
  83.8 4.0 %left.1.r_1_ = bf16[32,512,256]{2,1,0:T(8,128)(2,1)S(1)} custom-call(s32[1]{0:T(128)} %bitcast.4.r_0_, bf16[2048,128]{1,0:T(8,128)(2,1)S(1)} %spectra.1.r_1_, bf16[2048,128]{1,0:T(8,128)(2,1)S(1)} %bitcast.12, bf16[2048,128]{1,0:T(8,128)(2,1)S(1)} %bitcast.13, bf16[2048,128]{1,0:T(8,128)(2,1)S(1)} %bitcast.20), custom_call_target="tpu_custom_call" | custom-call | tf_op jit(solution)/shard_map/left/pallas_call | solution.py:168
  87.8 3.3 %copy-done = bf16[32,512,256]{2,1,0:T(8,128)(2,1)} copy-done((bf16[32,512,256]{2,1,0:T(8,128)(2,1)}, bf16[32,512,256]{2,1,0:T(8,128)(2,1)S(1)}, u32[]{:S(2)}) %copy-start) | copy-done | bytes 8388632
  92.6 6.8 %collective-permute-done.17.r_17_ = bf16[1,2048,128]{2,1,0:T(8,128)(2,1)S(1)} collective-permute-done((bf16[1,2048,128]{2,1,0:T(8,128)(2,1)S(1)}, bf16[1,2048,128]{2,1,0:T(8,128)(2,1)S(1)}, u32[]{:S(2)}, u32[]{:S(2)}) %collective-permute-start.17) | collective-permute-done | bytes 524320 | tf_op jit(solution)/shard_map/ppermute | solution.py:316
  108.4 2.3 %pad_maximum_fusion.4 = bf16[2,2048,128]{2,1,0:T(8,128)(2,1)} fusion(bf16[1,2048,128]{2,1,0:T(8,128)(2,1)} %collective-permute-done.20.r_19_, bf16[1,2048,128]{2,1,0:T(8,128)(2,1)} %collective-permute-done.19.r_18_), kind=kLoop, calls=%fused_computation.4 | loop fusion | flops 524288 | bytes 2097152 | tf_op jit(solution)/shard_map/concatenate | solution.py:320
  110.7 10.7 %collective-permute-start.22 = (bf16[2,2048,128]{2,1,0:T(8,128)(2,1)}, bf16[2,2048,128]{2,1,0:T(8,128)(2,1)}, u32[]{:S(2)}, u32[]{:S(2)}) collective-permute-start(bf16[2,2048,128]{2,1,0:T(8,128)(2,1)} %pad_maximum_fusion.4), channel_id=1, source_target_pairs={{0,4},{4,0},{8,12},{12,8},{16,20},{20,16},{24,28},{28,24},{1,5},{5... | collective-permute-start | bytes 3145736 | tf_op jit(solution)/shard_map/ppermute | solution.py:316
  121.5 2.5 %collective-permute-done.22.r_24_ = bf16[2,2048,128]{2,1,0:T(8,128)(2,1)} collective-permute-done((bf16[2,2048,128]{2,1,0:T(8,128)(2,1)}, bf16[2,2048,128]{2,1,0:T(8,128)(2,1)}, u32[]{:S(2)}, u32[]{:S(2)}) %collective-permute-start.22) | collective-permute-done | bytes 1048608 | tf_op jit(solution)/shard_map/ppermute | solution.py:316
  124.0 3.4 %copy-done.1 = bf16[32,512,256]{2,1,0:T(8,128)(2,1)S(1)} copy-done((bf16[32,512,256]{2,1,0:T(8,128)(2,1)S(1)}, bf16[32,512,256]{2,1,0:T(8,128)(2,1)}, u32[]{:S(2)}) %copy-start.1) | copy-done | bytes 8388632
  139.8 14.6 %pairs.1 = f32[32,3,128,128]{3,2,1,0:T(8,128)} custom-call(s32[12]{0:T(128)S(1)} %reshape.188.r_0_, bf16[32,512,256]{2,1,0:T(8,128)(2,1)S(1)} %copy-done.1, bf16[128,512]{1,0:T(8,128)(2,1)S(1)} %copy.14.r_2_, bf16[1,2048,128]{2,1,0:T(8,128)(2,1)S(1)} %bitcast.19, bf16[1,2048,128]{2,1,0:T(8,128)(2,1)S(1)} %select_select_fusion.2.r_4_, ...), custom_call_target="tpu_custom_call" | custom-call | tf_op jit(solution)/shard_map/pairs/pallas_call | solution.py:278
  (120 shorter events, 50.9 us)
Async XLA Ops:
  6.5 12.9 %collective-permute-start.3 = (bf16[1,2048,128]{2,1,0:T(8,128)(2,1)S(1)}, bf16[1,2048,128]{2,1,0:T(8,128)(2,1)S(1)}, u32[]{:S(2)}, u32[]{:S(2)}) collective-permute-start(bf16[1,2048,128]{2,1,0:T(8,128)(2,1)S(1)} %bitcast.14), channel_id=1, source_target_pairs={{0,8},{4,12},{8,0},{12,4},{16,24},{20,28},{24,16},{28,20},{1,9},{5... | collective-permute-start | bytes 1572872 | tf_op jit(solution)/shard_map/ppermute | solution.py:316
  7.8 14.4 %collective-permute-start.2 = (bf16[1,2048,128]{2,1,0:T(8,128)(2,1)S(1)}, bf16[1,2048,128]{2,1,0:T(8,128)(2,1)S(1)}, u32[]{:S(2)}, u32[]{:S(2)}) collective-permute-start(bf16[1,2048,128]{2,1,0:T(8,128)(2,1)S(1)} %bitcast.15), channel_id=1, source_target_pairs={{0,1},{1,2},{2,3},{4,5},{5,6},{6,7},{8,9},{9,10},{10,11},{12,13},{... | collective-permute-start | bytes 1572872 | tf_op jit(solution)/shard_map/ppermute | solution.py:348
  11.0 14.1 %collective-permute-start.1 = (bf16[1,2048,128]{2,1,0:T(8,128)(2,1)S(1)}, bf16[1,2048,128]{2,1,0:T(8,128)(2,1)S(1)}, u32[]{:S(2)}, u32[]{:S(2)}) collective-permute-start(bf16[1,2048,128]{2,1,0:T(8,128)(2,1)S(1)} %bitcast.16), channel_id=1, source_target_pairs={{3,2},{2,1},{1,0},{7,6},{6,5},{5,4},{11,10},{10,9},{9,8},{15,14},{... | collective-permute-start | bytes 1572872 | tf_op jit(solution)/shard_map/ppermute | solution.py:348
  13.1 12.0 %collective-permute-start = (bf16[1,2048,128]{2,1,0:T(8,128)(2,1)S(1)}, bf16[1,2048,128]{2,1,0:T(8,128)(2,1)S(1)}, u32[]{:S(2)}, u32[]{:S(2)}) collective-permute-start(bf16[1,2048,128]{2,1,0:T(8,128)(2,1)S(1)} %bitcast.17), channel_id=1, source_target_pairs={{16,0},{4,20},{24,8},{12,28},{17,1},{5,21},{25,9},{13,29},{18,2},{... | collective-permute-start | bytes 1572872 | tf_op jit(solution)/shard_map/ppermute | solution.py:316
  19.4 28.3 %copy-start.2 = (bf16[1,2048,128]{2,1,0:T(8,128)(2,1)}, bf16[1,2048,128]{2,1,0:T(8,128)(2,1)S(1)}, u32[]{:S(2)}) copy-start(bf16[1,2048,128]{2,1,0:T(8,128)(2,1)S(1)} %collective-permute-done.3.r_7_) | copy-start | bytes 1572868
  25.2 11.3 %collective-permute-start.8 = (bf16[1,2048,128]{2,1,0:T(8,128)(2,1)S(1)}, bf16[1,2048,128]{2,1,0:T(8,128)(2,1)S(1)}, u32[]{:S(2)}, u32[]{:S(2)}) collective-permute-start(bf16[1,2048,128]{2,1,0:T(8,128)(2,1)S(1)} %select_select_fusion.2.r_4_), channel_id=1, source_target_pairs={{0,8},{4,12},{8,0},{12,4},{16,24},{20,28},{24,16},{28,20},{1,9},{5... | collective-permute-start | bytes 1572872 | tf_op jit(solution)/shard_map/ppermute | solution.py:316
  25.5 11.0 %collective-permute-start.6 = (bf16[1,2048,128]{2,1,0:T(8,128)(2,1)S(1)}, bf16[1,2048,128]{2,1,0:T(8,128)(2,1)S(1)}, u32[]{:S(2)}, u32[]{:S(2)}) collective-permute-start(bf16[1,2048,128]{2,1,0:T(8,128)(2,1)S(1)} %select_select_fusion.2.r_4_), channel_id=1, source_target_pairs={{16,0},{4,20},{24,8},{12,28},{17,1},{5,21},{25,9},{13,29},{18,2},{... | collective-permute-start | bytes 1572872 | tf_op jit(solution)/shard_map/ppermute | solution.py:316
  28.7 12.8 %collective-permute-start.5 = (bf16[1,2048,128]{2,1,0:T(8,128)(2,1)S(1)}, bf16[1,2048,128]{2,1,0:T(8,128)(2,1)S(1)}, u32[]{:S(2)}, u32[]{:S(2)}) collective-permute-start(bf16[1,2048,128]{2,1,0:T(8,128)(2,1)S(1)} %collective-permute-done.1), channel_id=1, source_target_pairs={{2,1},{1,0},{6,5},{5,4},{10,9},{9,8},{14,13},{13,12},{18,17},{17,1... | collective-permute-start | bytes 1572872 | tf_op jit(solution)/shard_map/ppermute | solution.py:348
  30.8 14.5 %collective-permute-start.4 = (bf16[1,2048,128]{2,1,0:T(8,128)(2,1)S(1)}, bf16[1,2048,128]{2,1,0:T(8,128)(2,1)S(1)}, u32[]{:S(2)}, u32[]{:S(2)}) collective-permute-start(bf16[1,2048,128]{2,1,0:T(8,128)(2,1)S(1)} %collective-permute-done.2), channel_id=1, source_target_pairs={{1,2},{2,3},{5,6},{6,7},{9,10},{10,11},{13,14},{14,15},{17,18},{18... | collective-permute-start | bytes 1572872 | tf_op jit(solution)/shard_map/ppermute | solution.py:348
  32.7 13.4 %collective-permute-start.7 = (bf16[1,2048,128]{2,1,0:T(8,128)(2,1)S(1)}, bf16[1,2048,128]{2,1,0:T(8,128)(2,1)S(1)}, u32[]{:S(2)}, u32[]{:S(2)}) collective-permute-start(bf16[1,2048,128]{2,1,0:T(8,128)(2,1)S(1)} %collective-permute-done.3.r_7_), channel_id=1, source_target_pairs={{28,12},{0,16},{24,8},{4,20},{29,13},{1,17},{25,9},{5,21},{30,14},... | collective-permute-start | bytes 1572872 | tf_op jit(solution)/shard_map/ppermute | solution.py:316
  47.7 27.4 %collective-permute-start.10 = (bf16[4,2048,128]{2,1,0:T(8,128)(2,1)}, bf16[4,2048,128]{2,1,0:T(8,128)(2,1)}, u32[]{:S(2)}, u32[]{:S(2)}) collective-permute-start(bf16[4,2048,128]{2,1,0:T(8,128)(2,1)} %pad_maximum_fusion), channel_id=1, source_target_pairs={{0,4},{4,0},{8,12},{12,8},{16,20},{20,16},{24,28},{28,24},{1,5},{5... | collective-permute-start | bytes 6291464 | tf_op jit(solution)/shard_map/ppermute | solution.py:316
  51.0 13.2 %collective-permute-start.9 = (bf16[1,2048,128]{2,1,0:T(8,128)(2,1)S(1)}, bf16[1,2048,128]{2,1,0:T(8,128)(2,1)S(1)}, u32[]{:S(2)}, u32[]{:S(2)}) collective-permute-start(bf16[1,2048,128]{2,1,0:T(8,128)(2,1)S(1)} %get-tuple-element.56), channel_id=1, source_target_pairs={{2,3},{1,0},{6,7},{5,4},{10,11},{9,8},{14,15},{13,12},{18,19},{17,... | collective-permute-start | bytes 1572872 | tf_op jit(solution)/shard_map/ppermute | solution.py:348
  52.9 15.5 %collective-permute-start.13 = (bf16[1,2048,128]{2,1,0:T(8,128)(2,1)S(1)}, bf16[1,2048,128]{2,1,0:T(8,128)(2,1)S(1)}, u32[]{:S(2)}, u32[]{:S(2)}) collective-permute-start(bf16[1,2048,128]{2,1,0:T(8,128)(2,1)S(1)} %get-tuple-element.55.r_5_), channel_id=1, source_target_pairs={{0,8},{4,12},{8,0},{12,4},{16,24},{20,28},{24,16},{28,20},{1,9},{5... | collective-permute-start | bytes 1572872 | tf_op jit(solution)/shard_map/ppermute | solution.py:316
  56.4 12.1 %collective-permute-start.11 = (bf16[1,2048,128]{2,1,0:T(8,128)(2,1)S(1)}, bf16[1,2048,128]{2,1,0:T(8,128)(2,1)S(1)}, u32[]{:S(2)}, u32[]{:S(2)}) collective-permute-start(bf16[1,2048,128]{2,1,0:T(8,128)(2,1)S(1)} %get-tuple-element.55.r_5_), channel_id=1, source_target_pairs={{16,0},{4,20},{24,8},{12,28},{17,1},{5,21},{25,9},{13,29},{18,2},{... | collective-permute-start | bytes 1572872 | tf_op jit(solution)/shard_map/ppermute | solution.py:316
  57.7 17.3 %collective-permute-start.12 = (bf16[1,2048,128]{2,1,0:T(8,128)(2,1)S(1)}, bf16[1,2048,128]{2,1,0:T(8,128)(2,1)S(1)}, u32[]{:S(2)}, u32[]{:S(2)}) collective-permute-start(bf16[1,2048,128]{2,1,0:T(8,128)(2,1)S(1)} %copy-done.7), channel_id=1, source_target_pairs={{28,12},{0,16},{24,8},{4,20},{29,13},{1,17},{25,9},{5,21},{30,14},... | collective-permute-start | bytes 1572872 | tf_op jit(solution)/shard_map/ppermute | solution.py:316
  76.5 24.0 %collective-permute-start.14 = (bf16[4,2048,128]{2,1,0:T(8,128)(2,1)S(1)}, bf16[4,2048,128]{2,1,0:T(8,128)(2,1)S(1)}, u32[]{:S(2)}, u32[]{:S(2)}) collective-permute-start(bf16[4,2048,128]{2,1,0:T(8,128)(2,1)S(1)} %pad_maximum_fusion.1), channel_id=1, source_target_pairs={{0,4},{4,0},{8,12},{12,8},{16,20},{20,16},{24,28},{28,24},{1,5},{5... | collective-permute-start | bytes 6291464 | tf_op jit(solution)/shard_map/ppermute | solution.py:316
  77.0 22.4 %collective-permute-start.15 = (bf16[3,2048,128]{2,1,0:T(8,128)(2,1)S(1)}, bf16[3,2048,128]{2,1,0:T(8,128)(2,1)S(1)}, u32[]{:S(2)}, u32[]{:S(2)}) collective-permute-start(bf16[3,2048,128]{2,1,0:T(8,128)(2,1)S(1)} %pad_maximum_fusion.3), channel_id=1, source_target_pairs={{0,4},{4,0},{8,12},{12,8},{16,20},{20,16},{24,28},{28,24},{1,5},{5... | collective-permute-start | bytes 4718600 | tf_op jit(solution)/shard_map/ppermute | solution.py:316
  77.9 14.7 %collective-permute-start.18 = (bf16[1,2048,128]{2,1,0:T(8,128)(2,1)S(1)}, bf16[1,2048,128]{2,1,0:T(8,128)(2,1)S(1)}, u32[]{:S(2)}, u32[]{:S(2)}) collective-permute-start(bf16[1,2048,128]{2,1,0:T(8,128)(2,1)S(1)} %select_select_fusion.r_6_), channel_id=1, source_target_pairs={{0,8},{4,12},{8,0},{12,4},{16,24},{20,28},{24,16},{28,20},{1,9},{5... | collective-permute-start | bytes 1572872 | tf_op jit(solution)/shard_map/ppermute | solution.py:316
  81.1 11.5 %collective-permute-start.16 = (bf16[1,2048,128]{2,1,0:T(8,128)(2,1)S(1)}, bf16[1,2048,128]{2,1,0:T(8,128)(2,1)S(1)}, u32[]{:S(2)}, u32[]{:S(2)}) collective-permute-start(bf16[1,2048,128]{2,1,0:T(8,128)(2,1)S(1)} %select_select_fusion.r_6_), channel_id=1, source_target_pairs={{16,0},{4,20},{24,8},{12,28},{17,1},{5,21},{25,9},{13,29},{18,2},{... | collective-permute-start | bytes 1572872 | tf_op jit(solution)/shard_map/ppermute | solution.py:316
  82.4 17.0 %collective-permute-start.17 = (bf16[1,2048,128]{2,1,0:T(8,128)(2,1)S(1)}, bf16[1,2048,128]{2,1,0:T(8,128)(2,1)S(1)}, u32[]{:S(2)}, u32[]{:S(2)}) collective-permute-start(bf16[1,2048,128]{2,1,0:T(8,128)(2,1)S(1)} %collective-permute-done.13.r_9_), channel_id=1, source_target_pairs={{28,12},{0,16},{24,8},{4,20},{29,13},{1,17},{25,9},{5,21},{30,14},... | collective-permute-start | bytes 1572872 | tf_op jit(solution)/shard_map/ppermute | solution.py:316
  103.5 4.9 %collective-permute-start.21 = (bf16[4,2048,128]{2,1,0:T(8,128)(2,1)}, bf16[4,2048,128]{2,1,0:T(8,128)(2,1)}, u32[]{:S(2)}, u32[]{:S(2)}) collective-permute-start(bf16[4,2048,128]{2,1,0:T(8,128)(2,1)} %pad_maximum_fusion.2), channel_id=1, source_target_pairs={{0,4},{4,0},{8,12},{12,8},{16,20},{20,16},{24,28},{28,24},{1,5},{5... | collective-permute-start | bytes 6291464 | tf_op jit(solution)/shard_map/ppermute | solution.py:316
  104.3 3.4 %collective-permute-start.19 = (bf16[1,2048,128]{2,1,0:T(8,128)(2,1)}, bf16[1,2048,128]{2,1,0:T(8,128)(2,1)}, u32[]{:S(2)}, u32[]{:S(2)}) collective-permute-start(bf16[1,2048,128]{2,1,0:T(8,128)(2,1)} %copy-done.15), channel_id=1, source_target_pairs={{28,12},{0,16},{29,13},{1,17},{30,14},{2,18},{31,15},{3,19}} | collective-permute-start | bytes 1572872 | tf_op jit(solution)/shard_map/ppermute | solution.py:316
  105.8 1.9 %collective-permute-start.20 = (bf16[1,2048,128]{2,1,0:T(8,128)(2,1)}, bf16[1,2048,128]{2,1,0:T(8,128)(2,1)}, u32[]{:S(2)}, u32[]{:S(2)}) collective-permute-start(bf16[1,2048,128]{2,1,0:T(8,128)(2,1)} %copy-done.17), channel_id=1, source_target_pairs={{0,8},{28,20},{1,9},{29,21},{2,10},{30,22},{3,11},{31,23}} | collective-permute-start | bytes 1572872 | tf_op jit(solution)/shard_map/ppermute | solution.py:316
  110.7 13.4 %collective-permute-start.22 = (bf16[2,2048,128]{2,1,0:T(8,128)(2,1)}, bf16[2,2048,128]{2,1,0:T(8,128)(2,1)}, u32[]{:S(2)}, u32[]{:S(2)}) collective-permute-start(bf16[2,2048,128]{2,1,0:T(8,128)(2,1)} %pad_maximum_fusion.4), channel_id=1, source_target_pairs={{0,4},{4,0},{8,12},{12,8},{16,20},{20,16},{24,28},{28,24},{1,5},{5... | collective-permute-start | bytes 3145736 | tf_op jit(solution)/shard_map/ppermute | solution.py:316
  (33 other events, 173.4 us)

commit v6 on v5

--- a/solution.py
+++ b/solution.py
@@ -130,8 +130,8 @@
 def left_kernel(z, *refs, per_step):
     slabs, (out_ref, choice, mask) = refs[:-3], refs[-3:]
     m, k = mask.shape
-    channels = slabs[0].shape[1]
-    group_rows = k // len(slabs)
+    channels = slabs[0].shape[-1]
+    group_rows = slabs[0].shape[0] // per_step
     half = group_rows // 2
     rows_out = m // (2 * GROUP)
 
@@ -163,17 +163,15 @@
 def make_left(slabs, z, rows_out, bins):
     slab_rows, channels = slabs[0].shape
     groups = bins // GROUP
-    m, k = rows_out * GROUP * 2, slab_rows // groups * len(slabs)
+    m, k = rows_out * GROUP * 2, slab_rows // groups * 4
     per_step = 4
+    step_rows = slab_rows // groups * per_step
     return pl.pallas_call(
         lambda *r: left_kernel(*r, per_step=per_step),
         grid_spec=pltpu.PrefetchScalarGridSpec(
             num_scalar_prefetch=1,
             grid=(groups // per_step,),
-            in_specs=[
-                pl.BlockSpec((slab_rows // groups * per_step, channels), lambda i, s: (i, 0))
-            ]
-            * len(slabs),
+            in_specs=[pl.BlockSpec((step_rows, channels), lambda i, s: (i, 0))] * len(slabs),
             out_specs=pl.BlockSpec((per_step, m, k), lambda i, s: (i, 0, 0)),
             scratch_shapes=[
                 pltpu.VMEM((m, 2 * channels), jnp.bfloat16),
@@ -186,39 +184,46 @@
     )(z.reshape(1), *slabs)
 
 
-CHUNKS = 2
-GROUP_UNROLL = 4
-ROW_UNROLL = 4
-
-
-def pairs_kernel(slots, left_ref, lag_ref, *refs, arrays, norm):
-    sources, refs = refs[: len(arrays)], refs[len(arrays) :]
-    out_ref, partner, gram, stage, in_sems, out_sems = refs
-    groups, m, k = left_ref.shape
-    slot_count, slabs, slab_rows, channels = partner.shape
+CHUNKS = 4
+GROUP_UNROLL = 8
+ROW_UNROLL = 8
+
+
+def pairs_kernel(slots, left_ref, lag_ref, *refs, arrays, norm, aliased):
+    sources, refs = refs[: len(arrays)], refs[len(arrays) + aliased :]
+    out_ref, partner, left, gram, stage, in_sems, left_sems, out_sems = refs
+    groups, m, k = left.shape
+    chosen, slabs, slab_rows, channels = partner.shape
     group_rows = k // slabs
     chunk_rows = slab_rows // CHUNKS
-    lanes = slot_count * channels
+    per_chunk = groups // CHUNKS
 
     def fetch(source, s, r, chunk):
         rows = pl.ds(chunk * chunk_rows, chunk_rows)
         return pltpu.make_async_copy(source.at[rows], partner.at[s, r, rows], in_sems.at[chunk, s, r])
 
-    for s in range(slot_count):
+    def fetch_left(chunk):
+        some = pl.ds(chunk * per_chunk, per_chunk)
+        return pltpu.make_async_copy(left_ref.at[some], left.at[some], left_sems.at[chunk])
+
+    fetch_left(0).start()
+    for s in range(chosen):
         for r in range(slabs):
-            slot = slots[s * slabs + r]
+            place = slots[s * (slabs + 1) + 1 + r]
             for source, (first, count, holds) in zip(sources, arrays):
                 if r in holds:
 
-                    @pl.when((slot >= first) & (slot < first + count))
+                    @pl.when((place >= first) & (place < first + count))
                     def _():
                         for chunk in range(CHUNKS):
-                            fetch(source.at[slot - first], s, r, chunk).start()
-
-    per_chunk = groups // CHUNKS
+                            fetch(source.at[place - first], s, r, chunk).start()
+
+    for chunk in range(1, CHUNKS):
+        fetch_left(chunk).start()
 
     for chunk in range(CHUNKS):
-        for s in range(slot_count):
+        fetch_left(chunk).wait()
+        for s in range(chosen):
             for r in range(slabs):
                 fetch(sources[0].at[0], s, r, chunk).wait()
 
@@ -228,20 +233,33 @@
                 g = chunk * per_chunk + i * GROUP_UNROLL + u
                 rows = pl.ds(pl.multiple_of(g * group_rows, group_rows), group_rows)
                 right = jnp.concatenate(
-                    [partner[s, :, rows, :].reshape(k, channels) for s in range(slot_count)], 1
+                    [partner[s, :, rows, :].reshape(k, channels) for s in range(chosen)], 1
                 )
-                product = jnp.dot(left_ref[g], right, preferred_element_type=jnp.float32)
+                product = jnp.dot(left[g], right, preferred_element_type=jnp.float32)
                 cols = pl.ds(pl.multiple_of(g * 2 * GROUP, 2 * GROUP), 2 * GROUP)
                 gram[:, cols, :] = product.astype(jnp.bfloat16).reshape(
-                    m // (2 * GROUP), 2 * GROUP, lanes
+                    m // (2 * GROUP), 2 * GROUP, chosen * channels
                 )
 
     steps = gram.shape[0] // ROW_UNROLL
 
-    def write(i, b):
-        return pltpu.make_async_copy(
-            stage.at[b], out_ref.at[pl.ds(i * ROW_UNROLL, ROW_UNROLL)], out_sems.at[b]
-        )
+    class Write:
+        def __init__(self, i, b):
+            rows = pl.ds(i * ROW_UNROLL, ROW_UNROLL)
+            self.copies = [
+                pltpu.make_async_copy(
+                    stage.at[b, s], out_ref.at[rows, slots[s * (slabs + 1)]], out_sems.at[b, s]
+                )
+                for s in range(chosen)
+            ]
+
+        def start(self):
+            for copy in self.copies:
+                copy.start()
+
+        def wait(self):
+            for copy in self.copies:
+                copy.wait()
 
     @pl.loop(0, steps)
     def _(i):
@@ -249,21 +267,21 @@
 
         @pl.when(i >= 2)
         def _():
-            write(i - 2, b).wait()
+            Write(i - 2, b).wait()
 
         for u in range(ROW_UNROLL):
             lagged = jnp.dot(
                 lag_ref[...], gram[i * ROW_UNROLL + u], preferred_element_type=jnp.float32
             )
-            for s in range(slot_count):
-                stage[b, u, s] = (lagged[:, s * channels : (s + 1) * channels] * norm).T
-        write(i, b).start()
+            for s in range(chosen):
+                stage[b, s, u] = (lagged[:, s * channels : (s + 1) * channels] * norm).T
+        Write(i, b).start()
 
     for i in range(steps - 2, steps):
-        write(i, i % 2).wait()
-
-
-def correlate(slots, left, lag_rows, held, slot_count, norm):
+        Write(i, i % 2).wait()
+
+
+def correlate(slots, left, lag_rows, held, slot_count, norm, earlier=None):
     groups, m, k = left.shape
     rows_out = m // (2 * GROUP)
     arrays, first = [], 0
@@ -271,26 +289,39 @@
         arrays.append((first, value.shape[0], holds))
         first += value.shape[0]
     slab_rows, channels = held[0][0].shape[1:]
-    slabs = slots.shape[0] // slot_count
+    chosen, slabs = slots.shape[0], slots.shape[1] - 1
     lag_count, entries = lag_rows.shape
     anywhere = pl.BlockSpec(memory_space=pl.ANY)
     in_vmem = pl.BlockSpec(memory_space=pltpu.VMEM)
+    operands = [slots.reshape(-1), left, lag_rows] + [value for value, _ in held]
+    aliases = {}
+    if earlier is not None:
+        aliases = {len(operands): 0}
+        operands.append(earlier)
+    flops = 2 * groups * m * k * chosen * channels + 2 * rows_out * lag_count * entries * chosen * channels
     return pl.pallas_call(
-        lambda *r: pairs_kernel(*r, arrays=arrays, norm=norm),
-        in_specs=[pl.BlockSpec(memory_space=pltpu.SMEM), in_vmem, in_vmem] + [anywhere] * len(held),
+        lambda *r: pairs_kernel(*r, arrays=arrays, norm=norm, aliased=len(aliases)),
+        in_specs=[pl.BlockSpec(memory_space=pltpu.SMEM), anywhere, in_vmem]
+        + [anywhere] * (len(operands) - 3),
         out_specs=anywhere,
         scratch_shapes=[
-            pltpu.VMEM((slot_count, slabs, slab_rows, channels), jnp.bfloat16),
-            pltpu.VMEM((rows_out, entries, slot_count * channels), jnp.bfloat16),
-            pltpu.VMEM((2, ROW_UNROLL, slot_count, channels, lag_count), jnp.float32),
-            pltpu.SemaphoreType.DMA((CHUNKS, slot_count, slabs)),
-            pltpu.SemaphoreType.DMA((2,)),
+            pltpu.VMEM((chosen, slabs, slab_rows, channels), jnp.bfloat16),
+            pltpu.VMEM((groups, m, k), jnp.bfloat16),
+            pltpu.VMEM((rows_out, entries, chosen * channels), jnp.bfloat16),
+            pltpu.VMEM((2, chosen, ROW_UNROLL, channels, lag_count), jnp.float32),
+            pltpu.SemaphoreType.DMA((CHUNKS, chosen, slabs)),
+            pltpu.SemaphoreType.DMA((CHUNKS,)),
+            pltpu.SemaphoreType.DMA((2, chosen)),
         ],
         out_shape=jax.ShapeDtypeStruct((rows_out, slot_count, channels, lag_count), jnp.float32),
-        compiler_params=pltpu.CompilerParams(vmem_limit_bytes=25 << 20),
+        input_output_aliases=aliases,
+        cost_estimate=pl.CostEstimate(flops=flops, bytes_accessed=12 << 20, transcendentals=0),
+        compiler_params=pltpu.CompilerParams(vmem_limit_bytes=PAIRS_VMEM),
         name="pairs",
-    )(slots, left, lag_rows, *[value for value, _ in held])
-
+    )(*operands)
+
+
+PAIRS_VMEM = 58 << 20
 
 X_PAIRS = [(i, i ^ 2) for i in range(8)]
 Y_PAIRS = [(4, 0), (1, 5), (6, 2), (3, 7)]
@@ -348,7 +379,7 @@
         return lax.ppermute(value, "freq", pairs)
 
     def slab_of(value, r):
-        return Held(value, [[(i, r) for i in range(8)]])
+        return Held(lax.optimization_barrier(value), [[(i, r) for i in range(8)]])
 
     s0 = make_slab(traces, band_bins)[None]
     q0 = slab_of(s0, 0)
@@ -358,34 +389,37 @@
     y0, down1, up1, x0, lag_rows = together(y0, down1, up1, x0, lag_rows)
 
     q1 = slab_of(lax.select_n(z, down1, up1, down1, up1), 1)
+    c0 = x0.hop(Y_ON_ALL)
+    y1 = q1.hop(Y_PAIRS)
+    x1 = q1.hop(X_PAIRS)
     up2, down2 = along_z(up1, [(1, 2), (2, 3)]), along_z(down1, [(2, 1), (1, 0)])
-    x1 = q1.hop(X_PAIRS)
-    y1 = q1.hop(Y_PAIRS)
-    c0 = x0.hop(Y_ON_ALL)
-    up2, down2, y1, c0, x1 = together(up2, down2, y1, c0, x1)
+    first = join(q0, x0, y0, q1)
+    up2, down2, x1, y1, first = together(up2, down2, x1, y1, first)
 
     q2 = slab_of(lax.select_n(z, down2, down1, up1, up2), 2)
+    c1 = x1.hop(Y_ON_ALL)
+    y2 = q2.hop(Y_PAIRS)
+    x2 = q2.hop(X_PAIRS)
     last = along_z(jnp.where(z == 2, up2, down2), [(2, 3), (1, 0)])
-    a0 = join(q0, x0, y0, c0).hop(CORE_PAIRS)
-    x2 = q2.hop(X_PAIRS)
-    y2 = q2.hop(Y_PAIRS)
-    c1 = x1.hop(Y_ON_ALL)
-    last, a0, y2, c1, x2 = together(last, a0, y2, c1, x2)
+    second = join(x1, y1, q2)
+    last, c0, up2, down2, second = together(last, c0, up2, down2, second)
 
     q3 = slab_of(lax.select_n(z, last, down2, up2, last), 3)
-    a1 = join(q1, x1, y1, c1).hop(CORE_PAIRS)
-    a2 = join(q2, x2, y2).hop(CORE_PAIRS)
+    b = [first.hop(CORE_PAIRS), second.hop(CORE_PAIRS)]
+    y3 = q3.hop(Y_PAIRS)
     x3 = q3.hop(X_PAIRS)
-    y3 = q3.hop(Y_PAIRS)
-    c2 = x2.hop(Y_ON_ALL)
     left = make_left([q.value[0] for q in (q0, q1, q2, q3)], z, channels // 4, bins)
-    a1, a2, y3, c2, x3, left = together(a1, a2, y3, c2, x3, left)
-
-    a3 = join(c2, q3, x3, y3).hop(CORE_PAIRS)
-    c3, d3 = x3.hop(Y_ON), y3.hop(X_ON)
-
-    held = [q0, q1, q2, q3, x0, x1, x2, x3, y0, y1, y2, y3, c0, c1, c2, c3, d3, a0, a1, a2, a3]
-    whats = [h.what for h in held] + [moved(c3.what + d3.what, CORE_PAIRS)]
+    x2, y2, left = together(x2, y2, left)
+
+    c2, d2 = x2.hop(Y_ON), y2.hop(X_ON)
+    b += [c0.hop(CORE_PAIRS), q3.hop(CORE_PAIRS)]
+    ids = np.arange(8, dtype=np.int32)
+    third = [x2.what, y2.what, x3.what, y3.what]
+    held = [q0, q1, q2, q3, x0, x1, x2, x3, y0, y1, y2, y3, c0, c1] + b
+    whats = [h.what for h in held] + [moved(what, CORE_PAIRS) for what in third]
+    c3, d3 = moved(x3.what, Y_ON), moved(y3.what, X_ON)
+    whats += [c2.what, d2.what, c3, d3]
+    whats += [moved(what, CORE_PAIRS) for what in (c1.what, c2.what, d2.what, c3, d3)]
     table = np.zeros((8, 8, 4), np.int32)
     all_holds = [set() for _ in whats]
     index = sum(len(what) for what in whats)
@@ -396,18 +430,27 @@
                 if block_slab is not None:
                     table[device, block_slab[0], block_slab[1]] = index
                     holds.add(block_slab[1])
-    ids = np.arange(8, dtype=np.int32)
     wanted = (ids[None, None, :, None] == pair_blocks[0][:, None, None, None]) & (
         ids[None, :, None, None] == me
     )
-    slots = jnp.sum(jnp.where(wanted, table[None], 0), axis=(1, 2)).reshape(-1)
-
-    c3, d3, a3, slots = together(c3, d3, a3, slots)
-    a4 = join(c3, d3).hop(CORE_PAIRS)
-    held = [q0, q1, q2, q3, x0, x1, x2, x3, y0, y1, y2, y3, c0, c1, c2, c3, d3, a0, a1, a2, a3, a4]
+    slots = jnp.sum(jnp.where(wanted, table[None], 0), axis=(1, 2))
+    slots = jnp.concatenate([jnp.arange(slot_count, dtype=jnp.int32)[:, None], slots], 1)
+    swapped = slots[jnp.asarray([1, 0, 2])]
+    slots = jnp.where(me == 5, swapped, slots)
+
+    x3, y3, c1, slots = together(x3, y3, c1, slots)
+
+    c3, d3 = x3.hop(Y_ON), y3.hop(X_ON)
+    b += [h.hop(CORE_PAIRS) for h in (x2, y2, x3, y3)]
+    norm = 1.0 / math.sqrt(4 * windows * bins)
+    held = [q0, q1, q2, q3, x0, x1, x2, x3, y0, y1, y2, y3, c0, c1] + b
     places = [(h.value, holds) for h, holds in zip(held, all_holds)]
-    norm = 1.0 / math.sqrt(4 * windows * bins)
-    return correlate(slots, left, lag_rows, places, slot_count, norm)[None]
+    result = correlate(slots[:1], left, lag_rows, places, slot_count, norm)
+    c3, d3, c2, d2, result = together(c3, d3, c2, d2, result)
+    late = [h.hop(CORE_PAIRS) for h in (c1, c2, d2, c3, d3)]
+    held += [c2, d2, c3, d3] + late
+    places = [(h.value, holds) for h, holds in zip(held, all_holds)]
+    return correlate(slots[1:], left, lag_rows, places, slot_count, norm, result)[None]
 
 
 def solution(mesh):

time: 157 us -> 127 us (0.81)
  the two profiles are of different devices: /device:TPU:17 before, /device:TPU:0 now
where the time goes in v6:
time: 127 us
  starting transfers between devices  44.4 us (35%)
  waiting for transfers between devices  35.5 us (28%)
  Pallas kernels  26.3 us (21%)
  local copies, waits for them, and re-layouts  10.6 us (8%)
  other arithmetic  9.43 us (7%)
    ppermute x27, starting transfers between devices, hop(): lax.ppermute(self.value, 'chan', pairs)  35.6 us
    pallas_call x2, Pallas kernels, correlate(): pl.pallas_call(lambda *r: pairs_kernel(*r, arrays=arrays, norm=norm, alia...  20.2 us
    ppermute x5, waiting for transfers between devices, along_z(): return lax.ppermute(value, 'freq', pairs)  19.6 us
    ppermute x27, waiting for transfers between devices, hop(): lax.ppermute(self.value, 'chan', pairs)  15.8 us
    ppermute x5, starting transfers between devices, along_z(): return lax.ppermute(value, 'freq', pairs)  8.81 us
    unnamed x58, local copies, waits for them, and re-layouts  5.15 us
    pallas_call x1, Pallas kernels, make_left(): pl.pallas_call(lambda *r: left_kernel(*r, per_step=per_step), grid_spec=p...  4.04 us
    concatenate x2, other arithmetic, join(): jnp.concatenate([p.value for p in parts], 0)  2.91 us
  transfers between devices with their start and end apart: 32, of which 14 were waited for; matrix products, arithmetic and copies ran while one was open for 8% of the time, Pallas kernels for 11%

profile of v6, /device:TPU:0, one launch (start us, length us, event | category | flops | bytes accessed | tf_op | source)
XLA Modules:
  0.0 126.8 jit_solution(15014261432207292330)
XLA Ops:
  0.0 1.8 %fusion.6 = (f32[256,144]{1,0:T(8,128)S(1)}, f32[256,144]{1,0:T(8,128)S(1)}) fusion(s32[144]{0:T(256)S(1)} %pad_add_fusion.1, s32[256]{0:T(256)} %param.8), kind=kLoop, calls=%fused_computation.26 | loop fusion | flops 516096 | bytes 296512 | tf_op jit(solution)/shard_map/sin | solution.py:117
  1.9 2.7 %copy.16 = bf16[4,128,2048]{2,1,0:T(8,128)(2,1)S(1)} copy(bf16[4,128,2048]{2,0,1:T(4,128)(2,1)} %bitcast.26) | data formatting | bytes 4194304 | tf_op jit(solution)/shard_map/transpose | solution.py:113
  4.6 2.0 %spectra.1 = bf16[2048,128]{1,0:T(8,128)(2,1)S(1)} custom-call(bf16[512,2048]{1,0:T(8,128)(2,1)S(1)} %bitcast.25, f32[256,128]{1,0:T(8,128)S(1)} %slice.26.fine_cos, f32[256,128]{1,0:T(8,128)S(1)} %slice.27.fine_sin, f32[256,16]{1,0:T(8,128)S(1)} %slice.28.step_cos, f32[256,16]{1,0:T(8,128)S(1)} %slice.29.step_sin), custom_call_target="tpu_custom_call" | custom-call | tf_op jit(solution)/shard_map/spectra/pallas_call | solution.py:118
  6.6 3.0 %collective-permute-start.3 = (bf16[1,2048,128]{2,1,0:T(8,128)(2,1)S(1)}, bf16[1,2048,128]{2,1,0:T(8,128)(2,1)S(1)}, u32[]{:S(2)}, u32[]{:S(2)}) collective-permute-start(bf16[1,2048,128]{2,1,0:T(8,128)(2,1)S(1)} %bitcast.17), channel_id=1, source_target_pairs={{0,8},{4,12},{8,0},{12,4},{16,24},{20,28},{24,16},{28,20},{1,9},{5... | collective-permute-start | bytes 1572872 | tf_op jit(solution)/shard_map/ppermute | solution.py:347
  10.9 3.5 %collective-permute-start.2 = (bf16[1,2048,128]{2,1,0:T(8,128)(2,1)S(1)}, bf16[1,2048,128]{2,1,0:T(8,128)(2,1)S(1)}, u32[]{:S(2)}, u32[]{:S(2)}) collective-permute-start(bf16[1,2048,128]{2,1,0:T(8,128)(2,1)S(1)} %bitcast.19), channel_id=1, source_target_pairs={{0,1},{1,2},{2,3},{4,5},{5,6},{6,7},{8,9},{9,10},{10,11},{12,13},{... | collective-permute-start | bytes 1572872 | tf_op jit(solution)/shard_map/ppermute | solution.py:379
  16.5 5.0 %collective-permute-done.3.r_7_ = bf16[1,2048,128]{2,1,0:T(8,128)(2,1)S(1)} collective-permute-done((bf16[1,2048,128]{2,1,0:T(8,128)(2,1)S(1)}, bf16[1,2048,128]{2,1,0:T(8,128)(2,1)S(1)}, u32[]{:S(2)}, u32[]{:S(2)}) %collective-permute-start.3) | collective-permute-done | bytes 524320 | tf_op jit(solution)/shard_map/ppermute | solution.py:347
  21.6 4.8 %collective-permute-done.2 = bf16[1,2048,128]{2,1,0:T(8,128)(2,1)S(1)} collective-permute-done((bf16[1,2048,128]{2,1,0:T(8,128)(2,1)S(1)}, bf16[1,2048,128]{2,1,0:T(8,128)(2,1)S(1)}, u32[]{:S(2)}, u32[]{:S(2)}) %collective-permute-start.2) | collective-permute-done | bytes 524320 | tf_op jit(solution)/shard_map/ppermute | solution.py:379
  26.3 4.6 %collective-permute-done.1 = bf16[1,2048,128]{2,1,0:T(8,128)(2,1)S(1)} collective-permute-done((bf16[1,2048,128]{2,1,0:T(8,128)(2,1)S(1)}, bf16[1,2048,128]{2,1,0:T(8,128)(2,1)S(1)}, u32[]{:S(2)}, u32[]{:S(2)}) %collective-permute-start.1) | collective-permute-done | bytes 524320 | tf_op jit(solution)/shard_map/ppermute | solution.py:379
  36.5 5.5 %collective-permute-start.9 = (bf16[1,2048,128]{2,1,0:T(8,128)(2,1)S(1)}, bf16[1,2048,128]{2,1,0:T(8,128)(2,1)}, u32[]{:S(2)}, u32[]{:S(2)}) collective-permute-start(bf16[1,2048,128]{2,1,0:T(8,128)(2,1)S(1)} %collective-permute-done.3.r_7_), channel_id=1, source_target_pairs={{28,12},{0,16},{24,8},{4,20},{29,13},{1,17},{25,9},{5,21},{30,14},... | collective-permute-start | bytes 1572872 | tf_op jit(solution)/shard_map/ppermute | solution.py:347
  42.1 1.6 %pad_maximum_fusion = bf16[4,2048,128]{2,1,0:T(8,128)(2,1)} fusion(bf16[1,2048,128]{2,1,0:T(8,128)(2,1)S(1)} %select_select_fusion.2.r_4_, bf16[1,2048,128]{2,1,0:T(8,128)(2,1)S(1)} %collective-permute-done.r_11_, bf16[1,2048,128]{2,1,0:T(8,128)(2,1)S(1)} %collective-permute-done.3.r_7_, bf16[1,2048,128]{2,1,0:T(8,128)(2,1)S(1)} %bitcast.21), kind=kLoop, calls=%fused_computation.1 | loop fusion | flops 3145728 | bytes 4194304 | tf_op jit(solution)/shard_map/concatenate | solution.py:351
  43.7 3.5 %collective-permute-done.6.r_8_ = bf16[1,2048,128]{2,1,0:T(8,128)(2,1)S(1)} collective-permute-done((bf16[1,2048,128]{2,1,0:T(8,128)(2,1)S(1)}, bf16[1,2048,128]{2,1,0:T(8,128)(2,1)S(1)}, u32[]{:S(2)}, u32[]{:S(2)}) %collective-permute-start.6) | collective-permute-done | bytes 524320 | tf_op jit(solution)/shard_map/ppermute | solution.py:347
  47.2 6.2 %collective-permute-done.5 = bf16[1,2048,128]{2,1,0:T(8,128)(2,1)} collective-permute-done((bf16[1,2048,128]{2,1,0:T(8,128)(2,1)}, bf16[1,2048,128]{2,1,0:T(8,128)(2,1)}, u32[]{:S(2)}, u32[]{:S(2)}) %collective-permute-start.5) | collective-permute-done | bytes 524320 | tf_op jit(solution)/shard_map/ppermute | solution.py:379
  53.5 2.2 %select_select_fusion.1 = (bf16[1,2048,128]{2,1,0:T(8,128)(2,1)S(1)}, bf16[1,2048,128]{2,1,0:T(8,128)(2,1)}) fusion(bf16[1,2048,128]{2,1,0:T(8,128)(2,1)S(1)} %copy-done.17, bf16[1,2048,128]{2,1,0:T(8,128)(2,1)} %collective-permute-done.4, bf16[1,2048,128]{2,1,0:T(8,128)(2,1)} %collective-permute-done.5, bf16[1,2048,128]{2,1,0:T(8,128)(2,1)S(1)} %copy-done.19, ...), kind=kLoop, calls=%fused_computation.4 | loop fusion | flops 1048576 | bytes 3145732 | tf_op jit(solution)/shard_map/select_n | solution.py:399
  59.8 5.4 %collective-permute-start.12 = (bf16[1,2048,128]{2,1,0:T(8,128)(2,1)S(1)}, bf16[1,2048,128]{2,1,0:T(8,128)(2,1)}, u32[]{:S(2)}, u32[]{:S(2)}) collective-permute-start(bf16[1,2048,128]{2,1,0:T(8,128)(2,1)S(1)} %collective-permute-done.6.r_8_), channel_id=1, source_target_pairs={{28,12},{0,16},{24,8},{4,20},{29,13},{1,17},{25,9},{5,21},{30,14},... | collective-permute-start | bytes 1572872 | tf_op jit(solution)/shard_map/ppermute | solution.py:347
  66.6 4.0 %collective-permute-done.8 = bf16[1,2048,128]{2,1,0:T(8,128)(2,1)} collective-permute-done((bf16[1,2048,128]{2,1,0:T(8,128)(2,1)}, bf16[1,2048,128]{2,1,0:T(8,128)(2,1)}, u32[]{:S(2)}, u32[]{:S(2)}) %collective-permute-start.8) | collective-permute-done | bytes 524320 | tf_op jit(solution)/shard_map/ppermute | solution.py:379
  75.1 4.0 %left.1.r_1_ = bf16[32,512,256]{2,1,0:T(8,128)(2,1)S(1)} custom-call(s32[1]{0:T(128)} %bitcast.6.r_0_, bf16[2048,128]{1,0:T(8,128)(2,1)S(1)} %spectra.1, bf16[2048,128]{1,0:T(8,128)(2,1)S(1)} %bitcast.15, bf16[2048,128]{1,0:T(8,128)(2,1)S(1)} %bitcast.16, bf16[2048,128]{1,0:T(8,128)(2,1)S(1)} %bitcast.24), custom_call_target="tpu_custom_call" | custom-call | tf_op jit(solution)/shard_map/left/pallas_call | solution.py:169
  79.1 3.3 %copy-done = bf16[32,512,256]{2,1,0:T(8,128)(2,1)} copy-done((bf16[32,512,256]{2,1,0:T(8,128)(2,1)}, bf16[32,512,256]{2,1,0:T(8,128)(2,1)S(1)}, u32[]{:S(2)}) %copy-start) | copy-done | bytes 8388632
  83.1 2.9 %collective-permute-done.10.r_10_ = bf16[1,2048,128]{2,1,0:T(8,128)(2,1)} collective-permute-done((bf16[1,2048,128]{2,1,0:T(8,128)(2,1)S(1)}, bf16[1,2048,128]{2,1,0:T(8,128)(2,1)}, u32[]{:S(2)}, u32[]{:S(2)}) %collective-permute-start.10) | collective-permute-done | bytes 524320 | tf_op jit(solution)/shard_map/ppermute | solution.py:347
  89.2 3.6 %collective-permute-start.25 = (bf16[1,2048,128]{2,1,0:T(8,128)(2,1)}, bf16[1,2048,128]{2,1,0:T(8,128)(2,1)}, u32[]{:S(2)}, u32[]{:S(2)}) collective-permute-start(bf16[1,2048,128]{2,1,0:T(8,128)(2,1)} %collective-permute-done.13.r_9_), channel_id=1, source_target_pairs={{28,12},{0,16},{29,13},{1,17},{30,14},{2,18},{31,15},{3,19}} | collective-permute-start | bytes 1572872 | tf_op jit(solution)/shard_map/ppermute | solution.py:347
  92.8 2.4 %collective-permute-start.26 = (bf16[1,2048,128]{2,1,0:T(8,128)(2,1)S(1)}, bf16[1,2048,128]{2,1,0:T(8,128)(2,1)}, u32[]{:S(2)}, u32[]{:S(2)}) collective-permute-start(bf16[1,2048,128]{2,1,0:T(8,128)(2,1)S(1)} %copy-done.10), channel_id=1, source_target_pairs={{0,8},{28,20},{1,9},{29,21},{2,10},{30,22},{3,11},{31,23}} | collective-permute-start | bytes 1572872 | tf_op jit(solution)/shard_map/ppermute | solution.py:347
  95.2 2.1 %collective-permute-start.23 = (bf16[1,2048,128]{2,1,0:T(8,128)(2,1)}, bf16[1,2048,128]{2,1,0:T(8,128)(2,1)}, u32[]{:S(2)}, u32[]{:S(2)}) collective-permute-start(bf16[1,2048,128]{2,1,0:T(8,128)(2,1)} %collective-permute-done.10.r_10_), channel_id=1, source_target_pairs={{28,12},{0,16},{29,13},{1,17},{30,14},{2,18},{31,15},{3,19}} | collective-permute-start | bytes 1572872 | tf_op jit(solution)/shard_map/ppermute | solution.py:347
  97.3 2.1 %collective-permute-start.24 = (bf16[1,2048,128]{2,1,0:T(8,128)(2,1)}, bf16[1,2048,128]{2,1,0:T(8,128)(2,1)}, u32[]{:S(2)}, u32[]{:S(2)}) collective-permute-start(bf16[1,2048,128]{2,1,0:T(8,128)(2,1)} %collective-permute-done.11.r_14_), channel_id=1, source_target_pairs={{0,8},{28,20},{1,9},{29,21},{2,10},{30,22},{3,11},{31,23}} | collective-permute-start | bytes 1572872 | tf_op jit(solution)/shard_map/ppermute | solution.py:347
  100.8 9.4 %pairs.2.r_34_ = f32[32,3,128,128]{3,2,1,0:T(8,128)} custom-call(s32[5]{0:T(128)} %slice_bitcast_fusion.r_0_, bf16[32,512,256]{2,1,0:T(8,128)(2,1)} %copy-done, bf16[128,512]{1,0:T(8,128)(2,1)} %copy.19.r_2_, bf16[1,2048,128]{2,1,0:T(8,128)(2,1)} %bitcast.22, bf16[1,2048,128]{2,1,0:T(8,128)(2,1)} %copy-done.1, bf16[1,2048,128]{2,1,0:T(8,128)(2,1)} %copy-done.2, ...), custom_call_target="tpu_custom_call" | custom-call | flops 1610612736 | bytes 12582912 | tf_op jit(solution)/shard_map/pairs/pallas_call | solution.py:302
  115.8 10.8 %pairs.3 = f32[32,3,128,128]{3,2,1,0:T(8,128)} custom-call(s32[10]{0:T(128)} %reshape.190.r_0_, bf16[32,512,256]{2,1,0:T(8,128)(2,1)} %copy-done, bf16[128,512]{1,0:T(8,128)(2,1)} %copy.19.r_2_, bf16[1,2048,128]{2,1,0:T(8,128)(2,1)} %bitcast.23, bf16[1,2048,128]{2,1,0:T(8,128)(2,1)} %copy-done.1, ...), custom_call_target="tpu_custom_call", output_to_operand_aliasing={{}: (34, {})} | custom-call | flops 3221225472 | bytes 12582912 | tf_op jit(solution)/shard_map/pairs/pallas_call | solution.py:302
  (133 shorter events, 29.5 us)
Async XLA Ops:
  6.6 14.9 %collective-permute-start.3 = (bf16[1,2048,128]{2,1,0:T(8,128)(2,1)S(1)}, bf16[1,2048,128]{2,1,0:T(8,128)(2,1)S(1)}, u32[]{:S(2)}, u32[]{:S(2)}) collective-permute-start(bf16[1,2048,128]{2,1,0:T(8,128)(2,1)S(1)} %bitcast.17), channel_id=1, source_target_pairs={{0,8},{4,12},{8,0},{12,4},{16,24},{20,28},{24,16},{28,20},{1,9},{5... | collective-permute-start | bytes 1572872 | tf_op jit(solution)/shard_map/ppermute | solution.py:347
  9.6 11.9 %collective-permute-start = (bf16[1,2048,128]{2,1,0:T(8,128)(2,1)S(1)}, bf16[1,2048,128]{2,1,0:T(8,128)(2,1)S(1)}, u32[]{:S(2)}, u32[]{:S(2)}) collective-permute-start(bf16[1,2048,128]{2,1,0:T(8,128)(2,1)S(1)} %bitcast.18), channel_id=1, source_target_pairs={{16,0},{4,20},{24,8},{12,28},{17,1},{5,21},{25,9},{13,29},{18,2},{... | collective-permute-start | bytes 1572872 | tf_op jit(solution)/shard_map/ppermute | solution.py:347
  10.9 15.4 %collective-permute-start.2 = (bf16[1,2048,128]{2,1,0:T(8,128)(2,1)S(1)}, bf16[1,2048,128]{2,1,0:T(8,128)(2,1)S(1)}, u32[]{:S(2)}, u32[]{:S(2)}) collective-permute-start(bf16[1,2048,128]{2,1,0:T(8,128)(2,1)S(1)} %bitcast.19), channel_id=1, source_target_pairs={{0,1},{1,2},{2,3},{4,5},{5,6},{6,7},{8,9},{9,10},{10,11},{12,13},{... | collective-permute-start | bytes 1572872 | tf_op jit(solution)/shard_map/ppermute | solution.py:379
  14.4 16.5 %collective-permute-start.1 = (bf16[1,2048,128]{2,1,0:T(8,128)(2,1)S(1)}, bf16[1,2048,128]{2,1,0:T(8,128)(2,1)S(1)}, u32[]{:S(2)}, u32[]{:S(2)}) collective-permute-start(bf16[1,2048,128]{2,1,0:T(8,128)(2,1)S(1)} %bitcast.20), channel_id=1, source_target_pairs={{3,2},{2,1},{1,0},{7,6},{6,5},{5,4},{11,10},{10,9},{9,8},{15,14},{... | collective-permute-start | bytes 1572872 | tf_op jit(solution)/shard_map/ppermute | solution.py:379
  31.9 11.8 %collective-permute-start.7 = (bf16[1,2048,128]{2,1,0:T(8,128)(2,1)S(1)}, bf16[1,2048,128]{2,1,0:T(8,128)(2,1)S(1)}, u32[]{:S(2)}, u32[]{:S(2)}) collective-permute-start(bf16[1,2048,128]{2,1,0:T(8,128)(2,1)S(1)} %select_select_fusion.2.r_4_), channel_id=1, source_target_pairs={{16,0},{4,20},{24,8},{12,28},{17,1},{5,21},{25,9},{13,29},{18,2},{... | collective-permute-start | bytes 1572872 | tf_op jit(solution)/shard_map/ppermute | solution.py:347
  33.2 14.0 %collective-permute-start.6 = (bf16[1,2048,128]{2,1,0:T(8,128)(2,1)S(1)}, bf16[1,2048,128]{2,1,0:T(8,128)(2,1)S(1)}, u32[]{:S(2)}, u32[]{:S(2)}) collective-permute-start(bf16[1,2048,128]{2,1,0:T(8,128)(2,1)S(1)} %select_select_fusion.2.r_4_), channel_id=1, source_target_pairs={{0,8},{4,12},{8,0},{12,4},{16,24},{20,28},{24,16},{28,20},{1,9},{5... | collective-permute-start | bytes 1572872 | tf_op jit(solution)/shard_map/ppermute | solution.py:347
  33.8 13.4 %collective-permute-start.4 = (bf16[1,2048,128]{2,1,0:T(8,128)(2,1)}, bf16[1,2048,128]{2,1,0:T(8,128)(2,1)}, u32[]{:S(2)}, u32[]{:S(2)}) collective-permute-start(bf16[1,2048,128]{2,1,0:T(8,128)(2,1)} %copy-done.16), channel_id=1, source_target_pairs={{1,2},{2,3},{5,6},{6,7},{9,10},{10,11},{13,14},{14,15},{17,18},{18... | collective-permute-start | bytes 1572872 | tf_op jit(solution)/shard_map/ppermute | solution.py:379
  35.2 18.2 %collective-permute-start.5 = (bf16[1,2048,128]{2,1,0:T(8,128)(2,1)}, bf16[1,2048,128]{2,1,0:T(8,128)(2,1)}, u32[]{:S(2)}, u32[]{:S(2)}) collective-permute-start(bf16[1,2048,128]{2,1,0:T(8,128)(2,1)} %copy-done.18), channel_id=1, source_target_pairs={{2,1},{1,0},{6,5},{5,4},{10,9},{9,8},{14,13},{13,12},{18,17},{17,1... | collective-permute-start | bytes 1572872 | tf_op jit(solution)/shard_map/ppermute | solution.py:379
  36.5 30.0 %collective-permute-start.9 = (bf16[1,2048,128]{2,1,0:T(8,128)(2,1)S(1)}, bf16[1,2048,128]{2,1,0:T(8,128)(2,1)}, u32[]{:S(2)}, u32[]{:S(2)}) collective-permute-start(bf16[1,2048,128]{2,1,0:T(8,128)(2,1)S(1)} %collective-permute-done.3.r_7_), channel_id=1, source_target_pairs={{28,12},{0,16},{24,8},{4,20},{29,13},{1,17},{25,9},{5,21},{30,14},... | collective-permute-start | bytes 1572872 | tf_op jit(solution)/shard_map/ppermute | solution.py:347
  55.6 15.0 %collective-permute-start.8 = (bf16[1,2048,128]{2,1,0:T(8,128)(2,1)}, bf16[1,2048,128]{2,1,0:T(8,128)(2,1)}, u32[]{:S(2)}, u32[]{:S(2)}) collective-permute-start(bf16[1,2048,128]{2,1,0:T(8,128)(2,1)} %get-tuple-element.60), channel_id=1, source_target_pairs={{2,3},{1,0},{6,7},{5,4},{10,11},{9,8},{14,15},{13,12},{18,19},{17,... | collective-permute-start | bytes 1572872 | tf_op jit(solution)/shard_map/ppermute | solution.py:379
  56.9 16.3 %collective-permute-start.14 = (bf16[1,2048,128]{2,1,0:T(8,128)(2,1)S(1)}, bf16[1,2048,128]{2,1,0:T(8,128)(2,1)S(1)}, u32[]{:S(2)}, u32[]{:S(2)}) collective-permute-start(bf16[1,2048,128]{2,1,0:T(8,128)(2,1)S(1)} %get-tuple-element.59.r_5_), channel_id=1, source_target_pairs={{16,0},{4,20},{24,8},{12,28},{17,1},{5,21},{25,9},{13,29},{18,2},{... | collective-permute-start | bytes 1572872 | tf_op jit(solution)/shard_map/ppermute | solution.py:347
  58.2 16.6 %collective-permute-start.13 = (bf16[1,2048,128]{2,1,0:T(8,128)(2,1)S(1)}, bf16[1,2048,128]{2,1,0:T(8,128)(2,1)}, u32[]{:S(2)}, u32[]{:S(2)}) collective-permute-start(bf16[1,2048,128]{2,1,0:T(8,128)(2,1)S(1)} %get-tuple-element.59.r_5_), channel_id=1, source_target_pairs={{0,8},{4,12},{8,0},{12,4},{16,24},{20,28},{24,16},{28,20},{1,9},{5... | collective-permute-start | bytes 1572872 | tf_op jit(solution)/shard_map/ppermute | solution.py:347
  59.8 22.6 %collective-permute-start.12 = (bf16[1,2048,128]{2,1,0:T(8,128)(2,1)S(1)}, bf16[1,2048,128]{2,1,0:T(8,128)(2,1)}, u32[]{:S(2)}, u32[]{:S(2)}) collective-permute-start(bf16[1,2048,128]{2,1,0:T(8,128)(2,1)S(1)} %collective-permute-done.6.r_8_), channel_id=1, source_target_pairs={{28,12},{0,16},{24,8},{4,20},{29,13},{1,17},{25,9},{5,21},{30,14},... | collective-permute-start | bytes 1572872 | tf_op jit(solution)/shard_map/ppermute | solution.py:347
  66.5 34.2 %collective-permute-start.15 = (bf16[4,2048,128]{2,1,0:T(8,128)(2,1)}, bf16[4,2048,128]{2,1,0:T(8,128)(2,1)}, u32[]{:S(2)}, u32[]{:S(2)}) collective-permute-start(bf16[4,2048,128]{2,1,0:T(8,128)(2,1)} %pad_maximum_fusion), channel_id=1, source_target_pairs={{0,4},{4,0},{8,12},{12,8},{16,20},{20,16},{24,28},{28,24},{1,5},{5... | collective-permute-start | bytes 6291464 | tf_op jit(solution)/shard_map/ppermute | solution.py:347
  71.9 11.2 %collective-permute-start.11 = (bf16[1,2048,128]{2,1,0:T(8,128)(2,1)S(1)}, bf16[1,2048,128]{2,1,0:T(8,128)(2,1)}, u32[]{:S(2)}, u32[]{:S(2)}) collective-permute-start(bf16[1,2048,128]{2,1,0:T(8,128)(2,1)S(1)} %select_select_fusion.r_6_), channel_id=1, source_target_pairs={{16,0},{4,20},{24,8},{12,28},{17,1},{5,21},{25,9},{13,29},{18,2},{... | collective-permute-start | bytes 1572872 | tf_op jit(solution)/shard_map/ppermute | solution.py:347
  73.3 12.8 %collective-permute-start.10 = (bf16[1,2048,128]{2,1,0:T(8,128)(2,1)S(1)}, bf16[1,2048,128]{2,1,0:T(8,128)(2,1)}, u32[]{:S(2)}, u32[]{:S(2)}) collective-permute-start(bf16[1,2048,128]{2,1,0:T(8,128)(2,1)S(1)} %select_select_fusion.r_6_), channel_id=1, source_target_pairs={{0,8},{4,12},{8,0},{12,4},{16,24},{20,28},{24,16},{28,20},{1,9},{5... | collective-permute-start | bytes 1572872 | tf_op jit(solution)/shard_map/ppermute | solution.py:347
  74.8 22.5 %collective-permute-start.16 = (bf16[3,2048,128]{2,1,0:T(8,128)(2,1)}, bf16[3,2048,128]{2,1,0:T(8,128)(2,1)}, u32[]{:S(2)}, u32[]{:S(2)}) collective-permute-start(bf16[3,2048,128]{2,1,0:T(8,128)(2,1)} %pad_maximum_fusion.1), channel_id=1, source_target_pairs={{0,4},{4,0},{8,12},{12,8},{16,20},{20,16},{24,28},{28,24},{1,5},{5... | collective-permute-start | bytes 4718600 | tf_op jit(solution)/shard_map/ppermute | solution.py:347
  87.7 5.1 %collective-permute-start.21 = (bf16[1,2048,128]{2,1,0:T(8,128)(2,1)}, bf16[1,2048,128]{2,1,0:T(8,128)(2,1)S(1)}, u32[]{:S(2)}, u32[]{:S(2)}) collective-permute-start(bf16[1,2048,128]{2,1,0:T(8,128)(2,1)} %collective-permute-done.10.r_10_), channel_id=1, source_target_pairs={{0,4},{4,0},{8,12},{12,8},{16,20},{20,16},{24,28},{28,24},{1,5},{5... | collective-permute-start | bytes 1572872 | tf_op jit(solution)/shard_map/ppermute | solution.py:347
  88.2 7.0 %collective-permute-start.22 = (bf16[1,2048,128]{2,1,0:T(8,128)(2,1)}, bf16[1,2048,128]{2,1,0:T(8,128)(2,1)}, u32[]{:S(2)}, u32[]{:S(2)}) collective-permute-start(bf16[1,2048,128]{2,1,0:T(8,128)(2,1)} %collective-permute-done.11.r_14_), channel_id=1, source_target_pairs={{0,4},{4,0},{8,12},{12,8},{16,20},{20,16},{24,28},{28,24},{1,5},{5... | collective-permute-start | bytes 1572872 | tf_op jit(solution)/shard_map/ppermute | solution.py:347
  89.2 21.1 %collective-permute-start.25 = (bf16[1,2048,128]{2,1,0:T(8,128)(2,1)}, bf16[1,2048,128]{2,1,0:T(8,128)(2,1)}, u32[]{:S(2)}, u32[]{:S(2)}) collective-permute-start(bf16[1,2048,128]{2,1,0:T(8,128)(2,1)} %collective-permute-done.13.r_9_), channel_id=1, source_target_pairs={{28,12},{0,16},{29,13},{1,17},{30,14},{2,18},{31,15},{3,19}} | collective-permute-start | bytes 1572872 | tf_op jit(solution)/shard_map/ppermute | solution.py:347
  92.8 17.5 %collective-permute-start.26 = (bf16[1,2048,128]{2,1,0:T(8,128)(2,1)S(1)}, bf16[1,2048,128]{2,1,0:T(8,128)(2,1)}, u32[]{:S(2)}, u32[]{:S(2)}) collective-permute-start(bf16[1,2048,128]{2,1,0:T(8,128)(2,1)S(1)} %copy-done.10), channel_id=1, source_target_pairs={{0,8},{28,20},{1,9},{29,21},{2,10},{30,22},{3,11},{31,23}} | collective-permute-start | bytes 1572872 | tf_op jit(solution)/shard_map/ppermute | solution.py:347
  95.2 15.1 %collective-permute-start.23 = (bf16[1,2048,128]{2,1,0:T(8,128)(2,1)}, bf16[1,2048,128]{2,1,0:T(8,128)(2,1)}, u32[]{:S(2)}, u32[]{:S(2)}) collective-permute-start(bf16[1,2048,128]{2,1,0:T(8,128)(2,1)} %collective-permute-done.10.r_10_), channel_id=1, source_target_pairs={{28,12},{0,16},{29,13},{1,17},{30,14},{2,18},{31,15},{3,19}} | collective-permute-start | bytes 1572872 | tf_op jit(solution)/shard_map/ppermute | solution.py:347
  97.3 13.0 %collective-permute-start.24 = (bf16[1,2048,128]{2,1,0:T(8,128)(2,1)}, bf16[1,2048,128]{2,1,0:T(8,128)(2,1)}, u32[]{:S(2)}, u32[]{:S(2)}) collective-permute-start(bf16[1,2048,128]{2,1,0:T(8,128)(2,1)} %collective-permute-done.11.r_14_), channel_id=1, source_target_pairs={{0,8},{28,20},{1,9},{29,21},{2,10},{30,22},{3,11},{31,23}} | collective-permute-start | bytes 1572872 | tf_op jit(solution)/shard_map/ppermute | solution.py:347
  100.8 11.3 %collective-permute-start.27 = (bf16[1,2048,128]{2,1,0:T(8,128)(2,1)}, bf16[1,2048,128]{2,1,0:T(8,128)(2,1)}, u32[]{:S(2)}, u32[]{:S(2)}) collective-permute-start(bf16[1,2048,128]{2,1,0:T(8,128)(2,1)} %collective-permute-done.12.r_16_), channel_id=1, source_target_pairs={{0,4},{4,0},{8,12},{12,8},{16,20},{20,16},{24,28},{28,24},{1,5},{5... | collective-permute-start | bytes 1572872 | tf_op jit(solution)/shard_map/ppermute | solution.py:347
  (37 other events, 443.9 us)

commit v7 on v6

--- a/solution.py
+++ b/solution.py
@@ -84,25 +84,30 @@
 def spectra_kernel(traces_ref, fine_cos, fine_sin, step_cos, step_sin, out_ref, table, planes):
     bins, fine = fine_cos.shape
     groups, _, channels = planes.shape
-    windows = traces_ref.shape[0] // channels
+    windows, length = traces_ref.shape[1:]
+    series = windows * channels
     for h in range(step_cos.shape[1]):
         sc, ss = step_cos[:, h : h + 1], step_sin[:, h : h + 1]
         cols = slice(h * fine, (h + 1) * fine)
         table[:bins, cols] = (sc * fine_cos[...] - ss * fine_sin[...]).astype(jnp.bfloat16)
         table[bins:, cols] = (-(ss * fine_cos[...] + sc * fine_sin[...])).astype(jnp.bfloat16)
-    for half in range(windows // 2):
-        rows = traces_ref[half * 2 * channels : (half + 1) * 2 * channels, :]
-        spectra = lax.dot_general(
-            table[...], rows, (((1,), (1,)), ((), ())), preferred_element_type=jnp.float32
-        )
-        power = jnp.sum(spectra * spectra, axis=0, keepdims=True)
-        white = spectra / jnp.sqrt(power / bins + 1e-06)
-        for w in range(2):
-            for c in range(2):
-                first = c * GROUP * windows + half * 2 + w
-                planes[:, pl.ds(first, GROUP, stride=windows), :] = white[
-                    c * bins : (c + 1) * bins, w * channels : (w + 1) * channels
-                ].reshape(groups, GROUP, channels)
+    was = lax.broadcasted_iota(jnp.int32, (series, series), 0)
+    now = lax.broadcasted_iota(jnp.int32, (series, series), 1)
+    turned = jnp.where(was == now % channels * windows + now // channels, 1.0, 0.0)
+    turned = turned.astype(jnp.bfloat16)
+    rows = traces_ref[...].reshape(series, length)
+    spectra = lax.dot_general(
+        table[...], rows, (((1,), (1,)), ((), ())), preferred_element_type=jnp.float32
+    )
+    power = jnp.sum(spectra * spectra, axis=0, keepdims=True)
+    white = (spectra / jnp.sqrt(power / bins + 1e-06)).astype(jnp.bfloat16)
+    white = jnp.dot(white, turned, preferred_element_type=jnp.float32)
+    for w in range(windows):
+        for c in range(2):
+            first = c * GROUP * windows + w
+            planes[:, pl.ds(first, GROUP, stride=windows), :] = white[
+                c * bins : (c + 1) * bins, w * channels : (w + 1) * channels
+            ].reshape(groups, GROUP, channels)
     out_ref[...] = planes[...].reshape(out_ref.shape).astype(jnp.bfloat16)
 
 
@@ -110,7 +115,6 @@
     channels, windows, length = traces.shape
     bins = band_bins.shape[0]
     fine = 128
-    rows = traces.transpose(1, 0, 2).reshape(windows * channels, length)
     sample_idx = jnp.concatenate([jnp.arange(fine), jnp.arange(length // fine) * fine])
     phase_int = band_bins[:, None] * sample_idx[None, :].astype(jnp.int32) % length
     phases = phase_int.astype(jnp.float32) * (2.0 * math.pi / length)
@@ -122,9 +126,9 @@
             pltpu.VMEM((2 * bins, length), jnp.bfloat16),
             pltpu.VMEM((bins // GROUP, GROUP * windows * 2, channels), jnp.float32),
         ],
-        compiler_params=pltpu.CompilerParams(vmem_limit_bytes=12 << 20),
+        compiler_params=pltpu.CompilerParams(vmem_limit_bytes=16 << 20),
         name="spectra",
-    )(rows, cos[:, :fine], sin[:, :fine], cos[:, fine:], sin[:, fine:])
+    )(traces, cos[:, :fine], sin[:, :fine], cos[:, fine:], sin[:, fine:])
 
 
 def left_kernel(z, *refs, per_step):
@@ -179,7 +183,7 @@
             ],
         ),
         out_shape=jax.ShapeDtypeStruct((groups, m, k), jnp.bfloat16),
-        compiler_params=pltpu.CompilerParams(vmem_limit_bytes=10 << 20),
+        compiler_params=pltpu.CompilerParams(vmem_limit_bytes=32 << 20),
         name="left",
     )(z.reshape(1), *slabs)
 
@@ -383,43 +387,50 @@
 
     s0 = make_slab(traces, band_bins)[None]
     q0 = slab_of(s0, 0)
+    up1 = along_z(s0, [(0, 1), (1, 2), (2, 3)])
     y0 = q0.hop(Y_PAIRS)
     x0 = q0.hop(X_PAIRS)
-    down1, up1 = along_z(s0, [(3, 2), (2, 1), (1, 0)]), along_z(s0, [(0, 1), (1, 2), (2, 3)])
-    y0, down1, up1, x0, lag_rows = together(y0, down1, up1, x0, lag_rows)
+    down1 = along_z(s0, [(3, 2), (2, 1), (1, 0)])
+    down1, lag_rows, x0, up1 = together(down1, lag_rows, x0, up1)
 
     q1 = slab_of(lax.select_n(z, down1, up1, down1, up1), 1)
-    c0 = x0.hop(Y_ON_ALL)
     y1 = q1.hop(Y_PAIRS)
+    d0 = y0.hop(X_ON)
+    c0 = x0.hop(Y_ON)
     x1 = q1.hop(X_PAIRS)
-    up2, down2 = along_z(up1, [(1, 2), (2, 3)]), along_z(down1, [(2, 1), (1, 0)])
+    down2 = along_z(down1, [(2, 1), (1, 0)])
+    up2 = along_z(up1, [(1, 2), (2, 3)])
     first = join(q0, x0, y0, q1)
-    up2, down2, x1, y1, first = together(up2, down2, x1, y1, first)
+    x1, first, up2, y0, down2, y1 = together(x1, first, up2, y0, down2, y1)
 
     q2 = slab_of(lax.select_n(z, down2, down1, up1, up2), 2)
+    down3 = along_z(down2, [(1, 0)])
+    y2 = q2.hop(Y_PAIRS)
+    up3 = along_z(up2, [(2, 3)])
+    x2 = q2.hop(X_PAIRS)
     c1 = x1.hop(Y_ON_ALL)
-    y2 = q2.hop(Y_PAIRS)
-    x2 = q2.hop(X_PAIRS)
-    last = along_z(jnp.where(z == 2, up2, down2), [(2, 3), (1, 0)])
-    second = join(x1, y1, q2)
-    last, c0, up2, down2, second = together(last, c0, up2, down2, second)
-
-    q3 = slab_of(lax.select_n(z, last, down2, up2, last), 3)
-    b = [first.hop(CORE_PAIRS), second.hop(CORE_PAIRS)]
+    second = join(x1, y1)
+    c0, up3, d0, up2, down2, second, down3 = together(c0, up3, d0, up2, down2, second, down3)
+
+    q3 = slab_of(lax.select_n(z, down3, down2, up2, up3), 3)
+    b = [h.hop(CORE_PAIRS) for h in (first, second,)]
     y3 = q3.hop(Y_PAIRS)
     x3 = q3.hop(X_PAIRS)
     left = make_left([q.value[0] for q in (q0, q1, q2, q3)], z, channels // 4, bins)
-    x2, y2, left = together(x2, y2, left)
-
-    c2, d2 = x2.hop(Y_ON), y2.hop(X_ON)
-    b += [c0.hop(CORE_PAIRS), q3.hop(CORE_PAIRS)]
+    left, x2, y2 = together(left, x2, y2)
+
+    d2 = y2.hop(X_ON)
+    c2 = x2.hop(Y_ON)
+    b += [h.hop(CORE_PAIRS) for h in (q2, d0, q3, c0,)]
+
+
     ids = np.arange(8, dtype=np.int32)
-    third = [x2.what, y2.what, x3.what, y3.what]
-    held = [q0, q1, q2, q3, x0, x1, x2, x3, y0, y1, y2, y3, c0, c1] + b
+    third = [y2.what, x2.what, x3.what, y3.what]
+    held = [q0, q1, q2, q3, x0, x1, x2, x3, y0, y1, y2, y3, c0, d0, c1] + b
     whats = [h.what for h in held] + [moved(what, CORE_PAIRS) for what in third]
     c3, d3 = moved(x3.what, Y_ON), moved(y3.what, X_ON)
     whats += [c2.what, d2.what, c3, d3]
-    whats += [moved(what, CORE_PAIRS) for what in (c1.what, c2.what, d2.what, c3, d3)]
+    whats += [moved(what, CORE_PAIRS) for what in (c3, d2.what, c1.what, d3, c2.what)]
     table = np.zeros((8, 8, 4), np.int32)
     all_holds = [set() for _ in whats]
     index = sum(len(what) for what in whats)
@@ -438,16 +449,16 @@
     swapped = slots[jnp.asarray([1, 0, 2])]
     slots = jnp.where(me == 5, swapped, slots)
 
-    x3, y3, c1, slots = together(x3, y3, c1, slots)
+    c1, y3, slots, x3 = together(c1, y3, slots, x3)
 
     c3, d3 = x3.hop(Y_ON), y3.hop(X_ON)
-    b += [h.hop(CORE_PAIRS) for h in (x2, y2, x3, y3)]
+    b += [h.hop(CORE_PAIRS) for h in (y2, x2, x3, y3)]
     norm = 1.0 / math.sqrt(4 * windows * bins)
-    held = [q0, q1, q2, q3, x0, x1, x2, x3, y0, y1, y2, y3, c0, c1] + b
+    held = [q0, q1, q2, q3, x0, x1, x2, x3, y0, y1, y2, y3, c0, d0, c1] + b
     places = [(h.value, holds) for h, holds in zip(held, all_holds)]
     result = correlate(slots[:1], left, lag_rows, places, slot_count, norm)
-    c3, d3, c2, d2, result = together(c3, d3, c2, d2, result)
-    late = [h.hop(CORE_PAIRS) for h in (c1, c2, d2, c3, d3)]
+    c2, result, d2, d3, c3 = together(c2, result, d2, d3, c3)
+    late = [h.hop(CORE_PAIRS) for h in (c3, d2, c1, d3, c2)]
     held += [c2, d2, c3, d3] + late
     places = [(h.value, holds) for h, holds in zip(held, all_holds)]
     return correlate(slots[1:], left, lag_rows, places, slot_count, norm, result)[None]

time: 127 us -> 123 us (0.969)
  the two profiles are of different devices: /device:TPU:0 before, /device:TPU:17 now
where the time goes in v7:
time: 123 us
  starting transfers between devices  50.9 us (41%)
  Pallas kernels  26.9 us (22%)
  waiting for transfers between devices  25.9 us (21%)
  other arithmetic  9.25 us (8%)
  local copies, waits for them, and re-layouts  9.21 us (7%)
    ppermute x30, starting transfers between devices, hop(): lax.ppermute(self.value, 'chan', pairs)  38 us
    pallas_call x2, Pallas kernels, correlate(): pl.pallas_call(lambda *r: pairs_kernel(*r, arrays=arrays, norm=norm, alia...  20.3 us
    ppermute x30, waiting for transfers between devices, hop(): lax.ppermute(self.value, 'chan', pairs)  13.1 us
    ppermute x6, starting transfers between devices, along_z(): return lax.ppermute(value, 'freq', pairs)  13 us
    ppermute x6, waiting for transfers between devices, along_z(): return lax.ppermute(value, 'freq', pairs)  12.8 us
    unnamed x64, local copies, waits for them, and re-layouts  6.6 us
    pallas_call x1, Pallas kernels, make_left(): pl.pallas_call(lambda *r: left_kernel(*r, per_step=per_step), grid_spec=p...  4.03 us
    concatenate x2, other arithmetic, join(): jnp.concatenate([p.value for p in parts], 0)  3.69 us
  transfers between devices with their start and end apart: 36, of which 15 were waited for; matrix products, arithmetic and copies ran while one was open for 8% of the time, Pallas kernels for 11%

profile of v7, /device:TPU:17, one launch (start us, length us, event | category | flops | bytes accessed | tf_op | source)
XLA Modules:
  0.0 122.8 jit_solution(6721765013058976589)
XLA Ops:
  3.5 2.6 %spectra.1 = bf16[2048,128]{1,0:T(8,128)(2,1)S(1)} custom-call(bf16[128,4,2048]{2,1,0:T(4,128)(2,1)S(1)} %copy-done.5, f32[256,128]{1,0:T(8,128)S(1)} %slice.26.fine_cos, f32[256,128]{1,0:T(8,128)S(1)} %slice.27.fine_sin, f32[256,16]{1,0:T(8,128)S(1)} %slice.28.step_cos, f32[256,16]{1,0:T(8,128)S(1)} %slice.29.step_sin), custom_call_target="tpu_custom_call" | custom-call | tf_op jit(solution)/shard_map/spectra/pallas_call | solution.py:122
  7.3 3.2 %collective-permute-start.2 = (bf16[1,2048,128]{2,1,0:T(8,128)(2,1)S(1)}, bf16[1,2048,128]{2,1,0:T(8,128)(2,1)S(1)}, u32[]{:S(2)}, u32[]{:S(2)}) collective-permute-start(bf16[1,2048,128]{2,1,0:T(8,128)(2,1)S(1)} %bitcast.15), channel_id=1, source_target_pairs={{0,1},{1,2},{2,3},{4,5},{5,6},{6,7},{8,9},{9,10},{10,11},{12,13},{... | collective-permute-start | bytes 1572872 | tf_op jit(solution)/shard_map/ppermute | solution.py:383
  10.5 2.1 %collective-permute-start = (bf16[1,2048,128]{2,1,0:T(8,128)(2,1)S(1)}, bf16[1,2048,128]{2,1,0:T(8,128)(2,1)S(1)}, u32[]{:S(2)}, u32[]{:S(2)}) collective-permute-start(bf16[1,2048,128]{2,1,0:T(8,128)(2,1)S(1)} %bitcast.16), channel_id=1, source_target_pairs={{3,2},{2,1},{1,0},{7,6},{6,5},{5,4},{11,10},{10,9},{9,8},{15,14},{... | collective-permute-start | bytes 1572872 | tf_op jit(solution)/shard_map/ppermute | solution.py:383
  12.6 4.0 %collective-permute-start.4 = (bf16[1,2048,128]{2,1,0:T(8,128)(2,1)S(1)}, bf16[1,2048,128]{2,1,0:T(8,128)(2,1)}, u32[]{:S(2)}, u32[]{:S(2)}) collective-permute-start(bf16[1,2048,128]{2,1,0:T(8,128)(2,1)S(1)} %bitcast.17), channel_id=1, source_target_pairs={{16,0},{4,20},{24,8},{12,28},{17,1},{5,21},{25,9},{13,29},{18,2},{... | collective-permute-start | bytes 1572872 | tf_op jit(solution)/shard_map/ppermute | solution.py:351
  18.9 2.9 %collective-permute-done.2 = bf16[1,2048,128]{2,1,0:T(8,128)(2,1)S(1)} collective-permute-done((bf16[1,2048,128]{2,1,0:T(8,128)(2,1)S(1)}, bf16[1,2048,128]{2,1,0:T(8,128)(2,1)S(1)}, u32[]{:S(2)}, u32[]{:S(2)}) %collective-permute-start.2) | collective-permute-done | bytes 524320 | tf_op jit(solution)/shard_map/ppermute | solution.py:383
  21.8 2.9 %collective-permute-done = bf16[1,2048,128]{2,1,0:T(8,128)(2,1)S(1)} collective-permute-done((bf16[1,2048,128]{2,1,0:T(8,128)(2,1)S(1)}, bf16[1,2048,128]{2,1,0:T(8,128)(2,1)S(1)}, u32[]{:S(2)}, u32[]{:S(2)}) %collective-permute-start) | collective-permute-done | bytes 524320 | tf_op jit(solution)/shard_map/ppermute | solution.py:383
  25.5 3.1 %collective-permute-start.7 = (bf16[1,2048,128]{2,1,0:T(8,128)(2,1)S(1)}, bf16[1,2048,128]{2,1,0:T(8,128)(2,1)S(1)}, u32[]{:S(2)}, u32[]{:S(2)}) collective-permute-start(bf16[1,2048,128]{2,1,0:T(8,128)(2,1)S(1)} %select_select_fusion.2.r_4_), channel_id=1, source_target_pairs={{16,0},{4,20},{24,8},{12,28},{17,1},{5,21},{25,9},{13,29},{18,2},{... | collective-permute-start | bytes 1572872 | tf_op jit(solution)/shard_map/ppermute | solution.py:351
  28.9 2.8 %collective-permute-start.6 = (bf16[1,2048,128]{2,1,0:T(8,128)(2,1)}, bf16[1,2048,128]{2,1,0:T(8,128)(2,1)}, u32[]{:S(2)}, u32[]{:S(2)}) collective-permute-start(bf16[1,2048,128]{2,1,0:T(8,128)(2,1)} %copy-done.21), channel_id=1, source_target_pairs={{2,1},{1,0},{6,5},{5,4},{10,9},{9,8},{14,13},{13,12},{18,17},{17,1... | collective-permute-start | bytes 1572872 | tf_op jit(solution)/shard_map/ppermute | solution.py:383
  31.8 1.9 %collective-permute-start.5 = (bf16[1,2048,128]{2,1,0:T(8,128)(2,1)S(1)}, bf16[1,2048,128]{2,1,0:T(8,128)(2,1)}, u32[]{:S(2)}, u32[]{:S(2)}) collective-permute-start(bf16[1,2048,128]{2,1,0:T(8,128)(2,1)S(1)} %collective-permute-done.2), channel_id=1, source_target_pairs={{1,2},{2,3},{5,6},{6,7},{9,10},{10,11},{13,14},{14,15},{17,18},{18... | collective-permute-start | bytes 1572872 | tf_op jit(solution)/shard_map/ppermute | solution.py:383
  36.1 2.6 %pad_maximum_fusion = bf16[4,2048,128]{2,1,0:T(8,128)(2,1)} fusion(bf16[1,2048,128]{2,1,0:T(8,128)(2,1)S(1)} %select_select_fusion.2.r_4_, bf16[1,2048,128]{2,1,0:T(8,128)(2,1)} %collective-permute-done.4.r_11_, bf16[1,2048,128]{2,1,0:T(8,128)(2,1)S(1)} %collective-permute-done.1.r_7_, bf16[1,2048,128]{2,1,0:T(8,128)(2,1)S(1)} %bitcast.18), kind=kLoop, calls=%fused_computation.1 | loop fusion | flops 3145728 | bytes 4194304 | tf_op jit(solution)/shard_map/concatenate | solution.py:355
  38.8 3.3 %collective-permute-done.3.r_8_ = bf16[1,2048,128]{2,1,0:T(8,128)(2,1)S(1)} collective-permute-done((bf16[1,2048,128]{2,1,0:T(8,128)(2,1)S(1)}, bf16[1,2048,128]{2,1,0:T(8,128)(2,1)S(1)}, u32[]{:S(2)}, u32[]{:S(2)}) %collective-permute-start.3) | collective-permute-done | bytes 524320 | tf_op jit(solution)/shard_map/ppermute | solution.py:351
  42.0 4.4 %collective-permute-done.5 = bf16[1,2048,128]{2,1,0:T(8,128)(2,1)} collective-permute-done((bf16[1,2048,128]{2,1,0:T(8,128)(2,1)S(1)}, bf16[1,2048,128]{2,1,0:T(8,128)(2,1)}, u32[]{:S(2)}, u32[]{:S(2)}) %collective-permute-start.5) | collective-permute-done | bytes 524320 | tf_op jit(solution)/shard_map/ppermute | solution.py:383
  46.4 2.3 %collective-permute-start.10 = (bf16[1,2048,128]{2,1,0:T(8,128)(2,1)}, bf16[1,2048,128]{2,1,0:T(8,128)(2,1)S(1)}, u32[]{:S(2)}, u32[]{:S(2)}) collective-permute-start(bf16[1,2048,128]{2,1,0:T(8,128)(2,1)} %collective-permute-done.5), channel_id=1, source_target_pairs={{2,3},{6,7},{10,11},{14,15},{18,19},{22,23},{26,27},{30,31}} | collective-permute-start | bytes 1572872 | tf_op jit(solution)/shard_map/ppermute | solution.py:383
  56.0 2.7 %collective-permute-done.10 = bf16[1,2048,128]{2,1,0:T(8,128)(2,1)S(1)} collective-permute-done((bf16[1,2048,128]{2,1,0:T(8,128)(2,1)}, bf16[1,2048,128]{2,1,0:T(8,128)(2,1)S(1)}, u32[]{:S(2)}, u32[]{:S(2)}) %collective-permute-start.10) | collective-permute-done | bytes 524320 | tf_op jit(solution)/shard_map/ppermute | solution.py:383
  58.7 2.1 %collective-permute-start.8 = (bf16[1,2048,128]{2,1,0:T(8,128)(2,1)S(1)}, bf16[1,2048,128]{2,1,0:T(8,128)(2,1)}, u32[]{:S(2)}, u32[]{:S(2)}) collective-permute-start(bf16[1,2048,128]{2,1,0:T(8,128)(2,1)S(1)} %collective-permute-done.3.r_8_), channel_id=1, source_target_pairs={{28,12},{0,16},{24,8},{4,20},{29,13},{1,17},{25,9},{5,21},{30,14},... | collective-permute-start | bytes 1572872 | tf_op jit(solution)/shard_map/ppermute | solution.py:351
  60.8 2.3 %collective-permute-start.17 = (bf16[4,2048,128]{2,1,0:T(8,128)(2,1)}, bf16[4,2048,128]{2,1,0:T(8,128)(2,1)}, u32[]{:S(2)}, u32[]{:S(2)}) collective-permute-start(bf16[4,2048,128]{2,1,0:T(8,128)(2,1)} %pad_maximum_fusion), channel_id=1, source_target_pairs={{0,4},{4,0},{8,12},{12,8},{16,20},{20,16},{24,28},{28,24},{1,5},{5... | collective-permute-start | bytes 6291464 | tf_op jit(solution)/shard_map/ppermute | solution.py:351
  65.2 2.2 %collective-permute-done.15.r_9_ = bf16[1,2048,128]{2,1,0:T(8,128)(2,1)} collective-permute-done((bf16[1,2048,128]{2,1,0:T(8,128)(2,1)S(1)}, bf16[1,2048,128]{2,1,0:T(8,128)(2,1)}, u32[]{:S(2)}, u32[]{:S(2)}) %collective-permute-start.15) | collective-permute-done | bytes 524320 | tf_op jit(solution)/shard_map/ppermute | solution.py:351
  67.4 3.5 %collective-permute-start.13 = (bf16[1,2048,128]{2,1,0:T(8,128)(2,1)S(1)}, bf16[1,2048,128]{2,1,0:T(8,128)(2,1)}, u32[]{:S(2)}, u32[]{:S(2)}) collective-permute-start(bf16[1,2048,128]{2,1,0:T(8,128)(2,1)S(1)} %select_select_fusion.1.r_6_), channel_id=1, source_target_pairs={{16,0},{4,20},{24,8},{12,28},{17,1},{5,21},{25,9},{13,29},{18,2},{... | collective-permute-start | bytes 1572872 | tf_op jit(solution)/shard_map/ppermute | solution.py:351
  71.2 4.0 %left.1.r_1_ = bf16[32,512,256]{2,1,0:T(8,128)(2,1)S(1)} custom-call(s32[1]{0:T(128)} %bitcast.4.r_0_, bf16[2048,128]{1,0:T(8,128)(2,1)S(1)} %spectra.1, bf16[2048,128]{1,0:T(8,128)(2,1)S(1)} %bitcast.13, bf16[2048,128]{1,0:T(8,128)(2,1)S(1)} %bitcast.21, bf16[2048,128]{1,0:T(8,128)(2,1)S(1)} %bitcast.22), custom_call_target="tpu_custom_call" | custom-call | tf_op jit(solution)/shard_map/left/pallas_call | solution.py:173
  75.2 3.3 %copy-done = bf16[32,512,256]{2,1,0:T(8,128)(2,1)} copy-done((bf16[32,512,256]{2,1,0:T(8,128)(2,1)}, bf16[32,512,256]{2,1,0:T(8,128)(2,1)S(1)}, u32[]{:S(2)}) %copy-start) | copy-done | bytes 8388632
  81.5 2.1 %collective-permute-done.24.r_25_ = bf16[1,2048,128]{2,1,0:T(8,128)(2,1)S(1)} collective-permute-done((bf16[1,2048,128]{2,1,0:T(8,128)(2,1)}, bf16[1,2048,128]{2,1,0:T(8,128)(2,1)S(1)}, u32[]{:S(2)}, u32[]{:S(2)}) %collective-permute-start.24) | collective-permute-done | bytes 524320 | tf_op jit(solution)/shard_map/ppermute | solution.py:351
  91.7 5.3 %collective-permute-start.33 = (bf16[1,2048,128]{2,1,0:T(8,128)(2,1)}, bf16[1,2048,128]{2,1,0:T(8,128)(2,1)}, u32[]{:S(2)}, u32[]{:S(2)}) collective-permute-start(bf16[1,2048,128]{2,1,0:T(8,128)(2,1)} %collective-permute-done.8.r_17_), channel_id=1, source_target_pairs={{0,4},{4,0},{8,12},{12,8},{16,20},{20,16},{24,28},{28,24},{1,5},{5... | collective-permute-start | bytes 1572872 | tf_op jit(solution)/shard_map/ppermute | solution.py:351
  97.0 9.5 %pairs.2.r_37_ = f32[32,3,128,128]{3,2,1,0:T(8,128)} custom-call(s32[5]{0:T(128)} %slice_bitcast_fusion.r_0_, bf16[32,512,256]{2,1,0:T(8,128)(2,1)} %copy-done, bf16[128,512]{1,0:T(8,128)(2,1)} %copy.15.r_2_, bf16[1,2048,128]{2,1,0:T(8,128)(2,1)} %bitcast.19, bf16[1,2048,128]{2,1,0:T(8,128)(2,1)} %copy-done.1, bf16[1,2048,128]{2,1,0:T(8,128)(2,1)} %copy-done.3, ...), custom_call_target="tpu_custom_call" | custom-call | flops 1610612736 | bytes 12582912 | tf_op jit(solution)/shard_map/pairs/pallas_call | solution.py:306
  111.8 10.8 %pairs.3 = f32[32,3,128,128]{3,2,1,0:T(8,128)} custom-call(s32[10]{0:T(128)} %reshape.186.r_0_, bf16[32,512,256]{2,1,0:T(8,128)(2,1)} %copy-done, bf16[128,512]{1,0:T(8,128)(2,1)} %copy.15.r_2_, bf16[1,2048,128]{2,1,0:T(8,128)(2,1)} %bitcast.20, bf16[1,2048,128]{2,1,0:T(8,128)(2,1)} %copy-done.1, ...), custom_call_target="tpu_custom_call", output_to_operand_aliasing={{}: (37, {})} | custom-call | flops 3221225472 | bytes 12582912 | tf_op jit(solution)/shard_map/pairs/pallas_call | solution.py:306
  (146 shorter events, 36.3 us)
Async XLA Ops:
  6.1 12.9 %collective-permute-start.1 = (bf16[1,2048,128]{2,1,0:T(8,128)(2,1)S(1)}, bf16[1,2048,128]{2,1,0:T(8,128)(2,1)S(1)}, u32[]{:S(2)}, u32[]{:S(2)}) collective-permute-start(bf16[1,2048,128]{2,1,0:T(8,128)(2,1)S(1)} %bitcast.14), channel_id=1, source_target_pairs={{0,8},{4,12},{8,0},{12,4},{16,24},{20,28},{24,16},{28,20},{1,9},{5... | collective-permute-start | bytes 1572872 | tf_op jit(solution)/shard_map/ppermute | solution.py:351
  7.3 14.5 %collective-permute-start.2 = (bf16[1,2048,128]{2,1,0:T(8,128)(2,1)S(1)}, bf16[1,2048,128]{2,1,0:T(8,128)(2,1)S(1)}, u32[]{:S(2)}, u32[]{:S(2)}) collective-permute-start(bf16[1,2048,128]{2,1,0:T(8,128)(2,1)S(1)} %bitcast.15), channel_id=1, source_target_pairs={{0,1},{1,2},{2,3},{4,5},{5,6},{6,7},{8,9},{9,10},{10,11},{12,13},{... | collective-permute-start | bytes 1572872 | tf_op jit(solution)/shard_map/ppermute | solution.py:383
  10.5 14.2 %collective-permute-start = (bf16[1,2048,128]{2,1,0:T(8,128)(2,1)S(1)}, bf16[1,2048,128]{2,1,0:T(8,128)(2,1)S(1)}, u32[]{:S(2)}, u32[]{:S(2)}) collective-permute-start(bf16[1,2048,128]{2,1,0:T(8,128)(2,1)S(1)} %bitcast.16), channel_id=1, source_target_pairs={{3,2},{2,1},{1,0},{7,6},{6,5},{5,4},{11,10},{10,9},{9,8},{15,14},{... | collective-permute-start | bytes 1572872 | tf_op jit(solution)/shard_map/ppermute | solution.py:383
  12.6 21.1 %collective-permute-start.4 = (bf16[1,2048,128]{2,1,0:T(8,128)(2,1)S(1)}, bf16[1,2048,128]{2,1,0:T(8,128)(2,1)}, u32[]{:S(2)}, u32[]{:S(2)}) collective-permute-start(bf16[1,2048,128]{2,1,0:T(8,128)(2,1)S(1)} %bitcast.17), channel_id=1, source_target_pairs={{16,0},{4,20},{24,8},{12,28},{17,1},{5,21},{25,9},{13,29},{18,2},{... | collective-permute-start | bytes 1572872 | tf_op jit(solution)/shard_map/ppermute | solution.py:351
  28.6 13.4 %collective-permute-start.3 = (bf16[1,2048,128]{2,1,0:T(8,128)(2,1)S(1)}, bf16[1,2048,128]{2,1,0:T(8,128)(2,1)S(1)}, u32[]{:S(2)}, u32[]{:S(2)}) collective-permute-start(bf16[1,2048,128]{2,1,0:T(8,128)(2,1)S(1)} %select_select_fusion.2.r_4_), channel_id=1, source_target_pairs={{0,8},{4,12},{8,0},{12,4},{16,24},{20,28},{24,16},{28,20},{1,9},{5... | collective-permute-start | bytes 1572872 | tf_op jit(solution)/shard_map/ppermute | solution.py:351
  28.9 13.1 %collective-permute-start.6 = (bf16[1,2048,128]{2,1,0:T(8,128)(2,1)}, bf16[1,2048,128]{2,1,0:T(8,128)(2,1)}, u32[]{:S(2)}, u32[]{:S(2)}) collective-permute-start(bf16[1,2048,128]{2,1,0:T(8,128)(2,1)} %copy-done.21), channel_id=1, source_target_pairs={{2,1},{1,0},{6,5},{5,4},{10,9},{9,8},{14,13},{13,12},{18,17},{17,1... | collective-permute-start | bytes 1572872 | tf_op jit(solution)/shard_map/ppermute | solution.py:383
  31.8 14.6 %collective-permute-start.5 = (bf16[1,2048,128]{2,1,0:T(8,128)(2,1)S(1)}, bf16[1,2048,128]{2,1,0:T(8,128)(2,1)}, u32[]{:S(2)}, u32[]{:S(2)}) collective-permute-start(bf16[1,2048,128]{2,1,0:T(8,128)(2,1)S(1)} %collective-permute-done.2), channel_id=1, source_target_pairs={{1,2},{2,3},{5,6},{6,7},{9,10},{10,11},{13,14},{14,15},{17,18},{18... | collective-permute-start | bytes 1572872 | tf_op jit(solution)/shard_map/ppermute | solution.py:383
  33.7 19.9 %collective-permute-start.9 = (bf16[1,2048,128]{2,1,0:T(8,128)(2,1)S(1)}, bf16[1,2048,128]{2,1,0:T(8,128)(2,1)S(1)}, u32[]{:S(2)}, u32[]{:S(2)}) collective-permute-start(bf16[1,2048,128]{2,1,0:T(8,128)(2,1)S(1)} %collective-permute-done.1.r_7_), channel_id=1, source_target_pairs={{28,12},{0,16},{29,13},{1,17},{30,14},{2,18},{31,15},{3,19}} | collective-permute-start | bytes 1572872 | tf_op jit(solution)/shard_map/ppermute | solution.py:351
  34.7 17.7 %collective-permute-start.11 = (bf16[1,2048,128]{2,1,0:T(8,128)(2,1)}, bf16[1,2048,128]{2,1,0:T(8,128)(2,1)}, u32[]{:S(2)}, u32[]{:S(2)}) collective-permute-start(bf16[1,2048,128]{2,1,0:T(8,128)(2,1)} %collective-permute-done.4.r_11_), channel_id=1, source_target_pairs={{0,8},{28,20},{1,9},{29,21},{2,10},{30,22},{3,11},{31,23}} | collective-permute-start | bytes 1572872 | tf_op jit(solution)/shard_map/ppermute | solution.py:351
  46.4 12.3 %collective-permute-start.10 = (bf16[1,2048,128]{2,1,0:T(8,128)(2,1)}, bf16[1,2048,128]{2,1,0:T(8,128)(2,1)S(1)}, u32[]{:S(2)}, u32[]{:S(2)}) collective-permute-start(bf16[1,2048,128]{2,1,0:T(8,128)(2,1)} %collective-permute-done.5), channel_id=1, source_target_pairs={{2,3},{6,7},{10,11},{14,15},{18,19},{22,23},{26,27},{30,31}} | collective-permute-start | bytes 1572872 | tf_op jit(solution)/shard_map/ppermute | solution.py:383
  48.6 12.2 %collective-permute-start.12 = (bf16[1,2048,128]{2,1,0:T(8,128)(2,1)}, bf16[1,2048,128]{2,1,0:T(8,128)(2,1)S(1)}, u32[]{:S(2)}, u32[]{:S(2)}) collective-permute-start(bf16[1,2048,128]{2,1,0:T(8,128)(2,1)} %collective-permute-done.6), channel_id=1, source_target_pairs={{1,0},{5,4},{9,8},{13,12},{17,16},{21,20},{25,24},{29,28}} | collective-permute-start | bytes 1572872 | tf_op jit(solution)/shard_map/ppermute | solution.py:383
  50.6 13.9 %collective-permute-start.19 = (bf16[1,2048,128]{2,1,0:T(8,128)(2,1)S(1)}, bf16[1,2048,128]{2,1,0:T(8,128)(2,1)S(1)}, u32[]{:S(2)}, u32[]{:S(2)}) collective-permute-start(bf16[1,2048,128]{2,1,0:T(8,128)(2,1)S(1)} %select_select_fusion.r_5_), channel_id=1, source_target_pairs={{0,4},{4,0},{8,12},{12,8},{16,20},{20,16},{24,28},{28,24},{1,5},{5... | collective-permute-start | bytes 1572872 | tf_op jit(solution)/shard_map/ppermute | solution.py:351
  52.3 12.2 %collective-permute-start.16 = (bf16[1,2048,128]{2,1,0:T(8,128)(2,1)S(1)}, bf16[1,2048,128]{2,1,0:T(8,128)(2,1)S(1)}, u32[]{:S(2)}, u32[]{:S(2)}) collective-permute-start(bf16[1,2048,128]{2,1,0:T(8,128)(2,1)S(1)} %select_select_fusion.r_5_), channel_id=1, source_target_pairs={{16,0},{4,20},{24,8},{12,28},{17,1},{5,21},{25,9},{13,29},{18,2},{... | collective-permute-start | bytes 1572872 | tf_op jit(solution)/shard_map/ppermute | solution.py:351
  53.7 13.7 %collective-permute-start.15 = (bf16[1,2048,128]{2,1,0:T(8,128)(2,1)S(1)}, bf16[1,2048,128]{2,1,0:T(8,128)(2,1)}, u32[]{:S(2)}, u32[]{:S(2)}) collective-permute-start(bf16[1,2048,128]{2,1,0:T(8,128)(2,1)S(1)} %select_select_fusion.r_5_), channel_id=1, source_target_pairs={{0,8},{4,12},{8,0},{12,4},{16,24},{20,28},{24,16},{28,20},{1,9},{5... | collective-permute-start | bytes 1572872 | tf_op jit(solution)/shard_map/ppermute | solution.py:351
  58.7 19.8 %collective-permute-start.8 = (bf16[1,2048,128]{2,1,0:T(8,128)(2,1)S(1)}, bf16[1,2048,128]{2,1,0:T(8,128)(2,1)}, u32[]{:S(2)}, u32[]{:S(2)}) collective-permute-start(bf16[1,2048,128]{2,1,0:T(8,128)(2,1)S(1)} %collective-permute-done.3.r_8_), channel_id=1, source_target_pairs={{28,12},{0,16},{24,8},{4,20},{29,13},{1,17},{25,9},{5,21},{30,14},... | collective-permute-start | bytes 1572872 | tf_op jit(solution)/shard_map/ppermute | solution.py:351
  60.8 30.9 %collective-permute-start.17 = (bf16[4,2048,128]{2,1,0:T(8,128)(2,1)}, bf16[4,2048,128]{2,1,0:T(8,128)(2,1)}, u32[]{:S(2)}, u32[]{:S(2)}) collective-permute-start(bf16[4,2048,128]{2,1,0:T(8,128)(2,1)} %pad_maximum_fusion), channel_id=1, source_target_pairs={{0,4},{4,0},{8,12},{12,8},{16,20},{20,16},{24,28},{28,24},{1,5},{5... | collective-permute-start | bytes 6291464 | tf_op jit(solution)/shard_map/ppermute | solution.py:351
  64.5 14.1 %collective-permute-start.21 = (bf16[1,2048,128]{2,1,0:T(8,128)(2,1)S(1)}, bf16[1,2048,128]{2,1,0:T(8,128)(2,1)}, u32[]{:S(2)}, u32[]{:S(2)}) collective-permute-start(bf16[1,2048,128]{2,1,0:T(8,128)(2,1)S(1)} %select_select_fusion.1.r_6_), channel_id=1, source_target_pairs={{0,4},{4,0},{8,12},{12,8},{16,20},{20,16},{24,28},{28,24},{1,5},{5... | collective-permute-start | bytes 1572872 | tf_op jit(solution)/shard_map/ppermute | solution.py:351
  64.6 14.5 %collective-permute-start.14 = (bf16[1,2048,128]{2,1,0:T(8,128)(2,1)S(1)}, bf16[1,2048,128]{2,1,0:T(8,128)(2,1)}, u32[]{:S(2)}, u32[]{:S(2)}) collective-permute-start(bf16[1,2048,128]{2,1,0:T(8,128)(2,1)S(1)} %select_select_fusion.1.r_6_), channel_id=1, source_target_pairs={{0,8},{4,12},{8,0},{12,4},{16,24},{20,28},{24,16},{28,20},{1,9},{5... | collective-permute-start | bytes 1572872 | tf_op jit(solution)/shard_map/ppermute | solution.py:351
  67.4 12.0 %collective-permute-start.13 = (bf16[1,2048,128]{2,1,0:T(8,128)(2,1)S(1)}, bf16[1,2048,128]{2,1,0:T(8,128)(2,1)}, u32[]{:S(2)}, u32[]{:S(2)}) collective-permute-start(bf16[1,2048,128]{2,1,0:T(8,128)(2,1)S(1)} %select_select_fusion.1.r_6_), channel_id=1, source_target_pairs={{16,0},{4,20},{24,8},{12,28},{17,1},{5,21},{25,9},{13,29},{18,2},{... | collective-permute-start | bytes 1572872 | tf_op jit(solution)/shard_map/ppermute | solution.py:351
  84.4 22.1 %collective-permute-start.27 = (bf16[1,2048,128]{2,1,0:T(8,128)(2,1)}, bf16[1,2048,128]{2,1,0:T(8,128)(2,1)}, u32[]{:S(2)}, u32[]{:S(2)}) collective-permute-start(bf16[1,2048,128]{2,1,0:T(8,128)(2,1)} %collective-permute-done.15.r_9_), channel_id=1, source_target_pairs={{28,12},{0,16},{29,13},{1,17},{30,14},{2,18},{31,15},{3,19}} | collective-permute-start | bytes 1572872 | tf_op jit(solution)/shard_map/ppermute | solution.py:351
  85.9 20.6 %collective-permute-start.28 = (bf16[1,2048,128]{2,1,0:T(8,128)(2,1)}, bf16[1,2048,128]{2,1,0:T(8,128)(2,1)}, u32[]{:S(2)}, u32[]{:S(2)}) collective-permute-start(bf16[1,2048,128]{2,1,0:T(8,128)(2,1)} %copy-done.13), channel_id=1, source_target_pairs={{0,8},{28,20},{1,9},{29,21},{2,10},{30,22},{3,11},{31,23}} | collective-permute-start | bytes 1572872 | tf_op jit(solution)/shard_map/ppermute | solution.py:351
  87.4 19.1 %collective-permute-start.30 = (bf16[1,2048,128]{2,1,0:T(8,128)(2,1)}, bf16[1,2048,128]{2,1,0:T(8,128)(2,1)}, u32[]{:S(2)}, u32[]{:S(2)}) collective-permute-start(bf16[1,2048,128]{2,1,0:T(8,128)(2,1)} %collective-permute-done.14.r_10_), channel_id=1, source_target_pairs={{28,12},{0,16},{29,13},{1,17},{30,14},{2,18},{31,15},{3,19}} | collective-permute-start | bytes 1572872 | tf_op jit(solution)/shard_map/ppermute | solution.py:351
  88.9 17.6 %collective-permute-start.29 = (bf16[1,2048,128]{2,1,0:T(8,128)(2,1)}, bf16[1,2048,128]{2,1,0:T(8,128)(2,1)}, u32[]{:S(2)}, u32[]{:S(2)}) collective-permute-start(bf16[1,2048,128]{2,1,0:T(8,128)(2,1)} %collective-permute-done.13.r_14_), channel_id=1, source_target_pairs={{0,8},{28,20},{1,9},{29,21},{2,10},{30,22},{3,11},{31,23}} | collective-permute-start | bytes 1572872 | tf_op jit(solution)/shard_map/ppermute | solution.py:351
  91.7 16.6 %collective-permute-start.33 = (bf16[1,2048,128]{2,1,0:T(8,128)(2,1)}, bf16[1,2048,128]{2,1,0:T(8,128)(2,1)}, u32[]{:S(2)}, u32[]{:S(2)}) collective-permute-start(bf16[1,2048,128]{2,1,0:T(8,128)(2,1)} %collective-permute-done.8.r_17_), channel_id=1, source_target_pairs={{0,4},{4,0},{8,12},{12,8},{16,20},{20,16},{24,28},{28,24},{1,5},{5... | collective-permute-start | bytes 1572872 | tf_op jit(solution)/shard_map/ppermute | solution.py:351
  (44 other events, 475.6 us)

commit v8 on v7

--- a/solution.py
+++ b/solution.py
@@ -190,7 +190,7 @@
 
 CHUNKS = 4
 GROUP_UNROLL = 8
-ROW_UNROLL = 8
+ROW_UNROLL = 16
 
 
 def pairs_kernel(slots, left_ref, lag_ref, *refs, arrays, norm, aliased):

time: 123 us -> 122 us (level)
  no operation moved by 1% of the time
where the time goes in v8:
time: 122 us
  starting transfers between devices  50.9 us (42%)
  waiting for transfers between devices  25.9 us (21%)
  Pallas kernels  25.7 us (21%)
  other arithmetic  9.25 us (8%)
  local copies, waits for them, and re-layouts  9.21 us (8%)
    ppermute x30, starting transfers between devices, hop(): lax.ppermute(self.value, 'chan', pairs)  38 us
    pallas_call x2, Pallas kernels, correlate(): pl.pallas_call(lambda *r: pairs_kernel(*r, arrays=arrays, norm=norm, alia...  19.1 us
    ppermute x30, waiting for transfers between devices, hop(): lax.ppermute(self.value, 'chan', pairs)  13.1 us
    ppermute x6, starting transfers between devices, along_z(): return lax.ppermute(value, 'freq', pairs)  13 us
    ppermute x6, waiting for transfers between devices, along_z(): return lax.ppermute(value, 'freq', pairs)  12.8 us
    unnamed x64, local copies, waits for them, and re-layouts  6.6 us
    pallas_call x1, Pallas kernels, make_left(): pl.pallas_call(lambda *r: left_kernel(*r, per_step=per_step), grid_spec=p...  4.03 us
    concatenate x2, other arithmetic, join(): jnp.concatenate([p.value for p in parts], 0)  3.69 us
  transfers between devices with their start and end apart: 36, of which 15 were waited for; matrix products, arithmetic and copies ran while one was open for 8% of the time, Pallas kernels for 11%

profile of v8, /device:TPU:17, one launch (start us, length us, event | category | flops | bytes accessed | tf_op | source)
XLA Modules:
  0.0 121.6 jit_solution(11057727828808342567)
XLA Ops:
  3.5 2.6 %spectra.1 = bf16[2048,128]{1,0:T(8,128)(2,1)S(1)} custom-call(bf16[128,4,2048]{2,1,0:T(4,128)(2,1)S(1)} %copy-done.5, f32[256,128]{1,0:T(8,128)S(1)} %slice.26.fine_cos, f32[256,128]{1,0:T(8,128)S(1)} %slice.27.fine_sin, f32[256,16]{1,0:T(8,128)S(1)} %slice.28.step_cos, f32[256,16]{1,0:T(8,128)S(1)} %slice.29.step_sin), custom_call_target="tpu_custom_call" | custom-call | tf_op jit(solution)/shard_map/spectra/pallas_call | solution.py:122
  7.3 3.2 %collective-permute-start.2 = (bf16[1,2048,128]{2,1,0:T(8,128)(2,1)S(1)}, bf16[1,2048,128]{2,1,0:T(8,128)(2,1)S(1)}, u32[]{:S(2)}, u32[]{:S(2)}) collective-permute-start(bf16[1,2048,128]{2,1,0:T(8,128)(2,1)S(1)} %bitcast.15), channel_id=1, source_target_pairs={{0,1},{1,2},{2,3},{4,5},{5,6},{6,7},{8,9},{9,10},{10,11},{12,13},{... | collective-permute-start | bytes 1572872 | tf_op jit(solution)/shard_map/ppermute | solution.py:383
  10.5 2.1 %collective-permute-start = (bf16[1,2048,128]{2,1,0:T(8,128)(2,1)S(1)}, bf16[1,2048,128]{2,1,0:T(8,128)(2,1)S(1)}, u32[]{:S(2)}, u32[]{:S(2)}) collective-permute-start(bf16[1,2048,128]{2,1,0:T(8,128)(2,1)S(1)} %bitcast.16), channel_id=1, source_target_pairs={{3,2},{2,1},{1,0},{7,6},{6,5},{5,4},{11,10},{10,9},{9,8},{15,14},{... | collective-permute-start | bytes 1572872 | tf_op jit(solution)/shard_map/ppermute | solution.py:383
  12.6 4.0 %collective-permute-start.4 = (bf16[1,2048,128]{2,1,0:T(8,128)(2,1)S(1)}, bf16[1,2048,128]{2,1,0:T(8,128)(2,1)}, u32[]{:S(2)}, u32[]{:S(2)}) collective-permute-start(bf16[1,2048,128]{2,1,0:T(8,128)(2,1)S(1)} %bitcast.17), channel_id=1, source_target_pairs={{16,0},{4,20},{24,8},{12,28},{17,1},{5,21},{25,9},{13,29},{18,2},{... | collective-permute-start | bytes 1572872 | tf_op jit(solution)/shard_map/ppermute | solution.py:351
  18.9 2.9 %collective-permute-done.2 = bf16[1,2048,128]{2,1,0:T(8,128)(2,1)S(1)} collective-permute-done((bf16[1,2048,128]{2,1,0:T(8,128)(2,1)S(1)}, bf16[1,2048,128]{2,1,0:T(8,128)(2,1)S(1)}, u32[]{:S(2)}, u32[]{:S(2)}) %collective-permute-start.2) | collective-permute-done | bytes 524320 | tf_op jit(solution)/shard_map/ppermute | solution.py:383
  21.8 2.9 %collective-permute-done = bf16[1,2048,128]{2,1,0:T(8,128)(2,1)S(1)} collective-permute-done((bf16[1,2048,128]{2,1,0:T(8,128)(2,1)S(1)}, bf16[1,2048,128]{2,1,0:T(8,128)(2,1)S(1)}, u32[]{:S(2)}, u32[]{:S(2)}) %collective-permute-start) | collective-permute-done | bytes 524320 | tf_op jit(solution)/shard_map/ppermute | solution.py:383
  25.5 3.1 %collective-permute-start.7 = (bf16[1,2048,128]{2,1,0:T(8,128)(2,1)S(1)}, bf16[1,2048,128]{2,1,0:T(8,128)(2,1)S(1)}, u32[]{:S(2)}, u32[]{:S(2)}) collective-permute-start(bf16[1,2048,128]{2,1,0:T(8,128)(2,1)S(1)} %select_select_fusion.2.r_4_), channel_id=1, source_target_pairs={{16,0},{4,20},{24,8},{12,28},{17,1},{5,21},{25,9},{13,29},{18,2},{... | collective-permute-start | bytes 1572872 | tf_op jit(solution)/shard_map/ppermute | solution.py:351
  28.9 2.8 %collective-permute-start.6 = (bf16[1,2048,128]{2,1,0:T(8,128)(2,1)}, bf16[1,2048,128]{2,1,0:T(8,128)(2,1)}, u32[]{:S(2)}, u32[]{:S(2)}) collective-permute-start(bf16[1,2048,128]{2,1,0:T(8,128)(2,1)} %copy-done.21), channel_id=1, source_target_pairs={{2,1},{1,0},{6,5},{5,4},{10,9},{9,8},{14,13},{13,12},{18,17},{17,1... | collective-permute-start | bytes 1572872 | tf_op jit(solution)/shard_map/ppermute | solution.py:383
  31.8 1.9 %collective-permute-start.5 = (bf16[1,2048,128]{2,1,0:T(8,128)(2,1)S(1)}, bf16[1,2048,128]{2,1,0:T(8,128)(2,1)}, u32[]{:S(2)}, u32[]{:S(2)}) collective-permute-start(bf16[1,2048,128]{2,1,0:T(8,128)(2,1)S(1)} %collective-permute-done.2), channel_id=1, source_target_pairs={{1,2},{2,3},{5,6},{6,7},{9,10},{10,11},{13,14},{14,15},{17,18},{18... | collective-permute-start | bytes 1572872 | tf_op jit(solution)/shard_map/ppermute | solution.py:383
  36.1 2.6 %pad_maximum_fusion = bf16[4,2048,128]{2,1,0:T(8,128)(2,1)} fusion(bf16[1,2048,128]{2,1,0:T(8,128)(2,1)S(1)} %select_select_fusion.2.r_4_, bf16[1,2048,128]{2,1,0:T(8,128)(2,1)} %collective-permute-done.4.r_11_, bf16[1,2048,128]{2,1,0:T(8,128)(2,1)S(1)} %collective-permute-done.1.r_7_, bf16[1,2048,128]{2,1,0:T(8,128)(2,1)S(1)} %bitcast.18), kind=kLoop, calls=%fused_computation.1 | loop fusion | flops 3145728 | bytes 4194304 | tf_op jit(solution)/shard_map/concatenate | solution.py:355
  38.8 3.3 %collective-permute-done.3.r_8_ = bf16[1,2048,128]{2,1,0:T(8,128)(2,1)S(1)} collective-permute-done((bf16[1,2048,128]{2,1,0:T(8,128)(2,1)S(1)}, bf16[1,2048,128]{2,1,0:T(8,128)(2,1)S(1)}, u32[]{:S(2)}, u32[]{:S(2)}) %collective-permute-start.3) | collective-permute-done | bytes 524320 | tf_op jit(solution)/shard_map/ppermute | solution.py:351
  42.0 4.4 %collective-permute-done.5 = bf16[1,2048,128]{2,1,0:T(8,128)(2,1)} collective-permute-done((bf16[1,2048,128]{2,1,0:T(8,128)(2,1)S(1)}, bf16[1,2048,128]{2,1,0:T(8,128)(2,1)}, u32[]{:S(2)}, u32[]{:S(2)}) %collective-permute-start.5) | collective-permute-done | bytes 524320 | tf_op jit(solution)/shard_map/ppermute | solution.py:383
  46.4 2.3 %collective-permute-start.10 = (bf16[1,2048,128]{2,1,0:T(8,128)(2,1)}, bf16[1,2048,128]{2,1,0:T(8,128)(2,1)S(1)}, u32[]{:S(2)}, u32[]{:S(2)}) collective-permute-start(bf16[1,2048,128]{2,1,0:T(8,128)(2,1)} %collective-permute-done.5), channel_id=1, source_target_pairs={{2,3},{6,7},{10,11},{14,15},{18,19},{22,23},{26,27},{30,31}} | collective-permute-start | bytes 1572872 | tf_op jit(solution)/shard_map/ppermute | solution.py:383
  56.0 2.7 %collective-permute-done.10 = bf16[1,2048,128]{2,1,0:T(8,128)(2,1)S(1)} collective-permute-done((bf16[1,2048,128]{2,1,0:T(8,128)(2,1)}, bf16[1,2048,128]{2,1,0:T(8,128)(2,1)S(1)}, u32[]{:S(2)}, u32[]{:S(2)}) %collective-permute-start.10) | collective-permute-done | bytes 524320 | tf_op jit(solution)/shard_map/ppermute | solution.py:383
  58.7 2.1 %collective-permute-start.8 = (bf16[1,2048,128]{2,1,0:T(8,128)(2,1)S(1)}, bf16[1,2048,128]{2,1,0:T(8,128)(2,1)}, u32[]{:S(2)}, u32[]{:S(2)}) collective-permute-start(bf16[1,2048,128]{2,1,0:T(8,128)(2,1)S(1)} %collective-permute-done.3.r_8_), channel_id=1, source_target_pairs={{28,12},{0,16},{24,8},{4,20},{29,13},{1,17},{25,9},{5,21},{30,14},... | collective-permute-start | bytes 1572872 | tf_op jit(solution)/shard_map/ppermute | solution.py:351
  60.8 2.3 %collective-permute-start.17 = (bf16[4,2048,128]{2,1,0:T(8,128)(2,1)}, bf16[4,2048,128]{2,1,0:T(8,128)(2,1)}, u32[]{:S(2)}, u32[]{:S(2)}) collective-permute-start(bf16[4,2048,128]{2,1,0:T(8,128)(2,1)} %pad_maximum_fusion), channel_id=1, source_target_pairs={{0,4},{4,0},{8,12},{12,8},{16,20},{20,16},{24,28},{28,24},{1,5},{5... | collective-permute-start | bytes 6291464 | tf_op jit(solution)/shard_map/ppermute | solution.py:351
  65.2 2.2 %collective-permute-done.15.r_9_ = bf16[1,2048,128]{2,1,0:T(8,128)(2,1)} collective-permute-done((bf16[1,2048,128]{2,1,0:T(8,128)(2,1)S(1)}, bf16[1,2048,128]{2,1,0:T(8,128)(2,1)}, u32[]{:S(2)}, u32[]{:S(2)}) %collective-permute-start.15) | collective-permute-done | bytes 524320 | tf_op jit(solution)/shard_map/ppermute | solution.py:351
  67.4 3.5 %collective-permute-start.13 = (bf16[1,2048,128]{2,1,0:T(8,128)(2,1)S(1)}, bf16[1,2048,128]{2,1,0:T(8,128)(2,1)}, u32[]{:S(2)}, u32[]{:S(2)}) collective-permute-start(bf16[1,2048,128]{2,1,0:T(8,128)(2,1)S(1)} %select_select_fusion.1.r_6_), channel_id=1, source_target_pairs={{16,0},{4,20},{24,8},{12,28},{17,1},{5,21},{25,9},{13,29},{18,2},{... | collective-permute-start | bytes 1572872 | tf_op jit(solution)/shard_map/ppermute | solution.py:351
  71.2 4.0 %left.1.r_1_ = bf16[32,512,256]{2,1,0:T(8,128)(2,1)S(1)} custom-call(s32[1]{0:T(128)} %bitcast.4.r_0_, bf16[2048,128]{1,0:T(8,128)(2,1)S(1)} %spectra.1, bf16[2048,128]{1,0:T(8,128)(2,1)S(1)} %bitcast.13, bf16[2048,128]{1,0:T(8,128)(2,1)S(1)} %bitcast.21, bf16[2048,128]{1,0:T(8,128)(2,1)S(1)} %bitcast.22), custom_call_target="tpu_custom_call" | custom-call | tf_op jit(solution)/shard_map/left/pallas_call | solution.py:173
  75.2 3.3 %copy-done = bf16[32,512,256]{2,1,0:T(8,128)(2,1)} copy-done((bf16[32,512,256]{2,1,0:T(8,128)(2,1)}, bf16[32,512,256]{2,1,0:T(8,128)(2,1)S(1)}, u32[]{:S(2)}) %copy-start) | copy-done | bytes 8388632
  81.5 2.1 %collective-permute-done.24.r_25_ = bf16[1,2048,128]{2,1,0:T(8,128)(2,1)S(1)} collective-permute-done((bf16[1,2048,128]{2,1,0:T(8,128)(2,1)}, bf16[1,2048,128]{2,1,0:T(8,128)(2,1)S(1)}, u32[]{:S(2)}, u32[]{:S(2)}) %collective-permute-start.24) | collective-permute-done | bytes 524320 | tf_op jit(solution)/shard_map/ppermute | solution.py:351
  91.7 5.3 %collective-permute-start.33 = (bf16[1,2048,128]{2,1,0:T(8,128)(2,1)}, bf16[1,2048,128]{2,1,0:T(8,128)(2,1)}, u32[]{:S(2)}, u32[]{:S(2)}) collective-permute-start(bf16[1,2048,128]{2,1,0:T(8,128)(2,1)} %collective-permute-done.8.r_17_), channel_id=1, source_target_pairs={{0,4},{4,0},{8,12},{12,8},{16,20},{20,16},{24,28},{28,24},{1,5},{5... | collective-permute-start | bytes 1572872 | tf_op jit(solution)/shard_map/ppermute | solution.py:351
  97.0 8.9 %pairs.2.r_37_ = f32[32,3,128,128]{3,2,1,0:T(8,128)} custom-call(s32[5]{0:T(128)} %slice_bitcast_fusion.r_0_, bf16[32,512,256]{2,1,0:T(8,128)(2,1)} %copy-done, bf16[128,512]{1,0:T(8,128)(2,1)} %copy.15.r_2_, bf16[1,2048,128]{2,1,0:T(8,128)(2,1)} %bitcast.19, bf16[1,2048,128]{2,1,0:T(8,128)(2,1)} %copy-done.1, bf16[1,2048,128]{2,1,0:T(8,128)(2,1)} %copy-done.3, ...), custom_call_target="tpu_custom_call" | custom-call | flops 1610612736 | bytes 12582912 | tf_op jit(solution)/shard_map/pairs/pallas_call | solution.py:306
  111.3 10.2 %pairs.3 = f32[32,3,128,128]{3,2,1,0:T(8,128)} custom-call(s32[10]{0:T(128)} %reshape.186.r_0_, bf16[32,512,256]{2,1,0:T(8,128)(2,1)} %copy-done, bf16[128,512]{1,0:T(8,128)(2,1)} %copy.15.r_2_, bf16[1,2048,128]{2,1,0:T(8,128)(2,1)} %bitcast.20, bf16[1,2048,128]{2,1,0:T(8,128)(2,1)} %copy-done.1, ...), custom_call_target="tpu_custom_call", output_to_operand_aliasing={{}: (37, {})} | custom-call | flops 3221225472 | bytes 12582912 | tf_op jit(solution)/shard_map/pairs/pallas_call | solution.py:306
  (146 shorter events, 36.3 us)
Async XLA Ops:
  6.1 12.9 %collective-permute-start.1 = (bf16[1,2048,128]{2,1,0:T(8,128)(2,1)S(1)}, bf16[1,2048,128]{2,1,0:T(8,128)(2,1)S(1)}, u32[]{:S(2)}, u32[]{:S(2)}) collective-permute-start(bf16[1,2048,128]{2,1,0:T(8,128)(2,1)S(1)} %bitcast.14), channel_id=1, source_target_pairs={{0,8},{4,12},{8,0},{12,4},{16,24},{20,28},{24,16},{28,20},{1,9},{5... | collective-permute-start | bytes 1572872 | tf_op jit(solution)/shard_map/ppermute | solution.py:351
  7.3 14.5 %collective-permute-start.2 = (bf16[1,2048,128]{2,1,0:T(8,128)(2,1)S(1)}, bf16[1,2048,128]{2,1,0:T(8,128)(2,1)S(1)}, u32[]{:S(2)}, u32[]{:S(2)}) collective-permute-start(bf16[1,2048,128]{2,1,0:T(8,128)(2,1)S(1)} %bitcast.15), channel_id=1, source_target_pairs={{0,1},{1,2},{2,3},{4,5},{5,6},{6,7},{8,9},{9,10},{10,11},{12,13},{... | collective-permute-start | bytes 1572872 | tf_op jit(solution)/shard_map/ppermute | solution.py:383
  10.5 14.2 %collective-permute-start = (bf16[1,2048,128]{2,1,0:T(8,128)(2,1)S(1)}, bf16[1,2048,128]{2,1,0:T(8,128)(2,1)S(1)}, u32[]{:S(2)}, u32[]{:S(2)}) collective-permute-start(bf16[1,2048,128]{2,1,0:T(8,128)(2,1)S(1)} %bitcast.16), channel_id=1, source_target_pairs={{3,2},{2,1},{1,0},{7,6},{6,5},{5,4},{11,10},{10,9},{9,8},{15,14},{... | collective-permute-start | bytes 1572872 | tf_op jit(solution)/shard_map/ppermute | solution.py:383
  12.6 21.1 %collective-permute-start.4 = (bf16[1,2048,128]{2,1,0:T(8,128)(2,1)S(1)}, bf16[1,2048,128]{2,1,0:T(8,128)(2,1)}, u32[]{:S(2)}, u32[]{:S(2)}) collective-permute-start(bf16[1,2048,128]{2,1,0:T(8,128)(2,1)S(1)} %bitcast.17), channel_id=1, source_target_pairs={{16,0},{4,20},{24,8},{12,28},{17,1},{5,21},{25,9},{13,29},{18,2},{... | collective-permute-start | bytes 1572872 | tf_op jit(solution)/shard_map/ppermute | solution.py:351
  28.6 13.4 %collective-permute-start.3 = (bf16[1,2048,128]{2,1,0:T(8,128)(2,1)S(1)}, bf16[1,2048,128]{2,1,0:T(8,128)(2,1)S(1)}, u32[]{:S(2)}, u32[]{:S(2)}) collective-permute-start(bf16[1,2048,128]{2,1,0:T(8,128)(2,1)S(1)} %select_select_fusion.2.r_4_), channel_id=1, source_target_pairs={{0,8},{4,12},{8,0},{12,4},{16,24},{20,28},{24,16},{28,20},{1,9},{5... | collective-permute-start | bytes 1572872 | tf_op jit(solution)/shard_map/ppermute | solution.py:351
  28.9 13.1 %collective-permute-start.6 = (bf16[1,2048,128]{2,1,0:T(8,128)(2,1)}, bf16[1,2048,128]{2,1,0:T(8,128)(2,1)}, u32[]{:S(2)}, u32[]{:S(2)}) collective-permute-start(bf16[1,2048,128]{2,1,0:T(8,128)(2,1)} %copy-done.21), channel_id=1, source_target_pairs={{2,1},{1,0},{6,5},{5,4},{10,9},{9,8},{14,13},{13,12},{18,17},{17,1... | collective-permute-start | bytes 1572872 | tf_op jit(solution)/shard_map/ppermute | solution.py:383
  31.8 14.6 %collective-permute-start.5 = (bf16[1,2048,128]{2,1,0:T(8,128)(2,1)S(1)}, bf16[1,2048,128]{2,1,0:T(8,128)(2,1)}, u32[]{:S(2)}, u32[]{:S(2)}) collective-permute-start(bf16[1,2048,128]{2,1,0:T(8,128)(2,1)S(1)} %collective-permute-done.2), channel_id=1, source_target_pairs={{1,2},{2,3},{5,6},{6,7},{9,10},{10,11},{13,14},{14,15},{17,18},{18... | collective-permute-start | bytes 1572872 | tf_op jit(solution)/shard_map/ppermute | solution.py:383
  33.7 19.9 %collective-permute-start.9 = (bf16[1,2048,128]{2,1,0:T(8,128)(2,1)S(1)}, bf16[1,2048,128]{2,1,0:T(8,128)(2,1)S(1)}, u32[]{:S(2)}, u32[]{:S(2)}) collective-permute-start(bf16[1,2048,128]{2,1,0:T(8,128)(2,1)S(1)} %collective-permute-done.1.r_7_), channel_id=1, source_target_pairs={{28,12},{0,16},{29,13},{1,17},{30,14},{2,18},{31,15},{3,19}} | collective-permute-start | bytes 1572872 | tf_op jit(solution)/shard_map/ppermute | solution.py:351
  34.7 17.7 %collective-permute-start.11 = (bf16[1,2048,128]{2,1,0:T(8,128)(2,1)}, bf16[1,2048,128]{2,1,0:T(8,128)(2,1)}, u32[]{:S(2)}, u32[]{:S(2)}) collective-permute-start(bf16[1,2048,128]{2,1,0:T(8,128)(2,1)} %collective-permute-done.4.r_11_), channel_id=1, source_target_pairs={{0,8},{28,20},{1,9},{29,21},{2,10},{30,22},{3,11},{31,23}} | collective-permute-start | bytes 1572872 | tf_op jit(solution)/shard_map/ppermute | solution.py:351
  46.4 12.3 %collective-permute-start.10 = (bf16[1,2048,128]{2,1,0:T(8,128)(2,1)}, bf16[1,2048,128]{2,1,0:T(8,128)(2,1)S(1)}, u32[]{:S(2)}, u32[]{:S(2)}) collective-permute-start(bf16[1,2048,128]{2,1,0:T(8,128)(2,1)} %collective-permute-done.5), channel_id=1, source_target_pairs={{2,3},{6,7},{10,11},{14,15},{18,19},{22,23},{26,27},{30,31}} | collective-permute-start | bytes 1572872 | tf_op jit(solution)/shard_map/ppermute | solution.py:383
  48.6 12.2 %collective-permute-start.12 = (bf16[1,2048,128]{2,1,0:T(8,128)(2,1)}, bf16[1,2048,128]{2,1,0:T(8,128)(2,1)S(1)}, u32[]{:S(2)}, u32[]{:S(2)}) collective-permute-start(bf16[1,2048,128]{2,1,0:T(8,128)(2,1)} %collective-permute-done.6), channel_id=1, source_target_pairs={{1,0},{5,4},{9,8},{13,12},{17,16},{21,20},{25,24},{29,28}} | collective-permute-start | bytes 1572872 | tf_op jit(solution)/shard_map/ppermute | solution.py:383
  50.6 13.9 %collective-permute-start.19 = (bf16[1,2048,128]{2,1,0:T(8,128)(2,1)S(1)}, bf16[1,2048,128]{2,1,0:T(8,128)(2,1)S(1)}, u32[]{:S(2)}, u32[]{:S(2)}) collective-permute-start(bf16[1,2048,128]{2,1,0:T(8,128)(2,1)S(1)} %select_select_fusion.r_5_), channel_id=1, source_target_pairs={{0,4},{4,0},{8,12},{12,8},{16,20},{20,16},{24,28},{28,24},{1,5},{5... | collective-permute-start | bytes 1572872 | tf_op jit(solution)/shard_map/ppermute | solution.py:351
  52.3 12.2 %collective-permute-start.16 = (bf16[1,2048,128]{2,1,0:T(8,128)(2,1)S(1)}, bf16[1,2048,128]{2,1,0:T(8,128)(2,1)S(1)}, u32[]{:S(2)}, u32[]{:S(2)}) collective-permute-start(bf16[1,2048,128]{2,1,0:T(8,128)(2,1)S(1)} %select_select_fusion.r_5_), channel_id=1, source_target_pairs={{16,0},{4,20},{24,8},{12,28},{17,1},{5,21},{25,9},{13,29},{18,2},{... | collective-permute-start | bytes 1572872 | tf_op jit(solution)/shard_map/ppermute | solution.py:351
  53.7 13.7 %collective-permute-start.15 = (bf16[1,2048,128]{2,1,0:T(8,128)(2,1)S(1)}, bf16[1,2048,128]{2,1,0:T(8,128)(2,1)}, u32[]{:S(2)}, u32[]{:S(2)}) collective-permute-start(bf16[1,2048,128]{2,1,0:T(8,128)(2,1)S(1)} %select_select_fusion.r_5_), channel_id=1, source_target_pairs={{0,8},{4,12},{8,0},{12,4},{16,24},{20,28},{24,16},{28,20},{1,9},{5... | collective-permute-start | bytes 1572872 | tf_op jit(solution)/shard_map/ppermute | solution.py:351
  58.7 19.8 %collective-permute-start.8 = (bf16[1,2048,128]{2,1,0:T(8,128)(2,1)S(1)}, bf16[1,2048,128]{2,1,0:T(8,128)(2,1)}, u32[]{:S(2)}, u32[]{:S(2)}) collective-permute-start(bf16[1,2048,128]{2,1,0:T(8,128)(2,1)S(1)} %collective-permute-done.3.r_8_), channel_id=1, source_target_pairs={{28,12},{0,16},{24,8},{4,20},{29,13},{1,17},{25,9},{5,21},{30,14},... | collective-permute-start | bytes 1572872 | tf_op jit(solution)/shard_map/ppermute | solution.py:351
  60.8 30.9 %collective-permute-start.17 = (bf16[4,2048,128]{2,1,0:T(8,128)(2,1)}, bf16[4,2048,128]{2,1,0:T(8,128)(2,1)}, u32[]{:S(2)}, u32[]{:S(2)}) collective-permute-start(bf16[4,2048,128]{2,1,0:T(8,128)(2,1)} %pad_maximum_fusion), channel_id=1, source_target_pairs={{0,4},{4,0},{8,12},{12,8},{16,20},{20,16},{24,28},{28,24},{1,5},{5... | collective-permute-start | bytes 6291464 | tf_op jit(solution)/shard_map/ppermute | solution.py:351
  64.5 14.1 %collective-permute-start.21 = (bf16[1,2048,128]{2,1,0:T(8,128)(2,1)S(1)}, bf16[1,2048,128]{2,1,0:T(8,128)(2,1)}, u32[]{:S(2)}, u32[]{:S(2)}) collective-permute-start(bf16[1,2048,128]{2,1,0:T(8,128)(2,1)S(1)} %select_select_fusion.1.r_6_), channel_id=1, source_target_pairs={{0,4},{4,0},{8,12},{12,8},{16,20},{20,16},{24,28},{28,24},{1,5},{5... | collective-permute-start | bytes 1572872 | tf_op jit(solution)/shard_map/ppermute | solution.py:351
  64.6 14.5 %collective-permute-start.14 = (bf16[1,2048,128]{2,1,0:T(8,128)(2,1)S(1)}, bf16[1,2048,128]{2,1,0:T(8,128)(2,1)}, u32[]{:S(2)}, u32[]{:S(2)}) collective-permute-start(bf16[1,2048,128]{2,1,0:T(8,128)(2,1)S(1)} %select_select_fusion.1.r_6_), channel_id=1, source_target_pairs={{0,8},{4,12},{8,0},{12,4},{16,24},{20,28},{24,16},{28,20},{1,9},{5... | collective-permute-start | bytes 1572872 | tf_op jit(solution)/shard_map/ppermute | solution.py:351
  67.4 12.0 %collective-permute-start.13 = (bf16[1,2048,128]{2,1,0:T(8,128)(2,1)S(1)}, bf16[1,2048,128]{2,1,0:T(8,128)(2,1)}, u32[]{:S(2)}, u32[]{:S(2)}) collective-permute-start(bf16[1,2048,128]{2,1,0:T(8,128)(2,1)S(1)} %select_select_fusion.1.r_6_), channel_id=1, source_target_pairs={{16,0},{4,20},{24,8},{12,28},{17,1},{5,21},{25,9},{13,29},{18,2},{... | collective-permute-start | bytes 1572872 | tf_op jit(solution)/shard_map/ppermute | solution.py:351
  84.4 21.5 %collective-permute-start.27 = (bf16[1,2048,128]{2,1,0:T(8,128)(2,1)}, bf16[1,2048,128]{2,1,0:T(8,128)(2,1)}, u32[]{:S(2)}, u32[]{:S(2)}) collective-permute-start(bf16[1,2048,128]{2,1,0:T(8,128)(2,1)} %collective-permute-done.15.r_9_), channel_id=1, source_target_pairs={{28,12},{0,16},{29,13},{1,17},{30,14},{2,18},{31,15},{3,19}} | collective-permute-start | bytes 1572872 | tf_op jit(solution)/shard_map/ppermute | solution.py:351
  85.9 20.0 %collective-permute-start.28 = (bf16[1,2048,128]{2,1,0:T(8,128)(2,1)}, bf16[1,2048,128]{2,1,0:T(8,128)(2,1)}, u32[]{:S(2)}, u32[]{:S(2)}) collective-permute-start(bf16[1,2048,128]{2,1,0:T(8,128)(2,1)} %copy-done.13), channel_id=1, source_target_pairs={{0,8},{28,20},{1,9},{29,21},{2,10},{30,22},{3,11},{31,23}} | collective-permute-start | bytes 1572872 | tf_op jit(solution)/shard_map/ppermute | solution.py:351
  87.4 18.6 %collective-permute-start.30 = (bf16[1,2048,128]{2,1,0:T(8,128)(2,1)}, bf16[1,2048,128]{2,1,0:T(8,128)(2,1)}, u32[]{:S(2)}, u32[]{:S(2)}) collective-permute-start(bf16[1,2048,128]{2,1,0:T(8,128)(2,1)} %collective-permute-done.14.r_10_), channel_id=1, source_target_pairs={{28,12},{0,16},{29,13},{1,17},{30,14},{2,18},{31,15},{3,19}} | collective-permute-start | bytes 1572872 | tf_op jit(solution)/shard_map/ppermute | solution.py:351
  88.9 17.0 %collective-permute-start.29 = (bf16[1,2048,128]{2,1,0:T(8,128)(2,1)}, bf16[1,2048,128]{2,1,0:T(8,128)(2,1)}, u32[]{:S(2)}, u32[]{:S(2)}) collective-permute-start(bf16[1,2048,128]{2,1,0:T(8,128)(2,1)} %collective-permute-done.13.r_14_), channel_id=1, source_target_pairs={{0,8},{28,20},{1,9},{29,21},{2,10},{30,22},{3,11},{31,23}} | collective-permute-start | bytes 1572872 | tf_op jit(solution)/shard_map/ppermute | solution.py:351
  91.7 16.0 %collective-permute-start.33 = (bf16[1,2048,128]{2,1,0:T(8,128)(2,1)}, bf16[1,2048,128]{2,1,0:T(8,128)(2,1)}, u32[]{:S(2)}, u32[]{:S(2)}) collective-permute-start(bf16[1,2048,128]{2,1,0:T(8,128)(2,1)} %collective-permute-done.8.r_17_), channel_id=1, source_target_pairs={{0,4},{4,0},{8,12},{12,8},{16,20},{20,16},{24,28},{28,24},{1,5},{5... | collective-permute-start | bytes 1572872 | tf_op jit(solution)/shard_map/ppermute | solution.py:351
  (44 other events, 475.6 us)

commit v9 on v8

--- a/solution.py
+++ b/solution.py
@@ -126,7 +126,7 @@
             pltpu.VMEM((2 * bins, length), jnp.bfloat16),
             pltpu.VMEM((bins // GROUP, GROUP * windows * 2, channels), jnp.float32),
         ],
-        compiler_params=pltpu.CompilerParams(vmem_limit_bytes=16 << 20),
+        compiler_params=pltpu.CompilerParams(vmem_limit_bytes=48 << 20),
         name="spectra",
     )(traces, cos[:, :fine], sin[:, :fine], cos[:, fine:], sin[:, fine:])
 
@@ -387,50 +387,50 @@
 
     s0 = make_slab(traces, band_bins)[None]
     q0 = slab_of(s0, 0)
-    up1 = along_z(s0, [(0, 1), (1, 2), (2, 3)])
     y0 = q0.hop(Y_PAIRS)
     x0 = q0.hop(X_PAIRS)
     down1 = along_z(s0, [(3, 2), (2, 1), (1, 0)])
-    down1, lag_rows, x0, up1 = together(down1, lag_rows, x0, up1)
+    up1 = along_z(s0, [(0, 1), (1, 2), (2, 3)])
+    up1, down1, x0, lag_rows = together(up1, down1, x0, lag_rows)
 
     q1 = slab_of(lax.select_n(z, down1, up1, down1, up1), 1)
+    up2 = along_z(up1, [(1, 2), (2, 3)])
     y1 = q1.hop(Y_PAIRS)
+    c0 = x0.hop(Y_ON)
     d0 = y0.hop(X_ON)
-    c0 = x0.hop(Y_ON)
+    down2 = along_z(down1, [(2, 1), (1, 0)])
     x1 = q1.hop(X_PAIRS)
-    down2 = along_z(down1, [(2, 1), (1, 0)])
-    up2 = along_z(up1, [(1, 2), (2, 3)])
     first = join(q0, x0, y0, q1)
-    x1, first, up2, y0, down2, y1 = together(x1, first, up2, y0, down2, y1)
+    first, down2, x1, y0, y1, up2 = together(first, down2, x1, y0, y1, up2)
 
     q2 = slab_of(lax.select_n(z, down2, down1, up1, up2), 2)
+    y2 = q2.hop(Y_PAIRS)
     down3 = along_z(down2, [(1, 0)])
-    y2 = q2.hop(Y_PAIRS)
     up3 = along_z(up2, [(2, 3)])
+    c1 = x1.hop(Y_ON_ALL)
     x2 = q2.hop(X_PAIRS)
-    c1 = x1.hop(Y_ON_ALL)
     second = join(x1, y1)
-    c0, up3, d0, up2, down2, second, down3 = together(c0, up3, d0, up2, down2, second, down3)
+    c0, d0, up3, down2, up2, down3, second = together(c0, d0, up3, down2, up2, down3, second)
 
     q3 = slab_of(lax.select_n(z, down3, down2, up2, up3), 3)
     b = [h.hop(CORE_PAIRS) for h in (first, second,)]
     y3 = q3.hop(Y_PAIRS)
     x3 = q3.hop(X_PAIRS)
     left = make_left([q.value[0] for q in (q0, q1, q2, q3)], z, channels // 4, bins)
-    left, x2, y2 = together(left, x2, y2)
+    x2, y2, left = together(x2, y2, left)
 
     d2 = y2.hop(X_ON)
     c2 = x2.hop(Y_ON)
-    b += [h.hop(CORE_PAIRS) for h in (q2, d0, q3, c0,)]
+    b += [h.hop(CORE_PAIRS) for h in (d0, q3, q2, c0,)]
 
 
     ids = np.arange(8, dtype=np.int32)
-    third = [y2.what, x2.what, x3.what, y3.what]
+    third = [x3.what, y2.what, y3.what, x2.what]
     held = [q0, q1, q2, q3, x0, x1, x2, x3, y0, y1, y2, y3, c0, d0, c1] + b
     whats = [h.what for h in held] + [moved(what, CORE_PAIRS) for what in third]
     c3, d3 = moved(x3.what, Y_ON), moved(y3.what, X_ON)
     whats += [c2.what, d2.what, c3, d3]
-    whats += [moved(what, CORE_PAIRS) for what in (c3, d2.what, c1.what, d3, c2.what)]
+    whats += [moved(what, CORE_PAIRS) for what in (c2.what, c1.what, c3, d3, d2.what)]
     table = np.zeros((8, 8, 4), np.int32)
     all_holds = [set() for _ in whats]
     index = sum(len(what) for what in whats)
@@ -449,16 +449,16 @@
     swapped = slots[jnp.asarray([1, 0, 2])]
     slots = jnp.where(me == 5, swapped, slots)
 
-    c1, y3, slots, x3 = together(c1, y3, slots, x3)
+    slots, y3, x3, c1 = together(slots, y3, x3, c1)
 
     c3, d3 = x3.hop(Y_ON), y3.hop(X_ON)
-    b += [h.hop(CORE_PAIRS) for h in (y2, x2, x3, y3)]
+    b += [h.hop(CORE_PAIRS) for h in (x3, y2, y3, x2)]
     norm = 1.0 / math.sqrt(4 * windows * bins)
     held = [q0, q1, q2, q3, x0, x1, x2, x3, y0, y1, y2, y3, c0, d0, c1] + b
     places = [(h.value, holds) for h, holds in zip(held, all_holds)]
     result = correlate(slots[:1], left, lag_rows, places, slot_count, norm)
-    c2, result, d2, d3, c3 = together(c2, result, d2, d3, c3)
-    late = [h.hop(CORE_PAIRS) for h in (c3, d2, c1, d3, c2)]
+    result, d3, d2, c3, c2 = together(result, d3, d2, c3, c2)
+    late = [h.hop(CORE_PAIRS) for h in (c2, c1, c3, d3, d2)]
     held += [c2, d2, c3, d3] + late
     places = [(h.value, holds) for h, holds in zip(held, all_holds)]
     return correlate(slots[1:], left, lag_rows, places, slot_count, norm, result)[None]

time: 122 us -> 121 us (level)
  no operation moved by 1% of the time
where the time goes in v9:
time: 121 us
  starting transfers between devices  50.2 us (41%)
  Pallas kernels  25.7 us (21%)
  waiting for transfers between devices  25.5 us (21%)
  other arithmetic  9.25 us (8%)
  local copies, waits for them, and re-layouts  9.2 us (8%)
    ppermute x30, starting transfers between devices, hop(): lax.ppermute(self.value, 'chan', pairs)  37.3 us
    pallas_call x2, Pallas kernels, correlate(): pl.pallas_call(lambda *r: pairs_kernel(*r, arrays=arrays, norm=norm, alia...  19.1 us
    ppermute x30, waiting for transfers between devices, hop(): lax.ppermute(self.value, 'chan', pairs)  13 us
    ppermute x6, starting transfers between devices, along_z(): return lax.ppermute(value, 'freq', pairs)  13 us
    ppermute x6, waiting for transfers between devices, along_z(): return lax.ppermute(value, 'freq', pairs)  12.5 us
    unnamed x64, local copies, waits for them, and re-layouts  6.58 us
    pallas_call x1, Pallas kernels, make_left(): pl.pallas_call(lambda *r: left_kernel(*r, per_step=per_step), grid_spec=p...  4.04 us
    concatenate x2, other arithmetic, join(): jnp.concatenate([p.value for p in parts], 0)  3.69 us
  transfers between devices with their start and end apart: 36, of which 15 were waited for; matrix products, arithmetic and copies ran while one was open for 8% of the time, Pallas kernels for 11%

profile of v9, /device:TPU:17, one launch (start us, length us, event | category | flops | bytes accessed | tf_op | source)
XLA Modules:
  0.0 120.6 jit_solution(14708897503557928448)
XLA Ops:
  3.5 2.6 %spectra.1 = bf16[2048,128]{1,0:T(8,128)(2,1)S(1)} custom-call(bf16[128,4,2048]{2,1,0:T(4,128)(2,1)S(1)} %copy-done.5, f32[256,128]{1,0:T(8,128)S(1)} %slice.26.fine_cos, f32[256,128]{1,0:T(8,128)S(1)} %slice.27.fine_sin, f32[256,16]{1,0:T(8,128)S(1)} %slice.28.step_cos, f32[256,16]{1,0:T(8,128)S(1)} %slice.29.step_sin), custom_call_target="tpu_custom_call" | custom-call | tf_op jit(solution)/shard_map/spectra/pallas_call | solution.py:122
  7.3 2.1 %collective-permute-start.1 = (bf16[1,2048,128]{2,1,0:T(8,128)(2,1)S(1)}, bf16[1,2048,128]{2,1,0:T(8,128)(2,1)S(1)}, u32[]{:S(2)}, u32[]{:S(2)}) collective-permute-start(bf16[1,2048,128]{2,1,0:T(8,128)(2,1)S(1)} %bitcast.15), channel_id=1, source_target_pairs={{3,2},{2,1},{1,0},{7,6},{6,5},{5,4},{11,10},{10,9},{9,8},{15,14},{... | collective-permute-start | bytes 1572872 | tf_op jit(solution)/shard_map/ppermute | solution.py:383
  9.4 3.2 %collective-permute-start = (bf16[1,2048,128]{2,1,0:T(8,128)(2,1)S(1)}, bf16[1,2048,128]{2,1,0:T(8,128)(2,1)S(1)}, u32[]{:S(2)}, u32[]{:S(2)}) collective-permute-start(bf16[1,2048,128]{2,1,0:T(8,128)(2,1)S(1)} %bitcast.16), channel_id=1, source_target_pairs={{0,1},{1,2},{2,3},{4,5},{5,6},{6,7},{8,9},{9,10},{10,11},{12,13},{... | collective-permute-start | bytes 1572872 | tf_op jit(solution)/shard_map/ppermute | solution.py:383
  12.6 4.0 %collective-permute-start.4 = (bf16[1,2048,128]{2,1,0:T(8,128)(2,1)S(1)}, bf16[1,2048,128]{2,1,0:T(8,128)(2,1)}, u32[]{:S(2)}, u32[]{:S(2)}) collective-permute-start(bf16[1,2048,128]{2,1,0:T(8,128)(2,1)S(1)} %bitcast.17), channel_id=1, source_target_pairs={{16,0},{4,20},{24,8},{12,28},{17,1},{5,21},{25,9},{13,29},{18,2},{... | collective-permute-start | bytes 1572872 | tf_op jit(solution)/shard_map/ppermute | solution.py:351
  18.9 2.9 %collective-permute-done.1 = bf16[1,2048,128]{2,1,0:T(8,128)(2,1)S(1)} collective-permute-done((bf16[1,2048,128]{2,1,0:T(8,128)(2,1)S(1)}, bf16[1,2048,128]{2,1,0:T(8,128)(2,1)S(1)}, u32[]{:S(2)}, u32[]{:S(2)}) %collective-permute-start.1) | collective-permute-done | bytes 524320 | tf_op jit(solution)/shard_map/ppermute | solution.py:383
  21.8 1.8 %collective-permute-done = bf16[1,2048,128]{2,1,0:T(8,128)(2,1)S(1)} collective-permute-done((bf16[1,2048,128]{2,1,0:T(8,128)(2,1)S(1)}, bf16[1,2048,128]{2,1,0:T(8,128)(2,1)S(1)}, u32[]{:S(2)}, u32[]{:S(2)}) %collective-permute-start) | collective-permute-done | bytes 524320 | tf_op jit(solution)/shard_map/ppermute | solution.py:383
  24.4 3.0 %collective-permute-start.8 = (bf16[1,2048,128]{2,1,0:T(8,128)(2,1)S(1)}, bf16[1,2048,128]{2,1,0:T(8,128)(2,1)S(1)}, u32[]{:S(2)}, u32[]{:S(2)}) collective-permute-start(bf16[1,2048,128]{2,1,0:T(8,128)(2,1)S(1)} %select_select_fusion.2.r_4_), channel_id=1, source_target_pairs={{16,0},{4,20},{24,8},{12,28},{17,1},{5,21},{25,9},{13,29},{18,2},{... | collective-permute-start | bytes 1572872 | tf_op jit(solution)/shard_map/ppermute | solution.py:351
  27.8 2.9 %collective-permute-start.6 = (bf16[1,2048,128]{2,1,0:T(8,128)(2,1)S(1)}, bf16[1,2048,128]{2,1,0:T(8,128)(2,1)}, u32[]{:S(2)}, u32[]{:S(2)}) collective-permute-start(bf16[1,2048,128]{2,1,0:T(8,128)(2,1)S(1)} %collective-permute-done.1), channel_id=1, source_target_pairs={{2,1},{1,0},{6,5},{5,4},{10,9},{9,8},{14,13},{13,12},{18,17},{17,1... | collective-permute-start | bytes 1572872 | tf_op jit(solution)/shard_map/ppermute | solution.py:383
  30.7 1.9 %collective-permute-start.9 = (bf16[1,2048,128]{2,1,0:T(8,128)(2,1)}, bf16[1,2048,128]{2,1,0:T(8,128)(2,1)}, u32[]{:S(2)}, u32[]{:S(2)}) collective-permute-start(bf16[1,2048,128]{2,1,0:T(8,128)(2,1)} %copy-done.21), channel_id=1, source_target_pairs={{1,2},{2,3},{5,6},{6,7},{9,10},{10,11},{13,14},{14,15},{17,18},{18... | collective-permute-start | bytes 1572872 | tf_op jit(solution)/shard_map/ppermute | solution.py:383
  35.0 2.6 %pad_maximum_fusion = bf16[4,2048,128]{2,1,0:T(8,128)(2,1)} fusion(bf16[1,2048,128]{2,1,0:T(8,128)(2,1)S(1)} %select_select_fusion.2.r_4_, bf16[1,2048,128]{2,1,0:T(8,128)(2,1)} %collective-permute-done.4.r_11_, bf16[1,2048,128]{2,1,0:T(8,128)(2,1)S(1)} %collective-permute-done.2.r_7_, bf16[1,2048,128]{2,1,0:T(8,128)(2,1)S(1)} %bitcast.18), kind=kLoop, calls=%fused_computation.1 | loop fusion | flops 3145728 | bytes 4194304 | tf_op jit(solution)/shard_map/concatenate | solution.py:355
  37.6 3.2 %collective-permute-done.7.r_8_ = bf16[1,2048,128]{2,1,0:T(8,128)(2,1)S(1)} collective-permute-done((bf16[1,2048,128]{2,1,0:T(8,128)(2,1)S(1)}, bf16[1,2048,128]{2,1,0:T(8,128)(2,1)S(1)}, u32[]{:S(2)}, u32[]{:S(2)}) %collective-permute-start.7) | collective-permute-done | bytes 524320 | tf_op jit(solution)/shard_map/ppermute | solution.py:351
  40.9 4.8 %collective-permute-done.9 = bf16[1,2048,128]{2,1,0:T(8,128)(2,1)} collective-permute-done((bf16[1,2048,128]{2,1,0:T(8,128)(2,1)}, bf16[1,2048,128]{2,1,0:T(8,128)(2,1)}, u32[]{:S(2)}, u32[]{:S(2)}) %collective-permute-start.9) | collective-permute-done | bytes 524320 | tf_op jit(solution)/shard_map/ppermute | solution.py:383
  45.7 2.2 %collective-permute-start.10 = (bf16[1,2048,128]{2,1,0:T(8,128)(2,1)}, bf16[1,2048,128]{2,1,0:T(8,128)(2,1)S(1)}, u32[]{:S(2)}, u32[]{:S(2)}) collective-permute-start(bf16[1,2048,128]{2,1,0:T(8,128)(2,1)} %collective-permute-done.9), channel_id=1, source_target_pairs={{2,3},{6,7},{10,11},{14,15},{18,19},{22,23},{26,27},{30,31}} | collective-permute-start | bytes 1572872 | tf_op jit(solution)/shard_map/ppermute | solution.py:383
  55.1 3.0 %collective-permute-done.10 = bf16[1,2048,128]{2,1,0:T(8,128)(2,1)S(1)} collective-permute-done((bf16[1,2048,128]{2,1,0:T(8,128)(2,1)}, bf16[1,2048,128]{2,1,0:T(8,128)(2,1)S(1)}, u32[]{:S(2)}, u32[]{:S(2)}) %collective-permute-start.10) | collective-permute-done | bytes 524320 | tf_op jit(solution)/shard_map/ppermute | solution.py:383
  58.1 2.1 %collective-permute-start.14 = (bf16[1,2048,128]{2,1,0:T(8,128)(2,1)S(1)}, bf16[1,2048,128]{2,1,0:T(8,128)(2,1)}, u32[]{:S(2)}, u32[]{:S(2)}) collective-permute-start(bf16[1,2048,128]{2,1,0:T(8,128)(2,1)S(1)} %collective-permute-done.7.r_8_), channel_id=1, source_target_pairs={{28,12},{0,16},{24,8},{4,20},{29,13},{1,17},{25,9},{5,21},{30,14},... | collective-permute-start | bytes 1572872 | tf_op jit(solution)/shard_map/ppermute | solution.py:351
  60.2 2.2 %collective-permute-start.17 = (bf16[4,2048,128]{2,1,0:T(8,128)(2,1)}, bf16[4,2048,128]{2,1,0:T(8,128)(2,1)}, u32[]{:S(2)}, u32[]{:S(2)}) collective-permute-start(bf16[4,2048,128]{2,1,0:T(8,128)(2,1)} %pad_maximum_fusion), channel_id=1, source_target_pairs={{0,4},{4,0},{8,12},{12,8},{16,20},{20,16},{24,28},{28,24},{1,5},{5... | collective-permute-start | bytes 6291464 | tf_op jit(solution)/shard_map/ppermute | solution.py:351
  64.2 2.4 %collective-permute-done.15.r_9_ = bf16[1,2048,128]{2,1,0:T(8,128)(2,1)} collective-permute-done((bf16[1,2048,128]{2,1,0:T(8,128)(2,1)S(1)}, bf16[1,2048,128]{2,1,0:T(8,128)(2,1)}, u32[]{:S(2)}, u32[]{:S(2)}) %collective-permute-start.15) | collective-permute-done | bytes 524320 | tf_op jit(solution)/shard_map/ppermute | solution.py:351
  66.5 3.4 %collective-permute-start.12 = (bf16[1,2048,128]{2,1,0:T(8,128)(2,1)S(1)}, bf16[1,2048,128]{2,1,0:T(8,128)(2,1)}, u32[]{:S(2)}, u32[]{:S(2)}) collective-permute-start(bf16[1,2048,128]{2,1,0:T(8,128)(2,1)S(1)} %select_select_fusion.1.r_6_), channel_id=1, source_target_pairs={{16,0},{4,20},{24,8},{12,28},{17,1},{5,21},{25,9},{13,29},{18,2},{... | collective-permute-start | bytes 1572872 | tf_op jit(solution)/shard_map/ppermute | solution.py:351
  70.2 4.0 %left.1.r_1_ = bf16[32,512,256]{2,1,0:T(8,128)(2,1)S(1)} custom-call(s32[1]{0:T(128)} %bitcast.4.r_0_, bf16[2048,128]{1,0:T(8,128)(2,1)S(1)} %spectra.1, bf16[2048,128]{1,0:T(8,128)(2,1)S(1)} %bitcast.13, bf16[2048,128]{1,0:T(8,128)(2,1)S(1)} %bitcast.21, bf16[2048,128]{1,0:T(8,128)(2,1)S(1)} %bitcast.22), custom_call_target="tpu_custom_call" | custom-call | tf_op jit(solution)/shard_map/left/pallas_call | solution.py:173
  74.2 3.3 %copy-done = bf16[32,512,256]{2,1,0:T(8,128)(2,1)} copy-done((bf16[32,512,256]{2,1,0:T(8,128)(2,1)}, bf16[32,512,256]{2,1,0:T(8,128)(2,1)S(1)}, u32[]{:S(2)}) %copy-start) | copy-done | bytes 8388632
  80.6 2.1 %collective-permute-done.26.r_27_ = bf16[1,2048,128]{2,1,0:T(8,128)(2,1)S(1)} collective-permute-done((bf16[1,2048,128]{2,1,0:T(8,128)(2,1)}, bf16[1,2048,128]{2,1,0:T(8,128)(2,1)S(1)}, u32[]{:S(2)}, u32[]{:S(2)}) %collective-permute-start.26) | collective-permute-done | bytes 524320 | tf_op jit(solution)/shard_map/ppermute | solution.py:351
  90.7 5.3 %collective-permute-start.32 = (bf16[1,2048,128]{2,1,0:T(8,128)(2,1)}, bf16[1,2048,128]{2,1,0:T(8,128)(2,1)}, u32[]{:S(2)}, u32[]{:S(2)}) collective-permute-start(bf16[1,2048,128]{2,1,0:T(8,128)(2,1)} %collective-permute-done.14.r_17_), channel_id=1, source_target_pairs={{0,4},{4,0},{8,12},{12,8},{16,20},{20,16},{24,28},{28,24},{1,5},{5... | collective-permute-start | bytes 1572872 | tf_op jit(solution)/shard_map/ppermute | solution.py:351
  96.0 8.9 %pairs.2.r_37_ = f32[32,3,128,128]{3,2,1,0:T(8,128)} custom-call(s32[5]{0:T(128)} %slice_bitcast_fusion.r_0_, bf16[32,512,256]{2,1,0:T(8,128)(2,1)} %copy-done, bf16[128,512]{1,0:T(8,128)(2,1)} %copy.15.r_2_, bf16[1,2048,128]{2,1,0:T(8,128)(2,1)} %bitcast.19, bf16[1,2048,128]{2,1,0:T(8,128)(2,1)} %copy-done.1, bf16[1,2048,128]{2,1,0:T(8,128)(2,1)} %copy-done.3, ...), custom_call_target="tpu_custom_call" | custom-call | flops 1610612736 | bytes 12582912 | tf_op jit(solution)/shard_map/pairs/pallas_call | solution.py:306
  110.2 10.2 %pairs.3 = f32[32,3,128,128]{3,2,1,0:T(8,128)} custom-call(s32[10]{0:T(128)} %reshape.186.r_0_, bf16[32,512,256]{2,1,0:T(8,128)(2,1)} %copy-done, bf16[128,512]{1,0:T(8,128)(2,1)} %copy.15.r_2_, bf16[1,2048,128]{2,1,0:T(8,128)(2,1)} %bitcast.20, bf16[1,2048,128]{2,1,0:T(8,128)(2,1)} %copy-done.1, ...), custom_call_target="tpu_custom_call", output_to_operand_aliasing={{}: (37, {})} | custom-call | flops 3221225472 | bytes 12582912 | tf_op jit(solution)/shard_map/pairs/pallas_call | solution.py:306
  (146 shorter events, 35.7 us)
Async XLA Ops:
  6.1 12.9 %collective-permute-start.2 = (bf16[1,2048,128]{2,1,0:T(8,128)(2,1)S(1)}, bf16[1,2048,128]{2,1,0:T(8,128)(2,1)S(1)}, u32[]{:S(2)}, u32[]{:S(2)}) collective-permute-start(bf16[1,2048,128]{2,1,0:T(8,128)(2,1)S(1)} %bitcast.14), channel_id=1, source_target_pairs={{0,8},{4,12},{8,0},{12,4},{16,24},{20,28},{24,16},{28,20},{1,9},{5... | collective-permute-start | bytes 1572872 | tf_op jit(solution)/shard_map/ppermute | solution.py:351
  7.3 14.5 %collective-permute-start.1 = (bf16[1,2048,128]{2,1,0:T(8,128)(2,1)S(1)}, bf16[1,2048,128]{2,1,0:T(8,128)(2,1)S(1)}, u32[]{:S(2)}, u32[]{:S(2)}) collective-permute-start(bf16[1,2048,128]{2,1,0:T(8,128)(2,1)S(1)} %bitcast.15), channel_id=1, source_target_pairs={{3,2},{2,1},{1,0},{7,6},{6,5},{5,4},{11,10},{10,9},{9,8},{15,14},{... | collective-permute-start | bytes 1572872 | tf_op jit(solution)/shard_map/ppermute | solution.py:383
  9.4 14.2 %collective-permute-start = (bf16[1,2048,128]{2,1,0:T(8,128)(2,1)S(1)}, bf16[1,2048,128]{2,1,0:T(8,128)(2,1)S(1)}, u32[]{:S(2)}, u32[]{:S(2)}) collective-permute-start(bf16[1,2048,128]{2,1,0:T(8,128)(2,1)S(1)} %bitcast.16), channel_id=1, source_target_pairs={{0,1},{1,2},{2,3},{4,5},{5,6},{6,7},{8,9},{9,10},{10,11},{12,13},{... | collective-permute-start | bytes 1572872 | tf_op jit(solution)/shard_map/ppermute | solution.py:383
  12.6 20.0 %collective-permute-start.4 = (bf16[1,2048,128]{2,1,0:T(8,128)(2,1)S(1)}, bf16[1,2048,128]{2,1,0:T(8,128)(2,1)}, u32[]{:S(2)}, u32[]{:S(2)}) collective-permute-start(bf16[1,2048,128]{2,1,0:T(8,128)(2,1)S(1)} %bitcast.17), channel_id=1, source_target_pairs={{16,0},{4,20},{24,8},{12,28},{17,1},{5,21},{25,9},{13,29},{18,2},{... | collective-permute-start | bytes 1572872 | tf_op jit(solution)/shard_map/ppermute | solution.py:351
  27.5 13.4 %collective-permute-start.7 = (bf16[1,2048,128]{2,1,0:T(8,128)(2,1)S(1)}, bf16[1,2048,128]{2,1,0:T(8,128)(2,1)S(1)}, u32[]{:S(2)}, u32[]{:S(2)}) collective-permute-start(bf16[1,2048,128]{2,1,0:T(8,128)(2,1)S(1)} %select_select_fusion.2.r_4_), channel_id=1, source_target_pairs={{0,8},{4,12},{8,0},{12,4},{16,24},{20,28},{24,16},{28,20},{1,9},{5... | collective-permute-start | bytes 1572872 | tf_op jit(solution)/shard_map/ppermute | solution.py:351
  27.8 13.1 %collective-permute-start.6 = (bf16[1,2048,128]{2,1,0:T(8,128)(2,1)S(1)}, bf16[1,2048,128]{2,1,0:T(8,128)(2,1)}, u32[]{:S(2)}, u32[]{:S(2)}) collective-permute-start(bf16[1,2048,128]{2,1,0:T(8,128)(2,1)S(1)} %collective-permute-done.1), channel_id=1, source_target_pairs={{2,1},{1,0},{6,5},{5,4},{10,9},{9,8},{14,13},{13,12},{18,17},{17,1... | collective-permute-start | bytes 1572872 | tf_op jit(solution)/shard_map/ppermute | solution.py:383
  30.7 15.0 %collective-permute-start.9 = (bf16[1,2048,128]{2,1,0:T(8,128)(2,1)}, bf16[1,2048,128]{2,1,0:T(8,128)(2,1)}, u32[]{:S(2)}, u32[]{:S(2)}) collective-permute-start(bf16[1,2048,128]{2,1,0:T(8,128)(2,1)} %copy-done.21), channel_id=1, source_target_pairs={{1,2},{2,3},{5,6},{6,7},{9,10},{10,11},{13,14},{14,15},{17,18},{18... | collective-permute-start | bytes 1572872 | tf_op jit(solution)/shard_map/ppermute | solution.py:383
  32.6 20.1 %collective-permute-start.3 = (bf16[1,2048,128]{2,1,0:T(8,128)(2,1)S(1)}, bf16[1,2048,128]{2,1,0:T(8,128)(2,1)S(1)}, u32[]{:S(2)}, u32[]{:S(2)}) collective-permute-start(bf16[1,2048,128]{2,1,0:T(8,128)(2,1)S(1)} %collective-permute-done.2.r_7_), channel_id=1, source_target_pairs={{28,12},{0,16},{29,13},{1,17},{30,14},{2,18},{31,15},{3,19}} | collective-permute-start | bytes 1572872 | tf_op jit(solution)/shard_map/ppermute | solution.py:351
  33.5 17.9 %collective-permute-start.5 = (bf16[1,2048,128]{2,1,0:T(8,128)(2,1)}, bf16[1,2048,128]{2,1,0:T(8,128)(2,1)}, u32[]{:S(2)}, u32[]{:S(2)}) collective-permute-start(bf16[1,2048,128]{2,1,0:T(8,128)(2,1)} %collective-permute-done.4.r_11_), channel_id=1, source_target_pairs={{0,8},{28,20},{1,9},{29,21},{2,10},{30,22},{3,11},{31,23}} | collective-permute-start | bytes 1572872 | tf_op jit(solution)/shard_map/ppermute | solution.py:351
  45.7 12.4 %collective-permute-start.10 = (bf16[1,2048,128]{2,1,0:T(8,128)(2,1)}, bf16[1,2048,128]{2,1,0:T(8,128)(2,1)S(1)}, u32[]{:S(2)}, u32[]{:S(2)}) collective-permute-start(bf16[1,2048,128]{2,1,0:T(8,128)(2,1)} %collective-permute-done.9), channel_id=1, source_target_pairs={{2,3},{6,7},{10,11},{14,15},{18,19},{22,23},{26,27},{30,31}} | collective-permute-start | bytes 1572872 | tf_op jit(solution)/shard_map/ppermute | solution.py:383
  47.9 12.3 %collective-permute-start.11 = (bf16[1,2048,128]{2,1,0:T(8,128)(2,1)}, bf16[1,2048,128]{2,1,0:T(8,128)(2,1)S(1)}, u32[]{:S(2)}, u32[]{:S(2)}) collective-permute-start(bf16[1,2048,128]{2,1,0:T(8,128)(2,1)} %collective-permute-done.6), channel_id=1, source_target_pairs={{1,0},{5,4},{9,8},{13,12},{17,16},{21,20},{25,24},{29,28}} | collective-permute-start | bytes 1572872 | tf_op jit(solution)/shard_map/ppermute | solution.py:383
  49.8 13.9 %collective-permute-start.21 = (bf16[1,2048,128]{2,1,0:T(8,128)(2,1)S(1)}, bf16[1,2048,128]{2,1,0:T(8,128)(2,1)S(1)}, u32[]{:S(2)}, u32[]{:S(2)}) collective-permute-start(bf16[1,2048,128]{2,1,0:T(8,128)(2,1)S(1)} %select_select_fusion.r_5_), channel_id=1, source_target_pairs={{0,4},{4,0},{8,12},{12,8},{16,20},{20,16},{24,28},{28,24},{1,5},{5... | collective-permute-start | bytes 1572872 | tf_op jit(solution)/shard_map/ppermute | solution.py:351
  51.5 12.4 %collective-permute-start.16 = (bf16[1,2048,128]{2,1,0:T(8,128)(2,1)S(1)}, bf16[1,2048,128]{2,1,0:T(8,128)(2,1)S(1)}, u32[]{:S(2)}, u32[]{:S(2)}) collective-permute-start(bf16[1,2048,128]{2,1,0:T(8,128)(2,1)S(1)} %select_select_fusion.r_5_), channel_id=1, source_target_pairs={{16,0},{4,20},{24,8},{12,28},{17,1},{5,21},{25,9},{13,29},{18,2},{... | collective-permute-start | bytes 1572872 | tf_op jit(solution)/shard_map/ppermute | solution.py:351
  52.8 13.7 %collective-permute-start.15 = (bf16[1,2048,128]{2,1,0:T(8,128)(2,1)S(1)}, bf16[1,2048,128]{2,1,0:T(8,128)(2,1)}, u32[]{:S(2)}, u32[]{:S(2)}) collective-permute-start(bf16[1,2048,128]{2,1,0:T(8,128)(2,1)S(1)} %select_select_fusion.r_5_), channel_id=1, source_target_pairs={{0,8},{4,12},{8,0},{12,4},{16,24},{20,28},{24,16},{28,20},{1,9},{5... | collective-permute-start | bytes 1572872 | tf_op jit(solution)/shard_map/ppermute | solution.py:351
  58.1 19.4 %collective-permute-start.14 = (bf16[1,2048,128]{2,1,0:T(8,128)(2,1)S(1)}, bf16[1,2048,128]{2,1,0:T(8,128)(2,1)}, u32[]{:S(2)}, u32[]{:S(2)}) collective-permute-start(bf16[1,2048,128]{2,1,0:T(8,128)(2,1)S(1)} %collective-permute-done.7.r_8_), channel_id=1, source_target_pairs={{28,12},{0,16},{24,8},{4,20},{29,13},{1,17},{25,9},{5,21},{30,14},... | collective-permute-start | bytes 1572872 | tf_op jit(solution)/shard_map/ppermute | solution.py:351
  60.2 30.5 %collective-permute-start.17 = (bf16[4,2048,128]{2,1,0:T(8,128)(2,1)}, bf16[4,2048,128]{2,1,0:T(8,128)(2,1)}, u32[]{:S(2)}, u32[]{:S(2)}) collective-permute-start(bf16[4,2048,128]{2,1,0:T(8,128)(2,1)} %pad_maximum_fusion), channel_id=1, source_target_pairs={{0,4},{4,0},{8,12},{12,8},{16,20},{20,16},{24,28},{28,24},{1,5},{5... | collective-permute-start | bytes 6291464 | tf_op jit(solution)/shard_map/ppermute | solution.py:351
  63.7 13.8 %collective-permute-start.20 = (bf16[1,2048,128]{2,1,0:T(8,128)(2,1)S(1)}, bf16[1,2048,128]{2,1,0:T(8,128)(2,1)}, u32[]{:S(2)}, u32[]{:S(2)}) collective-permute-start(bf16[1,2048,128]{2,1,0:T(8,128)(2,1)S(1)} %select_select_fusion.1.r_6_), channel_id=1, source_target_pairs={{0,4},{4,0},{8,12},{12,8},{16,20},{20,16},{24,28},{28,24},{1,5},{5... | collective-permute-start | bytes 1572872 | tf_op jit(solution)/shard_map/ppermute | solution.py:351
  63.8 14.2 %collective-permute-start.13 = (bf16[1,2048,128]{2,1,0:T(8,128)(2,1)S(1)}, bf16[1,2048,128]{2,1,0:T(8,128)(2,1)}, u32[]{:S(2)}, u32[]{:S(2)}) collective-permute-start(bf16[1,2048,128]{2,1,0:T(8,128)(2,1)S(1)} %select_select_fusion.1.r_6_), channel_id=1, source_target_pairs={{0,8},{4,12},{8,0},{12,4},{16,24},{20,28},{24,16},{28,20},{1,9},{5... | collective-permute-start | bytes 1572872 | tf_op jit(solution)/shard_map/ppermute | solution.py:351
  66.5 12.0 %collective-permute-start.12 = (bf16[1,2048,128]{2,1,0:T(8,128)(2,1)S(1)}, bf16[1,2048,128]{2,1,0:T(8,128)(2,1)}, u32[]{:S(2)}, u32[]{:S(2)}) collective-permute-start(bf16[1,2048,128]{2,1,0:T(8,128)(2,1)S(1)} %select_select_fusion.1.r_6_), channel_id=1, source_target_pairs={{16,0},{4,20},{24,8},{12,28},{17,1},{5,21},{25,9},{13,29},{18,2},{... | collective-permute-start | bytes 1572872 | tf_op jit(solution)/shard_map/ppermute | solution.py:351
  83.4 21.5 %collective-permute-start.30 = (bf16[1,2048,128]{2,1,0:T(8,128)(2,1)}, bf16[1,2048,128]{2,1,0:T(8,128)(2,1)}, u32[]{:S(2)}, u32[]{:S(2)}) collective-permute-start(bf16[1,2048,128]{2,1,0:T(8,128)(2,1)} %collective-permute-done.15.r_9_), channel_id=1, source_target_pairs={{28,12},{0,16},{29,13},{1,17},{30,14},{2,18},{31,15},{3,19}} | collective-permute-start | bytes 1572872 | tf_op jit(solution)/shard_map/ppermute | solution.py:351
  84.9 20.0 %collective-permute-start.28 = (bf16[1,2048,128]{2,1,0:T(8,128)(2,1)}, bf16[1,2048,128]{2,1,0:T(8,128)(2,1)}, u32[]{:S(2)}, u32[]{:S(2)}) collective-permute-start(bf16[1,2048,128]{2,1,0:T(8,128)(2,1)} %copy-done.13), channel_id=1, source_target_pairs={{0,8},{28,20},{1,9},{29,21},{2,10},{30,22},{3,11},{31,23}} | collective-permute-start | bytes 1572872 | tf_op jit(solution)/shard_map/ppermute | solution.py:351
  86.4 18.5 %collective-permute-start.29 = (bf16[1,2048,128]{2,1,0:T(8,128)(2,1)}, bf16[1,2048,128]{2,1,0:T(8,128)(2,1)}, u32[]{:S(2)}, u32[]{:S(2)}) collective-permute-start(bf16[1,2048,128]{2,1,0:T(8,128)(2,1)} %collective-permute-done.13.r_10_), channel_id=1, source_target_pairs={{28,12},{0,16},{29,13},{1,17},{30,14},{2,18},{31,15},{3,19}} | collective-permute-start | bytes 1572872 | tf_op jit(solution)/shard_map/ppermute | solution.py:351
  87.9 17.0 %collective-permute-start.27 = (bf16[1,2048,128]{2,1,0:T(8,128)(2,1)}, bf16[1,2048,128]{2,1,0:T(8,128)(2,1)}, u32[]{:S(2)}, u32[]{:S(2)}) collective-permute-start(bf16[1,2048,128]{2,1,0:T(8,128)(2,1)} %collective-permute-done.12.r_14_), channel_id=1, source_target_pairs={{0,8},{28,20},{1,9},{29,21},{2,10},{30,22},{3,11},{31,23}} | collective-permute-start | bytes 1572872 | tf_op jit(solution)/shard_map/ppermute | solution.py:351
  90.7 16.0 %collective-permute-start.32 = (bf16[1,2048,128]{2,1,0:T(8,128)(2,1)}, bf16[1,2048,128]{2,1,0:T(8,128)(2,1)}, u32[]{:S(2)}, u32[]{:S(2)}) collective-permute-start(bf16[1,2048,128]{2,1,0:T(8,128)(2,1)} %collective-permute-done.14.r_17_), channel_id=1, source_target_pairs={{0,4},{4,0},{8,12},{12,8},{16,20},{20,16},{24,28},{28,24},{1,5},{5... | collective-permute-start | bytes 1572872 | tf_op jit(solution)/shard_map/ppermute | solution.py:351
  (44 other events, 472.4 us)

commit v10 on v9

--- a/solution.py
+++ b/solution.py
@@ -81,16 +81,24 @@
     return result[None]
 
 
-def spectra_kernel(traces_ref, fine_cos, fine_sin, step_cos, step_sin, out_ref, table, planes):
-    bins, fine = fine_cos.shape
+def spectra_kernel(traces_ref, bins_ref, out_ref, table, planes):
+    bins, fine = bins_ref.shape[0], 128
     groups, _, channels = planes.shape
     windows, length = traces_ref.shape[1:]
     series = windows * channels
-    for h in range(step_cos.shape[1]):
+
+    def angles(step):
+        sample = lax.broadcasted_iota(jnp.int32, (bins, fine), 1) * step
+        phase = lax.rem(bins_ref[...] * sample, length).astype(jnp.float32) * (2.0 * math.pi / length)
+        return jnp.cos(phase), jnp.sin(phase)
+
+    fine_cos, fine_sin = angles(1)
+    step_cos, step_sin = angles(fine)
+    for h in range(length // fine):
         sc, ss = step_cos[:, h : h + 1], step_sin[:, h : h + 1]
         cols = slice(h * fine, (h + 1) * fine)
-        table[:bins, cols] = (sc * fine_cos[...] - ss * fine_sin[...]).astype(jnp.bfloat16)
-        table[bins:, cols] = (-(ss * fine_cos[...] + sc * fine_sin[...])).astype(jnp.bfloat16)
+        table[:bins, cols] = (sc * fine_cos - ss * fine_sin).astype(jnp.bfloat16)
+        table[bins:, cols] = (-(ss * fine_cos + sc * fine_sin)).astype(jnp.bfloat16)
     was = lax.broadcasted_iota(jnp.int32, (series, series), 0)
     now = lax.broadcasted_iota(jnp.int32, (series, series), 1)
     turned = jnp.where(was == now % channels * windows + now // channels, 1.0, 0.0)
@@ -114,11 +122,6 @@
 def make_slab(traces, band_bins):
     channels, windows, length = traces.shape
     bins = band_bins.shape[0]
-    fine = 128
-    sample_idx = jnp.concatenate([jnp.arange(fine), jnp.arange(length // fine) * fine])
-    phase_int = band_bins[:, None] * sample_idx[None, :].astype(jnp.int32) % length
-    phases = phase_int.astype(jnp.float32) * (2.0 * math.pi / length)
-    cos, sin = jnp.cos(phases), jnp.sin(phases)
     return pl.pallas_call(
         spectra_kernel,
         out_shape=jax.ShapeDtypeStruct((bins * windows * 2, channels), jnp.bfloat16),
@@ -128,7 +131,7 @@
         ],
         compiler_params=pltpu.CompilerParams(vmem_limit_bytes=48 << 20),
         name="spectra",
-    )(traces, cos[:, :fine], sin[:, :fine], cos[:, fine:], sin[:, fine:])
+    )(traces, band_bins[:, None])
 
 
 def left_kernel(z, *refs, per_step):
@@ -421,11 +424,11 @@
 
     d2 = y2.hop(X_ON)
     c2 = x2.hop(Y_ON)
-    b += [h.hop(CORE_PAIRS) for h in (d0, q3, q2, c0,)]
+    b += [h.hop(CORE_PAIRS) for h in (d0, q3, q2, c0, x2, y2)]
 
 
     ids = np.arange(8, dtype=np.int32)
-    third = [x3.what, y2.what, y3.what, x2.what]
+    third = [x3.what, y3.what]
     held = [q0, q1, q2, q3, x0, x1, x2, x3, y0, y1, y2, y3, c0, d0, c1] + b
     whats = [h.what for h in held] + [moved(what, CORE_PAIRS) for what in third]
     c3, d3 = moved(x3.what, Y_ON), moved(y3.what, X_ON)
@@ -452,7 +455,7 @@
     slots, y3, x3, c1 = together(slots, y3, x3, c1)
 
     c3, d3 = x3.hop(Y_ON), y3.hop(X_ON)
-    b += [h.hop(CORE_PAIRS) for h in (x3, y2, y3, x2)]
+    b += [h.hop(CORE_PAIRS) for h in (x3, y3)]
     norm = 1.0 / math.sqrt(4 * windows * bins)
     held = [q0, q1, q2, q3, x0, x1, x2, x3, y0, y1, y2, y3, c0, d0, c1] + b
     places = [(h.value, holds) for h, holds in zip(held, all_holds)]

time: 121 us -> 121 us (level)
  other arithmetic: 9.25 us -> 7.46 us
    sin x1 -> x0, other arithmetic: 1.77 us -> none  [make_slab(): cos, sin = (jnp.cos(phases), jnp.sin(phases))]
where the time goes in v10:
time: 121 us
  starting transfers between devices  50.6 us (42%)
  Pallas kernels  26.6 us (22%)
  waiting for transfers between devices  25.3 us (21%)
  local copies, waits for them, and re-layouts  10.1 us (8%)
  other arithmetic  7.46 us (6%)
    ppermute x30, starting transfers between devices, hop(): lax.ppermute(self.value, 'chan', pairs)  37.6 us
    pallas_call x2, Pallas kernels, correlate(): pl.pallas_call(lambda *r: pairs_kernel(*r, arrays=arrays, norm=norm, alia...  19.1 us
    ppermute x30, waiting for transfers between devices, hop(): lax.ppermute(self.value, 'chan', pairs)  13.1 us
    ppermute x6, starting transfers between devices, along_z(): return lax.ppermute(value, 'freq', pairs)  13 us
    ppermute x6, waiting for transfers between devices, along_z(): return lax.ppermute(value, 'freq', pairs)  12.2 us
    unnamed x64, local copies, waits for them, and re-layouts  6.58 us
    pallas_call x1, Pallas kernels, make_left(): pl.pallas_call(lambda *r: left_kernel(*r, per_step=per_step), grid_spec=p...  4.04 us
    concatenate x2, other arithmetic, join(): jnp.concatenate([p.value for p in parts], 0)  3.68 us
  transfers between devices with their start and end apart: 36, of which 15 were waited for; matrix products, arithmetic and copies ran while one was open for 8% of the time, Pallas kernels for 11%

profile of v10, /device:TPU:17, one launch (start us, length us, event | category | flops | bytes accessed | tf_op | source)
XLA Modules:
  0.0 120.6 jit_solution(7408599886452082353)
XLA Ops:
  2.5 3.5 %spectra.1 = bf16[2048,128]{1,0:T(8,128)(2,1)S(1)} custom-call(bf16[128,4,2048]{2,1,0:T(4,128)(2,1)S(1)} %copy-done.5, s32[256,1]{1,0:T(8,128)S(1)} %copy.15.bins_ref), custom_call_target="tpu_custom_call" | custom-call | tf_op jit(solution)/shard_map/spectra/pallas_call | solution.py:125
  7.2 2.1 %collective-permute-start.1 = (bf16[1,2048,128]{2,1,0:T(8,128)(2,1)S(1)}, bf16[1,2048,128]{2,1,0:T(8,128)(2,1)S(1)}, u32[]{:S(2)}, u32[]{:S(2)}) collective-permute-start(bf16[1,2048,128]{2,1,0:T(8,128)(2,1)S(1)} %bitcast.16), channel_id=1, source_target_pairs={{3,2},{2,1},{1,0},{7,6},{6,5},{5,4},{11,10},{10,9},{9,8},{15,14},{... | collective-permute-start | bytes 1572872 | tf_op jit(solution)/shard_map/ppermute | solution.py:386
  9.3 3.2 %collective-permute-start = (bf16[1,2048,128]{2,1,0:T(8,128)(2,1)S(1)}, bf16[1,2048,128]{2,1,0:T(8,128)(2,1)S(1)}, u32[]{:S(2)}, u32[]{:S(2)}) collective-permute-start(bf16[1,2048,128]{2,1,0:T(8,128)(2,1)S(1)} %bitcast.17), channel_id=1, source_target_pairs={{0,1},{1,2},{2,3},{4,5},{5,6},{6,7},{8,9},{9,10},{10,11},{12,13},{... | collective-permute-start | bytes 1572872 | tf_op jit(solution)/shard_map/ppermute | solution.py:386
  12.5 4.0 %collective-permute-start.4 = (bf16[1,2048,128]{2,1,0:T(8,128)(2,1)S(1)}, bf16[1,2048,128]{2,1,0:T(8,128)(2,1)}, u32[]{:S(2)}, u32[]{:S(2)}) collective-permute-start(bf16[1,2048,128]{2,1,0:T(8,128)(2,1)S(1)} %bitcast.18), channel_id=1, source_target_pairs={{16,0},{4,20},{24,8},{12,28},{17,1},{5,21},{25,9},{13,29},{18,2},{... | collective-permute-start | bytes 1572872 | tf_op jit(solution)/shard_map/ppermute | solution.py:354
  18.8 2.9 %collective-permute-done.1 = bf16[1,2048,128]{2,1,0:T(8,128)(2,1)S(1)} collective-permute-done((bf16[1,2048,128]{2,1,0:T(8,128)(2,1)S(1)}, bf16[1,2048,128]{2,1,0:T(8,128)(2,1)S(1)}, u32[]{:S(2)}, u32[]{:S(2)}) %collective-permute-start.1) | collective-permute-done | bytes 524320 | tf_op jit(solution)/shard_map/ppermute | solution.py:386
  21.7 1.8 %collective-permute-done = bf16[1,2048,128]{2,1,0:T(8,128)(2,1)S(1)} collective-permute-done((bf16[1,2048,128]{2,1,0:T(8,128)(2,1)S(1)}, bf16[1,2048,128]{2,1,0:T(8,128)(2,1)S(1)}, u32[]{:S(2)}, u32[]{:S(2)}) %collective-permute-start) | collective-permute-done | bytes 524320 | tf_op jit(solution)/shard_map/ppermute | solution.py:386
  24.3 3.1 %collective-permute-start.8 = (bf16[1,2048,128]{2,1,0:T(8,128)(2,1)S(1)}, bf16[1,2048,128]{2,1,0:T(8,128)(2,1)S(1)}, u32[]{:S(2)}, u32[]{:S(2)}) collective-permute-start(bf16[1,2048,128]{2,1,0:T(8,128)(2,1)S(1)} %select_select_fusion.2.r_4_), channel_id=1, source_target_pairs={{16,0},{4,20},{24,8},{12,28},{17,1},{5,21},{25,9},{13,29},{18,2},{... | collective-permute-start | bytes 1572872 | tf_op jit(solution)/shard_map/ppermute | solution.py:354
  27.7 2.9 %collective-permute-start.6 = (bf16[1,2048,128]{2,1,0:T(8,128)(2,1)S(1)}, bf16[1,2048,128]{2,1,0:T(8,128)(2,1)}, u32[]{:S(2)}, u32[]{:S(2)}) collective-permute-start(bf16[1,2048,128]{2,1,0:T(8,128)(2,1)S(1)} %collective-permute-done.1), channel_id=1, source_target_pairs={{2,1},{1,0},{6,5},{5,4},{10,9},{9,8},{14,13},{13,12},{18,17},{17,1... | collective-permute-start | bytes 1572872 | tf_op jit(solution)/shard_map/ppermute | solution.py:386
  30.5 1.9 %collective-permute-start.9 = (bf16[1,2048,128]{2,1,0:T(8,128)(2,1)}, bf16[1,2048,128]{2,1,0:T(8,128)(2,1)}, u32[]{:S(2)}, u32[]{:S(2)}) collective-permute-start(bf16[1,2048,128]{2,1,0:T(8,128)(2,1)} %copy-done.21), channel_id=1, source_target_pairs={{1,2},{2,3},{5,6},{6,7},{9,10},{10,11},{13,14},{14,15},{17,18},{18... | collective-permute-start | bytes 1572872 | tf_op jit(solution)/shard_map/ppermute | solution.py:386
  34.9 2.6 %pad_maximum_fusion = bf16[4,2048,128]{2,1,0:T(8,128)(2,1)} fusion(bf16[1,2048,128]{2,1,0:T(8,128)(2,1)S(1)} %select_select_fusion.2.r_4_, bf16[1,2048,128]{2,1,0:T(8,128)(2,1)} %collective-permute-done.4.r_11_, bf16[1,2048,128]{2,1,0:T(8,128)(2,1)S(1)} %collective-permute-done.2.r_7_, bf16[1,2048,128]{2,1,0:T(8,128)(2,1)S(1)} %bitcast.19), kind=kLoop, calls=%fused_computation.1 | loop fusion | flops 3145728 | bytes 4194304 | tf_op jit(solution)/shard_map/concatenate | solution.py:358
  37.5 3.3 %collective-permute-done.7.r_8_ = bf16[1,2048,128]{2,1,0:T(8,128)(2,1)S(1)} collective-permute-done((bf16[1,2048,128]{2,1,0:T(8,128)(2,1)S(1)}, bf16[1,2048,128]{2,1,0:T(8,128)(2,1)S(1)}, u32[]{:S(2)}, u32[]{:S(2)}) %collective-permute-start.7) | collective-permute-done | bytes 524320 | tf_op jit(solution)/shard_map/ppermute | solution.py:354
  40.8 4.7 %collective-permute-done.9 = bf16[1,2048,128]{2,1,0:T(8,128)(2,1)} collective-permute-done((bf16[1,2048,128]{2,1,0:T(8,128)(2,1)}, bf16[1,2048,128]{2,1,0:T(8,128)(2,1)}, u32[]{:S(2)}, u32[]{:S(2)}) %collective-permute-start.9) | collective-permute-done | bytes 524320 | tf_op jit(solution)/shard_map/ppermute | solution.py:386
  45.5 2.2 %collective-permute-start.10 = (bf16[1,2048,128]{2,1,0:T(8,128)(2,1)}, bf16[1,2048,128]{2,1,0:T(8,128)(2,1)S(1)}, u32[]{:S(2)}, u32[]{:S(2)}) collective-permute-start(bf16[1,2048,128]{2,1,0:T(8,128)(2,1)} %collective-permute-done.9), channel_id=1, source_target_pairs={{2,3},{6,7},{10,11},{14,15},{18,19},{22,23},{26,27},{30,31}} | collective-permute-start | bytes 1572872 | tf_op jit(solution)/shard_map/ppermute | solution.py:386
  55.0 2.9 %collective-permute-done.10 = bf16[1,2048,128]{2,1,0:T(8,128)(2,1)S(1)} collective-permute-done((bf16[1,2048,128]{2,1,0:T(8,128)(2,1)}, bf16[1,2048,128]{2,1,0:T(8,128)(2,1)S(1)}, u32[]{:S(2)}, u32[]{:S(2)}) %collective-permute-start.10) | collective-permute-done | bytes 524320 | tf_op jit(solution)/shard_map/ppermute | solution.py:386
  57.9 2.1 %collective-permute-start.14 = (bf16[1,2048,128]{2,1,0:T(8,128)(2,1)S(1)}, bf16[1,2048,128]{2,1,0:T(8,128)(2,1)}, u32[]{:S(2)}, u32[]{:S(2)}) collective-permute-start(bf16[1,2048,128]{2,1,0:T(8,128)(2,1)S(1)} %collective-permute-done.7.r_8_), channel_id=1, source_target_pairs={{28,12},{0,16},{24,8},{4,20},{29,13},{1,17},{25,9},{5,21},{30,14},... | collective-permute-start | bytes 1572872 | tf_op jit(solution)/shard_map/ppermute | solution.py:354
  60.0 2.2 %collective-permute-start.17 = (bf16[4,2048,128]{2,1,0:T(8,128)(2,1)}, bf16[4,2048,128]{2,1,0:T(8,128)(2,1)}, u32[]{:S(2)}, u32[]{:S(2)}) collective-permute-start(bf16[4,2048,128]{2,1,0:T(8,128)(2,1)} %pad_maximum_fusion), channel_id=1, source_target_pairs={{0,4},{4,0},{8,12},{12,8},{16,20},{20,16},{24,28},{28,24},{1,5},{5... | collective-permute-start | bytes 6291464 | tf_op jit(solution)/shard_map/ppermute | solution.py:354
  64.1 2.3 %collective-permute-done.15.r_9_ = bf16[1,2048,128]{2,1,0:T(8,128)(2,1)} collective-permute-done((bf16[1,2048,128]{2,1,0:T(8,128)(2,1)S(1)}, bf16[1,2048,128]{2,1,0:T(8,128)(2,1)}, u32[]{:S(2)}, u32[]{:S(2)}) %collective-permute-start.15) | collective-permute-done | bytes 524320 | tf_op jit(solution)/shard_map/ppermute | solution.py:354
  66.4 3.5 %collective-permute-start.12 = (bf16[1,2048,128]{2,1,0:T(8,128)(2,1)S(1)}, bf16[1,2048,128]{2,1,0:T(8,128)(2,1)}, u32[]{:S(2)}, u32[]{:S(2)}) collective-permute-start(bf16[1,2048,128]{2,1,0:T(8,128)(2,1)S(1)} %select_select_fusion.1.r_6_), channel_id=1, source_target_pairs={{16,0},{4,20},{24,8},{12,28},{17,1},{5,21},{25,9},{13,29},{18,2},{... | collective-permute-start | bytes 1572872 | tf_op jit(solution)/shard_map/ppermute | solution.py:354
  70.1 4.0 %left.1.r_1_ = bf16[32,512,256]{2,1,0:T(8,128)(2,1)S(1)} custom-call(s32[1]{0:T(128)} %bitcast.5.r_0_, bf16[2048,128]{1,0:T(8,128)(2,1)S(1)} %spectra.1, bf16[2048,128]{1,0:T(8,128)(2,1)S(1)} %bitcast.14, bf16[2048,128]{1,0:T(8,128)(2,1)S(1)} %bitcast.22, bf16[2048,128]{1,0:T(8,128)(2,1)S(1)} %bitcast.23), custom_call_target="tpu_custom_call" | custom-call | tf_op jit(solution)/shard_map/left/pallas_call | solution.py:176
  74.2 3.3 %copy-done = bf16[32,512,256]{2,1,0:T(8,128)(2,1)} copy-done((bf16[32,512,256]{2,1,0:T(8,128)(2,1)}, bf16[32,512,256]{2,1,0:T(8,128)(2,1)S(1)}, u32[]{:S(2)}) %copy-start) | copy-done | bytes 8388632
  80.5 2.1 %collective-permute-done.23.r_24_ = bf16[1,2048,128]{2,1,0:T(8,128)(2,1)S(1)} collective-permute-done((bf16[1,2048,128]{2,1,0:T(8,128)(2,1)}, bf16[1,2048,128]{2,1,0:T(8,128)(2,1)S(1)}, u32[]{:S(2)}, u32[]{:S(2)}) %collective-permute-start.23) | collective-permute-done | bytes 524320 | tf_op jit(solution)/shard_map/ppermute | solution.py:354
  90.7 5.3 %collective-permute-start.32 = (bf16[1,2048,128]{2,1,0:T(8,128)(2,1)}, bf16[1,2048,128]{2,1,0:T(8,128)(2,1)}, u32[]{:S(2)}, u32[]{:S(2)}) collective-permute-start(bf16[1,2048,128]{2,1,0:T(8,128)(2,1)} %collective-permute-done.14.r_17_), channel_id=1, source_target_pairs={{0,4},{4,0},{8,12},{12,8},{16,20},{20,16},{24,28},{28,24},{1,5},{5... | collective-permute-start | bytes 1572872 | tf_op jit(solution)/shard_map/ppermute | solution.py:354
  96.0 8.9 %pairs.2.r_37_ = f32[32,3,128,128]{3,2,1,0:T(8,128)} custom-call(s32[5]{0:T(128)} %slice_bitcast_fusion.r_0_, bf16[32,512,256]{2,1,0:T(8,128)(2,1)} %copy-done, bf16[128,512]{1,0:T(8,128)(2,1)} %copy.18.r_2_, bf16[1,2048,128]{2,1,0:T(8,128)(2,1)} %bitcast.20, bf16[1,2048,128]{2,1,0:T(8,128)(2,1)} %copy-done.1, bf16[1,2048,128]{2,1,0:T(8,128)(2,1)} %copy-done.3, ...), custom_call_target="tpu_custom_call" | custom-call | flops 1610612736 | bytes 12582912 | tf_op jit(solution)/shard_map/pairs/pallas_call | solution.py:309
  110.3 10.2 %pairs.3 = f32[32,3,128,128]{3,2,1,0:T(8,128)} custom-call(s32[10]{0:T(128)} %reshape.184.r_0_, bf16[32,512,256]{2,1,0:T(8,128)(2,1)} %copy-done, bf16[128,512]{1,0:T(8,128)(2,1)} %copy.18.r_2_, bf16[1,2048,128]{2,1,0:T(8,128)(2,1)} %bitcast.21, bf16[1,2048,128]{2,1,0:T(8,128)(2,1)} %copy-done.1, ...), custom_call_target="tpu_custom_call", output_to_operand_aliasing={{}: (37, {})} | custom-call | flops 3221225472 | bytes 12582912 | tf_op jit(solution)/shard_map/pairs/pallas_call | solution.py:309
  (139 shorter events, 35.1 us)
Async XLA Ops:
  6.0 12.9 %collective-permute-start.2 = (bf16[1,2048,128]{2,1,0:T(8,128)(2,1)S(1)}, bf16[1,2048,128]{2,1,0:T(8,128)(2,1)S(1)}, u32[]{:S(2)}, u32[]{:S(2)}) collective-permute-start(bf16[1,2048,128]{2,1,0:T(8,128)(2,1)S(1)} %bitcast.15), channel_id=1, source_target_pairs={{0,8},{4,12},{8,0},{12,4},{16,24},{20,28},{24,16},{28,20},{1,9},{5... | collective-permute-start | bytes 1572872 | tf_op jit(solution)/shard_map/ppermute | solution.py:354
  7.2 14.5 %collective-permute-start.1 = (bf16[1,2048,128]{2,1,0:T(8,128)(2,1)S(1)}, bf16[1,2048,128]{2,1,0:T(8,128)(2,1)S(1)}, u32[]{:S(2)}, u32[]{:S(2)}) collective-permute-start(bf16[1,2048,128]{2,1,0:T(8,128)(2,1)S(1)} %bitcast.16), channel_id=1, source_target_pairs={{3,2},{2,1},{1,0},{7,6},{6,5},{5,4},{11,10},{10,9},{9,8},{15,14},{... | collective-permute-start | bytes 1572872 | tf_op jit(solution)/shard_map/ppermute | solution.py:386
  9.3 14.2 %collective-permute-start = (bf16[1,2048,128]{2,1,0:T(8,128)(2,1)S(1)}, bf16[1,2048,128]{2,1,0:T(8,128)(2,1)S(1)}, u32[]{:S(2)}, u32[]{:S(2)}) collective-permute-start(bf16[1,2048,128]{2,1,0:T(8,128)(2,1)S(1)} %bitcast.17), channel_id=1, source_target_pairs={{0,1},{1,2},{2,3},{4,5},{5,6},{6,7},{8,9},{9,10},{10,11},{12,13},{... | collective-permute-start | bytes 1572872 | tf_op jit(solution)/shard_map/ppermute | solution.py:386
  12.5 19.9 %collective-permute-start.4 = (bf16[1,2048,128]{2,1,0:T(8,128)(2,1)S(1)}, bf16[1,2048,128]{2,1,0:T(8,128)(2,1)}, u32[]{:S(2)}, u32[]{:S(2)}) collective-permute-start(bf16[1,2048,128]{2,1,0:T(8,128)(2,1)S(1)} %bitcast.18), channel_id=1, source_target_pairs={{16,0},{4,20},{24,8},{12,28},{17,1},{5,21},{25,9},{13,29},{18,2},{... | collective-permute-start | bytes 1572872 | tf_op jit(solution)/shard_map/ppermute | solution.py:354
  27.4 13.4 %collective-permute-start.7 = (bf16[1,2048,128]{2,1,0:T(8,128)(2,1)S(1)}, bf16[1,2048,128]{2,1,0:T(8,128)(2,1)S(1)}, u32[]{:S(2)}, u32[]{:S(2)}) collective-permute-start(bf16[1,2048,128]{2,1,0:T(8,128)(2,1)S(1)} %select_select_fusion.2.r_4_), channel_id=1, source_target_pairs={{0,8},{4,12},{8,0},{12,4},{16,24},{20,28},{24,16},{28,20},{1,9},{5... | collective-permute-start | bytes 1572872 | tf_op jit(solution)/shard_map/ppermute | solution.py:354
  27.7 13.1 %collective-permute-start.6 = (bf16[1,2048,128]{2,1,0:T(8,128)(2,1)S(1)}, bf16[1,2048,128]{2,1,0:T(8,128)(2,1)}, u32[]{:S(2)}, u32[]{:S(2)}) collective-permute-start(bf16[1,2048,128]{2,1,0:T(8,128)(2,1)S(1)} %collective-permute-done.1), channel_id=1, source_target_pairs={{2,1},{1,0},{6,5},{5,4},{10,9},{9,8},{14,13},{13,12},{18,17},{17,1... | collective-permute-start | bytes 1572872 | tf_op jit(solution)/shard_map/ppermute | solution.py:386
  30.5 15.0 %collective-permute-start.9 = (bf16[1,2048,128]{2,1,0:T(8,128)(2,1)}, bf16[1,2048,128]{2,1,0:T(8,128)(2,1)}, u32[]{:S(2)}, u32[]{:S(2)}) collective-permute-start(bf16[1,2048,128]{2,1,0:T(8,128)(2,1)} %copy-done.21), channel_id=1, source_target_pairs={{1,2},{2,3},{5,6},{6,7},{9,10},{10,11},{13,14},{14,15},{17,18},{18... | collective-permute-start | bytes 1572872 | tf_op jit(solution)/shard_map/ppermute | solution.py:386
  32.5 20.1 %collective-permute-start.3 = (bf16[1,2048,128]{2,1,0:T(8,128)(2,1)S(1)}, bf16[1,2048,128]{2,1,0:T(8,128)(2,1)S(1)}, u32[]{:S(2)}, u32[]{:S(2)}) collective-permute-start(bf16[1,2048,128]{2,1,0:T(8,128)(2,1)S(1)} %collective-permute-done.2.r_7_), channel_id=1, source_target_pairs={{28,12},{0,16},{29,13},{1,17},{30,14},{2,18},{31,15},{3,19}} | collective-permute-start | bytes 1572872 | tf_op jit(solution)/shard_map/ppermute | solution.py:354
  33.4 17.9 %collective-permute-start.5 = (bf16[1,2048,128]{2,1,0:T(8,128)(2,1)}, bf16[1,2048,128]{2,1,0:T(8,128)(2,1)}, u32[]{:S(2)}, u32[]{:S(2)}) collective-permute-start(bf16[1,2048,128]{2,1,0:T(8,128)(2,1)} %collective-permute-done.4.r_11_), channel_id=1, source_target_pairs={{0,8},{28,20},{1,9},{29,21},{2,10},{30,22},{3,11},{31,23}} | collective-permute-start | bytes 1572872 | tf_op jit(solution)/shard_map/ppermute | solution.py:354
  45.5 12.4 %collective-permute-start.10 = (bf16[1,2048,128]{2,1,0:T(8,128)(2,1)}, bf16[1,2048,128]{2,1,0:T(8,128)(2,1)S(1)}, u32[]{:S(2)}, u32[]{:S(2)}) collective-permute-start(bf16[1,2048,128]{2,1,0:T(8,128)(2,1)} %collective-permute-done.9), channel_id=1, source_target_pairs={{2,3},{6,7},{10,11},{14,15},{18,19},{22,23},{26,27},{30,31}} | collective-permute-start | bytes 1572872 | tf_op jit(solution)/shard_map/ppermute | solution.py:386
  47.7 12.3 %collective-permute-start.11 = (bf16[1,2048,128]{2,1,0:T(8,128)(2,1)}, bf16[1,2048,128]{2,1,0:T(8,128)(2,1)S(1)}, u32[]{:S(2)}, u32[]{:S(2)}) collective-permute-start(bf16[1,2048,128]{2,1,0:T(8,128)(2,1)} %collective-permute-done.6), channel_id=1, source_target_pairs={{1,0},{5,4},{9,8},{13,12},{17,16},{21,20},{25,24},{29,28}} | collective-permute-start | bytes 1572872 | tf_op jit(solution)/shard_map/ppermute | solution.py:386
  49.6 13.9 %collective-permute-start.21 = (bf16[1,2048,128]{2,1,0:T(8,128)(2,1)S(1)}, bf16[1,2048,128]{2,1,0:T(8,128)(2,1)S(1)}, u32[]{:S(2)}, u32[]{:S(2)}) collective-permute-start(bf16[1,2048,128]{2,1,0:T(8,128)(2,1)S(1)} %select_select_fusion.r_5_), channel_id=1, source_target_pairs={{0,4},{4,0},{8,12},{12,8},{16,20},{20,16},{24,28},{28,24},{1,5},{5... | collective-permute-start | bytes 1572872 | tf_op jit(solution)/shard_map/ppermute | solution.py:354
  51.3 12.3 %collective-permute-start.16 = (bf16[1,2048,128]{2,1,0:T(8,128)(2,1)S(1)}, bf16[1,2048,128]{2,1,0:T(8,128)(2,1)S(1)}, u32[]{:S(2)}, u32[]{:S(2)}) collective-permute-start(bf16[1,2048,128]{2,1,0:T(8,128)(2,1)S(1)} %select_select_fusion.r_5_), channel_id=1, source_target_pairs={{16,0},{4,20},{24,8},{12,28},{17,1},{5,21},{25,9},{13,29},{18,2},{... | collective-permute-start | bytes 1572872 | tf_op jit(solution)/shard_map/ppermute | solution.py:354
  52.6 13.7 %collective-permute-start.15 = (bf16[1,2048,128]{2,1,0:T(8,128)(2,1)S(1)}, bf16[1,2048,128]{2,1,0:T(8,128)(2,1)}, u32[]{:S(2)}, u32[]{:S(2)}) collective-permute-start(bf16[1,2048,128]{2,1,0:T(8,128)(2,1)S(1)} %select_select_fusion.r_5_), channel_id=1, source_target_pairs={{0,8},{4,12},{8,0},{12,4},{16,24},{20,28},{24,16},{28,20},{1,9},{5... | collective-permute-start | bytes 1572872 | tf_op jit(solution)/shard_map/ppermute | solution.py:354
  57.9 19.6 %collective-permute-start.14 = (bf16[1,2048,128]{2,1,0:T(8,128)(2,1)S(1)}, bf16[1,2048,128]{2,1,0:T(8,128)(2,1)}, u32[]{:S(2)}, u32[]{:S(2)}) collective-permute-start(bf16[1,2048,128]{2,1,0:T(8,128)(2,1)S(1)} %collective-permute-done.7.r_8_), channel_id=1, source_target_pairs={{28,12},{0,16},{24,8},{4,20},{29,13},{1,17},{25,9},{5,21},{30,14},... | collective-permute-start | bytes 1572872 | tf_op jit(solution)/shard_map/ppermute | solution.py:354
  60.0 30.7 %collective-permute-start.17 = (bf16[4,2048,128]{2,1,0:T(8,128)(2,1)}, bf16[4,2048,128]{2,1,0:T(8,128)(2,1)}, u32[]{:S(2)}, u32[]{:S(2)}) collective-permute-start(bf16[4,2048,128]{2,1,0:T(8,128)(2,1)} %pad_maximum_fusion), channel_id=1, source_target_pairs={{0,4},{4,0},{8,12},{12,8},{16,20},{20,16},{24,28},{28,24},{1,5},{5... | collective-permute-start | bytes 6291464 | tf_op jit(solution)/shard_map/ppermute | solution.py:354
  63.5 14.0 %collective-permute-start.20 = (bf16[1,2048,128]{2,1,0:T(8,128)(2,1)S(1)}, bf16[1,2048,128]{2,1,0:T(8,128)(2,1)}, u32[]{:S(2)}, u32[]{:S(2)}) collective-permute-start(bf16[1,2048,128]{2,1,0:T(8,128)(2,1)S(1)} %select_select_fusion.1.r_6_), channel_id=1, source_target_pairs={{0,4},{4,0},{8,12},{12,8},{16,20},{20,16},{24,28},{28,24},{1,5},{5... | collective-permute-start | bytes 1572872 | tf_op jit(solution)/shard_map/ppermute | solution.py:354
  63.6 14.4 %collective-permute-start.13 = (bf16[1,2048,128]{2,1,0:T(8,128)(2,1)S(1)}, bf16[1,2048,128]{2,1,0:T(8,128)(2,1)}, u32[]{:S(2)}, u32[]{:S(2)}) collective-permute-start(bf16[1,2048,128]{2,1,0:T(8,128)(2,1)S(1)} %select_select_fusion.1.r_6_), channel_id=1, source_target_pairs={{0,8},{4,12},{8,0},{12,4},{16,24},{20,28},{24,16},{28,20},{1,9},{5... | collective-permute-start | bytes 1572872 | tf_op jit(solution)/shard_map/ppermute | solution.py:354
  66.4 12.0 %collective-permute-start.12 = (bf16[1,2048,128]{2,1,0:T(8,128)(2,1)S(1)}, bf16[1,2048,128]{2,1,0:T(8,128)(2,1)}, u32[]{:S(2)}, u32[]{:S(2)}) collective-permute-start(bf16[1,2048,128]{2,1,0:T(8,128)(2,1)S(1)} %select_select_fusion.1.r_6_), channel_id=1, source_target_pairs={{16,0},{4,20},{24,8},{12,28},{17,1},{5,21},{25,9},{13,29},{18,2},{... | collective-permute-start | bytes 1572872 | tf_op jit(solution)/shard_map/ppermute | solution.py:354
  83.4 21.6 %collective-permute-start.30 = (bf16[1,2048,128]{2,1,0:T(8,128)(2,1)}, bf16[1,2048,128]{2,1,0:T(8,128)(2,1)}, u32[]{:S(2)}, u32[]{:S(2)}) collective-permute-start(bf16[1,2048,128]{2,1,0:T(8,128)(2,1)} %collective-permute-done.15.r_9_), channel_id=1, source_target_pairs={{28,12},{0,16},{29,13},{1,17},{30,14},{2,18},{31,15},{3,19}} | collective-permute-start | bytes 1572872 | tf_op jit(solution)/shard_map/ppermute | solution.py:354
  84.9 20.1 %collective-permute-start.28 = (bf16[1,2048,128]{2,1,0:T(8,128)(2,1)}, bf16[1,2048,128]{2,1,0:T(8,128)(2,1)}, u32[]{:S(2)}, u32[]{:S(2)}) collective-permute-start(bf16[1,2048,128]{2,1,0:T(8,128)(2,1)} %copy-done.13), channel_id=1, source_target_pairs={{0,8},{28,20},{1,9},{29,21},{2,10},{30,22},{3,11},{31,23}} | collective-permute-start | bytes 1572872 | tf_op jit(solution)/shard_map/ppermute | solution.py:354
  86.4 18.6 %collective-permute-start.29 = (bf16[1,2048,128]{2,1,0:T(8,128)(2,1)}, bf16[1,2048,128]{2,1,0:T(8,128)(2,1)}, u32[]{:S(2)}, u32[]{:S(2)}) collective-permute-start(bf16[1,2048,128]{2,1,0:T(8,128)(2,1)} %collective-permute-done.13.r_10_), channel_id=1, source_target_pairs={{28,12},{0,16},{29,13},{1,17},{30,14},{2,18},{31,15},{3,19}} | collective-permute-start | bytes 1572872 | tf_op jit(solution)/shard_map/ppermute | solution.py:354
  87.9 17.1 %collective-permute-start.27 = (bf16[1,2048,128]{2,1,0:T(8,128)(2,1)}, bf16[1,2048,128]{2,1,0:T(8,128)(2,1)}, u32[]{:S(2)}, u32[]{:S(2)}) collective-permute-start(bf16[1,2048,128]{2,1,0:T(8,128)(2,1)} %collective-permute-done.12.r_14_), channel_id=1, source_target_pairs={{0,8},{28,20},{1,9},{29,21},{2,10},{30,22},{3,11},{31,23}} | collective-permute-start | bytes 1572872 | tf_op jit(solution)/shard_map/ppermute | solution.py:354
  90.7 16.0 %collective-permute-start.32 = (bf16[1,2048,128]{2,1,0:T(8,128)(2,1)}, bf16[1,2048,128]{2,1,0:T(8,128)(2,1)}, u32[]{:S(2)}, u32[]{:S(2)}) collective-permute-start(bf16[1,2048,128]{2,1,0:T(8,128)(2,1)} %collective-permute-done.14.r_17_), channel_id=1, source_target_pairs={{0,4},{4,0},{8,12},{12,8},{16,20},{20,16},{24,28},{28,24},{1,5},{5... | collective-permute-start | bytes 1572872 | tf_op jit(solution)/shard_map/ppermute | solution.py:354
  (44 other events, 475.1 us)

commit v11 on v10

--- a/solution.py
+++ b/solution.py
@@ -191,8 +191,8 @@
     )(z.reshape(1), *slabs)
 
 
-CHUNKS = 4
-GROUP_UNROLL = 8
+CHUNKS = 2
+GROUP_UNROLL = 16
 ROW_UNROLL = 16
 
 

time: 121 us -> 121 us (level)
  no operation moved by 1% of the time
where the time goes in v11:
time: 121 us
  starting transfers between devices  50.6 us (42%)
  Pallas kernels  26.6 us (22%)
  waiting for transfers between devices  25.3 us (21%)
  local copies, waits for them, and re-layouts  10.1 us (8%)
  other arithmetic  7.46 us (6%)
    ppermute x30, starting transfers between devices, hop(): lax.ppermute(self.value, 'chan', pairs)  37.6 us
    pallas_call x2, Pallas kernels, correlate(): pl.pallas_call(lambda *r: pairs_kernel(*r, arrays=arrays, norm=norm, alia...  19.1 us
    ppermute x30, waiting for transfers between devices, hop(): lax.ppermute(self.value, 'chan', pairs)  13.1 us
    ppermute x6, starting transfers between devices, along_z(): return lax.ppermute(value, 'freq', pairs)  13 us
    ppermute x6, waiting for transfers between devices, along_z(): return lax.ppermute(value, 'freq', pairs)  12.2 us
    unnamed x64, local copies, waits for them, and re-layouts  6.58 us
    pallas_call x1, Pallas kernels, make_left(): pl.pallas_call(lambda *r: left_kernel(*r, per_step=per_step), grid_spec=p...  4.04 us
    concatenate x2, other arithmetic, join(): jnp.concatenate([p.value for p in parts], 0)  3.68 us
  transfers between devices with their start and end apart: 36, of which 15 were waited for; matrix products, arithmetic and copies ran while one was open for 8% of the time, Pallas kernels for 11%

profile of v11, /device:TPU:17, one launch (start us, length us, event | category | flops | bytes accessed | tf_op | source)
XLA Modules:
  0.0 120.6 jit_solution(6758049661700208081)
XLA Ops:
  2.5 3.5 %spectra.1 = bf16[2048,128]{1,0:T(8,128)(2,1)S(1)} custom-call(bf16[128,4,2048]{2,1,0:T(4,128)(2,1)S(1)} %copy-done.5, s32[256,1]{1,0:T(8,128)S(1)} %copy.15.bins_ref), custom_call_target="tpu_custom_call" | custom-call | tf_op jit(solution)/shard_map/spectra/pallas_call | solution.py:125
  7.2 2.1 %collective-permute-start.1 = (bf16[1,2048,128]{2,1,0:T(8,128)(2,1)S(1)}, bf16[1,2048,128]{2,1,0:T(8,128)(2,1)S(1)}, u32[]{:S(2)}, u32[]{:S(2)}) collective-permute-start(bf16[1,2048,128]{2,1,0:T(8,128)(2,1)S(1)} %bitcast.16), channel_id=1, source_target_pairs={{3,2},{2,1},{1,0},{7,6},{6,5},{5,4},{11,10},{10,9},{9,8},{15,14},{... | collective-permute-start | bytes 1572872 | tf_op jit(solution)/shard_map/ppermute | solution.py:386
  9.3 3.2 %collective-permute-start = (bf16[1,2048,128]{2,1,0:T(8,128)(2,1)S(1)}, bf16[1,2048,128]{2,1,0:T(8,128)(2,1)S(1)}, u32[]{:S(2)}, u32[]{:S(2)}) collective-permute-start(bf16[1,2048,128]{2,1,0:T(8,128)(2,1)S(1)} %bitcast.17), channel_id=1, source_target_pairs={{0,1},{1,2},{2,3},{4,5},{5,6},{6,7},{8,9},{9,10},{10,11},{12,13},{... | collective-permute-start | bytes 1572872 | tf_op jit(solution)/shard_map/ppermute | solution.py:386
  12.5 4.0 %collective-permute-start.4 = (bf16[1,2048,128]{2,1,0:T(8,128)(2,1)S(1)}, bf16[1,2048,128]{2,1,0:T(8,128)(2,1)}, u32[]{:S(2)}, u32[]{:S(2)}) collective-permute-start(bf16[1,2048,128]{2,1,0:T(8,128)(2,1)S(1)} %bitcast.18), channel_id=1, source_target_pairs={{16,0},{4,20},{24,8},{12,28},{17,1},{5,21},{25,9},{13,29},{18,2},{... | collective-permute-start | bytes 1572872 | tf_op jit(solution)/shard_map/ppermute | solution.py:354
  18.8 2.9 %collective-permute-done.1 = bf16[1,2048,128]{2,1,0:T(8,128)(2,1)S(1)} collective-permute-done((bf16[1,2048,128]{2,1,0:T(8,128)(2,1)S(1)}, bf16[1,2048,128]{2,1,0:T(8,128)(2,1)S(1)}, u32[]{:S(2)}, u32[]{:S(2)}) %collective-permute-start.1) | collective-permute-done | bytes 524320 | tf_op jit(solution)/shard_map/ppermute | solution.py:386
  21.7 1.8 %collective-permute-done = bf16[1,2048,128]{2,1,0:T(8,128)(2,1)S(1)} collective-permute-done((bf16[1,2048,128]{2,1,0:T(8,128)(2,1)S(1)}, bf16[1,2048,128]{2,1,0:T(8,128)(2,1)S(1)}, u32[]{:S(2)}, u32[]{:S(2)}) %collective-permute-start) | collective-permute-done | bytes 524320 | tf_op jit(solution)/shard_map/ppermute | solution.py:386
  24.3 3.1 %collective-permute-start.8 = (bf16[1,2048,128]{2,1,0:T(8,128)(2,1)S(1)}, bf16[1,2048,128]{2,1,0:T(8,128)(2,1)S(1)}, u32[]{:S(2)}, u32[]{:S(2)}) collective-permute-start(bf16[1,2048,128]{2,1,0:T(8,128)(2,1)S(1)} %select_select_fusion.2.r_4_), channel_id=1, source_target_pairs={{16,0},{4,20},{24,8},{12,28},{17,1},{5,21},{25,9},{13,29},{18,2},{... | collective-permute-start | bytes 1572872 | tf_op jit(solution)/shard_map/ppermute | solution.py:354
  27.7 2.9 %collective-permute-start.6 = (bf16[1,2048,128]{2,1,0:T(8,128)(2,1)S(1)}, bf16[1,2048,128]{2,1,0:T(8,128)(2,1)}, u32[]{:S(2)}, u32[]{:S(2)}) collective-permute-start(bf16[1,2048,128]{2,1,0:T(8,128)(2,1)S(1)} %collective-permute-done.1), channel_id=1, source_target_pairs={{2,1},{1,0},{6,5},{5,4},{10,9},{9,8},{14,13},{13,12},{18,17},{17,1... | collective-permute-start | bytes 1572872 | tf_op jit(solution)/shard_map/ppermute | solution.py:386
  30.5 1.9 %collective-permute-start.9 = (bf16[1,2048,128]{2,1,0:T(8,128)(2,1)}, bf16[1,2048,128]{2,1,0:T(8,128)(2,1)}, u32[]{:S(2)}, u32[]{:S(2)}) collective-permute-start(bf16[1,2048,128]{2,1,0:T(8,128)(2,1)} %copy-done.21), channel_id=1, source_target_pairs={{1,2},{2,3},{5,6},{6,7},{9,10},{10,11},{13,14},{14,15},{17,18},{18... | collective-permute-start | bytes 1572872 | tf_op jit(solution)/shard_map/ppermute | solution.py:386
  34.9 2.6 %pad_maximum_fusion = bf16[4,2048,128]{2,1,0:T(8,128)(2,1)} fusion(bf16[1,2048,128]{2,1,0:T(8,128)(2,1)S(1)} %select_select_fusion.2.r_4_, bf16[1,2048,128]{2,1,0:T(8,128)(2,1)} %collective-permute-done.4.r_11_, bf16[1,2048,128]{2,1,0:T(8,128)(2,1)S(1)} %collective-permute-done.2.r_7_, bf16[1,2048,128]{2,1,0:T(8,128)(2,1)S(1)} %bitcast.19), kind=kLoop, calls=%fused_computation.1 | loop fusion | flops 3145728 | bytes 4194304 | tf_op jit(solution)/shard_map/concatenate | solution.py:358
  37.5 3.3 %collective-permute-done.7.r_8_ = bf16[1,2048,128]{2,1,0:T(8,128)(2,1)S(1)} collective-permute-done((bf16[1,2048,128]{2,1,0:T(8,128)(2,1)S(1)}, bf16[1,2048,128]{2,1,0:T(8,128)(2,1)S(1)}, u32[]{:S(2)}, u32[]{:S(2)}) %collective-permute-start.7) | collective-permute-done | bytes 524320 | tf_op jit(solution)/shard_map/ppermute | solution.py:354
  40.8 4.7 %collective-permute-done.9 = bf16[1,2048,128]{2,1,0:T(8,128)(2,1)} collective-permute-done((bf16[1,2048,128]{2,1,0:T(8,128)(2,1)}, bf16[1,2048,128]{2,1,0:T(8,128)(2,1)}, u32[]{:S(2)}, u32[]{:S(2)}) %collective-permute-start.9) | collective-permute-done | bytes 524320 | tf_op jit(solution)/shard_map/ppermute | solution.py:386
  45.5 2.2 %collective-permute-start.10 = (bf16[1,2048,128]{2,1,0:T(8,128)(2,1)}, bf16[1,2048,128]{2,1,0:T(8,128)(2,1)S(1)}, u32[]{:S(2)}, u32[]{:S(2)}) collective-permute-start(bf16[1,2048,128]{2,1,0:T(8,128)(2,1)} %collective-permute-done.9), channel_id=1, source_target_pairs={{2,3},{6,7},{10,11},{14,15},{18,19},{22,23},{26,27},{30,31}} | collective-permute-start | bytes 1572872 | tf_op jit(solution)/shard_map/ppermute | solution.py:386
  55.0 2.9 %collective-permute-done.10 = bf16[1,2048,128]{2,1,0:T(8,128)(2,1)S(1)} collective-permute-done((bf16[1,2048,128]{2,1,0:T(8,128)(2,1)}, bf16[1,2048,128]{2,1,0:T(8,128)(2,1)S(1)}, u32[]{:S(2)}, u32[]{:S(2)}) %collective-permute-start.10) | collective-permute-done | bytes 524320 | tf_op jit(solution)/shard_map/ppermute | solution.py:386
  57.9 2.1 %collective-permute-start.14 = (bf16[1,2048,128]{2,1,0:T(8,128)(2,1)S(1)}, bf16[1,2048,128]{2,1,0:T(8,128)(2,1)}, u32[]{:S(2)}, u32[]{:S(2)}) collective-permute-start(bf16[1,2048,128]{2,1,0:T(8,128)(2,1)S(1)} %collective-permute-done.7.r_8_), channel_id=1, source_target_pairs={{28,12},{0,16},{24,8},{4,20},{29,13},{1,17},{25,9},{5,21},{30,14},... | collective-permute-start | bytes 1572872 | tf_op jit(solution)/shard_map/ppermute | solution.py:354
  60.0 2.2 %collective-permute-start.17 = (bf16[4,2048,128]{2,1,0:T(8,128)(2,1)}, bf16[4,2048,128]{2,1,0:T(8,128)(2,1)}, u32[]{:S(2)}, u32[]{:S(2)}) collective-permute-start(bf16[4,2048,128]{2,1,0:T(8,128)(2,1)} %pad_maximum_fusion), channel_id=1, source_target_pairs={{0,4},{4,0},{8,12},{12,8},{16,20},{20,16},{24,28},{28,24},{1,5},{5... | collective-permute-start | bytes 6291464 | tf_op jit(solution)/shard_map/ppermute | solution.py:354
  64.1 2.3 %collective-permute-done.15.r_9_ = bf16[1,2048,128]{2,1,0:T(8,128)(2,1)} collective-permute-done((bf16[1,2048,128]{2,1,0:T(8,128)(2,1)S(1)}, bf16[1,2048,128]{2,1,0:T(8,128)(2,1)}, u32[]{:S(2)}, u32[]{:S(2)}) %collective-permute-start.15) | collective-permute-done | bytes 524320 | tf_op jit(solution)/shard_map/ppermute | solution.py:354
  66.4 3.5 %collective-permute-start.12 = (bf16[1,2048,128]{2,1,0:T(8,128)(2,1)S(1)}, bf16[1,2048,128]{2,1,0:T(8,128)(2,1)}, u32[]{:S(2)}, u32[]{:S(2)}) collective-permute-start(bf16[1,2048,128]{2,1,0:T(8,128)(2,1)S(1)} %select_select_fusion.1.r_6_), channel_id=1, source_target_pairs={{16,0},{4,20},{24,8},{12,28},{17,1},{5,21},{25,9},{13,29},{18,2},{... | collective-permute-start | bytes 1572872 | tf_op jit(solution)/shard_map/ppermute | solution.py:354
  70.1 4.0 %left.1.r_1_ = bf16[32,512,256]{2,1,0:T(8,128)(2,1)S(1)} custom-call(s32[1]{0:T(128)} %bitcast.5.r_0_, bf16[2048,128]{1,0:T(8,128)(2,1)S(1)} %spectra.1, bf16[2048,128]{1,0:T(8,128)(2,1)S(1)} %bitcast.14, bf16[2048,128]{1,0:T(8,128)(2,1)S(1)} %bitcast.22, bf16[2048,128]{1,0:T(8,128)(2,1)S(1)} %bitcast.23), custom_call_target="tpu_custom_call" | custom-call | tf_op jit(solution)/shard_map/left/pallas_call | solution.py:176
  74.2 3.3 %copy-done = bf16[32,512,256]{2,1,0:T(8,128)(2,1)} copy-done((bf16[32,512,256]{2,1,0:T(8,128)(2,1)}, bf16[32,512,256]{2,1,0:T(8,128)(2,1)S(1)}, u32[]{:S(2)}) %copy-start) | copy-done | bytes 8388632
  80.5 2.1 %collective-permute-done.23.r_24_ = bf16[1,2048,128]{2,1,0:T(8,128)(2,1)S(1)} collective-permute-done((bf16[1,2048,128]{2,1,0:T(8,128)(2,1)}, bf16[1,2048,128]{2,1,0:T(8,128)(2,1)S(1)}, u32[]{:S(2)}, u32[]{:S(2)}) %collective-permute-start.23) | collective-permute-done | bytes 524320 | tf_op jit(solution)/shard_map/ppermute | solution.py:354
  90.7 5.3 %collective-permute-start.32 = (bf16[1,2048,128]{2,1,0:T(8,128)(2,1)}, bf16[1,2048,128]{2,1,0:T(8,128)(2,1)}, u32[]{:S(2)}, u32[]{:S(2)}) collective-permute-start(bf16[1,2048,128]{2,1,0:T(8,128)(2,1)} %collective-permute-done.14.r_17_), channel_id=1, source_target_pairs={{0,4},{4,0},{8,12},{12,8},{16,20},{20,16},{24,28},{28,24},{1,5},{5... | collective-permute-start | bytes 1572872 | tf_op jit(solution)/shard_map/ppermute | solution.py:354
  96.0 8.9 %pairs.2.r_37_ = f32[32,3,128,128]{3,2,1,0:T(8,128)} custom-call(s32[5]{0:T(128)} %slice_bitcast_fusion.r_0_, bf16[32,512,256]{2,1,0:T(8,128)(2,1)} %copy-done, bf16[128,512]{1,0:T(8,128)(2,1)} %copy.18.r_2_, bf16[1,2048,128]{2,1,0:T(8,128)(2,1)} %bitcast.20, bf16[1,2048,128]{2,1,0:T(8,128)(2,1)} %copy-done.1, bf16[1,2048,128]{2,1,0:T(8,128)(2,1)} %copy-done.3, ...), custom_call_target="tpu_custom_call" | custom-call | flops 1610612736 | bytes 12582912 | tf_op jit(solution)/shard_map/pairs/pallas_call | solution.py:309
  110.3 10.2 %pairs.3 = f32[32,3,128,128]{3,2,1,0:T(8,128)} custom-call(s32[10]{0:T(128)} %reshape.184.r_0_, bf16[32,512,256]{2,1,0:T(8,128)(2,1)} %copy-done, bf16[128,512]{1,0:T(8,128)(2,1)} %copy.18.r_2_, bf16[1,2048,128]{2,1,0:T(8,128)(2,1)} %bitcast.21, bf16[1,2048,128]{2,1,0:T(8,128)(2,1)} %copy-done.1, ...), custom_call_target="tpu_custom_call", output_to_operand_aliasing={{}: (37, {})} | custom-call | flops 3221225472 | bytes 12582912 | tf_op jit(solution)/shard_map/pairs/pallas_call | solution.py:309
  (139 shorter events, 35.1 us)
Async XLA Ops:
  6.0 12.9 %collective-permute-start.2 = (bf16[1,2048,128]{2,1,0:T(8,128)(2,1)S(1)}, bf16[1,2048,128]{2,1,0:T(8,128)(2,1)S(1)}, u32[]{:S(2)}, u32[]{:S(2)}) collective-permute-start(bf16[1,2048,128]{2,1,0:T(8,128)(2,1)S(1)} %bitcast.15), channel_id=1, source_target_pairs={{0,8},{4,12},{8,0},{12,4},{16,24},{20,28},{24,16},{28,20},{1,9},{5... | collective-permute-start | bytes 1572872 | tf_op jit(solution)/shard_map/ppermute | solution.py:354
  7.2 14.5 %collective-permute-start.1 = (bf16[1,2048,128]{2,1,0:T(8,128)(2,1)S(1)}, bf16[1,2048,128]{2,1,0:T(8,128)(2,1)S(1)}, u32[]{:S(2)}, u32[]{:S(2)}) collective-permute-start(bf16[1,2048,128]{2,1,0:T(8,128)(2,1)S(1)} %bitcast.16), channel_id=1, source_target_pairs={{3,2},{2,1},{1,0},{7,6},{6,5},{5,4},{11,10},{10,9},{9,8},{15,14},{... | collective-permute-start | bytes 1572872 | tf_op jit(solution)/shard_map/ppermute | solution.py:386
  9.3 14.2 %collective-permute-start = (bf16[1,2048,128]{2,1,0:T(8,128)(2,1)S(1)}, bf16[1,2048,128]{2,1,0:T(8,128)(2,1)S(1)}, u32[]{:S(2)}, u32[]{:S(2)}) collective-permute-start(bf16[1,2048,128]{2,1,0:T(8,128)(2,1)S(1)} %bitcast.17), channel_id=1, source_target_pairs={{0,1},{1,2},{2,3},{4,5},{5,6},{6,7},{8,9},{9,10},{10,11},{12,13},{... | collective-permute-start | bytes 1572872 | tf_op jit(solution)/shard_map/ppermute | solution.py:386
  12.5 19.9 %collective-permute-start.4 = (bf16[1,2048,128]{2,1,0:T(8,128)(2,1)S(1)}, bf16[1,2048,128]{2,1,0:T(8,128)(2,1)}, u32[]{:S(2)}, u32[]{:S(2)}) collective-permute-start(bf16[1,2048,128]{2,1,0:T(8,128)(2,1)S(1)} %bitcast.18), channel_id=1, source_target_pairs={{16,0},{4,20},{24,8},{12,28},{17,1},{5,21},{25,9},{13,29},{18,2},{... | collective-permute-start | bytes 1572872 | tf_op jit(solution)/shard_map/ppermute | solution.py:354
  27.4 13.4 %collective-permute-start.7 = (bf16[1,2048,128]{2,1,0:T(8,128)(2,1)S(1)}, bf16[1,2048,128]{2,1,0:T(8,128)(2,1)S(1)}, u32[]{:S(2)}, u32[]{:S(2)}) collective-permute-start(bf16[1,2048,128]{2,1,0:T(8,128)(2,1)S(1)} %select_select_fusion.2.r_4_), channel_id=1, source_target_pairs={{0,8},{4,12},{8,0},{12,4},{16,24},{20,28},{24,16},{28,20},{1,9},{5... | collective-permute-start | bytes 1572872 | tf_op jit(solution)/shard_map/ppermute | solution.py:354
  27.7 13.1 %collective-permute-start.6 = (bf16[1,2048,128]{2,1,0:T(8,128)(2,1)S(1)}, bf16[1,2048,128]{2,1,0:T(8,128)(2,1)}, u32[]{:S(2)}, u32[]{:S(2)}) collective-permute-start(bf16[1,2048,128]{2,1,0:T(8,128)(2,1)S(1)} %collective-permute-done.1), channel_id=1, source_target_pairs={{2,1},{1,0},{6,5},{5,4},{10,9},{9,8},{14,13},{13,12},{18,17},{17,1... | collective-permute-start | bytes 1572872 | tf_op jit(solution)/shard_map/ppermute | solution.py:386
  30.5 15.0 %collective-permute-start.9 = (bf16[1,2048,128]{2,1,0:T(8,128)(2,1)}, bf16[1,2048,128]{2,1,0:T(8,128)(2,1)}, u32[]{:S(2)}, u32[]{:S(2)}) collective-permute-start(bf16[1,2048,128]{2,1,0:T(8,128)(2,1)} %copy-done.21), channel_id=1, source_target_pairs={{1,2},{2,3},{5,6},{6,7},{9,10},{10,11},{13,14},{14,15},{17,18},{18... | collective-permute-start | bytes 1572872 | tf_op jit(solution)/shard_map/ppermute | solution.py:386
  32.5 20.1 %collective-permute-start.3 = (bf16[1,2048,128]{2,1,0:T(8,128)(2,1)S(1)}, bf16[1,2048,128]{2,1,0:T(8,128)(2,1)S(1)}, u32[]{:S(2)}, u32[]{:S(2)}) collective-permute-start(bf16[1,2048,128]{2,1,0:T(8,128)(2,1)S(1)} %collective-permute-done.2.r_7_), channel_id=1, source_target_pairs={{28,12},{0,16},{29,13},{1,17},{30,14},{2,18},{31,15},{3,19}} | collective-permute-start | bytes 1572872 | tf_op jit(solution)/shard_map/ppermute | solution.py:354
  33.4 17.9 %collective-permute-start.5 = (bf16[1,2048,128]{2,1,0:T(8,128)(2,1)}, bf16[1,2048,128]{2,1,0:T(8,128)(2,1)}, u32[]{:S(2)}, u32[]{:S(2)}) collective-permute-start(bf16[1,2048,128]{2,1,0:T(8,128)(2,1)} %collective-permute-done.4.r_11_), channel_id=1, source_target_pairs={{0,8},{28,20},{1,9},{29,21},{2,10},{30,22},{3,11},{31,23}} | collective-permute-start | bytes 1572872 | tf_op jit(solution)/shard_map/ppermute | solution.py:354
  45.5 12.4 %collective-permute-start.10 = (bf16[1,2048,128]{2,1,0:T(8,128)(2,1)}, bf16[1,2048,128]{2,1,0:T(8,128)(2,1)S(1)}, u32[]{:S(2)}, u32[]{:S(2)}) collective-permute-start(bf16[1,2048,128]{2,1,0:T(8,128)(2,1)} %collective-permute-done.9), channel_id=1, source_target_pairs={{2,3},{6,7},{10,11},{14,15},{18,19},{22,23},{26,27},{30,31}} | collective-permute-start | bytes 1572872 | tf_op jit(solution)/shard_map/ppermute | solution.py:386
  47.7 12.3 %collective-permute-start.11 = (bf16[1,2048,128]{2,1,0:T(8,128)(2,1)}, bf16[1,2048,128]{2,1,0:T(8,128)(2,1)S(1)}, u32[]{:S(2)}, u32[]{:S(2)}) collective-permute-start(bf16[1,2048,128]{2,1,0:T(8,128)(2,1)} %collective-permute-done.6), channel_id=1, source_target_pairs={{1,0},{5,4},{9,8},{13,12},{17,16},{21,20},{25,24},{29,28}} | collective-permute-start | bytes 1572872 | tf_op jit(solution)/shard_map/ppermute | solution.py:386
  49.6 13.9 %collective-permute-start.21 = (bf16[1,2048,128]{2,1,0:T(8,128)(2,1)S(1)}, bf16[1,2048,128]{2,1,0:T(8,128)(2,1)S(1)}, u32[]{:S(2)}, u32[]{:S(2)}) collective-permute-start(bf16[1,2048,128]{2,1,0:T(8,128)(2,1)S(1)} %select_select_fusion.r_5_), channel_id=1, source_target_pairs={{0,4},{4,0},{8,12},{12,8},{16,20},{20,16},{24,28},{28,24},{1,5},{5... | collective-permute-start | bytes 1572872 | tf_op jit(solution)/shard_map/ppermute | solution.py:354
  51.3 12.3 %collective-permute-start.16 = (bf16[1,2048,128]{2,1,0:T(8,128)(2,1)S(1)}, bf16[1,2048,128]{2,1,0:T(8,128)(2,1)S(1)}, u32[]{:S(2)}, u32[]{:S(2)}) collective-permute-start(bf16[1,2048,128]{2,1,0:T(8,128)(2,1)S(1)} %select_select_fusion.r_5_), channel_id=1, source_target_pairs={{16,0},{4,20},{24,8},{12,28},{17,1},{5,21},{25,9},{13,29},{18,2},{... | collective-permute-start | bytes 1572872 | tf_op jit(solution)/shard_map/ppermute | solution.py:354
  52.6 13.7 %collective-permute-start.15 = (bf16[1,2048,128]{2,1,0:T(8,128)(2,1)S(1)}, bf16[1,2048,128]{2,1,0:T(8,128)(2,1)}, u32[]{:S(2)}, u32[]{:S(2)}) collective-permute-start(bf16[1,2048,128]{2,1,0:T(8,128)(2,1)S(1)} %select_select_fusion.r_5_), channel_id=1, source_target_pairs={{0,8},{4,12},{8,0},{12,4},{16,24},{20,28},{24,16},{28,20},{1,9},{5... | collective-permute-start | bytes 1572872 | tf_op jit(solution)/shard_map/ppermute | solution.py:354
  57.9 19.6 %collective-permute-start.14 = (bf16[1,2048,128]{2,1,0:T(8,128)(2,1)S(1)}, bf16[1,2048,128]{2,1,0:T(8,128)(2,1)}, u32[]{:S(2)}, u32[]{:S(2)}) collective-permute-start(bf16[1,2048,128]{2,1,0:T(8,128)(2,1)S(1)} %collective-permute-done.7.r_8_), channel_id=1, source_target_pairs={{28,12},{0,16},{24,8},{4,20},{29,13},{1,17},{25,9},{5,21},{30,14},... | collective-permute-start | bytes 1572872 | tf_op jit(solution)/shard_map/ppermute | solution.py:354
  60.0 30.7 %collective-permute-start.17 = (bf16[4,2048,128]{2,1,0:T(8,128)(2,1)}, bf16[4,2048,128]{2,1,0:T(8,128)(2,1)}, u32[]{:S(2)}, u32[]{:S(2)}) collective-permute-start(bf16[4,2048,128]{2,1,0:T(8,128)(2,1)} %pad_maximum_fusion), channel_id=1, source_target_pairs={{0,4},{4,0},{8,12},{12,8},{16,20},{20,16},{24,28},{28,24},{1,5},{5... | collective-permute-start | bytes 6291464 | tf_op jit(solution)/shard_map/ppermute | solution.py:354
  63.5 14.0 %collective-permute-start.20 = (bf16[1,2048,128]{2,1,0:T(8,128)(2,1)S(1)}, bf16[1,2048,128]{2,1,0:T(8,128)(2,1)}, u32[]{:S(2)}, u32[]{:S(2)}) collective-permute-start(bf16[1,2048,128]{2,1,0:T(8,128)(2,1)S(1)} %select_select_fusion.1.r_6_), channel_id=1, source_target_pairs={{0,4},{4,0},{8,12},{12,8},{16,20},{20,16},{24,28},{28,24},{1,5},{5... | collective-permute-start | bytes 1572872 | tf_op jit(solution)/shard_map/ppermute | solution.py:354
  63.6 14.4 %collective-permute-start.13 = (bf16[1,2048,128]{2,1,0:T(8,128)(2,1)S(1)}, bf16[1,2048,128]{2,1,0:T(8,128)(2,1)}, u32[]{:S(2)}, u32[]{:S(2)}) collective-permute-start(bf16[1,2048,128]{2,1,0:T(8,128)(2,1)S(1)} %select_select_fusion.1.r_6_), channel_id=1, source_target_pairs={{0,8},{4,12},{8,0},{12,4},{16,24},{20,28},{24,16},{28,20},{1,9},{5... | collective-permute-start | bytes 1572872 | tf_op jit(solution)/shard_map/ppermute | solution.py:354
  66.4 12.0 %collective-permute-start.12 = (bf16[1,2048,128]{2,1,0:T(8,128)(2,1)S(1)}, bf16[1,2048,128]{2,1,0:T(8,128)(2,1)}, u32[]{:S(2)}, u32[]{:S(2)}) collective-permute-start(bf16[1,2048,128]{2,1,0:T(8,128)(2,1)S(1)} %select_select_fusion.1.r_6_), channel_id=1, source_target_pairs={{16,0},{4,20},{24,8},{12,28},{17,1},{5,21},{25,9},{13,29},{18,2},{... | collective-permute-start | bytes 1572872 | tf_op jit(solution)/shard_map/ppermute | solution.py:354
  83.4 21.6 %collective-permute-start.30 = (bf16[1,2048,128]{2,1,0:T(8,128)(2,1)}, bf16[1,2048,128]{2,1,0:T(8,128)(2,1)}, u32[]{:S(2)}, u32[]{:S(2)}) collective-permute-start(bf16[1,2048,128]{2,1,0:T(8,128)(2,1)} %collective-permute-done.15.r_9_), channel_id=1, source_target_pairs={{28,12},{0,16},{29,13},{1,17},{30,14},{2,18},{31,15},{3,19}} | collective-permute-start | bytes 1572872 | tf_op jit(solution)/shard_map/ppermute | solution.py:354
  84.9 20.1 %collective-permute-start.28 = (bf16[1,2048,128]{2,1,0:T(8,128)(2,1)}, bf16[1,2048,128]{2,1,0:T(8,128)(2,1)}, u32[]{:S(2)}, u32[]{:S(2)}) collective-permute-start(bf16[1,2048,128]{2,1,0:T(8,128)(2,1)} %copy-done.13), channel_id=1, source_target_pairs={{0,8},{28,20},{1,9},{29,21},{2,10},{30,22},{3,11},{31,23}} | collective-permute-start | bytes 1572872 | tf_op jit(solution)/shard_map/ppermute | solution.py:354
  86.4 18.6 %collective-permute-start.29 = (bf16[1,2048,128]{2,1,0:T(8,128)(2,1)}, bf16[1,2048,128]{2,1,0:T(8,128)(2,1)}, u32[]{:S(2)}, u32[]{:S(2)}) collective-permute-start(bf16[1,2048,128]{2,1,0:T(8,128)(2,1)} %collective-permute-done.13.r_10_), channel_id=1, source_target_pairs={{28,12},{0,16},{29,13},{1,17},{30,14},{2,18},{31,15},{3,19}} | collective-permute-start | bytes 1572872 | tf_op jit(solution)/shard_map/ppermute | solution.py:354
  87.9 17.1 %collective-permute-start.27 = (bf16[1,2048,128]{2,1,0:T(8,128)(2,1)}, bf16[1,2048,128]{2,1,0:T(8,128)(2,1)}, u32[]{:S(2)}, u32[]{:S(2)}) collective-permute-start(bf16[1,2048,128]{2,1,0:T(8,128)(2,1)} %collective-permute-done.12.r_14_), channel_id=1, source_target_pairs={{0,8},{28,20},{1,9},{29,21},{2,10},{30,22},{3,11},{31,23}} | collective-permute-start | bytes 1572872 | tf_op jit(solution)/shard_map/ppermute | solution.py:354
  90.7 16.0 %collective-permute-start.32 = (bf16[1,2048,128]{2,1,0:T(8,128)(2,1)}, bf16[1,2048,128]{2,1,0:T(8,128)(2,1)}, u32[]{:S(2)}, u32[]{:S(2)}) collective-permute-start(bf16[1,2048,128]{2,1,0:T(8,128)(2,1)} %collective-permute-done.14.r_17_), channel_id=1, source_target_pairs={{0,4},{4,0},{8,12},{12,8},{16,20},{20,16},{24,28},{28,24},{1,5},{5... | collective-permute-start | bytes 1572872 | tf_op jit(solution)/shard_map/ppermute | solution.py:354
  (44 other events, 475.1 us)
